TPU v7x, 32 devices: a whole 2x2x4 slice. The times are simulated.
32 devices in a mesh: groups: 2 (over y), dp: 4 (over z), query: 4 (over x, core).
Axes of the slice: x: 2, y: 2, z: 4, core: 2. Of those that a mesh axis runs over, the one named last changes fastest.
Arguments:
- activations: bfloat16 [2048, 4096], P(('groups', 'dp'), 'query'), parts along dimension 0, may hold values from -6 to 6
- out_grads: bfloat16 [2048, 14336], P(('groups', 'dp'), 'query'), parts along dimension 0, may hold values from -6 to 6
- proj_in: bfloat16 [4096, 64], P('query'), may hold values from -0.09375 to 0.09375
- proj_out: bfloat16 [14336, 64], P('query')
- queries: bfloat16 [8192, 1024], P(('groups', 'dp'), 'query'), parts along dimension 0, may hold values from -2 to 2
- lengths: int32 [16], P(('groups', 'dp')), parts along dimension 0, may hold values from 32 to 128
- credit: int32 [16], P(('groups', 'dp')), parts along dimension 0, may hold values from 1 to 10
Outputs:
- hessian: float32 [8192, 4096], P(('groups', 'dp')), parts along dimension 0
- scores: bfloat16 [2048, 1024], P(('groups', 'dp'), 'query'), parts along dimension 0
There are 2 independent parts, one for each index of `groups`. A program takes and returns all parts, laid end to end along the dimension named above; an argument that names none is the same for every part. Nothing has to cross between parts.
All inputs are finite; a program needn't handle non-finite values.
Results may differ from a plain program's by a relative error of at most 0.008.
Values may be sent and summed in bfloat16 or wider, within the bound.
No kernel may reach another device: no remote copies, remote signals or barrier semaphores. Data moves between devices by JAX's collectives and lax.ppermute only.
A program may use at most 128 MiB of HBM per device.

v0:
```python
import jax
import jax.numpy as jnp
from jax import lax
from jax.sharding import PartitionSpec as P


def kron_columns(grad_rows, act_rows, start, count):
    rank = grad_rows.shape[1]
    tokens_here = grad_rows.shape[0]
    grad_cols = lax.dynamic_slice_in_dim(grad_rows, start // rank, count // rank, 1)
    outer = grad_cols.astype(jnp.float32)[:, :, None] * act_rows.astype(jnp.float32)[:, None, :]
    return outer.reshape(tokens_here, count).astype(jnp.bfloat16)


def hessian_block(total, pieces, row_start, rows_own, col_start, col_count):
    grad_rows, act_rows, weights = pieces
    left = kron_columns(grad_rows, act_rows, row_start, rows_own)
    weighted = (weights.astype(jnp.float32)[:, None] * left.astype(jnp.float32)).astype(
        jnp.bfloat16
    )
    right = kron_columns(grad_rows, act_rows, col_start, col_count)
    return total + lax.dot_general(
        weighted, right, (((0,), (0,)), ((), ())), preferred_element_type=jnp.float32
    )


def fold_blocks(total, pieces, step_fn):
    count = pieces[0].shape[0]
    shaped = tuple((p.reshape((count // 512, 512) + p.shape[1:]) for p in pieces))

    def inner(carry, block):
        return (step_fn(carry, block), None)

    return lax.scan(inner, total, shaped)[0]


def split_parts(matrix):
    high_part = matrix.astype(jnp.bfloat16)
    first_rest = matrix - high_part.astype(jnp.float32)
    middle_part = first_rest.astype(jnp.bfloat16)
    low_part = (first_rest - middle_part.astype(jnp.float32)).astype(jnp.bfloat16)
    return (high_part, middle_part, low_part)


def per_device(activations, out_grads, proj_in, proj_out, queries, lengths, credit):
    tok_rows = activations.shape[0]
    seq_len = tok_rows // lengths.shape[0]
    dp_count = lax.axis_size("dp")
    query_count = lax.axis_size("query")
    dp_index = lax.axis_index("dp")
    query_index = lax.axis_index("query")
    part_act = jnp.dot(activations, proj_in, preferred_element_type=jnp.float32)
    part_grad = jnp.dot(out_grads, proj_out, preferred_element_type=jnp.float32)
    sum_act, sum_grad = lax.psum((part_act, part_grad), "query")
    act_proj = sum_act.astype(jnp.bfloat16)
    grad_proj = sum_grad.astype(jnp.bfloat16)
    rank = act_proj.shape[1]
    feat = rank * rank
    live = jnp.arange(seq_len, dtype=jnp.int32)[None, :] < lengths[:, None]
    weight = (credit[:, None].astype(jnp.float32) * live.astype(jnp.float32)).reshape(-1)
    mask = live.astype(jnp.float32).reshape(-1)
    weight_wire = weight.astype(jnp.bfloat16)
    rows_own = feat // dp_count
    row_start = dp_index * rows_own
    all_tokens = tok_rows * dp_count
    col_count = feat // query_count
    col_start = query_index * col_count
    owned = fold_blocks(
        jnp.zeros((rows_own, col_count), jnp.float32),
        (
            lax.all_gather(grad_proj, "dp", axis=0, tiled=True),
            lax.all_gather(act_proj, "dp", axis=0, tiled=True),
            lax.all_gather(weight_wire, "dp", axis=0, tiled=True),
        ),
        lambda carry, block: hessian_block(carry, block, row_start, rows_own, col_start, col_count),
    )
    hessian = lax.all_gather(owned, "query", axis=1, tiled=True) / all_tokens
    diagonal_block = lax.dynamic_slice_in_dim(hessian, row_start, rows_own, 1)
    level = lax.psum(jnp.trace(diagonal_block), "dp") / feat
    step = 1.1 * level
    high_part, middle_part, low_part = split_parts(hessian)
    piece = lax.all_gather(queries, "dp", axis=0, tiled=True)
    result = jnp.zeros(queries.shape, jnp.float32)
    for part_matrix in (low_part, middle_part, high_part):
        columns = part_matrix
        result = result + jnp.dot(columns, piece, preferred_element_type=jnp.float32)
    query_f = queries.astype(jnp.float32)
    precond = ((2.0 * query_f - (result + 0.1 * level * query_f) / step) / step).astype(
        jnp.bfloat16
    )
    local_features = kron_columns(grad_proj, act_proj, 0, feat)
    piece = lax.all_gather(precond, "dp", axis=0, tiled=True)
    columns = lax.slice_in_dim(local_features, 0, piece.shape[0], axis=1)
    scores = jnp.zeros((tok_rows, precond.shape[1]), jnp.float32) + jnp.dot(
        columns, piece, preferred_element_type=jnp.float32
    )
    return (hessian, (scores * mask[:, None]).astype(jnp.bfloat16))


def solution(mesh):
    placed = (
        P(("groups", "dp"), "query"),
        P(("groups", "dp"), "query"),
        P("query", None),
        P("query", None),
        P(("groups", "dp"), "query"),
        P(("groups", "dp")),
        P(("groups", "dp")),
    )
    return jax.shard_map(
        per_device,
        mesh=mesh,
        in_specs=placed,
        out_specs=(P(("groups", "dp"), None), P(("groups", "dp"), "query")),
        check_vma=False,
    )
```

profile of v0, /device:TPU:0, one launch (start us, length us, event | category | flops | bytes accessed | tf_op | source)
XLA Modules:
  0.0 302.7 jit_solution(5617856460040371665)
XLA Ops:
  7.2 0.0 copy-start
  7.2 0.0 all-gather.5.cloned.1.call-start
  7.3 1.4 copy-done
  8.7 1.7 fusion.14
  10.4 1.3 fusion.15
  11.7 14.5 %all-reduce.2 = (bf16[256,64]{0,1:T(8,128)(2,1)S(1)}, bf16[256,64]{0,1:T(8,128)(2,1)S(1)}) all-reduce(f32[256,64]{0,1:T(8,128)S(1)} %fusion.14, f32[256,64]{0,1:T(8,128)S(1)} %fusion.15), channel_id=1, replica_groups=mesh['groups'=2,'dp'=4,'query'=4] {'query'}, use_global_device_ids=true, to_apply=%region_0.0 | all-reduce | flops 32768 | bytes 196608 | tf_op jit(solution)/shard_map/psum | solution.py:54
  26.2 13.7 %all_gather.20 = bf16[1024,64]{0,1:T(8,128)(2,1)S(1)} all-gather(bf16[256,64]{0,1:T(8,128)(2,1)S(1)} %get-tuple-element.330), channel_id=1, replica_groups=mesh['groups'=2,'dp'=4,'query'=4] {'dp'}, dimensions={0}, use_global_device_ids=true | all-gather | bytes 163840 | tf_op jit(solution)/shard_map/all_gather | solution.py:72
  39.9 13.4 %all_gather.19 = bf16[1024,64]{0,1:T(8,128)(2,1)S(1)} all-gather(bf16[256,64]{0,1:T(8,128)(2,1)S(1)} %get-tuple-element.329), channel_id=1, replica_groups=mesh['groups'=2,'dp'=4,'query'=4] {'dp'}, dimensions={0}, use_global_device_ids=true | all-gather | bytes 163840 | tf_op jit(solution)/shard_map/all_gather | solution.py:71
  53.4 0.7 convert_element_type.180
  54.0 0.7 select_convert_fusion
  54.8 10.8 %all-gather = bf16[4,1,256]{2,1,0:T(2,128)(2,1)S(1)} all-gather(bf16[1,1,256]{2,1,0:T(2,128)(2,1)S(1)} %reshape.153), channel_id=1, replica_groups=mesh['groups'=2,'dp'=4,'query'=4] {'dp'}, dimensions={0}, use_global_device_ids=true | all-gather | bytes 2560 | tf_op jit(solution)/shard_map/all_gather | solution.py:73
  65.6 13.4 %while.14 = (s32[]{:T(128)}, f32[1024,1024]{1,0:T(8,128)}, bf16[2,512]{1,0:T(2,128)(2,1)S(1)}, bf16[2,512,64]{1,2,0:T(8,128)(2,1)S(1)}, s32[]{:T(128)}, /*index=...) while((s32[]{:T(128)}, f32[1024,1024]{1,0:T(8,128)}, ...), condition=%wide.region_3.4_spmd.clone, body=%wide.region_2.3_spmd.clone.sunk | while | flops 1079558656 | bytes 13079691 | solution.py:34
  65.7 1.4 multiply_convert_fusion.5
  67.2 4.5 %select_add_fusion.2 = f32[1024,1024]{1,0:T(8,128)} fusion(f32[1024,1024]{1,0:T(8,128)} %get-tuple-element.396, bf16[512,1024]{0,1:T(8,128)(2,1)} %bitcast.49, bf16[512,1024]{0,1:T(8,128)(2,1)S(1)} %bitcast.48, pred[]{:T(512)S(6)} %compare.15), kind=kOutput, calls=%fused_computation.clone.1 | convolution fusion | flops 1075838976 | bytes 10485761 | tf_op jit(solution)/shard_map/while/body/eval_jaxpr/dot_general | solution.py:22
  71.8 1.4 multiply_convert_fusion.5
  73.2 5.8 %select_add_fusion.2 = f32[1024,1024]{1,0:T(8,128)} fusion(f32[1024,1024]{1,0:T(8,128)} %get-tuple-element.396, bf16[512,1024]{0,1:T(8,128)(2,1)} %bitcast.49, bf16[512,1024]{0,1:T(8,128)(2,1)S(1)} %bitcast.48, pred[]{:T(512)S(6)} %compare.15), kind=kOutput, calls=%fused_computation.clone.1 | convolution fusion | flops 1075838976 | bytes 10485761 | tf_op jit(solution)/shard_map/while/body/eval_jaxpr/dot_general | solution.py:22
  79.0 0.0 all-gather.5.cloned.1.call-update
  79.0 0.0 all-gather.7.cloned.1.call-start
  79.1 0.7 all-gather.7.cloned.1.call-update
  79.8 0.0 all-gather.9.cloned.1.call-start
  79.8 102.6 %all-gather.5.cloned.1.call-done = f32[1024,4096]{1,0:T(8,128)} async-done(((f32[1024,1024]{1,0:T(8,128)}), f32[1024,4096]{1,0:T(8,128)}) %all-gather.5.cloned.1.call-update) | async-done | bytes 16777232 | tf_op jit(solution)/shard_map/all_gather | solution.py:77
  182.5 6.5 %broadcast_multiply_fusion = f32[1024,4096]{1,0:T(8,128)S(1)} fusion(f32[1024,4096]{1,0:T(8,128)} %all-gather.5.cloned.1.call-done), kind=kLoop, calls=%fused_computation.15 | loop fusion | flops 4194304 | bytes 33554432 | tf_op jit(solution)/shard_map/div | solution.py:77
  189.0 0.0 copy-start.1
  189.0 6.2 %copy-done.1 = f32[1024,4096]{1,0:T(8,128)} copy-done((f32[1024,4096]{1,0:T(8,128)}, f32[1024,4096]{1,0:T(8,128)S(1)}, u32[]{:S(2)}) %copy-start.1) | copy-done | bytes 16777240
  195.1 0.7 select_reduce_fusion
  195.9 12.6 %psum.23 = f32[]{:T(128)} all-reduce(f32[]{:T(128)} %select_reduce_fusion), channel_id=1, replica_groups=mesh['groups'=2,'dp'=4,'query'=4] {'dp'}, use_global_device_ids=true, to_apply=%region_5.6 | all-reduce | flops 1 | bytes 8 | tf_op jit(solution)/shard_map/psum | solution.py:79
  209.8 20.5 %all-gather.7.cloned.1.call-done = bf16[4096,256]{1,0:T(8,128)(2,1)} async-done(((bf16[1024,256]{1,0:T(8,128)(2,1)}), bf16[4096,256]{1,0:T(8,128)(2,1)}) %all-gather.7.cloned.1.call-update) | async-done | bytes 2097168 | tf_op jit(solution)/shard_map/all_gather | solution.py:82
  230.2 0.0 copy-start.2
  230.2 0.0 copy-start.3
  230.2 8.8 %fusion.1 = f32[1024,256]{1,0:T(8,128)S(1)} fusion(bf16[4096,256]{1,0:T(8,128)(2,1)} %all-gather.7.cloned.1.call-done, f32[1024,4096]{1,0:T(8,128)} %copy-done.1), kind=kOutput, calls=%fused_computation.11 | convolution fusion | flops 2151677952 | bytes 19922944 | tf_op jit(solution)/shard_map/dot_general | solution.py:86
  239.1 2.3 copy-done.2
  241.4 0.6 copy-done.3
  242.0 0.0 copy-start.4
  242.0 2.3 fusion.3
  244.3 0.0 copy-done.4
  244.3 0.0 copy-start.5
  244.3 3.3 %fusion.12 = bf16[1024,256]{1,0:T(8,128)(2,1)} fusion(f32[1024,256]{1,0:T(8,128)S(1)} %fusion.1, f32[1024,256]{1,0:T(8,128)S(1)} %fusion.3, bf16[4096,256]{1,0:T(8,128)(2,1)S(1)} %copy-done.3, f32[1024,4096]{1,0:T(8,128)S(1)} %copy-done.2, bf16[1024,256]{1,0:T(8,128)(2,1)S(1)} %copy-done.4, f32[]{:T(128)S(6)} %mul_shard_map.7, f32[]{:T(128)S(6)} %mul_shard_map.6), kind=kOutput, calls=%fused_computation.27 | convolution fusion | flops 2179465216 | bytes 22020104 | tf_op jit(solution)/shard_map/dot_general | solution.py:86
  247.6 0.0 all-gather.9.cloned.1.call-update
  247.7 0.0 copy-done.5
  247.7 0.1 convert_bitcast_fusion
  247.8 2.0 multiply_convert_fusion.3
  249.8 42.7 %all-gather.9.cloned.1.call-done = bf16[4096,256]{1,0:T(8,128)(2,1)} async-done(((bf16[1024,256]{1,0:T(8,128)(2,1)}), bf16[4096,256]{1,0:T(8,128)(2,1)}) %all-gather.9.cloned.1.call-update) | async-done | bytes 2097168 | tf_op jit(solution)/shard_map/all_gather | solution.py:92
  292.5 3.6 %fusion.13 = bf16[256,256]{1,0:T(8,128)(2,1)} fusion(bf16[256,4096]{0,1:T(8,128)(2,1)} %bitcast.50, bf16[4096,256]{1,0:T(8,128)(2,1)} %all-gather.9.cloned.1.call-done, f32[256]{0:T(256)S(1)} %convert_bitcast_fusion), kind=kOutput, calls=%fused_computation.29 | convolution fusion | flops 537001984 | bytes 4326400 | tf_op jit(solution)/shard_map/dot_general | solution.py:94
  (14 shorter events, 0.2 us)
Async XLA Ops:
  7.2 1.5 copy-start
  7.2 175.3 %all-gather.5.cloned.1.call-start = ((), (), s32[]{:S(2)}) async-start(), calls=%async_computation | async-start | bytes 20971520 | tf_op jit(solution)/shard_map/all_gather | solution.py:77
  79.0 151.2 %all-gather.7.cloned.1.call-start = ((), (), s32[]{:S(2)}) async-start(), calls=%async_computation.1 | async-start | bytes 2621440 | tf_op jit(solution)/shard_map/all_gather | solution.py:82
  79.8 212.7 %all-gather.9.cloned.1.call-start = ((), (), s32[]{:S(2)}) async-start(), calls=%async_computation.2 | async-start | bytes 2621440 | tf_op jit(solution)/shard_map/all_gather | solution.py:92
  189.0 6.2 %copy-start.1 = (f32[1024,4096]{1,0:T(8,128)}, f32[1024,4096]{1,0:T(8,128)S(1)}, u32[]{:S(2)}) copy-start(f32[1024,4096]{1,0:T(8,128)S(1)} %broadcast_multiply_fusion) | copy-start | bytes 50331652
  230.2 11.1 %copy-start.2 = (f32[1024,4096]{1,0:T(8,128)S(1)}, f32[1024,4096]{1,0:T(8,128)}, u32[]{:S(2)}) copy-start(f32[1024,4096]{1,0:T(8,128)} %copy-done.1) | copy-start | bytes 50331652
  230.2 11.7 %copy-start.3 = (bf16[4096,256]{1,0:T(8,128)(2,1)S(1)}, bf16[4096,256]{1,0:T(8,128)(2,1)}, u32[]{:S(2)}) copy-start(bf16[4096,256]{1,0:T(8,128)(2,1)} %all-gather.7.cloned.1.call-done) | copy-start | bytes 6291460
  242.0 2.3 copy-start.4
  244.3 3.4 %copy-start.5 = (s32[2]{0:T(128)S(1)}, s32[2]{0:T(128)}, u32[]{:S(2)}) copy-start(s32[2]{0:T(128)} %param.14) | copy-start | bytes 28
Sparse Core Ops, SparseCore 0:
  79.2 103.2 all-gather.4
  184.0 46.1 all-gather.6
  247.8 44.6 all-gather.8
where the time goes:
time: 303 us
  waiting for transfers between devices  167 us (55%)
  blocking collectives  65 us (21%)
  matrix products  31.5 us (10%)
  between operations  15.2 us (5%)
  other arithmetic  13.8 us (5%)
  local copies, waits for them, and re-layouts  10.5 us (3%)
    all_gather x1, waiting for transfers between devices, per_device(): hessian = lax.all_gather(owned, 'query', axis=1, tiled=True) / all_tokens  103 us
    all_gather x1, waiting for transfers between devices, per_device(): piece = lax.all_gather(precond, 'dp', axis=0, tiled=True)  42.7 us
    all_gather x1, waiting for transfers between devices, per_device(): piece = lax.all_gather(queries, 'dp', axis=0, tiled=True)  20.5 us
    dot_general x4, matrix products, per_device(): jnp.dot(columns, piece, preferred_element_type=jnp.float32)  18.1 us
    psum x1, blocking collectives, per_device(): sum_act, sum_grad = lax.psum((part_act, part_grad), 'query')  14.5 us
    all_gather x1, blocking collectives, per_device(): lax.all_gather(act_proj, 'dp', axis=0, tiled=True)  13.7 us
    all_gather x1, blocking collectives, per_device(): lax.all_gather(grad_proj, 'dp', axis=0, tiled=True)  13.4 us
    psum x1, blocking collectives, per_device(): level = lax.psum(jnp.trace(diagonal_block), 'dp') / feat  12.6 us
  transfers between devices with their start and end apart: 3, of which 3 were waited for; matrix products, arithmetic and copies ran while one was open for 3% of the time, Pallas kernels for 0%

commit v1 on v0

--- a/solution.py
+++ b/solution.py
@@ -1,6 +1,9 @@
+import functools
 import jax
 import jax.numpy as jnp
 from jax import lax
+from jax.experimental import pallas as pl
+from jax.experimental.pallas import tpu as pltpu
 from jax.sharding import PartitionSpec as P
 
 
@@ -42,7 +45,7 @@
     return (high_part, middle_part, low_part)
 
 
-def per_device(activations, out_grads, proj_in, proj_out, queries, lengths, credit):
+def many_tokens(activations, out_grads, proj_in, proj_out, queries, lengths, credit):
     tok_rows = activations.shape[0]
     seq_len = tok_rows // lengths.shape[0]
     dp_count = lax.axis_size("dp")
@@ -97,6 +100,224 @@
     return (hessian, (scores * mask[:, None]).astype(jnp.bfloat16))
 
 
+MEM = pltpu.CompilerParams(vmem_limit_bytes=48 * 1024 * 1024)
+NT = (((1,), (1,)), ((), ()))
+
+
+def project_kernel(act_ref, grad_ref, pin_ref, pout_ref, out_ref):
+    @pl.when(pl.program_id(0) == 0)
+    def _():
+        out_ref[...] = jnp.zeros_like(out_ref)
+
+    part_act = jnp.dot(act_ref[...], pin_ref[...], preferred_element_type=jnp.float32)
+    part_grad = jnp.dot(grad_ref[...], pout_ref[...], preferred_element_type=jnp.float32)
+    out_ref[...] += jnp.concatenate([part_act, part_grad], axis=1)
+
+
+def project(activations, out_grads, proj_in, proj_out, steps=4):
+    tok, d_here = activations.shape
+    f_here = out_grads.shape[1]
+    rank = proj_in.shape[1]
+    return pl.pallas_call(
+        project_kernel,
+        grid=(steps,),
+        in_specs=[
+            pl.BlockSpec((tok, d_here // steps), lambda s: (0, s)),
+            pl.BlockSpec((tok, f_here // steps), lambda s: (0, s)),
+            pl.BlockSpec((d_here // steps, rank), lambda s: (s, 0)),
+            pl.BlockSpec((f_here // steps, rank), lambda s: (s, 0)),
+        ],
+        out_specs=pl.BlockSpec((tok, 2 * rank), lambda s: (0, 0)),
+        out_shape=jax.ShapeDtypeStruct((tok, 2 * rank), jnp.float32),
+        compiler_params=MEM,
+    )(activations, out_grads, proj_in, proj_out)
+
+
+def total_kernel(*refs):
+    out_ref = refs[-1]
+    total = refs[0][...]
+    for ref in refs[1:-1]:
+        total = total + ref[...]
+    out_ref[...] = total.T.astype(out_ref.dtype)
+
+
+def add_projections(parts):
+    tok, width = parts[0].shape
+    return pl.pallas_call(
+        total_kernel,
+        out_shape=jax.ShapeDtypeStruct((width, tok), jnp.bfloat16),
+        compiler_params=MEM,
+    )(*parts)
+
+
+def lay_out_factors(factor_refs, weight_refs, factors, weights):
+    tok = factor_refs[0].shape[1]
+    for k, (factor_ref, weight_ref) in enumerate(zip(factor_refs, weight_refs)):
+        factors[:, k * tok : (k + 1) * tok] = factor_ref[...].astype(jnp.float32)
+        weights[:, k * tok : (k + 1) * tok] = weight_ref[...]
+
+
+def range_scale(values):
+    top = jnp.max(jnp.abs(values), keepdims=True)
+    scale = jnp.ones_like(top)
+    for low in (16, 48, 80, 112):
+        scale = jnp.where(top > 2.0**low, 2.0 ** -min(low + 16, 126), scale)
+        scale = jnp.where(top < 2.0**-low, 2.0 ** min(low + 16, 126), scale)
+    return scale
+
+
+def share_kernel(blocks, row_count, *refs):
+    factor_refs, weight_refs = refs[:blocks], refs[blocks : 2 * blocks]
+    query_ref = refs[2 * blocks]
+    out_refs = refs[2 * blocks + 1 : 3 * blocks + 1]
+    factors, weights, features = refs[3 * blocks + 1 :]
+    lay_out_factors(factor_refs, weight_refs, factors, weights)
+    rank = factors.shape[0] // 2
+    tokens = factors.shape[1]
+    tok = tokens // blocks
+    first = rank + lax.axis_index("dp") * row_count
+    act = factors[:rank, :]
+    for i in range(row_count):
+        row = factors[pl.ds(first + i, 1), :]
+        features[i * rank : (i + 1) * rank, :] = (row * act).astype(jnp.bfloat16)
+    plain = jnp.dot(query_ref[...], features[...], preferred_element_type=jnp.float32)
+    weight = weights[...]
+    live = weight > 0.0
+    act = jnp.where(live, act, 0.0)
+    grad = jnp.where(live, factors[rank:, :], 0.0)
+    act_scale, grad_scale = range_scale(act), range_scale(grad)
+    act, grad = act * act_scale, grad * grad_scale
+    norms = jnp.sum(act * act, axis=0, keepdims=True) * jnp.sum(grad * grad, axis=0, keepdims=True)
+    level = jnp.sum(weight * norms, axis=1, keepdims=True) / (tokens * rank * rank)
+    step = 1.1 * level
+    act_b, grad_b = act.astype(jnp.bfloat16), grad.astype(jnp.bfloat16)
+    gram = jnp.dot(act.T.astype(jnp.bfloat16), act_b, preferred_element_type=jnp.float32) * jnp.dot(
+        grad.T.astype(jnp.bfloat16), grad_b, preferred_element_type=jnp.float32
+    )
+    gram = (gram * (1.0 / (tokens * step))).astype(jnp.bfloat16)
+    image = jnp.dot((plain * weight).astype(jnp.bfloat16), gram, preferred_element_type=jnp.float32)
+    scale = act_scale * grad_scale
+    share = ((2.0 - 0.1 / 1.1) * plain - image) * scale * (scale / step)
+    for k, out_ref in enumerate(out_refs):
+        out_ref[...] = share[:, k * tok : (k + 1) * tok].astype(jnp.bfloat16)
+
+
+def score_shares(factors, weights, queries_t, row_count):
+    blocks = len(factors)
+    width, tok = factors[0].shape
+    rows = queries_t.shape[1]
+    out = jax.ShapeDtypeStruct((queries_t.shape[0], tok), jnp.bfloat16)
+    return pl.pallas_call(
+        functools.partial(share_kernel, blocks, row_count),
+        out_shape=[out] * blocks,
+        scratch_shapes=[
+            pltpu.VMEM((width, tok * blocks), jnp.float32),
+            pltpu.VMEM((1, tok * blocks), jnp.float32),
+            pltpu.VMEM((rows, tok * blocks), jnp.bfloat16),
+        ],
+        compiler_params=MEM,
+    )(*factors, *weights, queries_t)
+
+
+def hessian_kernel(blocks, row_count, col_count, *refs):
+    factor_refs, weight_refs = refs[:blocks], refs[blocks : 2 * blocks]
+    out_ref, factors, weights, weighted, right = refs[2 * blocks :]
+    rank = factors.shape[0] // 2
+    tokens = factors.shape[1]
+
+    @pl.when(pl.program_id(0) == 0)
+    def _():
+        lay_out_factors(factor_refs, weight_refs, factors, weights)
+        first = rank + lax.axis_index("dp") * row_count
+        act, weight = factors[:rank, :], weights[...]
+        for i in range(row_count):
+            left = (factors[pl.ds(first + i, 1), :] * act).astype(jnp.bfloat16)
+            left = (weight * left.astype(jnp.float32)).astype(jnp.bfloat16)
+            weighted[i * rank : (i + 1) * rank, :] = left
+
+    act = factors[:rank, :]
+    first = rank + pl.program_id(0) * col_count
+    for i in range(col_count):
+        row = factors[pl.ds(first + i, 1), :]
+        right[i * rank : (i + 1) * rank, :] = (row * act).astype(jnp.bfloat16)
+    block = lax.dot_general(weighted[...], right[...], NT, preferred_element_type=jnp.float32)
+    out_ref[...] = block / tokens
+
+
+def hessian_rows(factors, weights, row_count, col_count=8):
+    blocks = len(factors)
+    width, tok = factors[0].shape
+    rank = width // 2
+    feat = rank * rank
+    rows, cols = row_count * rank, col_count * rank
+    return pl.pallas_call(
+        functools.partial(hessian_kernel, blocks, row_count, col_count),
+        grid=(feat // cols,),
+        in_specs=[pl.BlockSpec((width, tok), lambda s: (0, 0))] * blocks
+        + [pl.BlockSpec((1, tok), lambda s: (0, 0))] * blocks,
+        out_specs=pl.BlockSpec((rows, cols), lambda s: (0, s)),
+        out_shape=jax.ShapeDtypeStruct((rows, feat), jnp.float32),
+        scratch_shapes=[
+            pltpu.VMEM((width, tok * blocks), jnp.float32),
+            pltpu.VMEM((1, tok * blocks), jnp.float32),
+            pltpu.VMEM((rows, tok * blocks), jnp.bfloat16),
+            pltpu.VMEM((cols, tok * blocks), jnp.bfloat16),
+        ],
+        compiler_params=MEM,
+    )(*factors, *weights)
+
+
+def finish_kernel(*refs):
+    weight_ref, out_ref = refs[-2], refs[-1]
+    total = refs[0][...].astype(jnp.float32)
+    for ref in refs[1:-2]:
+        total = total + ref[...].astype(jnp.float32)
+    total = jnp.where(weight_ref[...] > 0.0, total, 0.0)
+    out_ref[...] = total.T.astype(out_ref.dtype)
+
+
+def finish_scores(shares, weight):
+    count, tok = shares[0].shape
+    return pl.pallas_call(
+        finish_kernel,
+        out_shape=jax.ShapeDtypeStruct((tok, count), jnp.bfloat16),
+        compiler_params=MEM,
+    )(*shares, weight)
+
+
+def shifted(array, axis, by):
+    count = lax.axis_size(axis)
+    return lax.ppermute(array, axis, [(i, (i + by) % count) for i in range(count)])
+
+
+def from_all(array, axis):
+    return [array] + [shifted(array, axis, k) for k in range(1, lax.axis_size(axis))]
+
+
+def few_tokens(activations, out_grads, proj_in, proj_out, queries, lengths, credit):
+    tok_rows = activations.shape[0]
+    seq_len = tok_rows // lengths.shape[0]
+    dp_count = lax.axis_size("dp")
+    rank = proj_in.shape[1]
+    row_count = rank // dp_count
+    live = jnp.arange(seq_len, dtype=jnp.int32)[None, :] < lengths[:, None]
+    weight = (credit[:, None].astype(jnp.float32) * live.astype(jnp.float32)).reshape(1, -1)
+    weights = from_all(weight, "dp")
+    part = project(activations, out_grads, proj_in, proj_out)
+    factors = from_all(add_projections(from_all(part, "query")), "dp")
+    shares = score_shares(factors, weights, queries.T, row_count)
+    arrived = [shares[0]] + [shifted(shares[k], "dp", -k) for k in range(1, dp_count)]
+    hessian = hessian_rows(factors, weights, row_count)
+    return hessian, finish_scores(arrived, weight)
+
+
+def per_device(activations, *others):
+    rank = others[1].shape[1]
+    if activations.shape[0] * lax.axis_size("dp") > rank * rank:
+        return many_tokens(activations, *others)
+    return few_tokens(activations, *others)
+
+
 def solution(mesh):
     placed = (
         P(("groups", "dp"), "query"),

time: 303 us -> 51.9 us (0.17)
  waiting for transfers between devices: 167 us -> 8.71 us
  blocking collectives: 65 us -> 0 us
  matrix products: 31.5 us -> 0 us
  Pallas kernels: 0 us -> 17.8 us
  starting transfers between devices: 0.12 us -> 16.7 us
  between operations: 15.2 us -> 0.71 us
  other arithmetic: 13.8 us -> 1.38 us
  local copies, waits for them, and re-layouts: 10.5 us -> 6.3 us
    all_gather x3 -> x0, waiting for transfers between devices: 166 us -> none  [the longest x1 103 us: per_device(): hessian = lax.all_gather(owned, 'query', axis=1, tiled=True) / all_tokens]
    all_gather x3 -> x0, blocking collectives: 38 us -> none  [the longest x1 13.7 us: per_device(): lax.all_gather(act_proj, 'dp', axis=0, tiled=True)]
    dot_general x8 -> x0, matrix products: 31.5 us -> none  [the longest x4 18.1 us: per_device(): jnp.dot(columns, piece, preferred_element_type=jnp.float32)]
    psum x2 -> x0, blocking collectives: 27.1 us -> none  [the longest x1 14.5 us: per_device(): sum_act, sum_grad = lax.psum((part_act, part_grad), 'query')]
    pallas_call x0 -> x5, Pallas kernels: none -> 17.8 us  [the longest x1 12.5 us: hessian_rows(): pl.pallas_call(functools.partial(hessian_kernel, blocks, row_count, col_c...]
    ppermute x0 -> x12, starting transfers between devices: none -> 16.7 us  [shifted(): lax.ppermute(array, axis, [(i, (i + by) % count) for i in range(count)])]
    ppermute x0 -> x12, waiting for transfers between devices: none -> 8.71 us  [shifted(): lax.ppermute(array, axis, [(i, (i + by) % count) for i in range(count)])]
    div x1 -> x0, other arithmetic: 6.52 us -> none  [per_device(): hessian = lax.all_gather(owned, 'query', axis=1, tiled=True) / all_tokens]
  transfers between devices with their start and end apart: 3 -> 12, of which waited for: 3 -> 4; matrix products, arithmetic and copies ran while one was open for 3% -> 5% of each run, Pallas kernels for 0% -> 24%
where the time goes in v1:
time: 51.9 us; the launch traced here: 51.5 us
  Pallas kernels  17.8 us (34%)
  starting transfers between devices  16.7 us (32%)
  waiting for transfers between devices  8.71 us (17%)
  local copies, waits for them, and re-layouts  6.3 us (12%)
  other arithmetic  1.38 us (3%)
  between operations  0.71 us (1%)
    ppermute x12, starting transfers between devices, shifted(): lax.ppermute(array, axis, [(i, (i + by) % count) for i in range(count)])  16.7 us
    pallas_call x1, Pallas kernels, hessian_rows(): pl.pallas_call(functools.partial(hessian_kernel, blocks, row_count, col_c...  12.5 us
    ppermute x12, waiting for transfers between devices, shifted(): lax.ppermute(array, axis, [(i, (i + by) % count) for i in range(count)])  8.71 us
    unnamed x7, local copies, waits for them, and re-layouts  6.3 us
    pallas_call x1, Pallas kernels, score_shares(): pl.pallas_call(functools.partial(share_kernel, blocks, row_count), out_sh...  2.55 us
    pallas_call x1, Pallas kernels, project(): pl.pallas_call(project_kernel, grid=(steps,), in_specs=[pl.BlockSpec((tok...  1.82 us
  transfers between devices with their start and end apart: 12, of which 4 were waited for; matrix products, arithmetic and copies ran while one was open for 5% of the time, Pallas kernels for 24%

profile of v1, /device:TPU:0, one launch (start us, length us, event | category | flops | bytes accessed | tf_op | source)
XLA Modules:
  0.0 51.5 jit_solution(2808974912317054268)
XLA Ops:
  0.6 1.1 %copy.9.pin_ref = bf16[1024,64]{1,0:T(8,128)(2,1)S(1)} copy(bf16[1024,64]{0,1:T(8,128)(2,1)} %param.9) | data formatting | bytes 262144 | tf_op args[2]
  1.7 1.4 %copy.10.pout_ref = bf16[3584,64]{1,0:T(8,128)(2,1)S(1)} copy(bf16[3584,64]{0,1:T(8,128)(2,1)} %param.10) | data formatting | bytes 917504 | tf_op args[3]
  3.2 0.0 copy-start
  3.2 1.5 %copy-done = bf16[256,3584]{1,0:T(8,128)(2,1)S(1)} copy-done((bf16[256,3584]{1,0:T(8,128)(2,1)S(1)}, bf16[256,3584]{1,0:T(8,128)(2,1)}, u32[]{:S(2)}) %copy-start) | copy-done | bytes 1835032
  4.7 0.0 copy-start.1
  4.7 1.0 %copy-done.1 = bf16[256,1024]{1,0:T(8,128)(2,1)S(1)} copy-done((bf16[256,1024]{1,0:T(8,128)(2,1)S(1)}, bf16[256,1024]{1,0:T(8,128)(2,1)}, u32[]{:S(2)}) %copy-start.1) | copy-done | bytes 524312
  5.7 1.8 %shard_map.86.refs_0_ = f32[256,128]{1,0:T(8,128)S(1)} custom-call(bf16[256,1024]{1,0:T(8,128)(2,1)S(1)} %copy-done.1, bf16[256,3584]{1,0:T(8,128)(2,1)S(1)} %copy-done, bf16[1024,64]{1,0:T(8,128)(2,1)S(1)} %copy.9.pin_ref, bf16[3584,64]{1,0:T(8,128)(2,1)S(1)} %copy.10.pout_ref), custom_call_target="tpu_custom_call" | custom-call | tf_op jit(solution)/shard_map/pallas_call | solution.py:121
  7.5 2.4 %collective-permute-start.2 = (f32[256,128]{1,0:T(8,128)S(1)}, f32[256,128]{1,0:T(8,128)S(1)}, u32[]{:S(2)}, u32[]{:S(2)}) collective-permute-start(f32[256,128]{1,0:T(8,128)S(1)} %shard_map.86.refs_0_), channel_id=1, source_target_pairs={{0,3},{1,0},{2,1},{3,2},{4,7},{5,4},{6,5},{7,6},{8,11},{9,8},{10,9... | collective-permute-start | bytes 393224 | tf_op jit(solution)/shard_map/ppermute | solution.py:290
  10.0 0.6 %collective-permute-start.1 = (f32[256,128]{1,0:T(8,128)S(1)}, f32[256,128]{1,0:T(8,128)S(1)}, u32[]{:S(2)}, u32[]{:S(2)}) collective-permute-start(f32[256,128]{1,0:T(8,128)S(1)} %shard_map.86.refs_0_), channel_id=1, source_target_pairs={{0,2},{1,3},{2,0},{3,1},{4,6},{5,7},{6,4},{7,5},{8,10},{9,11},{10,... | collective-permute-start | bytes 393224 | tf_op jit(solution)/shard_map/ppermute | solution.py:290
  10.6 0.2 collective-permute-start
  10.8 0.7 %convert_element_type.5 = f32[2]{0:T(128)S(1)} convert(s32[2]{0:T(128)} %param.13) | non-fusion elementwise | flops 2 | bytes 16 | tf_op jit(solution)/shard_map/convert_element_type | solution.py:304
  11.4 2.3 %collective-permute-done.2.refs_3_ = f32[256,128]{1,0:T(8,128)S(1)} collective-permute-done((f32[256,128]{1,0:T(8,128)S(1)}, f32[256,128]{1,0:T(8,128)S(1)}, u32[]{:S(2)}, u32[]{:S(2)}) %collective-permute-start.2) | collective-permute-done | bytes 131104 | tf_op jit(solution)/shard_map/ppermute | solution.py:290
  13.7 3.8 %collective-permute-done.1.refs_2_ = f32[256,128]{1,0:T(8,128)S(1)} collective-permute-done((f32[256,128]{1,0:T(8,128)S(1)}, f32[256,128]{1,0:T(8,128)S(1)}, u32[]{:S(2)}, u32[]{:S(2)}) %collective-permute-start.1) | collective-permute-done | bytes 131104 | tf_op jit(solution)/shard_map/ppermute | solution.py:290
  17.5 0.0 collective-permute-done.refs_1_
  17.5 0.1 shard_map.87.refs_0_
  17.6 3.8 %collective-permute-start.5 = (bf16[128,256]{1,0:T(8,128)(2,1)S(1)}, bf16[128,256]{1,0:T(8,128)(2,1)S(1)}, u32[]{:S(2)}, u32[]{:S(2)}) collective-permute-start(bf16[128,256]{1,0:T(8,128)(2,1)S(1)} %shard_map.87.refs_0_), channel_id=1, source_target_pairs={{0,12},{4,0},{8,4},{12,8},{1,13},{5,1},{9,5},{13,9},{2,14},{6,2},{... | collective-permute-start | bytes 196616 | tf_op jit(solution)/shard_map/ppermute | solution.py:290
  21.5 0.0 collective-permute-start.4
  21.5 1.0 %collective-permute-start.3 = (bf16[128,256]{1,0:T(8,128)(2,1)S(1)}, bf16[128,256]{1,0:T(8,128)(2,1)S(1)}, u32[]{:S(2)}, u32[]{:S(2)}) collective-permute-start(bf16[128,256]{1,0:T(8,128)(2,1)S(1)} %shard_map.87.refs_0_), channel_id=1, source_target_pairs={{0,4},{4,8},{8,12},{12,0},{1,5},{5,9},{9,13},{13,1},{2,6},{6,10},{... | collective-permute-start | bytes 196616 | tf_op jit(solution)/shard_map/ppermute | solution.py:290
  22.5 0.7 %compare_select_fusion = f32[2,128]{1,0:T(2,128)S(1)} fusion(f32[2]{0:T(128)S(1)} %convert_element_type.5, s32[2]{0:T(128)} %param.12), kind=kLoop, calls=%fused_computation | loop fusion | flops 512 | bytes 1040 | tf_op jit(solution)/shard_map/mul | solution.py:304
  23.2 2.8 %collective-permute-start.8 = (f32[1,256]{1,0:T(1,128)S(1)}, f32[1,256]{1,0:T(1,128)S(1)}, u32[]{:S(2)}, u32[]{:S(2)}) collective-permute-start(f32[1,256]{1,0:T(1,128)S(1)} %bitcast.3), channel_id=1, source_target_pairs={{0,12},{4,0},{8,4},{12,8},{1,13},{5,1},{9,5},{13,9},{2,14},{6,2},{... | collective-permute-start | bytes 3080 | tf_op jit(solution)/shard_map/ppermute | solution.py:290
  26.0 1.1 %collective-permute-start.7 = (f32[1,256]{1,0:T(1,128)S(1)}, f32[1,256]{1,0:T(1,128)S(1)}, u32[]{:S(2)}, u32[]{:S(2)}) collective-permute-start(f32[1,256]{1,0:T(1,128)S(1)} %bitcast.4), channel_id=1, source_target_pairs={{0,8},{4,12},{8,0},{12,4},{1,9},{5,13},{9,1},{13,5},{2,10},{6,14},... | collective-permute-start | bytes 3080 | tf_op jit(solution)/shard_map/ppermute | solution.py:290
  27.1 0.2 collective-permute-done.8.refs_7_
  27.3 1.9 %collective-permute-start.6 = (f32[1,256]{1,0:T(1,128)S(1)}, f32[1,256]{1,0:T(1,128)S(1)}, u32[]{:S(2)}, u32[]{:S(2)}) collective-permute-start(f32[1,256]{1,0:T(1,128)S(1)} %bitcast.5), channel_id=1, source_target_pairs={{0,4},{4,8},{8,12},{12,0},{1,5},{5,9},{9,13},{13,1},{2,6},{6,10},{... | collective-permute-start | bytes 3080 | tf_op jit(solution)/shard_map/ppermute | solution.py:290
  29.2 1.2 %copy.11 = bf16[1024,256]{0,1:T(8,128)(2,1)S(1)} copy(bf16[1024,256]{1,0:T(8,128)(2,1)} %param.11) | data formatting | bytes 1048576 | tf_op args[4]
  30.5 0.0 collective-permute-done.7.refs_6_
  30.5 2.4 %collective-permute-done.6.refs_5_ = f32[1,256]{1,0:T(1,128)S(1)} collective-permute-done((f32[1,256]{1,0:T(1,128)S(1)}, f32[1,256]{1,0:T(1,128)S(1)}, u32[]{:S(2)}, u32[]{:S(2)}) %collective-permute-start.6) | collective-permute-done | bytes 1056 | tf_op jit(solution)/shard_map/ppermute | solution.py:290
  32.9 0.0 collective-permute-done.5.refs_3_
  32.9 0.0 collective-permute-done.4.refs_2_
  32.9 0.0 collective-permute-done.3.refs_1_
  32.9 2.6 %shard_map.89 = (bf16[256,256]{1,0:T(8,128)(2,1)S(1)}, bf16[256,256]{1,0:T(8,128)(2,1)S(1)}, bf16[256,256]{1,0:T(8,128)(2,1)S(1)}, bf16[256,256]{1,0:T(8,128)(2,1)S(1)}) custom-call(bf16[128,256]{1,0:T(8,128)(2,1)S(1)} %shard_map.87.refs_0_, bf16[128,256]{1,0:T(8,128)(2,1)S(1)} %collective-permute-done.3.refs_1_, ...), custom_call_target="tpu_custom_call" | custom-call | tf_op jit(solution)/shard_map/pallas_call | solution.py:210
  35.5 2.1 %collective-permute-start.9 = (bf16[256,256]{1,0:T(8,128)(2,1)S(1)}, bf16[256,256]{1,0:T(8,128)(2,1)S(1)}, u32[]{:S(2)}, u32[]{:S(2)}) collective-permute-start(bf16[256,256]{1,0:T(8,128)(2,1)S(1)} %get-tuple-element.7), channel_id=1, source_target_pairs={{0,12},{4,0},{8,4},{12,8},{1,13},{5,1},{9,5},{13,9},{2,14},{6,2},{... | collective-permute-start | bytes 393224 | tf_op jit(solution)/shard_map/ppermute | solution.py:290
  37.6 0.0 collective-permute-start.10
  37.6 0.6 %collective-permute-start.11 = (bf16[256,256]{1,0:T(8,128)(2,1)S(1)}, bf16[256,256]{1,0:T(8,128)(2,1)S(1)}, u32[]{:S(2)}, u32[]{:S(2)}) collective-permute-start(bf16[256,256]{1,0:T(8,128)(2,1)S(1)} %get-tuple-element.9), channel_id=1, source_target_pairs={{0,4},{4,8},{8,12},{12,0},{1,5},{5,9},{9,13},{13,1},{2,6},{6,10},{... | collective-permute-start | bytes 393224 | tf_op jit(solution)/shard_map/ppermute | solution.py:290
  38.2 12.5 %shard_map.88 = f32[1024,4096]{1,0:T(8,128)} custom-call(bf16[128,256]{1,0:T(8,128)(2,1)S(1)} %shard_map.87.refs_0_, bf16[128,256]{1,0:T(8,128)(2,1)S(1)} %collective-permute-done.3.refs_1_, bf16[128,256]{1,0:T(8,128)(2,1)S(1)} %collective-permute-done.4.refs_2_, bf16[128,256]{1,0:T(8,128)(2,1)S(1)} %collective-permute-done.5.refs_3_, f32[1,256]{1,0:T(1,128)S(1)} %bitcast.7, ...), custom_call_target="tpu_custom_call" | custom-call | tf_op jit(solution)/shard_map/pallas_call | solution.py:253
  50.7 0.0 collective-permute-done.9.refs_1_
  50.7 0.0 collective-permute-done.10.refs_2_
  50.7 0.0 collective-permute-done.11.refs_3_
  50.7 0.8 %shard_map.90 = bf16[256,256]{1,0:T(8,128)(2,1)} custom-call(bf16[256,256]{1,0:T(8,128)(2,1)S(1)} %get-tuple-element.6.refs_0_, bf16[256,256]{1,0:T(8,128)(2,1)S(1)} %collective-permute-done.9.refs_1_, bf16[256,256]{1,0:T(8,128)(2,1)S(1)} %collective-permute-done.10.refs_2_, bf16[256,256]{1,0:T(8,128)(2,1)S(1)} %collective-permute-done.11.refs_3_, ...), custom_call_target="tpu_custom_call" | custom-call | tf_op jit(solution)/shard_map/pallas_call | solution.py:281
Async XLA Ops:
  3.2 1.5 %copy-start = (bf16[256,3584]{1,0:T(8,128)(2,1)S(1)}, bf16[256,3584]{1,0:T(8,128)(2,1)}, u32[]{:S(2)}) copy-start(bf16[256,3584]{1,0:T(8,128)(2,1)} %grad_ref.1) | copy-start | bytes 5505028
  4.7 1.0 %copy-start.1 = (bf16[256,1024]{1,0:T(8,128)(2,1)S(1)}, bf16[256,1024]{1,0:T(8,128)(2,1)}, u32[]{:S(2)}) copy-start(bf16[256,1024]{1,0:T(8,128)(2,1)} %act_ref.1) | copy-start | bytes 1572868
  7.5 6.2 %collective-permute-start.2 = (f32[256,128]{1,0:T(8,128)S(1)}, f32[256,128]{1,0:T(8,128)S(1)}, u32[]{:S(2)}, u32[]{:S(2)}) collective-permute-start(f32[256,128]{1,0:T(8,128)S(1)} %shard_map.86.refs_0_), channel_id=1, source_target_pairs={{0,3},{1,0},{2,1},{3,2},{4,7},{5,4},{6,5},{7,6},{8,11},{9,8},{10,9... | collective-permute-start | bytes 393224 | tf_op jit(solution)/shard_map/ppermute | solution.py:290
  10.0 7.5 %collective-permute-start.1 = (f32[256,128]{1,0:T(8,128)S(1)}, f32[256,128]{1,0:T(8,128)S(1)}, u32[]{:S(2)}, u32[]{:S(2)}) collective-permute-start(f32[256,128]{1,0:T(8,128)S(1)} %shard_map.86.refs_0_), channel_id=1, source_target_pairs={{0,2},{1,3},{2,0},{3,1},{4,6},{5,7},{6,4},{7,5},{8,10},{9,11},{10,... | collective-permute-start | bytes 393224 | tf_op jit(solution)/shard_map/ppermute | solution.py:290
  10.6 6.9 %collective-permute-start = (f32[256,128]{1,0:T(8,128)S(1)}, f32[256,128]{1,0:T(8,128)S(1)}, u32[]{:S(2)}, u32[]{:S(2)}) collective-permute-start(f32[256,128]{1,0:T(8,128)S(1)} %shard_map.86.refs_0_), channel_id=1, source_target_pairs={{0,1},{1,2},{2,3},{3,0},{4,5},{5,6},{6,7},{7,4},{8,9},{9,10},{10,1... | collective-permute-start | bytes 393224 | tf_op jit(solution)/shard_map/ppermute | solution.py:290
  17.6 15.3 %collective-permute-start.5 = (bf16[128,256]{1,0:T(8,128)(2,1)S(1)}, bf16[128,256]{1,0:T(8,128)(2,1)S(1)}, u32[]{:S(2)}, u32[]{:S(2)}) collective-permute-start(bf16[128,256]{1,0:T(8,128)(2,1)S(1)} %shard_map.87.refs_0_), channel_id=1, source_target_pairs={{0,12},{4,0},{8,4},{12,8},{1,13},{5,1},{9,5},{13,9},{2,14},{6,2},{... | collective-permute-start | bytes 196616 | tf_op jit(solution)/shard_map/ppermute | solution.py:290
  21.5 11.5 %collective-permute-start.4 = (bf16[128,256]{1,0:T(8,128)(2,1)S(1)}, bf16[128,256]{1,0:T(8,128)(2,1)S(1)}, u32[]{:S(2)}, u32[]{:S(2)}) collective-permute-start(bf16[128,256]{1,0:T(8,128)(2,1)S(1)} %shard_map.87.refs_0_), channel_id=1, source_target_pairs={{0,8},{4,12},{8,0},{12,4},{1,9},{5,13},{9,1},{13,5},{2,10},{6,14},... | collective-permute-start | bytes 196616 | tf_op jit(solution)/shard_map/ppermute | solution.py:290
  21.5 11.5 %collective-permute-start.3 = (bf16[128,256]{1,0:T(8,128)(2,1)S(1)}, bf16[128,256]{1,0:T(8,128)(2,1)S(1)}, u32[]{:S(2)}, u32[]{:S(2)}) collective-permute-start(bf16[128,256]{1,0:T(8,128)(2,1)S(1)} %shard_map.87.refs_0_), channel_id=1, source_target_pairs={{0,4},{4,8},{8,12},{12,0},{1,5},{5,9},{9,13},{13,1},{2,6},{6,10},{... | collective-permute-start | bytes 196616 | tf_op jit(solution)/shard_map/ppermute | solution.py:290
  23.2 4.1 %collective-permute-start.8 = (f32[1,256]{1,0:T(1,128)S(1)}, f32[1,256]{1,0:T(1,128)S(1)}, u32[]{:S(2)}, u32[]{:S(2)}) collective-permute-start(f32[1,256]{1,0:T(1,128)S(1)} %bitcast.3), channel_id=1, source_target_pairs={{0,12},{4,0},{8,4},{12,8},{1,13},{5,1},{9,5},{13,9},{2,14},{6,2},{... | collective-permute-start | bytes 3080 | tf_op jit(solution)/shard_map/ppermute | solution.py:290
  26.0 4.5 %collective-permute-start.7 = (f32[1,256]{1,0:T(1,128)S(1)}, f32[1,256]{1,0:T(1,128)S(1)}, u32[]{:S(2)}, u32[]{:S(2)}) collective-permute-start(f32[1,256]{1,0:T(1,128)S(1)} %bitcast.4), channel_id=1, source_target_pairs={{0,8},{4,12},{8,0},{12,4},{1,9},{5,13},{9,1},{13,5},{2,10},{6,14},... | collective-permute-start | bytes 3080 | tf_op jit(solution)/shard_map/ppermute | solution.py:290
  27.3 5.6 %collective-permute-start.6 = (f32[1,256]{1,0:T(1,128)S(1)}, f32[1,256]{1,0:T(1,128)S(1)}, u32[]{:S(2)}, u32[]{:S(2)}) collective-permute-start(f32[1,256]{1,0:T(1,128)S(1)} %bitcast.5), channel_id=1, source_target_pairs={{0,4},{4,8},{8,12},{12,0},{1,5},{5,9},{9,13},{13,1},{2,6},{6,10},{... | collective-permute-start | bytes 3080 | tf_op jit(solution)/shard_map/ppermute | solution.py:290
  35.5 15.2 %collective-permute-start.9 = (bf16[256,256]{1,0:T(8,128)(2,1)S(1)}, bf16[256,256]{1,0:T(8,128)(2,1)S(1)}, u32[]{:S(2)}, u32[]{:S(2)}) collective-permute-start(bf16[256,256]{1,0:T(8,128)(2,1)S(1)} %get-tuple-element.7), channel_id=1, source_target_pairs={{0,12},{4,0},{8,4},{12,8},{1,13},{5,1},{9,5},{13,9},{2,14},{6,2},{... | collective-permute-start | bytes 393224 | tf_op jit(solution)/shard_map/ppermute | solution.py:290
  37.6 13.2 %collective-permute-start.10 = (bf16[256,256]{1,0:T(8,128)(2,1)S(1)}, bf16[256,256]{1,0:T(8,128)(2,1)S(1)}, u32[]{:S(2)}, u32[]{:S(2)}) collective-permute-start(bf16[256,256]{1,0:T(8,128)(2,1)S(1)} %get-tuple-element.8), channel_id=1, source_target_pairs={{0,8},{4,12},{8,0},{12,4},{1,9},{5,13},{9,1},{13,5},{2,10},{6,14},... | collective-permute-start | bytes 393224 | tf_op jit(solution)/shard_map/ppermute | solution.py:290
  37.6 13.2 %collective-permute-start.11 = (bf16[256,256]{1,0:T(8,128)(2,1)S(1)}, bf16[256,256]{1,0:T(8,128)(2,1)S(1)}, u32[]{:S(2)}, u32[]{:S(2)}) collective-permute-start(bf16[256,256]{1,0:T(8,128)(2,1)S(1)} %get-tuple-element.9), channel_id=1, source_target_pairs={{0,4},{4,8},{8,12},{12,0},{1,5},{5,9},{9,13},{13,1},{2,6},{6,10},{... | collective-permute-start | bytes 393224 | tf_op jit(solution)/shard_map/ppermute | solution.py:290

commit v2 on v1

--- a/solution.py
+++ b/solution.py
@@ -100,61 +100,100 @@
     return (hessian, (scores * mask[:, None]).astype(jnp.bfloat16))
 
 
-MEM = pltpu.CompilerParams(vmem_limit_bytes=48 * 1024 * 1024)
+MIB = 1024 * 1024
 NT = (((1,), (1,)), ((), ()))
-
-
-def project_kernel(act_ref, grad_ref, pin_ref, pout_ref, out_ref):
-    @pl.when(pl.program_id(0) == 0)
-    def _():
-        out_ref[...] = jnp.zeros_like(out_ref)
-
-    part_act = jnp.dot(act_ref[...], pin_ref[...], preferred_element_type=jnp.float32)
-    part_grad = jnp.dot(grad_ref[...], pout_ref[...], preferred_element_type=jnp.float32)
-    out_ref[...] += jnp.concatenate([part_act, part_grad], axis=1)
-
-
-def project(activations, out_grads, proj_in, proj_out, steps=4):
+TN = (((0,), (0,)), ((), ()))
+
+
+def params(mib):
+    return pltpu.CompilerParams(vmem_limit_bytes=mib * MIB)
+
+
+def project_kernel(act, grad, pin, pout, out_ref, act_v, grad_v, pin_v, pout_v, sems):
+    chunk = act.shape[1] // 2
+    copies, jobs = [], []
+    for source, weight, source_v, weight_v, is_grad in (
+        (grad, pout, grad_v, pout_v, 1),
+        (act, pin, act_v, pin_v, 0),
+    ):
+        for c in range(source.shape[1] // chunk):
+            span = pl.ds(c * chunk, chunk)
+            n = len(copies)
+            pair = [
+                pltpu.make_async_copy(weight.at[:, span], weight_v.at[:, span], sems.at[n]),
+                pltpu.make_async_copy(source.at[:, span], source_v.at[:, span], sems.at[n + 1]),
+            ]
+            for copy in pair:
+                copy.start()
+            copies += pair
+            jobs.append((pair, weight_v, source_v, span, is_grad))
+    rank = pin.shape[0]
+    totals = [jnp.zeros((rank, act.shape[0]), jnp.float32) for _ in range(2)]
+    for pair, weight_v, source_v, span, is_grad in jobs:
+        for copy in pair:
+            copy.wait()
+        totals[is_grad] += lax.dot_general(
+            weight_v[:, span], source_v[:, span], NT, preferred_element_type=jnp.float32
+        )
+    rows = out_ref.shape[1]
+    for q in range(out_ref.shape[0]):
+        total = totals[q * rows // rank]
+        start = q * rows % rank
+        out_ref[q] = total[start : start + rows]
+
+
+def project(activations, out_grads, proj_in_t, proj_out_t, parts):
     tok, d_here = activations.shape
     f_here = out_grads.shape[1]
-    rank = proj_in.shape[1]
+    rank = proj_in_t.shape[0]
+    copies = 2 * (2 + 2 * f_here // d_here)
     return pl.pallas_call(
         project_kernel,
-        grid=(steps,),
-        in_specs=[
-            pl.BlockSpec((tok, d_here // steps), lambda s: (0, s)),
-            pl.BlockSpec((tok, f_here // steps), lambda s: (0, s)),
-            pl.BlockSpec((d_here // steps, rank), lambda s: (s, 0)),
-            pl.BlockSpec((f_here // steps, rank), lambda s: (s, 0)),
+        in_specs=[pl.BlockSpec(memory_space=pl.ANY)] * 4,
+        out_shape=jax.ShapeDtypeStruct((parts, 2 * rank // parts, tok), jnp.float32),
+        scratch_shapes=[
+            pltpu.VMEM((tok, d_here), jnp.bfloat16),
+            pltpu.VMEM((tok, f_here), jnp.bfloat16),
+            pltpu.VMEM((rank, d_here), jnp.bfloat16),
+            pltpu.VMEM((rank, f_here), jnp.bfloat16),
+            pltpu.SemaphoreType.DMA((copies,)),
         ],
-        out_specs=pl.BlockSpec((tok, 2 * rank), lambda s: (0, 0)),
-        out_shape=jax.ShapeDtypeStruct((tok, 2 * rank), jnp.float32),
-        compiler_params=MEM,
-    )(activations, out_grads, proj_in, proj_out)
-
-
-def total_kernel(*refs):
-    out_ref = refs[-1]
-    total = refs[0][...]
-    for ref in refs[1:-1]:
-        total = total + ref[...]
-    out_ref[...] = total.T.astype(out_ref.dtype)
-
-
-def add_projections(parts):
-    tok, width = parts[0].shape
+        compiler_params=params(60),
+    )(activations, out_grads, proj_in_t, proj_out_t)
+
+
+def total_kernel(part_ref, weight_ref, out_ref):
+    rows = part_ref.shape[1]
+    total = part_ref[0]
+    for q in range(1, part_ref.shape[0]):
+        total = total + part_ref[q]
+    weight = jnp.broadcast_to(weight_ref[...], (out_ref.shape[1] - rows, weight_ref.shape[1]))
+    payload = jnp.concatenate([total, weight], axis=0).astype(out_ref.dtype)
+    for k in range(out_ref.shape[0]):
+        out_ref[k] = payload
+
+
+def add_projections(parts, weight, copies):
+    _, rows, tok = parts.shape
     return pl.pallas_call(
         total_kernel,
-        out_shape=jax.ShapeDtypeStruct((width, tok), jnp.bfloat16),
-        compiler_params=MEM,
-    )(*parts)
-
-
-def lay_out_factors(factor_refs, weight_refs, factors, weights):
-    tok = factor_refs[0].shape[1]
-    for k, (factor_ref, weight_ref) in enumerate(zip(factor_refs, weight_refs)):
-        factors[:, k * tok : (k + 1) * tok] = factor_ref[...].astype(jnp.float32)
-        weights[:, k * tok : (k + 1) * tok] = weight_ref[...]
+        out_shape=jax.ShapeDtypeStruct((copies, rows + 16, tok), jnp.bfloat16),
+        compiler_params=params(48),
+    )(parts, weight)
+
+
+def lay_out_factors(gathered, blocks, factors, weights):
+    per_block = gathered.shape[0] // blocks
+    tok = gathered.shape[2]
+    rows = factors.shape[0] // per_block
+    for k in range(blocks):
+        source = lax.rem(lax.axis_index("dp") + blocks - k, blocks) * per_block
+        span = slice(k * tok, (k + 1) * tok)
+        for q in range(per_block):
+            part = gathered[source + q]
+            factors[q * rows : (q + 1) * rows, span] = part[:rows].astype(jnp.float32)
+            if q == 0:
+                weights[:, span] = part[rows:].astype(jnp.float32)[:1]
 
 
 def range_scale(values):
@@ -166,12 +205,12 @@
     return scale
 
 
-def share_kernel(blocks, row_count, *refs):
-    factor_refs, weight_refs = refs[:blocks], refs[blocks : 2 * blocks]
-    query_ref = refs[2 * blocks]
-    out_refs = refs[2 * blocks + 1 : 3 * blocks + 1]
-    factors, weights, features = refs[3 * blocks + 1 :]
-    lay_out_factors(factor_refs, weight_refs, factors, weights)
+def share_kernel(blocks, row_count, gathered, query_ref, *refs):
+    out_refs = refs[:blocks]
+    factors, weights, features, query_v, sem = refs[blocks:]
+    fetch = pltpu.make_async_copy(query_ref, query_v, sem)
+    fetch.start()
+    lay_out_factors(gathered, blocks, factors, weights)
     rank = factors.shape[0] // 2
     tokens = factors.shape[1]
     tok = tokens // blocks
@@ -180,7 +219,8 @@
     for i in range(row_count):
         row = factors[pl.ds(first + i, 1), :]
         features[i * rank : (i + 1) * rank, :] = (row * act).astype(jnp.bfloat16)
-    plain = jnp.dot(query_ref[...], features[...], preferred_element_type=jnp.float32)
+    fetch.wait()
+    plain = lax.dot_general(query_v[...], features[...], TN, preferred_element_type=jnp.float32)
     weight = weights[...]
     live = weight > 0.0
     act = jnp.where(live, act, 0.0)
@@ -202,32 +242,32 @@
         out_ref[...] = share[:, k * tok : (k + 1) * tok].astype(jnp.bfloat16)
 
 
-def score_shares(factors, weights, queries_t, row_count):
-    blocks = len(factors)
-    width, tok = factors[0].shape
-    rows = queries_t.shape[1]
-    out = jax.ShapeDtypeStruct((queries_t.shape[0], tok), jnp.bfloat16)
+def score_shares(gathered, queries, blocks, rank, row_count):
+    tok = gathered.shape[2]
+    rows, count = queries.shape
+    out = jax.ShapeDtypeStruct((count, tok), jnp.bfloat16)
     return pl.pallas_call(
         functools.partial(share_kernel, blocks, row_count),
+        in_specs=[pl.BlockSpec(memory_space=pltpu.VMEM), pl.BlockSpec(memory_space=pl.ANY)],
         out_shape=[out] * blocks,
         scratch_shapes=[
-            pltpu.VMEM((width, tok * blocks), jnp.float32),
+            pltpu.VMEM((2 * rank, tok * blocks), jnp.float32),
             pltpu.VMEM((1, tok * blocks), jnp.float32),
             pltpu.VMEM((rows, tok * blocks), jnp.bfloat16),
+            pltpu.VMEM(queries.shape, queries.dtype),
+            pltpu.SemaphoreType.DMA,
         ],
-        compiler_params=MEM,
-    )(*factors, *weights, queries_t)
-
-
-def hessian_kernel(blocks, row_count, col_count, *refs):
-    factor_refs, weight_refs = refs[:blocks], refs[blocks : 2 * blocks]
-    out_ref, factors, weights, weighted, right = refs[2 * blocks :]
+        compiler_params=params(60),
+    )(gathered, queries)
+
+
+def hessian_kernel(blocks, row_count, col_count, gathered, out_ref, factors, weights, weighted, right):
     rank = factors.shape[0] // 2
     tokens = factors.shape[1]
 
     @pl.when(pl.program_id(0) == 0)
     def _():
-        lay_out_factors(factor_refs, weight_refs, factors, weights)
+        lay_out_factors(gathered, blocks, factors, weights)
         first = rank + lax.axis_index("dp") * row_count
         act, weight = factors[:rank, :], weights[...]
         for i in range(row_count):
@@ -244,27 +284,24 @@
     out_ref[...] = block / tokens
 
 
-def hessian_rows(factors, weights, row_count, col_count=8):
-    blocks = len(factors)
-    width, tok = factors[0].shape
-    rank = width // 2
+def hessian_rows(gathered, blocks, rank, row_count, col_count=8):
+    tok = gathered.shape[2]
     feat = rank * rank
     rows, cols = row_count * rank, col_count * rank
     return pl.pallas_call(
         functools.partial(hessian_kernel, blocks, row_count, col_count),
         grid=(feat // cols,),
-        in_specs=[pl.BlockSpec((width, tok), lambda s: (0, 0))] * blocks
-        + [pl.BlockSpec((1, tok), lambda s: (0, 0))] * blocks,
+        in_specs=[pl.BlockSpec(gathered.shape, lambda s: (0, 0, 0))],
         out_specs=pl.BlockSpec((rows, cols), lambda s: (0, s)),
         out_shape=jax.ShapeDtypeStruct((rows, feat), jnp.float32),
         scratch_shapes=[
-            pltpu.VMEM((width, tok * blocks), jnp.float32),
+            pltpu.VMEM((2 * rank, tok * blocks), jnp.float32),
             pltpu.VMEM((1, tok * blocks), jnp.float32),
             pltpu.VMEM((rows, tok * blocks), jnp.bfloat16),
             pltpu.VMEM((cols, tok * blocks), jnp.bfloat16),
         ],
-        compiler_params=MEM,
-    )(*factors, *weights)
+        compiler_params=params(48),
+    )(gathered)
 
 
 def finish_kernel(*refs):
@@ -281,33 +318,31 @@
     return pl.pallas_call(
         finish_kernel,
         out_shape=jax.ShapeDtypeStruct((tok, count), jnp.bfloat16),
-        compiler_params=MEM,
+        compiler_params=params(48),
     )(*shares, weight)
 
 
 def shifted(array, axis, by):
     count = lax.axis_size(axis)
     return lax.ppermute(array, axis, [(i, (i + by) % count) for i in range(count)])
-
-
-def from_all(array, axis):
-    return [array] + [shifted(array, axis, k) for k in range(1, lax.axis_size(axis))]
 
 
 def few_tokens(activations, out_grads, proj_in, proj_out, queries, lengths, credit):
     tok_rows = activations.shape[0]
     seq_len = tok_rows // lengths.shape[0]
     dp_count = lax.axis_size("dp")
+    query_count = lax.axis_size("query")
     rank = proj_in.shape[1]
     row_count = rank // dp_count
     live = jnp.arange(seq_len, dtype=jnp.int32)[None, :] < lengths[:, None]
     weight = (credit[:, None].astype(jnp.float32) * live.astype(jnp.float32)).reshape(1, -1)
-    weights = from_all(weight, "dp")
-    part = project(activations, out_grads, proj_in, proj_out)
-    factors = from_all(add_projections(from_all(part, "query")), "dp")
-    shares = score_shares(factors, weights, queries.T, row_count)
+    parts = project(activations, out_grads, proj_in.T, proj_out.T, query_count)
+    parts = lax.all_to_all(parts, "query", 0, 0, tiled=True)
+    payloads = add_projections(parts, weight, dp_count * query_count)
+    gathered = lax.all_to_all(payloads, ("dp", "query"), 0, 0, tiled=True)
+    shares = score_shares(gathered, queries, dp_count, rank, row_count)
     arrived = [shares[0]] + [shifted(shares[k], "dp", -k) for k in range(1, dp_count)]
-    hessian = hessian_rows(factors, weights, row_count)
+    hessian = hessian_rows(gathered, dp_count, rank, row_count)
     return hessian, finish_scores(arrived, weight)
 
 

time: 51.9 us -> 54.5 us (1.050)
  blocking collectives: 0 us -> 17.6 us
  starting transfers between devices: 16.7 us -> 8.01 us
  waiting for transfers between devices: 8.71 us -> 3.26 us
  local copies, waits for them, and re-layouts: 6.3 us -> 1 us
  Pallas kernels: 17.8 us -> 22.1 us
    all_to_all x0 -> x1, blocking collectives: none -> 17.6 us  [few_tokens(): gathered = lax.all_to_all(payloads, ('dp', 'query'), 0, 0, tiled=True)]
    ppermute x12 -> x3, starting transfers between devices: 16.7 us -> 3.79 us  [shifted(): lax.ppermute(array, axis, [(i, (i + by) % count) for i in range(count)])]
    ppermute x12 -> x3, waiting for transfers between devices: 8.71 us -> 0.01 us  [shifted(): lax.ppermute(array, axis, [(i, (i + by) % count) for i in range(count)])]
    unnamed x7 -> x4, local copies, waits for them, and re-layouts: 6.3 us -> 1 us
    pallas_call x3, Pallas kernels: 4.47 us -> 8.82 us  [the longest x1 5.21 us: score_shares(): pl.pallas_call(functools.partial(share_kernel, blocks, row_count), in_spe...]
    all_to_all x0 -> x1, starting transfers between devices: none -> 4.22 us  [few_tokens(): parts = lax.all_to_all(parts, 'query', 0, 0, tiled=True)]
    all_to_all x0 -> x1, waiting for transfers between devices: none -> 3.25 us  [few_tokens(): parts = lax.all_to_all(parts, 'query', 0, 0, tiled=True)]
  transfers between devices with their start and end apart: 12 -> 4, of which waited for: 4 -> 1; matrix products, arithmetic and copies ran while one was open for 5% -> 3% of each run, Pallas kernels for 24% -> 23%
where the time goes in v2:
time: 54.5 us; the launch traced here: 54.1 us
  Pallas kernels  22.1 us (41%)
  blocking collectives  17.6 us (32%)
  starting transfers between devices  8.01 us (15%)
  waiting for transfers between devices  3.26 us (6%)
  other arithmetic  1.38 us (3%)
  local copies, waits for them, and re-layouts  1 us (2%)
  between operations  0.67 us (1%)
    all_to_all x1, blocking collectives, few_tokens(): gathered = lax.all_to_all(payloads, ('dp', 'query'), 0, 0, tiled=True)  17.6 us
    pallas_call x1, Pallas kernels, hessian_rows(): pl.pallas_call(functools.partial(hessian_kernel, blocks, row_count, col_c...  12.5 us
    pallas_call x1, Pallas kernels, score_shares(): pl.pallas_call(functools.partial(share_kernel, blocks, row_count), in_spe...  5.21 us
    all_to_all x1, starting transfers between devices, few_tokens(): parts = lax.all_to_all(parts, 'query', 0, 0, tiled=True)  4.22 us
    ppermute x3, starting transfers between devices, shifted(): lax.ppermute(array, axis, [(i, (i + by) % count) for i in range(count)])  3.79 us
    pallas_call x1, Pallas kernels, project(): pl.pallas_call(project_kernel, in_specs=[pl.BlockSpec(memory_space=pl.ANY...  3.58 us
    all_to_all x1, waiting for transfers between devices, few_tokens(): parts = lax.all_to_all(parts, 'query', 0, 0, tiled=True)  3.25 us
  transfers between devices with their start and end apart: 4, of which 1 were waited for; matrix products, arithmetic and copies ran while one was open for 3% of the time, Pallas kernels for 23%

profile of v2, /device:TPU:0, one launch (start us, length us, event | category | flops | bytes accessed | tf_op | source)
XLA Modules:
  0.0 54.1 jit_solution(10034101913952797295)
XLA Ops:
  0.6 3.6 %shard_map.86 = f32[4,32,256]{2,1,0:T(8,128)} custom-call(bf16[256,1024]{1,0:T(8,128)(2,1)} %act.1, bf16[256,3584]{1,0:T(8,128)(2,1)} %grad.1, bf16[64,1024]{1,0:T(8,128)(2,1)} %bitcast.6, bf16[64,3584]{1,0:T(8,128)(2,1)} %bitcast.5), custom_call_target="tpu_custom_call" | custom-call | tf_op jit(solution)/shard_map/pallas_call | solution.py:150
  4.2 4.2 %all-to-all-start = ((f32[4,32,256]{2,1,0:T(8,128)}), f32[4,32,256]{2,1,0:T(8,128)S(1)}, u32[]{:S(2)}, u32[]{:S(2)}) async-start(f32[4,32,256]{2,1,0:T(8,128)} %shard_map.86), calls=%async_computation | async-start | bytes 262144 | tf_op jit(solution)/shard_map/all_to_all | solution.py:340
  8.4 0.7 %convert_element_type.5 = f32[2]{0:T(128)S(1)} convert(s32[2]{0:T(128)} %param.13) | non-fusion elementwise | flops 2 | bytes 16 | tf_op jit(solution)/shard_map/convert_element_type | solution.py:338
  9.1 0.7 %compare_select_fusion = f32[2,128]{1,0:T(2,128)S(1)} fusion(f32[2]{0:T(128)S(1)} %convert_element_type.5, s32[2]{0:T(128)} %param.12), kind=kLoop, calls=%fused_computation | loop fusion | flops 512 | bytes 1040 | tf_op jit(solution)/shard_map/mul | solution.py:338
  9.8 3.3 %all-to-all-done.part_ref = f32[4,32,256]{2,1,0:T(8,128)S(1)} async-done(((f32[4,32,256]{2,1,0:T(8,128)}), f32[4,32,256]{2,1,0:T(8,128)S(1)}, u32[]{:S(2)}, u32[]{:S(2)}) %all-to-all-start) | async-done | bytes 131104 | tf_op jit(solution)/shard_map/all_to_all | solution.py:340
  13.1 17.6 %all_to_all.10.gathered = bf16[16,48,256]{2,1,0:T(8,128)(2,1)} all-to-all(bf16[16,48,256]{2,1,0:T(8,128)(2,1)S(1)} %shard_map.87), channel_id=1, replica_groups=mesh['groups'=2,'dp'=4,'query'=4] {'dp','query'}, dimensions={0} | all-to-all | bytes 786432 | tf_op jit(solution)/shard_map/all_to_all | solution.py:342
  30.7 5.2 %shard_map.89 = (bf16[256,256]{1,0:T(8,128)(2,1)}, bf16[256,256]{1,0:T(8,128)(2,1)}, bf16[256,256]{1,0:T(8,128)(2,1)}, bf16[256,256]{1,0:T(8,128)(2,1)}) custom-call(bf16[16,48,256]{2,1,0:T(8,128)(2,1)} %all_to_all.10.gathered, bf16[1024,256]{1,0:T(8,128)(2,1)} %query_ref.1), custom_call_target="tpu_custom_call" | custom-call | tf_op jit(solution)/shard_map/pallas_call | solution.py:249
  36.0 1.3 %collective-permute-start = (bf16[256,256]{1,0:T(8,128)(2,1)}, bf16[256,256]{1,0:T(8,128)(2,1)S(1)}, u32[]{:S(2)}, u32[]{:S(2)}) collective-permute-start(bf16[256,256]{1,0:T(8,128)(2,1)} %get-tuple-element.7), channel_id=1, source_target_pairs={{0,12},{4,0},{8,4},{12,8},{1,13},{5,1},{9,5},{13,9},{2,14},{6,2},{... | collective-permute-start | bytes 393224 | tf_op jit(solution)/shard_map/ppermute | solution.py:327
  37.3 0.9 %collective-permute-start.1 = (bf16[256,256]{1,0:T(8,128)(2,1)}, bf16[256,256]{1,0:T(8,128)(2,1)S(1)}, u32[]{:S(2)}, u32[]{:S(2)}) collective-permute-start(bf16[256,256]{1,0:T(8,128)(2,1)} %get-tuple-element.8), channel_id=1, source_target_pairs={{0,8},{4,12},{8,0},{12,4},{1,9},{5,13},{9,1},{13,5},{2,10},{6,14},... | collective-permute-start | bytes 393224 | tf_op jit(solution)/shard_map/ppermute | solution.py:327
  38.2 1.6 %collective-permute-start.2 = (bf16[256,256]{1,0:T(8,128)(2,1)}, bf16[256,256]{1,0:T(8,128)(2,1)S(1)}, u32[]{:S(2)}, u32[]{:S(2)}) collective-permute-start(bf16[256,256]{1,0:T(8,128)(2,1)} %get-tuple-element.9), channel_id=1, source_target_pairs={{0,4},{4,8},{8,12},{12,0},{1,5},{5,9},{9,13},{13,1},{2,6},{6,10},{... | collective-permute-start | bytes 393224 | tf_op jit(solution)/shard_map/ppermute | solution.py:327
  39.7 0.0 copy-start
  39.7 1.0 %copy-done = bf16[16,48,256]{2,1,0:T(8,128)(2,1)S(1)} copy-done((bf16[16,48,256]{2,1,0:T(8,128)(2,1)S(1)}, bf16[16,48,256]{2,1,0:T(8,128)(2,1)}, u32[]{:S(2)}) %copy-start) | copy-done | bytes 393240
  40.7 0.0 copy-start.1
  40.7 12.5 %shard_map.88 = f32[1024,4096]{1,0:T(8,128)} custom-call(bf16[16,48,256]{2,1,0:T(8,128)(2,1)S(1)} %copy-done), custom_call_target="tpu_custom_call" | custom-call | tf_op jit(solution)/shard_map/pallas_call | solution.py:291
  53.2 0.0 collective-permute-done.refs_1_
  53.2 0.0 collective-permute-done.1.refs_2_
  53.3 0.0 collective-permute-done.2.refs_3_
  53.3 0.0 copy-done.1
  53.3 0.8 %shard_map.90 = bf16[256,256]{1,0:T(8,128)(2,1)} custom-call(bf16[256,256]{1,0:T(8,128)(2,1)S(1)} %copy-done.1, bf16[256,256]{1,0:T(8,128)(2,1)S(1)} %collective-permute-done.refs_1_, bf16[256,256]{1,0:T(8,128)(2,1)S(1)} %collective-permute-done.1.refs_2_, bf16[256,256]{1,0:T(8,128)(2,1)S(1)} %collective-permute-done.2.refs_3_, f32[1,256]{1,0:T(1,128)S(1)} %bitcast.4), custom_call_target="tpu_custom_call" | custom-call | tf_op jit(solution)/shard_map/pallas_call | solution.py:318
  (1 shorter events, 0.0 us)
Async XLA Ops:
  4.2 8.9 %all-to-all-start = ((f32[4,32,256]{2,1,0:T(8,128)}), f32[4,32,256]{2,1,0:T(8,128)S(1)}, u32[]{:S(2)}, u32[]{:S(2)}) async-start(f32[4,32,256]{2,1,0:T(8,128)} %shard_map.86), calls=%async_computation | async-start | bytes 262144 | tf_op jit(solution)/shard_map/all_to_all | solution.py:340
  36.0 17.3 %collective-permute-start = (bf16[256,256]{1,0:T(8,128)(2,1)}, bf16[256,256]{1,0:T(8,128)(2,1)S(1)}, u32[]{:S(2)}, u32[]{:S(2)}) collective-permute-start(bf16[256,256]{1,0:T(8,128)(2,1)} %get-tuple-element.7), channel_id=1, source_target_pairs={{0,12},{4,0},{8,4},{12,8},{1,13},{5,1},{9,5},{13,9},{2,14},{6,2},{... | collective-permute-start | bytes 393224 | tf_op jit(solution)/shard_map/ppermute | solution.py:327
  37.3 16.0 %collective-permute-start.1 = (bf16[256,256]{1,0:T(8,128)(2,1)}, bf16[256,256]{1,0:T(8,128)(2,1)S(1)}, u32[]{:S(2)}, u32[]{:S(2)}) collective-permute-start(bf16[256,256]{1,0:T(8,128)(2,1)} %get-tuple-element.8), channel_id=1, source_target_pairs={{0,8},{4,12},{8,0},{12,4},{1,9},{5,13},{9,1},{13,5},{2,10},{6,14},... | collective-permute-start | bytes 393224 | tf_op jit(solution)/shard_map/ppermute | solution.py:327
  38.2 15.1 %collective-permute-start.2 = (bf16[256,256]{1,0:T(8,128)(2,1)}, bf16[256,256]{1,0:T(8,128)(2,1)S(1)}, u32[]{:S(2)}, u32[]{:S(2)}) collective-permute-start(bf16[256,256]{1,0:T(8,128)(2,1)} %get-tuple-element.9), channel_id=1, source_target_pairs={{0,4},{4,8},{8,12},{12,0},{1,5},{5,9},{9,13},{13,1},{2,6},{6,10},{... | collective-permute-start | bytes 393224 | tf_op jit(solution)/shard_map/ppermute | solution.py:327
  39.7 1.0 %copy-start = (bf16[16,48,256]{2,1,0:T(8,128)(2,1)S(1)}, bf16[16,48,256]{2,1,0:T(8,128)(2,1)}, u32[]{:S(2)}) copy-start(bf16[16,48,256]{2,1,0:T(8,128)(2,1)} %all_to_all.10.gathered) | copy-start | bytes 1179652
  40.7 12.5 %copy-start.1 = (bf16[256,256]{1,0:T(8,128)(2,1)S(1)}, bf16[256,256]{1,0:T(8,128)(2,1)}, u32[]{:S(2)}) copy-start(bf16[256,256]{1,0:T(8,128)(2,1)} %get-tuple-element.6.refs_0_) | copy-start | bytes 393220

commit v3 on v0

--- a/solution.py
+++ b/solution.py
@@ -1,6 +1,9 @@
+import functools
 import jax
 import jax.numpy as jnp
 from jax import lax
+from jax.experimental import pallas as pl
+from jax.experimental.pallas import tpu as pltpu
 from jax.sharding import PartitionSpec as P
 
 
@@ -42,7 +45,7 @@
     return (high_part, middle_part, low_part)
 
 
-def per_device(activations, out_grads, proj_in, proj_out, queries, lengths, credit):
+def many_tokens(activations, out_grads, proj_in, proj_out, queries, lengths, credit):
     tok_rows = activations.shape[0]
     seq_len = tok_rows // lengths.shape[0]
     dp_count = lax.axis_size("dp")
@@ -97,6 +100,295 @@
     return (hessian, (scores * mask[:, None]).astype(jnp.bfloat16))
 
 
+MIB = 1024 * 1024
+NT = (((1,), (1,)), ((), ()))
+
+
+def params(mib):
+    return pltpu.CompilerParams(vmem_limit_bytes=int(mib * MIB))
+
+
+def project_kernel(act, grad, pin, pout, keep_ref, send_ref, act_v, grad_v, pin_v, pout_v, sems):
+    chunk = act.shape[1]
+    while grad.shape[1] % chunk:
+        chunk //= 2
+    spans = [pl.ds(c, chunk) for c in range(0, grad.shape[1], chunk)]
+    copies = [pltpu.make_async_copy(s, d, sems.at[n]) for n, (s, d) in enumerate(((pin, pin_v), (act, act_v), (pout, pout_v)))]
+    copies += [
+        pltpu.make_async_copy(grad.at[:, span], grad_v.at[:, span], sems.at[3 + n])
+        for n, span in enumerate(spans)
+    ]
+    for copy in copies:
+        copy.start()
+    copies[0].wait()
+    copies[1].wait()
+    part_act = lax.dot_general(pin_v[...], act_v[...], NT, preferred_element_type=jnp.float32)
+    copies[2].wait()
+    part_grad = jnp.zeros_like(part_act)
+    for copy, span in zip(copies[3:], spans):
+        copy.wait()
+        part_grad += lax.dot_general(
+            pout_v[:, span], grad_v[:, span], NT, preferred_element_type=jnp.float32
+        )
+    even = lax.rem(lax.axis_index("query"), 2) == 0
+    keep_ref[...] = jnp.where(even, part_act, part_grad)
+    send_ref[...] = jnp.where(even, part_grad, part_act)
+
+
+def project(activations, out_grads, proj_in_t, proj_out_t):
+    tok, d_here = activations.shape
+    f_here = out_grads.shape[1]
+    rank = proj_in_t.shape[0]
+    out = jax.ShapeDtypeStruct((rank, tok), jnp.float32)
+    return pl.pallas_call(
+        project_kernel,
+        in_specs=[pl.BlockSpec(memory_space=pl.ANY)] * 4,
+        out_shape=[out, out],
+        scratch_shapes=[
+            pltpu.VMEM((tok, d_here), jnp.bfloat16),
+            pltpu.VMEM((tok, f_here), jnp.bfloat16),
+            pltpu.VMEM((rank, d_here), jnp.bfloat16),
+            pltpu.VMEM((rank, f_here), jnp.bfloat16),
+            pltpu.SemaphoreType.DMA((3 + f_here // 128,)),
+        ],
+        compiler_params=params(53.75),
+    )(activations, out_grads, proj_in_t, proj_out_t)
+
+
+def add_kernel(one_ref, other_ref, out_ref):
+    out_ref[...] = one_ref[...] + other_ref[...]
+
+
+def add(one, other):
+    return pl.pallas_call(
+        add_kernel,
+        out_shape=jax.ShapeDtypeStruct(one.shape, one.dtype),
+        compiler_params=params(40),
+    )(one, other)
+
+
+def payload_kernel(one_ref, other_ref, weight_ref, out_ref):
+    total = one_ref[...] + other_ref[...]
+    weight = jnp.broadcast_to(weight_ref[...], (16, weight_ref.shape[1]))
+    out_ref[...] = jnp.concatenate([total, weight], axis=0).astype(out_ref.dtype)
+
+
+def add_to_payload(one, other, weight):
+    rows, tok = one.shape
+    return pl.pallas_call(
+        payload_kernel,
+        out_shape=jax.ShapeDtypeStruct((rows + 16, tok), jnp.bfloat16),
+        compiler_params=params(40),
+    )(one, other, weight)
+
+
+def stack_kernel(*refs):
+    for k, ref in enumerate(refs[:-1]):
+        refs[-1][k] = ref[...]
+
+
+def stack(parts):
+    return pl.pallas_call(
+        stack_kernel,
+        out_shape=jax.ShapeDtypeStruct((len(parts),) + parts[0].shape, parts[0].dtype),
+        compiler_params=params(40),
+    )(*parts)
+
+
+def lay_out_factors(mine, other, factors, weights):
+    blocks, _, tok = mine.shape
+    rank = factors.shape[0] // 2
+    here = pl.multiple_of(lax.rem(lax.axis_index("query"), 2) * rank, rank)
+    there = pl.multiple_of(rank - here, rank)
+    for k in range(blocks):
+        span = slice(k * tok, (k + 1) * tok)
+        factors[pl.ds(here, rank), span] = mine[k, :rank].astype(jnp.float32)
+        factors[pl.ds(there, rank), span] = other[k, :rank].astype(jnp.float32)
+        weights[:, span] = mine[k, rank:].astype(jnp.float32)[:1]
+
+
+def range_scale(values):
+    top = jnp.max(jnp.abs(values), keepdims=True)
+    scale = jnp.ones_like(top)
+    for low in (16, 48, 80, 112):
+        scale = jnp.where(top > 2.0**low, 2.0 ** -min(low + 16, 126), scale)
+        scale = jnp.where(top < 2.0**-low, 2.0 ** min(low + 16, 126), scale)
+    return scale
+
+
+def share_kernel(row_count, mine, other, query_ref, *refs):
+    factors, weights, features = refs[-3:]
+    out_refs = refs[:-3]
+    lay_out_factors(mine, other, factors, weights)
+    rank = factors.shape[0] // 2
+    tokens = factors.shape[1]
+    tok = tokens // len(out_refs)
+    first = rank + lax.axis_index("dp") * row_count
+    act = factors[:rank, :]
+    for i in range(row_count):
+        row = factors[pl.ds(first + i, 1), :]
+        features[i * rank : (i + 1) * rank, :] = (row * act).astype(jnp.bfloat16)
+    plain = jnp.dot(query_ref[...], features[...], preferred_element_type=jnp.float32)
+    weight = weights[...]
+    live = weight > 0.0
+    act = jnp.where(live, act, 0.0)
+    grad = jnp.where(live, factors[rank:, :], 0.0)
+    act_scale, grad_scale = range_scale(act), range_scale(grad)
+    act, grad = act * act_scale, grad * grad_scale
+    norms = jnp.sum(act * act, axis=0, keepdims=True) * jnp.sum(grad * grad, axis=0, keepdims=True)
+    level = jnp.sum(weight * norms, axis=1, keepdims=True) / (tokens * rank * rank)
+    step = 1.1 * level
+    act_b, grad_b = act.astype(jnp.bfloat16), grad.astype(jnp.bfloat16)
+    gram = jnp.dot(act.T.astype(jnp.bfloat16), act_b, preferred_element_type=jnp.float32) * jnp.dot(
+        grad.T.astype(jnp.bfloat16), grad_b, preferred_element_type=jnp.float32
+    )
+    gram = (gram * (1.0 / (tokens * step))).astype(jnp.bfloat16)
+    image = jnp.dot((plain * weight).astype(jnp.bfloat16), gram, preferred_element_type=jnp.float32)
+    scale = act_scale * grad_scale
+    share = ((2.0 - 0.1 / 1.1) * plain - image) * scale * (scale / step)
+    for k, out_ref in enumerate(out_refs):
+        out_ref[...] = share[:, k * tok : (k + 1) * tok].astype(jnp.bfloat16)
+
+
+def score_shares(mine, other, queries_t, rank, row_count):
+    blocks, _, tok = mine.shape
+    count, rows = queries_t.shape
+    out = jax.ShapeDtypeStruct((count, tok), jnp.bfloat16)
+    return pl.pallas_call(
+        functools.partial(share_kernel, row_count),
+        out_shape=[out] * blocks,
+        scratch_shapes=[
+            pltpu.VMEM((2 * rank, tok * blocks), jnp.float32),
+            pltpu.VMEM((1, tok * blocks), jnp.float32),
+            pltpu.VMEM((rows, tok * blocks), jnp.bfloat16),
+        ],
+        compiler_params=params(40),
+    )(mine, other, queries_t)
+
+
+def hessian_kernel(row_count, col_count, mine, other, out, factors, weights, weighted, *scratch):
+    rights, results, sems = scratch[:2], scratch[2:4], scratch[4]
+    rank = factors.shape[0] // 2
+    tokens = factors.shape[1]
+    cols = col_count * rank
+    steps = rank // col_count
+    lay_out_factors(mine, other, factors, weights)
+    act, weight = factors[:rank, :], weights[...]
+    first = rank + lax.axis_index("dp") * row_count
+    for i in range(row_count):
+        left = (factors[pl.ds(first + i, 1), :] * act).astype(jnp.bfloat16)
+        left = (weight * left.astype(jnp.float32)).astype(jnp.bfloat16)
+        weighted[i * rank : (i + 1) * rank, :] = left
+
+    def build(step):
+        for i in range(col_count):
+            row = rank + step * col_count + i
+            right = (factors[row : row + 1, :] * act).astype(jnp.bfloat16)
+            rights[step % 2][i * rank : (i + 1) * rank, :] = right
+
+    def store(step):
+        return pltpu.make_async_copy(
+            results[step % 2], out.at[:, pl.ds(step * cols, cols)], sems.at[step % 2]
+        )
+
+    build(0)
+    for step in range(steps):
+        if step + 1 < steps:
+            build(step + 1)
+        if step > 1:
+            store(step - 2).wait()
+        block = lax.dot_general(
+            weighted[...], rights[step % 2][...], NT, preferred_element_type=jnp.float32
+        )
+        results[step % 2][...] = block * (1.0 / tokens)
+        store(step).start()
+    for step in range(max(steps - 2, 0), steps):
+        store(step).wait()
+
+
+def hessian_rows(mine, other, rank, row_count, col_count=8):
+    blocks, _, tok = mine.shape
+    feat = rank * rank
+    rows, cols = row_count * rank, col_count * rank
+    return pl.pallas_call(
+        functools.partial(hessian_kernel, row_count, col_count),
+        out_specs=pl.BlockSpec(memory_space=pl.ANY),
+        out_shape=jax.ShapeDtypeStruct((rows, feat), jnp.float32),
+        scratch_shapes=[
+            pltpu.VMEM((2 * rank, tok * blocks), jnp.float32),
+            pltpu.VMEM((1, tok * blocks), jnp.float32),
+            pltpu.VMEM((rows, tok * blocks), jnp.bfloat16),
+            pltpu.VMEM((cols, tok * blocks), jnp.bfloat16),
+            pltpu.VMEM((cols, tok * blocks), jnp.bfloat16),
+            pltpu.VMEM((rows, cols), jnp.float32),
+            pltpu.VMEM((rows, cols), jnp.float32),
+            pltpu.SemaphoreType.DMA((2,)),
+        ],
+        compiler_params=params(40),
+    )(mine, other)
+
+
+def finish_kernel(*refs):
+    weight_ref, out_ref = refs[-2], refs[-1]
+    total = refs[0][...].astype(jnp.float32)
+    for ref in refs[1:-2]:
+        total = total + ref[...].astype(jnp.float32)
+    total = jnp.where(weight_ref[...] > 0.0, total, 0.0)
+    out_ref[...] = total.T.astype(out_ref.dtype)
+
+
+def finish_scores(shares, weight):
+    count, tok = shares[0].shape
+    return pl.pallas_call(
+        finish_kernel,
+        out_shape=jax.ShapeDtypeStruct((tok, count), jnp.bfloat16),
+        compiler_params=params(40),
+    )(*shares, weight)
+
+
+def swapped(array, axis, distance):
+    return lax.ppermute(array, axis, [(i, i ^ distance) for i in range(lax.axis_size(axis))])
+
+
+def few_tokens(activations, out_grads, proj_in, proj_out, queries, lengths, credit):
+    tok_rows = activations.shape[0]
+    seq_len = tok_rows // lengths.shape[0]
+    dp_count = lax.axis_size("dp")
+    query_count = lax.axis_size("query")
+    rank = proj_in.shape[1]
+    row_count = rank // dp_count
+    live = jnp.arange(seq_len, dtype=jnp.int32)[None, :] < lengths[:, None]
+    weight = (credit[:, None].astype(jnp.float32) * live.astype(jnp.float32)).reshape(1, -1)
+    keep, send = project(activations, out_grads, proj_in.T, proj_out.T)
+    other = swapped(send, "query", 1)
+    distance = 2
+    while distance < query_count:
+        keep = add(keep, other)
+        other = swapped(keep, "query", distance)
+        distance *= 2
+    payload = add_to_payload(keep, other, weight)
+    others = [swapped(payload, "dp", k) for k in reversed(range(1, dp_count))]
+    mine = stack([payload] + others[::-1])
+    other = swapped(mine, "query", 1)
+    shares = score_shares(mine, other, queries.T, rank, row_count)
+    arrived = [swapped(shares[k], "dp", k) for k in reversed(range(1, dp_count))]
+    hessian = hessian_rows(mine, other, rank, row_count)
+    return hessian, finish_scores([shares[0]] + arrived, weight)
+
+
+def power_of_two(count):
+    return count & (count - 1) == 0
+
+
+def per_device(activations, *others):
+    rank = others[1].shape[1]
+    dp_count, query_count = lax.axis_size("dp"), lax.axis_size("query")
+    pairs = query_count > 1 and power_of_two(query_count) and power_of_two(dp_count)
+    if pairs and activations.shape[0] * dp_count <= rank * rank:
+        return few_tokens(activations, *others)
+    return many_tokens(activations, *others)
+
+
 def solution(mesh):
     placed = (
         P(("groups", "dp"), "query"),

time: 303 us -> 41.4 us (0.14)
  waiting for transfers between devices: 167 us -> 6.33 us
  blocking collectives: 65 us -> 0 us
  matrix products: 31.5 us -> 0 us
  Pallas kernels: 0 us -> 18.9 us
  between operations: 15.2 us -> 0.71 us
  starting transfers between devices: 0.12 us -> 12.6 us
  other arithmetic: 13.8 us -> 1.38 us
  local copies, waits for them, and re-layouts: 10.5 us -> 1.25 us
    all_gather x3 -> x0, waiting for transfers between devices: 166 us -> none  [the longest x1 103 us: per_device(): hessian = lax.all_gather(owned, 'query', axis=1, tiled=True) / all_tokens]
    all_gather x3 -> x0, blocking collectives: 38 us -> none  [the longest x1 13.7 us: per_device(): lax.all_gather(act_proj, 'dp', axis=0, tiled=True)]
    dot_general x8 -> x0, matrix products: 31.5 us -> none  [the longest x4 18.1 us: per_device(): jnp.dot(columns, piece, preferred_element_type=jnp.float32)]
    psum x2 -> x0, blocking collectives: 27.1 us -> none  [the longest x1 14.5 us: per_device(): sum_act, sum_grad = lax.psum((part_act, part_grad), 'query')]
    pallas_call x0 -> x7, Pallas kernels: none -> 18.9 us  [the longest x1 12.4 us: hessian_rows(): pl.pallas_call(functools.partial(hessian_kernel, row_count, col_count), o...]
    ppermute x0 -> x9, starting transfers between devices: none -> 12.6 us  [swapped(): lax.ppermute(array, axis, [(i, i ^ distance) for i in range(lax.axis_size...]
    unnamed x13 -> x1, local copies, waits for them, and re-layouts: 10.5 us -> 1.25 us
    div x1 -> x0, other arithmetic: 6.52 us -> none  [per_device(): hessian = lax.all_gather(owned, 'query', axis=1, tiled=True) / all_tokens]
  transfers between devices with their start and end apart: 3 -> 9, of which waited for: 3 -> 5; matrix products, arithmetic and copies ran while one was open for 3% -> 6% of each run, Pallas kernels for 0% -> 30%
where the time goes in v3:
time: 41.4 us; the launch traced here: 41.2 us
  Pallas kernels  18.9 us (46%)
  starting transfers between devices  12.6 us (30%)
  waiting for transfers between devices  6.33 us (15%)
  other arithmetic  1.38 us (3%)
  local copies, waits for them, and re-layouts  1.25 us (3%)
  between operations  0.71 us (2%)
    ppermute x9, starting transfers between devices, swapped(): lax.ppermute(array, axis, [(i, i ^ distance) for i in range(lax.axis_size...  12.6 us
    pallas_call x1, Pallas kernels, hessian_rows(): pl.pallas_call(functools.partial(hessian_kernel, row_count, col_count), o...  12.4 us
    ppermute x9, waiting for transfers between devices, swapped(): lax.ppermute(array, axis, [(i, i ^ distance) for i in range(lax.axis_size...  6.33 us
    pallas_call x1, Pallas kernels, project(): pl.pallas_call(project_kernel, in_specs=[pl.BlockSpec(memory_space=pl.ANY...  3.04 us
    pallas_call x1, Pallas kernels, score_shares(): pl.pallas_call(functools.partial(share_kernel, row_count), out_shape=[out...  2.6 us
    unnamed x1, local copies, waits for them, and re-layouts  1.25 us
  transfers between devices with their start and end apart: 9, of which 5 were waited for; matrix products, arithmetic and copies ran while one was open for 6% of the time, Pallas kernels for 30%

profile of v3, /device:TPU:0, one launch (start us, length us, event | category | flops | bytes accessed | tf_op | source)
XLA Modules:
  0.0 41.2 jit_solution(15541337701347353714)
XLA Ops:
  0.6 3.0 %shard_map.86 = (f32[64,256]{1,0:T(8,128)S(1)}, f32[64,256]{1,0:T(8,128)S(1)}) custom-call(bf16[256,1024]{1,0:T(8,128)(2,1)} %act.1, bf16[256,3584]{1,0:T(8,128)(2,1)} %grad.1, bf16[64,1024]{1,0:T(8,128)(2,1)} %bitcast.8, bf16[64,3584]{1,0:T(8,128)(2,1)} %bitcast.7), custom_call_target="tpu_custom_call" | custom-call | tf_op jit(solution)/shard_map/pallas_call | solution.py:143
  3.7 0.5 %collective-permute-start = (f32[64,256]{1,0:T(8,128)S(1)}, f32[64,256]{1,0:T(8,128)S(1)}, u32[]{:S(2)}, u32[]{:S(2)}) collective-permute-start(f32[64,256]{1,0:T(8,128)S(1)} %get-tuple-element.9), channel_id=1, source_target_pairs={{0,1},{1,0},{2,3},{3,2},{4,5},{5,4},{6,7},{7,6},{8,9},{9,8},{10,11... | collective-permute-start | bytes 196616 | tf_op jit(solution)/shard_map/ppermute | solution.py:350
  4.2 0.7 %convert_element_type.5 = f32[2]{0:T(128)S(1)} convert(s32[2]{0:T(128)} %param.13) | non-fusion elementwise | flops 2 | bytes 16 | tf_op jit(solution)/shard_map/convert_element_type | solution.py:361
  4.9 0.2 collective-permute-done.other_ref
  5.1 2.9 %collective-permute-start.1 = (f32[64,256]{1,0:T(8,128)S(1)}, f32[64,256]{1,0:T(8,128)S(1)}, u32[]{:S(2)}, u32[]{:S(2)}) collective-permute-start(f32[64,256]{1,0:T(8,128)S(1)} %shard_map.87.one_ref), channel_id=1, source_target_pairs={{0,2},{1,3},{2,0},{3,1},{4,6},{5,7},{6,4},{7,5},{8,10},{9,11},{10,... | collective-permute-start | bytes 196616 | tf_op jit(solution)/shard_map/ppermute | solution.py:350
  8.0 0.7 %compare_select_fusion = f32[2,128]{1,0:T(2,128)S(1)} fusion(f32[2]{0:T(128)S(1)} %convert_element_type.5, s32[2]{0:T(128)} %param.12), kind=kLoop, calls=%fused_computation | loop fusion | flops 512 | bytes 1040 | tf_op jit(solution)/shard_map/mul | solution.py:361
  8.7 1.7 %collective-permute-done.1.other_ref = f32[64,256]{1,0:T(8,128)S(1)} collective-permute-done((f32[64,256]{1,0:T(8,128)S(1)}, f32[64,256]{1,0:T(8,128)S(1)}, u32[]{:S(2)}, u32[]{:S(2)}) %collective-permute-start.1) | collective-permute-done | bytes 65568 | tf_op jit(solution)/shard_map/ppermute | solution.py:350
  10.4 4.0 %collective-permute-start.4 = (bf16[80,256]{1,0:T(8,128)(2,1)S(1)}, bf16[80,256]{1,0:T(8,128)(2,1)S(1)}, u32[]{:S(2)}, u32[]{:S(2)}) collective-permute-start(bf16[80,256]{1,0:T(8,128)(2,1)S(1)} %shard_map.88.refs_0_), channel_id=1, source_target_pairs={{0,12},{4,8},{8,4},{12,0},{1,13},{5,9},{9,5},{13,1},{2,14},{6,10},... | collective-permute-start | bytes 122888 | tf_op jit(solution)/shard_map/ppermute | solution.py:350
  14.5 0.0 collective-permute-start.3
  14.5 0.6 %collective-permute-start.2 = (bf16[80,256]{1,0:T(8,128)(2,1)S(1)}, bf16[80,256]{1,0:T(8,128)(2,1)S(1)}, u32[]{:S(2)}, u32[]{:S(2)}) collective-permute-start(bf16[80,256]{1,0:T(8,128)(2,1)S(1)} %shard_map.88.refs_0_), channel_id=1, source_target_pairs={{0,4},{4,0},{8,12},{12,8},{1,5},{5,1},{9,13},{13,9},{2,6},{6,2},{1... | collective-permute-start | bytes 122888 | tf_op jit(solution)/shard_map/ppermute | solution.py:350
  15.1 1.6 %collective-permute-done.4.refs_3_ = bf16[80,256]{1,0:T(8,128)(2,1)S(1)} collective-permute-done((bf16[80,256]{1,0:T(8,128)(2,1)S(1)}, bf16[80,256]{1,0:T(8,128)(2,1)S(1)}, u32[]{:S(2)}, u32[]{:S(2)}) %collective-permute-start.4) | collective-permute-done | bytes 40992 | tf_op jit(solution)/shard_map/ppermute | solution.py:350
  16.7 2.7 %collective-permute-done.3.refs_2_ = bf16[80,256]{1,0:T(8,128)(2,1)S(1)} collective-permute-done((bf16[80,256]{1,0:T(8,128)(2,1)S(1)}, bf16[80,256]{1,0:T(8,128)(2,1)S(1)}, u32[]{:S(2)}, u32[]{:S(2)}) %collective-permute-start.3) | collective-permute-done | bytes 40992 | tf_op jit(solution)/shard_map/ppermute | solution.py:350
  19.4 0.0 collective-permute-done.2.refs_1_
  19.4 0.1 collective-permute-start.5
  19.5 1.2 %copy.9 = bf16[1024,256]{0,1:T(8,128)(2,1)S(1)} copy(bf16[1024,256]{1,0:T(8,128)(2,1)} %param.11) | data formatting | bytes 1048576 | tf_op args[4]
  20.7 0.1 collective-permute-done.5.other
  20.9 2.6 %shard_map.91 = (bf16[256,256]{1,0:T(8,128)(2,1)S(1)}, bf16[256,256]{1,0:T(8,128)(2,1)S(1)}, bf16[256,256]{1,0:T(8,128)(2,1)S(1)}, bf16[256,256]{1,0:T(8,128)(2,1)S(1)}) custom-call(bf16[4,80,256]{2,1,0:T(8,128)(2,1)S(1)} %shard_map.89.mine, bf16[4,80,256]{2,1,0:T(8,128)(2,1)S(1)} %collective-permute-done.5.other, bf16[256,1024]{1,0:T(8,128)(2,1)S(1)} %bitcast.4), custom_call_target="tpu_custom_call" | custom-call | tf_op jit(solution)/shard_map/pallas_call | solution.py:257
  23.5 1.5 %collective-permute-start.6 = (bf16[256,256]{1,0:T(8,128)(2,1)S(1)}, bf16[256,256]{1,0:T(8,128)(2,1)S(1)}, u32[]{:S(2)}, u32[]{:S(2)}) collective-permute-start(bf16[256,256]{1,0:T(8,128)(2,1)S(1)} %get-tuple-element.11), channel_id=1, source_target_pairs={{0,12},{4,8},{8,4},{12,0},{1,13},{5,9},{9,5},{13,1},{2,14},{6,10},... | collective-permute-start | bytes 393224 | tf_op jit(solution)/shard_map/ppermute | solution.py:350
  25.0 0.6 %collective-permute-start.7 = (bf16[256,256]{1,0:T(8,128)(2,1)S(1)}, bf16[256,256]{1,0:T(8,128)(2,1)S(1)}, u32[]{:S(2)}, u32[]{:S(2)}) collective-permute-start(bf16[256,256]{1,0:T(8,128)(2,1)S(1)} %get-tuple-element.12), channel_id=1, source_target_pairs={{0,8},{4,12},{8,0},{12,4},{1,9},{5,13},{9,1},{13,5},{2,10},{6,14},... | collective-permute-start | bytes 393224 | tf_op jit(solution)/shard_map/ppermute | solution.py:350
  25.7 2.3 %collective-permute-start.8 = (bf16[256,256]{1,0:T(8,128)(2,1)S(1)}, bf16[256,256]{1,0:T(8,128)(2,1)S(1)}, u32[]{:S(2)}, u32[]{:S(2)}) collective-permute-start(bf16[256,256]{1,0:T(8,128)(2,1)S(1)} %get-tuple-element.13), channel_id=1, source_target_pairs={{0,4},{4,0},{8,12},{12,8},{1,5},{5,1},{9,13},{13,9},{2,6},{6,2},{1... | collective-permute-start | bytes 393224 | tf_op jit(solution)/shard_map/ppermute | solution.py:350
  27.9 12.4 %shard_map.90 = f32[1024,4096]{1,0:T(8,128)} custom-call(bf16[4,80,256]{2,1,0:T(8,128)(2,1)S(1)} %shard_map.89.mine, bf16[4,80,256]{2,1,0:T(8,128)(2,1)S(1)} %collective-permute-done.5.other), custom_call_target="tpu_custom_call" | custom-call | tf_op jit(solution)/shard_map/pallas_call | solution.py:313
  40.4 0.0 collective-permute-done.6.refs_1_
  40.4 0.0 collective-permute-done.7.refs_2_
  40.4 0.0 collective-permute-done.8.refs_3_
  40.4 0.8 %shard_map.92 = bf16[256,256]{1,0:T(8,128)(2,1)} custom-call(bf16[256,256]{1,0:T(8,128)(2,1)S(1)} %get-tuple-element.10.refs_0_, bf16[256,256]{1,0:T(8,128)(2,1)S(1)} %collective-permute-done.6.refs_1_, bf16[256,256]{1,0:T(8,128)(2,1)S(1)} %collective-permute-done.7.refs_2_, bf16[256,256]{1,0:T(8,128)(2,1)S(1)} %collective-permute-done.8.refs_3_, ...), custom_call_target="tpu_custom_call" | custom-call | tf_op jit(solution)/shard_map/pallas_call | solution.py:342
  (3 shorter events, 0.0 us)
Async XLA Ops:
  3.7 1.4 %collective-permute-start = (f32[64,256]{1,0:T(8,128)S(1)}, f32[64,256]{1,0:T(8,128)S(1)}, u32[]{:S(2)}, u32[]{:S(2)}) collective-permute-start(f32[64,256]{1,0:T(8,128)S(1)} %get-tuple-element.9), channel_id=1, source_target_pairs={{0,1},{1,0},{2,3},{3,2},{4,5},{5,4},{6,7},{7,6},{8,9},{9,8},{10,11... | collective-permute-start | bytes 196616 | tf_op jit(solution)/shard_map/ppermute | solution.py:350
  5.1 5.3 %collective-permute-start.1 = (f32[64,256]{1,0:T(8,128)S(1)}, f32[64,256]{1,0:T(8,128)S(1)}, u32[]{:S(2)}, u32[]{:S(2)}) collective-permute-start(f32[64,256]{1,0:T(8,128)S(1)} %shard_map.87.one_ref), channel_id=1, source_target_pairs={{0,2},{1,3},{2,0},{3,1},{4,6},{5,7},{6,4},{7,5},{8,10},{9,11},{10,... | collective-permute-start | bytes 196616 | tf_op jit(solution)/shard_map/ppermute | solution.py:350
  10.4 6.2 %collective-permute-start.4 = (bf16[80,256]{1,0:T(8,128)(2,1)S(1)}, bf16[80,256]{1,0:T(8,128)(2,1)S(1)}, u32[]{:S(2)}, u32[]{:S(2)}) collective-permute-start(bf16[80,256]{1,0:T(8,128)(2,1)S(1)} %shard_map.88.refs_0_), channel_id=1, source_target_pairs={{0,12},{4,8},{8,4},{12,0},{1,13},{5,9},{9,5},{13,1},{2,14},{6,10},... | collective-permute-start | bytes 122888 | tf_op jit(solution)/shard_map/ppermute | solution.py:350
  14.5 4.9 %collective-permute-start.3 = (bf16[80,256]{1,0:T(8,128)(2,1)S(1)}, bf16[80,256]{1,0:T(8,128)(2,1)S(1)}, u32[]{:S(2)}, u32[]{:S(2)}) collective-permute-start(bf16[80,256]{1,0:T(8,128)(2,1)S(1)} %shard_map.88.refs_0_), channel_id=1, source_target_pairs={{0,8},{4,12},{8,0},{12,4},{1,9},{5,13},{9,1},{13,5},{2,10},{6,14},... | collective-permute-start | bytes 122888 | tf_op jit(solution)/shard_map/ppermute | solution.py:350
  14.5 4.9 %collective-permute-start.2 = (bf16[80,256]{1,0:T(8,128)(2,1)S(1)}, bf16[80,256]{1,0:T(8,128)(2,1)S(1)}, u32[]{:S(2)}, u32[]{:S(2)}) collective-permute-start(bf16[80,256]{1,0:T(8,128)(2,1)S(1)} %shard_map.88.refs_0_), channel_id=1, source_target_pairs={{0,4},{4,0},{8,12},{12,8},{1,5},{5,1},{9,13},{13,9},{2,6},{6,2},{1... | collective-permute-start | bytes 122888 | tf_op jit(solution)/shard_map/ppermute | solution.py:350
  19.4 1.5 %collective-permute-start.5 = (bf16[4,80,256]{2,1,0:T(8,128)(2,1)S(1)}, bf16[4,80,256]{2,1,0:T(8,128)(2,1)S(1)}, u32[]{:S(2)}, u32[]{:S(2)}) collective-permute-start(bf16[4,80,256]{2,1,0:T(8,128)(2,1)S(1)} %shard_map.89.mine), channel_id=1, source_target_pairs={{0,1},{1,0},{2,3},{3,2},{4,5},{5,4},{6,7},{7,6},{8,9},{9,8},{10,11... | collective-permute-start | bytes 491528 | tf_op jit(solution)/shard_map/ppermute | solution.py:350
  23.5 16.9 %collective-permute-start.6 = (bf16[256,256]{1,0:T(8,128)(2,1)S(1)}, bf16[256,256]{1,0:T(8,128)(2,1)S(1)}, u32[]{:S(2)}, u32[]{:S(2)}) collective-permute-start(bf16[256,256]{1,0:T(8,128)(2,1)S(1)} %get-tuple-element.11), channel_id=1, source_target_pairs={{0,12},{4,8},{8,4},{12,0},{1,13},{5,9},{9,5},{13,1},{2,14},{6,10},... | collective-permute-start | bytes 393224 | tf_op jit(solution)/shard_map/ppermute | solution.py:350
  25.0 15.4 %collective-permute-start.7 = (bf16[256,256]{1,0:T(8,128)(2,1)S(1)}, bf16[256,256]{1,0:T(8,128)(2,1)S(1)}, u32[]{:S(2)}, u32[]{:S(2)}) collective-permute-start(bf16[256,256]{1,0:T(8,128)(2,1)S(1)} %get-tuple-element.12), channel_id=1, source_target_pairs={{0,8},{4,12},{8,0},{12,4},{1,9},{5,13},{9,1},{13,5},{2,10},{6,14},... | collective-permute-start | bytes 393224 | tf_op jit(solution)/shard_map/ppermute | solution.py:350
  25.7 14.7 %collective-permute-start.8 = (bf16[256,256]{1,0:T(8,128)(2,1)S(1)}, bf16[256,256]{1,0:T(8,128)(2,1)S(1)}, u32[]{:S(2)}, u32[]{:S(2)}) collective-permute-start(bf16[256,256]{1,0:T(8,128)(2,1)S(1)} %get-tuple-element.13), channel_id=1, source_target_pairs={{0,4},{4,0},{8,12},{12,8},{1,5},{5,1},{9,13},{13,9},{2,6},{6,2},{1... | collective-permute-start | bytes 393224 | tf_op jit(solution)/shard_map/ppermute | solution.py:350

commit v4 on v3

--- a/solution.py
+++ b/solution.py
@@ -279,12 +279,17 @@
         left = (factors[pl.ds(first + i, 1), :] * act).astype(jnp.bfloat16)
         left = (weight * left.astype(jnp.float32)).astype(jnp.bfloat16)
         weighted[i * rank : (i + 1) * rank, :] = left
+    act_rows = jnp.concatenate([act, act], axis=0).T
+    grad_rows = factors[rank:, :].T.astype(jnp.bfloat16)
+    spread_row = lax.broadcasted_iota(jnp.int32, (rank, cols), 0)
+    spread_col = lax.broadcasted_iota(jnp.int32, (rank, cols), 1) // rank
 
     def build(step):
-        for i in range(col_count):
-            row = rank + step * col_count + i
-            right = (factors[row : row + 1, :] * act).astype(jnp.bfloat16)
-            rights[step % 2][i * rank : (i + 1) * rank, :] = right
+        spread = jnp.where(spread_row == spread_col + step * col_count, 1.0, 0.0)
+        grad = jnp.dot(grad_rows, spread.astype(jnp.bfloat16), preferred_element_type=jnp.float32)
+        for i in range(0, cols, 2 * rank):
+            span = slice(i, i + 2 * rank)
+            rights[step % 2][:, span] = (grad[:, span] * act_rows).astype(jnp.bfloat16)
 
     def store(step):
         return pltpu.make_async_copy(
@@ -297,8 +302,8 @@
             build(step + 1)
         if step > 1:
             store(step - 2).wait()
-        block = lax.dot_general(
-            weighted[...], rights[step % 2][...], NT, preferred_element_type=jnp.float32
+        block = jnp.dot(
+            weighted[...], rights[step % 2][...], preferred_element_type=jnp.float32
         )
         results[step % 2][...] = block * (1.0 / tokens)
         store(step).start()
@@ -318,8 +323,8 @@
             pltpu.VMEM((2 * rank, tok * blocks), jnp.float32),
             pltpu.VMEM((1, tok * blocks), jnp.float32),
             pltpu.VMEM((rows, tok * blocks), jnp.bfloat16),
-            pltpu.VMEM((cols, tok * blocks), jnp.bfloat16),
-            pltpu.VMEM((cols, tok * blocks), jnp.bfloat16),
+            pltpu.VMEM((tok * blocks, cols), jnp.bfloat16),
+            pltpu.VMEM((tok * blocks, cols), jnp.bfloat16),
             pltpu.VMEM((rows, cols), jnp.float32),
             pltpu.VMEM((rows, cols), jnp.float32),
             pltpu.SemaphoreType.DMA((2,)),

time: 41.4 us -> 42.4 us (1.024)
  Pallas kernels: 18.9 us -> 19.9 us
    pallas_call x1, Pallas kernels: 12.4 us -> 13.4 us  [hessian_rows(): pl.pallas_call(functools.partial(hessian_kernel, row_count, col_count), o...]
  transfers between devices with their start and end apart: 9 -> 9, of which waited for: 5 -> 5; matrix products, arithmetic and copies ran while one was open for 6% -> 6% of each run, Pallas kernels for 30% -> 32%
where the time goes in v4:
time: 42.4 us; the launch traced here: 42.2 us
  Pallas kernels  19.9 us (47%)
  starting transfers between devices  12.6 us (30%)
  waiting for transfers between devices  6.33 us (15%)
  other arithmetic  1.38 us (3%)
  local copies, waits for them, and re-layouts  1.25 us (3%)
  between operations  0.71 us (2%)
    pallas_call x1, Pallas kernels, hessian_rows(): pl.pallas_call(functools.partial(hessian_kernel, row_count, col_count), o...  13.4 us
    ppermute x9, starting transfers between devices, swapped(): lax.ppermute(array, axis, [(i, i ^ distance) for i in range(lax.axis_size...  12.6 us
    ppermute x9, waiting for transfers between devices, swapped(): lax.ppermute(array, axis, [(i, i ^ distance) for i in range(lax.axis_size...  6.33 us
    pallas_call x1, Pallas kernels, project(): pl.pallas_call(project_kernel, in_specs=[pl.BlockSpec(memory_space=pl.ANY...  3.04 us
    pallas_call x1, Pallas kernels, score_shares(): pl.pallas_call(functools.partial(share_kernel, row_count), out_shape=[out...  2.6 us
    unnamed x1, local copies, waits for them, and re-layouts  1.25 us
  transfers between devices with their start and end apart: 9, of which 5 were waited for; matrix products, arithmetic and copies ran while one was open for 6% of the time, Pallas kernels for 32%

profile of v4, /device:TPU:0, one launch (start us, length us, event | category | flops | bytes accessed | tf_op | source)
XLA Modules:
  0.0 42.2 jit_solution(2511128952988604838)
XLA Ops:
  0.6 3.0 %shard_map.86 = (f32[64,256]{1,0:T(8,128)S(1)}, f32[64,256]{1,0:T(8,128)S(1)}) custom-call(bf16[256,1024]{1,0:T(8,128)(2,1)} %act.1, bf16[256,3584]{1,0:T(8,128)(2,1)} %grad.1, bf16[64,1024]{1,0:T(8,128)(2,1)} %bitcast.8, bf16[64,3584]{1,0:T(8,128)(2,1)} %bitcast.7), custom_call_target="tpu_custom_call" | custom-call | tf_op jit(solution)/shard_map/pallas_call | solution.py:143
  3.7 0.5 %collective-permute-start = (f32[64,256]{1,0:T(8,128)S(1)}, f32[64,256]{1,0:T(8,128)S(1)}, u32[]{:S(2)}, u32[]{:S(2)}) collective-permute-start(f32[64,256]{1,0:T(8,128)S(1)} %get-tuple-element.9), channel_id=1, source_target_pairs={{0,1},{1,0},{2,3},{3,2},{4,5},{5,4},{6,7},{7,6},{8,9},{9,8},{10,11... | collective-permute-start | bytes 196616 | tf_op jit(solution)/shard_map/ppermute | solution.py:355
  4.2 0.7 %convert_element_type.5 = f32[2]{0:T(128)S(1)} convert(s32[2]{0:T(128)} %param.13) | non-fusion elementwise | flops 2 | bytes 16 | tf_op jit(solution)/shard_map/convert_element_type | solution.py:366
  4.9 0.2 collective-permute-done.other_ref
  5.1 2.9 %collective-permute-start.1 = (f32[64,256]{1,0:T(8,128)S(1)}, f32[64,256]{1,0:T(8,128)S(1)}, u32[]{:S(2)}, u32[]{:S(2)}) collective-permute-start(f32[64,256]{1,0:T(8,128)S(1)} %shard_map.87.one_ref), channel_id=1, source_target_pairs={{0,2},{1,3},{2,0},{3,1},{4,6},{5,7},{6,4},{7,5},{8,10},{9,11},{10,... | collective-permute-start | bytes 196616 | tf_op jit(solution)/shard_map/ppermute | solution.py:355
  8.0 0.7 %compare_select_fusion = f32[2,128]{1,0:T(2,128)S(1)} fusion(f32[2]{0:T(128)S(1)} %convert_element_type.5, s32[2]{0:T(128)} %param.12), kind=kLoop, calls=%fused_computation | loop fusion | flops 512 | bytes 1040 | tf_op jit(solution)/shard_map/mul | solution.py:366
  8.7 1.7 %collective-permute-done.1.other_ref = f32[64,256]{1,0:T(8,128)S(1)} collective-permute-done((f32[64,256]{1,0:T(8,128)S(1)}, f32[64,256]{1,0:T(8,128)S(1)}, u32[]{:S(2)}, u32[]{:S(2)}) %collective-permute-start.1) | collective-permute-done | bytes 65568 | tf_op jit(solution)/shard_map/ppermute | solution.py:355
  10.4 4.0 %collective-permute-start.4 = (bf16[80,256]{1,0:T(8,128)(2,1)S(1)}, bf16[80,256]{1,0:T(8,128)(2,1)S(1)}, u32[]{:S(2)}, u32[]{:S(2)}) collective-permute-start(bf16[80,256]{1,0:T(8,128)(2,1)S(1)} %shard_map.88.refs_0_), channel_id=1, source_target_pairs={{0,12},{4,8},{8,4},{12,0},{1,13},{5,9},{9,5},{13,1},{2,14},{6,10},... | collective-permute-start | bytes 122888 | tf_op jit(solution)/shard_map/ppermute | solution.py:355
  14.5 0.0 collective-permute-start.3
  14.5 0.6 %collective-permute-start.2 = (bf16[80,256]{1,0:T(8,128)(2,1)S(1)}, bf16[80,256]{1,0:T(8,128)(2,1)S(1)}, u32[]{:S(2)}, u32[]{:S(2)}) collective-permute-start(bf16[80,256]{1,0:T(8,128)(2,1)S(1)} %shard_map.88.refs_0_), channel_id=1, source_target_pairs={{0,4},{4,0},{8,12},{12,8},{1,5},{5,1},{9,13},{13,9},{2,6},{6,2},{1... | collective-permute-start | bytes 122888 | tf_op jit(solution)/shard_map/ppermute | solution.py:355
  15.1 1.6 %collective-permute-done.4.refs_3_ = bf16[80,256]{1,0:T(8,128)(2,1)S(1)} collective-permute-done((bf16[80,256]{1,0:T(8,128)(2,1)S(1)}, bf16[80,256]{1,0:T(8,128)(2,1)S(1)}, u32[]{:S(2)}, u32[]{:S(2)}) %collective-permute-start.4) | collective-permute-done | bytes 40992 | tf_op jit(solution)/shard_map/ppermute | solution.py:355
  16.7 2.7 %collective-permute-done.3.refs_2_ = bf16[80,256]{1,0:T(8,128)(2,1)S(1)} collective-permute-done((bf16[80,256]{1,0:T(8,128)(2,1)S(1)}, bf16[80,256]{1,0:T(8,128)(2,1)S(1)}, u32[]{:S(2)}, u32[]{:S(2)}) %collective-permute-start.3) | collective-permute-done | bytes 40992 | tf_op jit(solution)/shard_map/ppermute | solution.py:355
  19.4 0.0 collective-permute-done.2.refs_1_
  19.4 0.1 collective-permute-start.5
  19.5 1.2 %copy.9 = bf16[1024,256]{0,1:T(8,128)(2,1)S(1)} copy(bf16[1024,256]{1,0:T(8,128)(2,1)} %param.11) | data formatting | bytes 1048576 | tf_op args[4]
  20.7 0.1 collective-permute-done.5.other
  20.9 2.6 %shard_map.91 = (bf16[256,256]{1,0:T(8,128)(2,1)S(1)}, bf16[256,256]{1,0:T(8,128)(2,1)S(1)}, bf16[256,256]{1,0:T(8,128)(2,1)S(1)}, bf16[256,256]{1,0:T(8,128)(2,1)S(1)}) custom-call(bf16[4,80,256]{2,1,0:T(8,128)(2,1)S(1)} %shard_map.89.mine, bf16[4,80,256]{2,1,0:T(8,128)(2,1)S(1)} %collective-permute-done.5.other, bf16[256,1024]{1,0:T(8,128)(2,1)S(1)} %bitcast.4), custom_call_target="tpu_custom_call" | custom-call | tf_op jit(solution)/shard_map/pallas_call | solution.py:257
  23.5 1.5 %collective-permute-start.6 = (bf16[256,256]{1,0:T(8,128)(2,1)S(1)}, bf16[256,256]{1,0:T(8,128)(2,1)S(1)}, u32[]{:S(2)}, u32[]{:S(2)}) collective-permute-start(bf16[256,256]{1,0:T(8,128)(2,1)S(1)} %get-tuple-element.11), channel_id=1, source_target_pairs={{0,12},{4,8},{8,4},{12,0},{1,13},{5,9},{9,5},{13,1},{2,14},{6,10},... | collective-permute-start | bytes 393224 | tf_op jit(solution)/shard_map/ppermute | solution.py:355
  25.0 0.6 %collective-permute-start.7 = (bf16[256,256]{1,0:T(8,128)(2,1)S(1)}, bf16[256,256]{1,0:T(8,128)(2,1)S(1)}, u32[]{:S(2)}, u32[]{:S(2)}) collective-permute-start(bf16[256,256]{1,0:T(8,128)(2,1)S(1)} %get-tuple-element.12), channel_id=1, source_target_pairs={{0,8},{4,12},{8,0},{12,4},{1,9},{5,13},{9,1},{13,5},{2,10},{6,14},... | collective-permute-start | bytes 393224 | tf_op jit(solution)/shard_map/ppermute | solution.py:355
  25.7 2.3 %collective-permute-start.8 = (bf16[256,256]{1,0:T(8,128)(2,1)S(1)}, bf16[256,256]{1,0:T(8,128)(2,1)S(1)}, u32[]{:S(2)}, u32[]{:S(2)}) collective-permute-start(bf16[256,256]{1,0:T(8,128)(2,1)S(1)} %get-tuple-element.13), channel_id=1, source_target_pairs={{0,4},{4,0},{8,12},{12,8},{1,5},{5,1},{9,13},{13,9},{2,6},{6,2},{1... | collective-permute-start | bytes 393224 | tf_op jit(solution)/shard_map/ppermute | solution.py:355
  27.9 13.4 %shard_map.90 = f32[1024,4096]{1,0:T(8,128)} custom-call(bf16[4,80,256]{2,1,0:T(8,128)(2,1)S(1)} %shard_map.89.mine, bf16[4,80,256]{2,1,0:T(8,128)(2,1)S(1)} %collective-permute-done.5.other), custom_call_target="tpu_custom_call" | custom-call | tf_op jit(solution)/shard_map/pallas_call | solution.py:318
  41.4 0.0 collective-permute-done.6.refs_1_
  41.4 0.0 collective-permute-done.7.refs_2_
  41.4 0.0 collective-permute-done.8.refs_3_
  41.4 0.8 %shard_map.92 = bf16[256,256]{1,0:T(8,128)(2,1)} custom-call(bf16[256,256]{1,0:T(8,128)(2,1)S(1)} %get-tuple-element.10.refs_0_, bf16[256,256]{1,0:T(8,128)(2,1)S(1)} %collective-permute-done.6.refs_1_, bf16[256,256]{1,0:T(8,128)(2,1)S(1)} %collective-permute-done.7.refs_2_, bf16[256,256]{1,0:T(8,128)(2,1)S(1)} %collective-permute-done.8.refs_3_, ...), custom_call_target="tpu_custom_call" | custom-call | tf_op jit(solution)/shard_map/pallas_call | solution.py:347
  (3 shorter events, 0.0 us)
Async XLA Ops:
  3.7 1.4 %collective-permute-start = (f32[64,256]{1,0:T(8,128)S(1)}, f32[64,256]{1,0:T(8,128)S(1)}, u32[]{:S(2)}, u32[]{:S(2)}) collective-permute-start(f32[64,256]{1,0:T(8,128)S(1)} %get-tuple-element.9), channel_id=1, source_target_pairs={{0,1},{1,0},{2,3},{3,2},{4,5},{5,4},{6,7},{7,6},{8,9},{9,8},{10,11... | collective-permute-start | bytes 196616 | tf_op jit(solution)/shard_map/ppermute | solution.py:355
  5.1 5.3 %collective-permute-start.1 = (f32[64,256]{1,0:T(8,128)S(1)}, f32[64,256]{1,0:T(8,128)S(1)}, u32[]{:S(2)}, u32[]{:S(2)}) collective-permute-start(f32[64,256]{1,0:T(8,128)S(1)} %shard_map.87.one_ref), channel_id=1, source_target_pairs={{0,2},{1,3},{2,0},{3,1},{4,6},{5,7},{6,4},{7,5},{8,10},{9,11},{10,... | collective-permute-start | bytes 196616 | tf_op jit(solution)/shard_map/ppermute | solution.py:355
  10.4 6.2 %collective-permute-start.4 = (bf16[80,256]{1,0:T(8,128)(2,1)S(1)}, bf16[80,256]{1,0:T(8,128)(2,1)S(1)}, u32[]{:S(2)}, u32[]{:S(2)}) collective-permute-start(bf16[80,256]{1,0:T(8,128)(2,1)S(1)} %shard_map.88.refs_0_), channel_id=1, source_target_pairs={{0,12},{4,8},{8,4},{12,0},{1,13},{5,9},{9,5},{13,1},{2,14},{6,10},... | collective-permute-start | bytes 122888 | tf_op jit(solution)/shard_map/ppermute | solution.py:355
  14.5 4.9 %collective-permute-start.3 = (bf16[80,256]{1,0:T(8,128)(2,1)S(1)}, bf16[80,256]{1,0:T(8,128)(2,1)S(1)}, u32[]{:S(2)}, u32[]{:S(2)}) collective-permute-start(bf16[80,256]{1,0:T(8,128)(2,1)S(1)} %shard_map.88.refs_0_), channel_id=1, source_target_pairs={{0,8},{4,12},{8,0},{12,4},{1,9},{5,13},{9,1},{13,5},{2,10},{6,14},... | collective-permute-start | bytes 122888 | tf_op jit(solution)/shard_map/ppermute | solution.py:355
  14.5 4.9 %collective-permute-start.2 = (bf16[80,256]{1,0:T(8,128)(2,1)S(1)}, bf16[80,256]{1,0:T(8,128)(2,1)S(1)}, u32[]{:S(2)}, u32[]{:S(2)}) collective-permute-start(bf16[80,256]{1,0:T(8,128)(2,1)S(1)} %shard_map.88.refs_0_), channel_id=1, source_target_pairs={{0,4},{4,0},{8,12},{12,8},{1,5},{5,1},{9,13},{13,9},{2,6},{6,2},{1... | collective-permute-start | bytes 122888 | tf_op jit(solution)/shard_map/ppermute | solution.py:355
  19.4 1.5 %collective-permute-start.5 = (bf16[4,80,256]{2,1,0:T(8,128)(2,1)S(1)}, bf16[4,80,256]{2,1,0:T(8,128)(2,1)S(1)}, u32[]{:S(2)}, u32[]{:S(2)}) collective-permute-start(bf16[4,80,256]{2,1,0:T(8,128)(2,1)S(1)} %shard_map.89.mine), channel_id=1, source_target_pairs={{0,1},{1,0},{2,3},{3,2},{4,5},{5,4},{6,7},{7,6},{8,9},{9,8},{10,11... | collective-permute-start | bytes 491528 | tf_op jit(solution)/shard_map/ppermute | solution.py:355
  23.5 17.9 %collective-permute-start.6 = (bf16[256,256]{1,0:T(8,128)(2,1)S(1)}, bf16[256,256]{1,0:T(8,128)(2,1)S(1)}, u32[]{:S(2)}, u32[]{:S(2)}) collective-permute-start(bf16[256,256]{1,0:T(8,128)(2,1)S(1)} %get-tuple-element.11), channel_id=1, source_target_pairs={{0,12},{4,8},{8,4},{12,0},{1,13},{5,9},{9,5},{13,1},{2,14},{6,10},... | collective-permute-start | bytes 393224 | tf_op jit(solution)/shard_map/ppermute | solution.py:355
  25.0 16.4 %collective-permute-start.7 = (bf16[256,256]{1,0:T(8,128)(2,1)S(1)}, bf16[256,256]{1,0:T(8,128)(2,1)S(1)}, u32[]{:S(2)}, u32[]{:S(2)}) collective-permute-start(bf16[256,256]{1,0:T(8,128)(2,1)S(1)} %get-tuple-element.12), channel_id=1, source_target_pairs={{0,8},{4,12},{8,0},{12,4},{1,9},{5,13},{9,1},{13,5},{2,10},{6,14},... | collective-permute-start | bytes 393224 | tf_op jit(solution)/shard_map/ppermute | solution.py:355
  25.7 15.8 %collective-permute-start.8 = (bf16[256,256]{1,0:T(8,128)(2,1)S(1)}, bf16[256,256]{1,0:T(8,128)(2,1)S(1)}, u32[]{:S(2)}, u32[]{:S(2)}) collective-permute-start(bf16[256,256]{1,0:T(8,128)(2,1)S(1)} %get-tuple-element.13), channel_id=1, source_target_pairs={{0,4},{4,0},{8,12},{12,8},{1,5},{5,1},{9,13},{13,9},{2,6},{6,2},{1... | collective-permute-start | bytes 393224 | tf_op jit(solution)/shard_map/ppermute | solution.py:355

commit v5 on v3

--- a/solution.py
+++ b/solution.py
@@ -101,6 +101,7 @@
 
 
 MIB = 1024 * 1024
+TILE = 256
 NT = (((1,), (1,)), ((), ()))
 
 
@@ -270,7 +271,7 @@
     rights, results, sems = scratch[:2], scratch[2:4], scratch[4]
     rank = factors.shape[0] // 2
     tokens = factors.shape[1]
-    cols = col_count * rank
+    rows, cols = row_count * rank, col_count * rank
     steps = rank // col_count
     lay_out_factors(mine, other, factors, weights)
     act, weight = factors[:rank, :], weights[...]
@@ -297,10 +298,15 @@
             build(step + 1)
         if step > 1:
             store(step - 2).wait()
-        block = lax.dot_general(
-            weighted[...], rights[step % 2][...], NT, preferred_element_type=jnp.float32
-        )
-        results[step % 2][...] = block * (1.0 / tokens)
+        for col in range(0, cols, TILE):
+            for row in range(0, rows, TILE):
+                tile = lax.dot_general(
+                    weighted[row : row + TILE, :],
+                    rights[step % 2][col : col + TILE, :],
+                    NT,
+                    preferred_element_type=jnp.float32,
+                )
+                results[step % 2][row : row + TILE, col : col + TILE] = tile * (1.0 / tokens)
         store(step).start()
     for step in range(max(steps - 2, 0), steps):
         store(step).wait()

time: 41.4 us -> 41.5 us (level)
  no operation moved by 1% of the time
where the time goes in v5:
time: 41.5 us; the launch traced here: 41.3 us
  Pallas kernels  19 us (46%)
  starting transfers between devices  12.6 us (30%)
  waiting for transfers between devices  6.33 us (15%)
  other arithmetic  1.38 us (3%)
  local copies, waits for them, and re-layouts  1.25 us (3%)
  between operations  0.71 us (2%)
    ppermute x9, starting transfers between devices, swapped(): lax.ppermute(array, axis, [(i, i ^ distance) for i in range(lax.axis_size...  12.6 us
    pallas_call x1, Pallas kernels, hessian_rows(): pl.pallas_call(functools.partial(hessian_kernel, row_count, col_count), o...  12.5 us
    ppermute x9, waiting for transfers between devices, swapped(): lax.ppermute(array, axis, [(i, i ^ distance) for i in range(lax.axis_size...  6.33 us
    pallas_call x1, Pallas kernels, project(): pl.pallas_call(project_kernel, in_specs=[pl.BlockSpec(memory_space=pl.ANY...  3.04 us
    pallas_call x1, Pallas kernels, score_shares(): pl.pallas_call(functools.partial(share_kernel, row_count), out_shape=[out...  2.6 us
    unnamed x1, local copies, waits for them, and re-layouts  1.25 us
  transfers between devices with their start and end apart: 9, of which 5 were waited for; matrix products, arithmetic and copies ran while one was open for 6% of the time, Pallas kernels for 30%

profile of v5, /device:TPU:0, one launch (start us, length us, event | category | flops | bytes accessed | tf_op | source)
XLA Modules:
  0.0 41.3 jit_solution(413815573164271534)
XLA Ops:
  0.6 3.0 %shard_map.86 = (f32[64,256]{1,0:T(8,128)S(1)}, f32[64,256]{1,0:T(8,128)S(1)}) custom-call(bf16[256,1024]{1,0:T(8,128)(2,1)} %act.1, bf16[256,3584]{1,0:T(8,128)(2,1)} %grad.1, bf16[64,1024]{1,0:T(8,128)(2,1)} %bitcast.8, bf16[64,3584]{1,0:T(8,128)(2,1)} %bitcast.7), custom_call_target="tpu_custom_call" | custom-call | tf_op jit(solution)/shard_map/pallas_call | solution.py:144
  3.7 0.5 %collective-permute-start = (f32[64,256]{1,0:T(8,128)S(1)}, f32[64,256]{1,0:T(8,128)S(1)}, u32[]{:S(2)}, u32[]{:S(2)}) collective-permute-start(f32[64,256]{1,0:T(8,128)S(1)} %get-tuple-element.9), channel_id=1, source_target_pairs={{0,1},{1,0},{2,3},{3,2},{4,5},{5,4},{6,7},{7,6},{8,9},{9,8},{10,11... | collective-permute-start | bytes 196616 | tf_op jit(solution)/shard_map/ppermute | solution.py:356
  4.2 0.7 %convert_element_type.5 = f32[2]{0:T(128)S(1)} convert(s32[2]{0:T(128)} %param.13) | non-fusion elementwise | flops 2 | bytes 16 | tf_op jit(solution)/shard_map/convert_element_type | solution.py:367
  4.9 0.2 collective-permute-done.other_ref
  5.1 2.9 %collective-permute-start.1 = (f32[64,256]{1,0:T(8,128)S(1)}, f32[64,256]{1,0:T(8,128)S(1)}, u32[]{:S(2)}, u32[]{:S(2)}) collective-permute-start(f32[64,256]{1,0:T(8,128)S(1)} %shard_map.87.one_ref), channel_id=1, source_target_pairs={{0,2},{1,3},{2,0},{3,1},{4,6},{5,7},{6,4},{7,5},{8,10},{9,11},{10,... | collective-permute-start | bytes 196616 | tf_op jit(solution)/shard_map/ppermute | solution.py:356
  8.0 0.7 %compare_select_fusion = f32[2,128]{1,0:T(2,128)S(1)} fusion(f32[2]{0:T(128)S(1)} %convert_element_type.5, s32[2]{0:T(128)} %param.12), kind=kLoop, calls=%fused_computation | loop fusion | flops 512 | bytes 1040 | tf_op jit(solution)/shard_map/mul | solution.py:367
  8.7 1.7 %collective-permute-done.1.other_ref = f32[64,256]{1,0:T(8,128)S(1)} collective-permute-done((f32[64,256]{1,0:T(8,128)S(1)}, f32[64,256]{1,0:T(8,128)S(1)}, u32[]{:S(2)}, u32[]{:S(2)}) %collective-permute-start.1) | collective-permute-done | bytes 65568 | tf_op jit(solution)/shard_map/ppermute | solution.py:356
  10.4 4.0 %collective-permute-start.4 = (bf16[80,256]{1,0:T(8,128)(2,1)S(1)}, bf16[80,256]{1,0:T(8,128)(2,1)S(1)}, u32[]{:S(2)}, u32[]{:S(2)}) collective-permute-start(bf16[80,256]{1,0:T(8,128)(2,1)S(1)} %shard_map.88.refs_0_), channel_id=1, source_target_pairs={{0,12},{4,8},{8,4},{12,0},{1,13},{5,9},{9,5},{13,1},{2,14},{6,10},... | collective-permute-start | bytes 122888 | tf_op jit(solution)/shard_map/ppermute | solution.py:356
  14.5 0.0 collective-permute-start.3
  14.5 0.6 %collective-permute-start.2 = (bf16[80,256]{1,0:T(8,128)(2,1)S(1)}, bf16[80,256]{1,0:T(8,128)(2,1)S(1)}, u32[]{:S(2)}, u32[]{:S(2)}) collective-permute-start(bf16[80,256]{1,0:T(8,128)(2,1)S(1)} %shard_map.88.refs_0_), channel_id=1, source_target_pairs={{0,4},{4,0},{8,12},{12,8},{1,5},{5,1},{9,13},{13,9},{2,6},{6,2},{1... | collective-permute-start | bytes 122888 | tf_op jit(solution)/shard_map/ppermute | solution.py:356
  15.1 1.6 %collective-permute-done.4.refs_3_ = bf16[80,256]{1,0:T(8,128)(2,1)S(1)} collective-permute-done((bf16[80,256]{1,0:T(8,128)(2,1)S(1)}, bf16[80,256]{1,0:T(8,128)(2,1)S(1)}, u32[]{:S(2)}, u32[]{:S(2)}) %collective-permute-start.4) | collective-permute-done | bytes 40992 | tf_op jit(solution)/shard_map/ppermute | solution.py:356
  16.7 2.7 %collective-permute-done.3.refs_2_ = bf16[80,256]{1,0:T(8,128)(2,1)S(1)} collective-permute-done((bf16[80,256]{1,0:T(8,128)(2,1)S(1)}, bf16[80,256]{1,0:T(8,128)(2,1)S(1)}, u32[]{:S(2)}, u32[]{:S(2)}) %collective-permute-start.3) | collective-permute-done | bytes 40992 | tf_op jit(solution)/shard_map/ppermute | solution.py:356
  19.4 0.0 collective-permute-done.2.refs_1_
  19.4 0.1 collective-permute-start.5
  19.5 1.2 %copy.9 = bf16[1024,256]{0,1:T(8,128)(2,1)S(1)} copy(bf16[1024,256]{1,0:T(8,128)(2,1)} %param.11) | data formatting | bytes 1048576 | tf_op args[4]
  20.7 0.1 collective-permute-done.5.other
  20.9 2.6 %shard_map.91 = (bf16[256,256]{1,0:T(8,128)(2,1)S(1)}, bf16[256,256]{1,0:T(8,128)(2,1)S(1)}, bf16[256,256]{1,0:T(8,128)(2,1)S(1)}, bf16[256,256]{1,0:T(8,128)(2,1)S(1)}) custom-call(bf16[4,80,256]{2,1,0:T(8,128)(2,1)S(1)} %shard_map.89.mine, bf16[4,80,256]{2,1,0:T(8,128)(2,1)S(1)} %collective-permute-done.5.other, bf16[256,1024]{1,0:T(8,128)(2,1)S(1)} %bitcast.4), custom_call_target="tpu_custom_call" | custom-call | tf_op jit(solution)/shard_map/pallas_call | solution.py:258
  23.5 1.5 %collective-permute-start.6 = (bf16[256,256]{1,0:T(8,128)(2,1)S(1)}, bf16[256,256]{1,0:T(8,128)(2,1)S(1)}, u32[]{:S(2)}, u32[]{:S(2)}) collective-permute-start(bf16[256,256]{1,0:T(8,128)(2,1)S(1)} %get-tuple-element.11), channel_id=1, source_target_pairs={{0,12},{4,8},{8,4},{12,0},{1,13},{5,9},{9,5},{13,1},{2,14},{6,10},... | collective-permute-start | bytes 393224 | tf_op jit(solution)/shard_map/ppermute | solution.py:356
  25.0 0.6 %collective-permute-start.7 = (bf16[256,256]{1,0:T(8,128)(2,1)S(1)}, bf16[256,256]{1,0:T(8,128)(2,1)S(1)}, u32[]{:S(2)}, u32[]{:S(2)}) collective-permute-start(bf16[256,256]{1,0:T(8,128)(2,1)S(1)} %get-tuple-element.12), channel_id=1, source_target_pairs={{0,8},{4,12},{8,0},{12,4},{1,9},{5,13},{9,1},{13,5},{2,10},{6,14},... | collective-permute-start | bytes 393224 | tf_op jit(solution)/shard_map/ppermute | solution.py:356
  25.7 2.3 %collective-permute-start.8 = (bf16[256,256]{1,0:T(8,128)(2,1)S(1)}, bf16[256,256]{1,0:T(8,128)(2,1)S(1)}, u32[]{:S(2)}, u32[]{:S(2)}) collective-permute-start(bf16[256,256]{1,0:T(8,128)(2,1)S(1)} %get-tuple-element.13), channel_id=1, source_target_pairs={{0,4},{4,0},{8,12},{12,8},{1,5},{5,1},{9,13},{13,9},{2,6},{6,2},{1... | collective-permute-start | bytes 393224 | tf_op jit(solution)/shard_map/ppermute | solution.py:356
  27.9 12.5 %shard_map.90 = f32[1024,4096]{1,0:T(8,128)} custom-call(bf16[4,80,256]{2,1,0:T(8,128)(2,1)S(1)} %shard_map.89.mine, bf16[4,80,256]{2,1,0:T(8,128)(2,1)S(1)} %collective-permute-done.5.other), custom_call_target="tpu_custom_call" | custom-call | tf_op jit(solution)/shard_map/pallas_call | solution.py:319
  40.5 0.0 collective-permute-done.6.refs_1_
  40.5 0.0 collective-permute-done.7.refs_2_
  40.5 0.0 collective-permute-done.8.refs_3_
  40.5 0.8 %shard_map.92 = bf16[256,256]{1,0:T(8,128)(2,1)} custom-call(bf16[256,256]{1,0:T(8,128)(2,1)S(1)} %get-tuple-element.10.refs_0_, bf16[256,256]{1,0:T(8,128)(2,1)S(1)} %collective-permute-done.6.refs_1_, bf16[256,256]{1,0:T(8,128)(2,1)S(1)} %collective-permute-done.7.refs_2_, bf16[256,256]{1,0:T(8,128)(2,1)S(1)} %collective-permute-done.8.refs_3_, ...), custom_call_target="tpu_custom_call" | custom-call | tf_op jit(solution)/shard_map/pallas_call | solution.py:348
  (3 shorter events, 0.0 us)
Async XLA Ops:
  3.7 1.4 %collective-permute-start = (f32[64,256]{1,0:T(8,128)S(1)}, f32[64,256]{1,0:T(8,128)S(1)}, u32[]{:S(2)}, u32[]{:S(2)}) collective-permute-start(f32[64,256]{1,0:T(8,128)S(1)} %get-tuple-element.9), channel_id=1, source_target_pairs={{0,1},{1,0},{2,3},{3,2},{4,5},{5,4},{6,7},{7,6},{8,9},{9,8},{10,11... | collective-permute-start | bytes 196616 | tf_op jit(solution)/shard_map/ppermute | solution.py:356
  5.1 5.3 %collective-permute-start.1 = (f32[64,256]{1,0:T(8,128)S(1)}, f32[64,256]{1,0:T(8,128)S(1)}, u32[]{:S(2)}, u32[]{:S(2)}) collective-permute-start(f32[64,256]{1,0:T(8,128)S(1)} %shard_map.87.one_ref), channel_id=1, source_target_pairs={{0,2},{1,3},{2,0},{3,1},{4,6},{5,7},{6,4},{7,5},{8,10},{9,11},{10,... | collective-permute-start | bytes 196616 | tf_op jit(solution)/shard_map/ppermute | solution.py:356
  10.4 6.2 %collective-permute-start.4 = (bf16[80,256]{1,0:T(8,128)(2,1)S(1)}, bf16[80,256]{1,0:T(8,128)(2,1)S(1)}, u32[]{:S(2)}, u32[]{:S(2)}) collective-permute-start(bf16[80,256]{1,0:T(8,128)(2,1)S(1)} %shard_map.88.refs_0_), channel_id=1, source_target_pairs={{0,12},{4,8},{8,4},{12,0},{1,13},{5,9},{9,5},{13,1},{2,14},{6,10},... | collective-permute-start | bytes 122888 | tf_op jit(solution)/shard_map/ppermute | solution.py:356
  14.5 4.9 %collective-permute-start.3 = (bf16[80,256]{1,0:T(8,128)(2,1)S(1)}, bf16[80,256]{1,0:T(8,128)(2,1)S(1)}, u32[]{:S(2)}, u32[]{:S(2)}) collective-permute-start(bf16[80,256]{1,0:T(8,128)(2,1)S(1)} %shard_map.88.refs_0_), channel_id=1, source_target_pairs={{0,8},{4,12},{8,0},{12,4},{1,9},{5,13},{9,1},{13,5},{2,10},{6,14},... | collective-permute-start | bytes 122888 | tf_op jit(solution)/shard_map/ppermute | solution.py:356
  14.5 4.9 %collective-permute-start.2 = (bf16[80,256]{1,0:T(8,128)(2,1)S(1)}, bf16[80,256]{1,0:T(8,128)(2,1)S(1)}, u32[]{:S(2)}, u32[]{:S(2)}) collective-permute-start(bf16[80,256]{1,0:T(8,128)(2,1)S(1)} %shard_map.88.refs_0_), channel_id=1, source_target_pairs={{0,4},{4,0},{8,12},{12,8},{1,5},{5,1},{9,13},{13,9},{2,6},{6,2},{1... | collective-permute-start | bytes 122888 | tf_op jit(solution)/shard_map/ppermute | solution.py:356
  19.4 1.5 %collective-permute-start.5 = (bf16[4,80,256]{2,1,0:T(8,128)(2,1)S(1)}, bf16[4,80,256]{2,1,0:T(8,128)(2,1)S(1)}, u32[]{:S(2)}, u32[]{:S(2)}) collective-permute-start(bf16[4,80,256]{2,1,0:T(8,128)(2,1)S(1)} %shard_map.89.mine), channel_id=1, source_target_pairs={{0,1},{1,0},{2,3},{3,2},{4,5},{5,4},{6,7},{7,6},{8,9},{9,8},{10,11... | collective-permute-start | bytes 491528 | tf_op jit(solution)/shard_map/ppermute | solution.py:356
  23.5 17.0 %collective-permute-start.6 = (bf16[256,256]{1,0:T(8,128)(2,1)S(1)}, bf16[256,256]{1,0:T(8,128)(2,1)S(1)}, u32[]{:S(2)}, u32[]{:S(2)}) collective-permute-start(bf16[256,256]{1,0:T(8,128)(2,1)S(1)} %get-tuple-element.11), channel_id=1, source_target_pairs={{0,12},{4,8},{8,4},{12,0},{1,13},{5,9},{9,5},{13,1},{2,14},{6,10},... | collective-permute-start | bytes 393224 | tf_op jit(solution)/shard_map/ppermute | solution.py:356
  25.0 15.5 %collective-permute-start.7 = (bf16[256,256]{1,0:T(8,128)(2,1)S(1)}, bf16[256,256]{1,0:T(8,128)(2,1)S(1)}, u32[]{:S(2)}, u32[]{:S(2)}) collective-permute-start(bf16[256,256]{1,0:T(8,128)(2,1)S(1)} %get-tuple-element.12), channel_id=1, source_target_pairs={{0,8},{4,12},{8,0},{12,4},{1,9},{5,13},{9,1},{13,5},{2,10},{6,14},... | collective-permute-start | bytes 393224 | tf_op jit(solution)/shard_map/ppermute | solution.py:356
  25.7 14.9 %collective-permute-start.8 = (bf16[256,256]{1,0:T(8,128)(2,1)S(1)}, bf16[256,256]{1,0:T(8,128)(2,1)S(1)}, u32[]{:S(2)}, u32[]{:S(2)}) collective-permute-start(bf16[256,256]{1,0:T(8,128)(2,1)S(1)} %get-tuple-element.13), channel_id=1, source_target_pairs={{0,4},{4,0},{8,12},{12,8},{1,5},{5,1},{9,13},{13,9},{2,6},{6,2},{1... | collective-permute-start | bytes 393224 | tf_op jit(solution)/shard_map/ppermute | solution.py:356

commit v6 on v3

--- a/solution.py
+++ b/solution.py
@@ -101,6 +101,7 @@
 
 
 MIB = 1024 * 1024
+TILE = 256
 NT = (((1,), (1,)), ((), ()))
 
 
@@ -267,10 +268,10 @@
 
 
 def hessian_kernel(row_count, col_count, mine, other, out, factors, weights, weighted, *scratch):
-    rights, results, sems = scratch[:2], scratch[2:4], scratch[4]
+    rights, result, sems = scratch[:2], scratch[2], scratch[3]
     rank = factors.shape[0] // 2
     tokens = factors.shape[1]
-    cols = col_count * rank
+    rows, cols = row_count * rank, col_count * rank
     steps = rank // col_count
     lay_out_factors(mine, other, factors, weights)
     act, weight = factors[:rank, :], weights[...]
@@ -286,24 +287,25 @@
             right = (factors[row : row + 1, :] * act).astype(jnp.bfloat16)
             rights[step % 2][i * rank : (i + 1) * rank, :] = right
 
-    def store(step):
-        return pltpu.make_async_copy(
-            results[step % 2], out.at[:, pl.ds(step * cols, cols)], sems.at[step % 2]
-        )
-
+    copies = []
     build(0)
     for step in range(steps):
         if step + 1 < steps:
             build(step + 1)
-        if step > 1:
-            store(step - 2).wait()
-        block = lax.dot_general(
-            weighted[...], rights[step % 2][...], NT, preferred_element_type=jnp.float32
-        )
-        results[step % 2][...] = block * (1.0 / tokens)
-        store(step).start()
-    for step in range(max(steps - 2, 0), steps):
-        store(step).wait()
+        for row in range(0, rows, TILE):
+            here = pl.ds(row, TILE), pl.ds(step * cols, cols)
+            tile = lax.dot_general(
+                weighted[row : row + TILE, :],
+                rights[step % 2][...],
+                NT,
+                preferred_element_type=jnp.float32,
+            )
+            result[here] = tile * (1.0 / tokens)
+            copy = pltpu.make_async_copy(result.at[here], out.at[here], sems.at[len(copies)])
+            copy.start()
+            copies.append(copy)
+    for copy in copies:
+        copy.wait()
 
 
 def hessian_rows(mine, other, rank, row_count, col_count=8):
@@ -320,9 +322,8 @@
             pltpu.VMEM((rows, tok * blocks), jnp.bfloat16),
             pltpu.VMEM((cols, tok * blocks), jnp.bfloat16),
             pltpu.VMEM((cols, tok * blocks), jnp.bfloat16),
-            pltpu.VMEM((rows, cols), jnp.float32),
-            pltpu.VMEM((rows, cols), jnp.float32),
-            pltpu.SemaphoreType.DMA((2,)),
+            pltpu.VMEM((rows, feat), jnp.float32),
+            pltpu.SemaphoreType.DMA((feat // cols * (rows // TILE),)),
         ],
         compiler_params=params(40),
     )(mine, other)

time: 41.4 us -> 39 us (0.942)
  Pallas kernels: 18.9 us -> 16.5 us
    pallas_call x1, Pallas kernels: 12.4 us -> 10 us  [hessian_rows(): pl.pallas_call(functools.partial(hessian_kernel, row_count, col_count), o...]
  transfers between devices with their start and end apart: 9 -> 9, of which waited for: 5 -> 6; matrix products, arithmetic and copies ran while one was open for 6% -> 7% of each run, Pallas kernels for 30% -> 26%
where the time goes in v6:
time: 39 us; the launch traced here: 38.8 us
  Pallas kernels  16.5 us (42%)
  starting transfers between devices  12.6 us (32%)
  waiting for transfers between devices  6.38 us (16%)
  other arithmetic  1.38 us (4%)
  local copies, waits for them, and re-layouts  1.25 us (3%)
  between operations  0.69 us (2%)
    ppermute x9, starting transfers between devices, swapped(): lax.ppermute(array, axis, [(i, i ^ distance) for i in range(lax.axis_size...  12.6 us
    pallas_call x1, Pallas kernels, hessian_rows(): pl.pallas_call(functools.partial(hessian_kernel, row_count, col_count), o...  10 us
    ppermute x9, waiting for transfers between devices, swapped(): lax.ppermute(array, axis, [(i, i ^ distance) for i in range(lax.axis_size...  6.38 us
    pallas_call x1, Pallas kernels, project(): pl.pallas_call(project_kernel, in_specs=[pl.BlockSpec(memory_space=pl.ANY...  3.04 us
    pallas_call x1, Pallas kernels, score_shares(): pl.pallas_call(functools.partial(share_kernel, row_count), out_shape=[out...  2.6 us
    unnamed x1, local copies, waits for them, and re-layouts  1.25 us
    pallas_call x1, Pallas kernels, finish_scores(): pl.pallas_call(finish_kernel, out_shape=jax.ShapeDtypeStruct((tok, count)...  0.8 us
  transfers between devices with their start and end apart: 9, of which 6 were waited for; matrix products, arithmetic and copies ran while one was open for 7% of the time, Pallas kernels for 26%

profile of v6, /device:TPU:0, one launch (start us, length us, event | category | flops | bytes accessed | tf_op | source)
XLA Modules:
  0.0 38.8 jit_solution(8629920861982863005)
XLA Ops:
  0.6 3.0 %shard_map.86 = (f32[64,256]{1,0:T(8,128)S(1)}, f32[64,256]{1,0:T(8,128)S(1)}) custom-call(bf16[256,1024]{1,0:T(8,128)(2,1)} %act.1, bf16[256,3584]{1,0:T(8,128)(2,1)} %grad.1, bf16[64,1024]{1,0:T(8,128)(2,1)} %bitcast.8, bf16[64,3584]{1,0:T(8,128)(2,1)} %bitcast.7), custom_call_target="tpu_custom_call" | custom-call | tf_op jit(solution)/shard_map/pallas_call | solution.py:144
  3.7 0.5 %collective-permute-start = (f32[64,256]{1,0:T(8,128)S(1)}, f32[64,256]{1,0:T(8,128)S(1)}, u32[]{:S(2)}, u32[]{:S(2)}) collective-permute-start(f32[64,256]{1,0:T(8,128)S(1)} %get-tuple-element.9), channel_id=1, source_target_pairs={{0,1},{1,0},{2,3},{3,2},{4,5},{5,4},{6,7},{7,6},{8,9},{9,8},{10,11... | collective-permute-start | bytes 196616 | tf_op jit(solution)/shard_map/ppermute | solution.py:351
  4.2 0.7 %convert_element_type.5 = f32[2]{0:T(128)S(1)} convert(s32[2]{0:T(128)} %param.13) | non-fusion elementwise | flops 2 | bytes 16 | tf_op jit(solution)/shard_map/convert_element_type | solution.py:362
  4.9 0.2 collective-permute-done.other_ref
  5.1 2.9 %collective-permute-start.1 = (f32[64,256]{1,0:T(8,128)S(1)}, f32[64,256]{1,0:T(8,128)S(1)}, u32[]{:S(2)}, u32[]{:S(2)}) collective-permute-start(f32[64,256]{1,0:T(8,128)S(1)} %shard_map.87.one_ref), channel_id=1, source_target_pairs={{0,2},{1,3},{2,0},{3,1},{4,6},{5,7},{6,4},{7,5},{8,10},{9,11},{10,... | collective-permute-start | bytes 196616 | tf_op jit(solution)/shard_map/ppermute | solution.py:351
  8.0 0.7 %compare_select_fusion = f32[2,128]{1,0:T(2,128)S(1)} fusion(f32[2]{0:T(128)S(1)} %convert_element_type.5, s32[2]{0:T(128)} %param.12), kind=kLoop, calls=%fused_computation | loop fusion | flops 512 | bytes 1040 | tf_op jit(solution)/shard_map/mul | solution.py:362
  8.7 1.7 %collective-permute-done.1.other_ref = f32[64,256]{1,0:T(8,128)S(1)} collective-permute-done((f32[64,256]{1,0:T(8,128)S(1)}, f32[64,256]{1,0:T(8,128)S(1)}, u32[]{:S(2)}, u32[]{:S(2)}) %collective-permute-start.1) | collective-permute-done | bytes 65568 | tf_op jit(solution)/shard_map/ppermute | solution.py:351
  10.4 4.0 %collective-permute-start.4 = (bf16[80,256]{1,0:T(8,128)(2,1)S(1)}, bf16[80,256]{1,0:T(8,128)(2,1)S(1)}, u32[]{:S(2)}, u32[]{:S(2)}) collective-permute-start(bf16[80,256]{1,0:T(8,128)(2,1)S(1)} %shard_map.88.refs_0_), channel_id=1, source_target_pairs={{0,12},{4,8},{8,4},{12,0},{1,13},{5,9},{9,5},{13,1},{2,14},{6,10},... | collective-permute-start | bytes 122888 | tf_op jit(solution)/shard_map/ppermute | solution.py:351
  14.5 0.0 collective-permute-start.3
  14.5 0.6 %collective-permute-start.2 = (bf16[80,256]{1,0:T(8,128)(2,1)S(1)}, bf16[80,256]{1,0:T(8,128)(2,1)S(1)}, u32[]{:S(2)}, u32[]{:S(2)}) collective-permute-start(bf16[80,256]{1,0:T(8,128)(2,1)S(1)} %shard_map.88.refs_0_), channel_id=1, source_target_pairs={{0,4},{4,0},{8,12},{12,8},{1,5},{5,1},{9,13},{13,9},{2,6},{6,2},{1... | collective-permute-start | bytes 122888 | tf_op jit(solution)/shard_map/ppermute | solution.py:351
  15.1 1.6 %collective-permute-done.4.refs_3_ = bf16[80,256]{1,0:T(8,128)(2,1)S(1)} collective-permute-done((bf16[80,256]{1,0:T(8,128)(2,1)S(1)}, bf16[80,256]{1,0:T(8,128)(2,1)S(1)}, u32[]{:S(2)}, u32[]{:S(2)}) %collective-permute-start.4) | collective-permute-done | bytes 40992 | tf_op jit(solution)/shard_map/ppermute | solution.py:351
  16.7 2.7 %collective-permute-done.3.refs_2_ = bf16[80,256]{1,0:T(8,128)(2,1)S(1)} collective-permute-done((bf16[80,256]{1,0:T(8,128)(2,1)S(1)}, bf16[80,256]{1,0:T(8,128)(2,1)S(1)}, u32[]{:S(2)}, u32[]{:S(2)}) %collective-permute-start.3) | collective-permute-done | bytes 40992 | tf_op jit(solution)/shard_map/ppermute | solution.py:351
  19.4 0.0 collective-permute-done.2.refs_1_
  19.4 0.1 collective-permute-start.5
  19.5 1.2 %copy.9 = bf16[1024,256]{0,1:T(8,128)(2,1)S(1)} copy(bf16[1024,256]{1,0:T(8,128)(2,1)} %param.11) | data formatting | bytes 1048576 | tf_op args[4]
  20.7 0.1 collective-permute-done.5.other
  20.9 2.6 %shard_map.91 = (bf16[256,256]{1,0:T(8,128)(2,1)S(1)}, bf16[256,256]{1,0:T(8,128)(2,1)S(1)}, bf16[256,256]{1,0:T(8,128)(2,1)S(1)}, bf16[256,256]{1,0:T(8,128)(2,1)S(1)}) custom-call(bf16[4,80,256]{2,1,0:T(8,128)(2,1)S(1)} %shard_map.89.mine, bf16[4,80,256]{2,1,0:T(8,128)(2,1)S(1)} %collective-permute-done.5.other, bf16[256,1024]{1,0:T(8,128)(2,1)S(1)} %bitcast.4), custom_call_target="tpu_custom_call" | custom-call | tf_op jit(solution)/shard_map/pallas_call | solution.py:258
  23.5 1.5 %collective-permute-start.6 = (bf16[256,256]{1,0:T(8,128)(2,1)S(1)}, bf16[256,256]{1,0:T(8,128)(2,1)S(1)}, u32[]{:S(2)}, u32[]{:S(2)}) collective-permute-start(bf16[256,256]{1,0:T(8,128)(2,1)S(1)} %get-tuple-element.11), channel_id=1, source_target_pairs={{0,12},{4,8},{8,4},{12,0},{1,13},{5,9},{9,5},{13,1},{2,14},{6,10},... | collective-permute-start | bytes 393224 | tf_op jit(solution)/shard_map/ppermute | solution.py:351
  25.0 0.6 %collective-permute-start.7 = (bf16[256,256]{1,0:T(8,128)(2,1)S(1)}, bf16[256,256]{1,0:T(8,128)(2,1)S(1)}, u32[]{:S(2)}, u32[]{:S(2)}) collective-permute-start(bf16[256,256]{1,0:T(8,128)(2,1)S(1)} %get-tuple-element.12), channel_id=1, source_target_pairs={{0,8},{4,12},{8,0},{12,4},{1,9},{5,13},{9,1},{13,5},{2,10},{6,14},... | collective-permute-start | bytes 393224 | tf_op jit(solution)/shard_map/ppermute | solution.py:351
  25.7 2.3 %collective-permute-start.8 = (bf16[256,256]{1,0:T(8,128)(2,1)S(1)}, bf16[256,256]{1,0:T(8,128)(2,1)S(1)}, u32[]{:S(2)}, u32[]{:S(2)}) collective-permute-start(bf16[256,256]{1,0:T(8,128)(2,1)S(1)} %get-tuple-element.13), channel_id=1, source_target_pairs={{0,4},{4,0},{8,12},{12,8},{1,5},{5,1},{9,13},{13,9},{2,6},{6,2},{1... | collective-permute-start | bytes 393224 | tf_op jit(solution)/shard_map/ppermute | solution.py:351
  27.9 10.0 %shard_map.90 = f32[1024,4096]{1,0:T(8,128)} custom-call(bf16[4,80,256]{2,1,0:T(8,128)(2,1)S(1)} %shard_map.89.mine, bf16[4,80,256]{2,1,0:T(8,128)(2,1)S(1)} %collective-permute-done.5.other), custom_call_target="tpu_custom_call" | custom-call | tf_op jit(solution)/shard_map/pallas_call | solution.py:315
  38.0 0.0 collective-permute-done.6.refs_1_
  38.0 0.1 collective-permute-done.7.refs_2_
  38.0 0.0 collective-permute-done.8.refs_3_
  38.0 0.8 %shard_map.92 = bf16[256,256]{1,0:T(8,128)(2,1)} custom-call(bf16[256,256]{1,0:T(8,128)(2,1)S(1)} %get-tuple-element.10.refs_0_, bf16[256,256]{1,0:T(8,128)(2,1)S(1)} %collective-permute-done.6.refs_1_, bf16[256,256]{1,0:T(8,128)(2,1)S(1)} %collective-permute-done.7.refs_2_, bf16[256,256]{1,0:T(8,128)(2,1)S(1)} %collective-permute-done.8.refs_3_, ...), custom_call_target="tpu_custom_call" | custom-call | tf_op jit(solution)/shard_map/pallas_call | solution.py:343
  (3 shorter events, 0.0 us)
Async XLA Ops:
  3.7 1.4 %collective-permute-start = (f32[64,256]{1,0:T(8,128)S(1)}, f32[64,256]{1,0:T(8,128)S(1)}, u32[]{:S(2)}, u32[]{:S(2)}) collective-permute-start(f32[64,256]{1,0:T(8,128)S(1)} %get-tuple-element.9), channel_id=1, source_target_pairs={{0,1},{1,0},{2,3},{3,2},{4,5},{5,4},{6,7},{7,6},{8,9},{9,8},{10,11... | collective-permute-start | bytes 196616 | tf_op jit(solution)/shard_map/ppermute | solution.py:351
  5.1 5.3 %collective-permute-start.1 = (f32[64,256]{1,0:T(8,128)S(1)}, f32[64,256]{1,0:T(8,128)S(1)}, u32[]{:S(2)}, u32[]{:S(2)}) collective-permute-start(f32[64,256]{1,0:T(8,128)S(1)} %shard_map.87.one_ref), channel_id=1, source_target_pairs={{0,2},{1,3},{2,0},{3,1},{4,6},{5,7},{6,4},{7,5},{8,10},{9,11},{10,... | collective-permute-start | bytes 196616 | tf_op jit(solution)/shard_map/ppermute | solution.py:351
  10.4 6.2 %collective-permute-start.4 = (bf16[80,256]{1,0:T(8,128)(2,1)S(1)}, bf16[80,256]{1,0:T(8,128)(2,1)S(1)}, u32[]{:S(2)}, u32[]{:S(2)}) collective-permute-start(bf16[80,256]{1,0:T(8,128)(2,1)S(1)} %shard_map.88.refs_0_), channel_id=1, source_target_pairs={{0,12},{4,8},{8,4},{12,0},{1,13},{5,9},{9,5},{13,1},{2,14},{6,10},... | collective-permute-start | bytes 122888 | tf_op jit(solution)/shard_map/ppermute | solution.py:351
  14.5 4.9 %collective-permute-start.3 = (bf16[80,256]{1,0:T(8,128)(2,1)S(1)}, bf16[80,256]{1,0:T(8,128)(2,1)S(1)}, u32[]{:S(2)}, u32[]{:S(2)}) collective-permute-start(bf16[80,256]{1,0:T(8,128)(2,1)S(1)} %shard_map.88.refs_0_), channel_id=1, source_target_pairs={{0,8},{4,12},{8,0},{12,4},{1,9},{5,13},{9,1},{13,5},{2,10},{6,14},... | collective-permute-start | bytes 122888 | tf_op jit(solution)/shard_map/ppermute | solution.py:351
  14.5 4.9 %collective-permute-start.2 = (bf16[80,256]{1,0:T(8,128)(2,1)S(1)}, bf16[80,256]{1,0:T(8,128)(2,1)S(1)}, u32[]{:S(2)}, u32[]{:S(2)}) collective-permute-start(bf16[80,256]{1,0:T(8,128)(2,1)S(1)} %shard_map.88.refs_0_), channel_id=1, source_target_pairs={{0,4},{4,0},{8,12},{12,8},{1,5},{5,1},{9,13},{13,9},{2,6},{6,2},{1... | collective-permute-start | bytes 122888 | tf_op jit(solution)/shard_map/ppermute | solution.py:351
  19.4 1.5 %collective-permute-start.5 = (bf16[4,80,256]{2,1,0:T(8,128)(2,1)S(1)}, bf16[4,80,256]{2,1,0:T(8,128)(2,1)S(1)}, u32[]{:S(2)}, u32[]{:S(2)}) collective-permute-start(bf16[4,80,256]{2,1,0:T(8,128)(2,1)S(1)} %shard_map.89.mine), channel_id=1, source_target_pairs={{0,1},{1,0},{2,3},{3,2},{4,5},{5,4},{6,7},{7,6},{8,9},{9,8},{10,11... | collective-permute-start | bytes 491528 | tf_op jit(solution)/shard_map/ppermute | solution.py:351
  23.5 14.5 %collective-permute-start.6 = (bf16[256,256]{1,0:T(8,128)(2,1)S(1)}, bf16[256,256]{1,0:T(8,128)(2,1)S(1)}, u32[]{:S(2)}, u32[]{:S(2)}) collective-permute-start(bf16[256,256]{1,0:T(8,128)(2,1)S(1)} %get-tuple-element.11), channel_id=1, source_target_pairs={{0,12},{4,8},{8,4},{12,0},{1,13},{5,9},{9,5},{13,1},{2,14},{6,10},... | collective-permute-start | bytes 393224 | tf_op jit(solution)/shard_map/ppermute | solution.py:351
  25.0 13.0 %collective-permute-start.7 = (bf16[256,256]{1,0:T(8,128)(2,1)S(1)}, bf16[256,256]{1,0:T(8,128)(2,1)S(1)}, u32[]{:S(2)}, u32[]{:S(2)}) collective-permute-start(bf16[256,256]{1,0:T(8,128)(2,1)S(1)} %get-tuple-element.12), channel_id=1, source_target_pairs={{0,8},{4,12},{8,0},{12,4},{1,9},{5,13},{9,1},{13,5},{2,10},{6,14},... | collective-permute-start | bytes 393224 | tf_op jit(solution)/shard_map/ppermute | solution.py:351
  25.7 12.4 %collective-permute-start.8 = (bf16[256,256]{1,0:T(8,128)(2,1)S(1)}, bf16[256,256]{1,0:T(8,128)(2,1)S(1)}, u32[]{:S(2)}, u32[]{:S(2)}) collective-permute-start(bf16[256,256]{1,0:T(8,128)(2,1)S(1)} %get-tuple-element.13), channel_id=1, source_target_pairs={{0,4},{4,0},{8,12},{12,8},{1,5},{5,1},{9,13},{13,9},{2,6},{6,2},{1... | collective-permute-start | bytes 393224 | tf_op jit(solution)/shard_map/ppermute | solution.py:351

commit v7 on v6

--- a/solution.py
+++ b/solution.py
@@ -217,13 +217,11 @@
     return scale
 
 
-def share_kernel(row_count, mine, other, query_ref, *refs):
-    factors, weights, features = refs[-3:]
-    out_refs = refs[:-3]
+def share_kernel(row_count, mine, other, query_ref, out_ref, factors, weights, features):
     lay_out_factors(mine, other, factors, weights)
     rank = factors.shape[0] // 2
     tokens = factors.shape[1]
-    tok = tokens // len(out_refs)
+    tok = tokens // out_ref.shape[0]
     first = rank + lax.axis_index("dp") * row_count
     act = factors[:rank, :]
     for i in range(row_count):
@@ -247,17 +245,16 @@
     image = jnp.dot((plain * weight).astype(jnp.bfloat16), gram, preferred_element_type=jnp.float32)
     scale = act_scale * grad_scale
     share = ((2.0 - 0.1 / 1.1) * plain - image) * scale * (scale / step)
-    for k, out_ref in enumerate(out_refs):
-        out_ref[...] = share[:, k * tok : (k + 1) * tok].astype(jnp.bfloat16)
+    for k in range(out_ref.shape[0]):
+        out_ref[lax.axis_index("dp") ^ k] = share[:, k * tok : (k + 1) * tok].astype(jnp.bfloat16)
 
 
 def score_shares(mine, other, queries_t, rank, row_count):
     blocks, _, tok = mine.shape
     count, rows = queries_t.shape
-    out = jax.ShapeDtypeStruct((count, tok), jnp.bfloat16)
     return pl.pallas_call(
         functools.partial(share_kernel, row_count),
-        out_shape=[out] * blocks,
+        out_shape=jax.ShapeDtypeStruct((blocks, count, tok), jnp.bfloat16),
         scratch_shapes=[
             pltpu.VMEM((2 * rank, tok * blocks), jnp.float32),
             pltpu.VMEM((1, tok * blocks), jnp.float32),
@@ -372,9 +369,9 @@
     mine = stack([payload] + others[::-1])
     other = swapped(mine, "query", 1)
     shares = score_shares(mine, other, queries.T, rank, row_count)
-    arrived = [swapped(shares[k], "dp", k) for k in reversed(range(1, dp_count))]
+    arrived = lax.psum_scatter(shares, "dp", scatter_dimension=0)
     hessian = hessian_rows(mine, other, rank, row_count)
-    return hessian, finish_scores([shares[0]] + arrived, weight)
+    return hessian, finish_scores([arrived], weight)
 
 
 def power_of_two(count):

time: 39 us -> 61.1 us (1.57)
  between operations: 0.69 us -> 14.1 us
  waiting for transfers between devices: 6.38 us -> 17.8 us
  starting transfers between devices: 12.6 us -> 8.19 us
  local copies, waits for them, and re-layouts: 1.25 us -> 2.15 us
  Pallas kernels: 16.5 us -> 17.2 us
    reduce_scatter x0 -> x1, waiting for transfers between devices: none -> 11.5 us  [few_tokens(): arrived = lax.psum_scatter(shares, 'dp', scatter_dimension=0)]
    ppermute x9 -> x6, starting transfers between devices: 12.6 us -> 8.16 us  [swapped(): lax.ppermute(array, axis, [(i, i ^ distance) for i in range(lax.axis_size...]
    unnamed x1 -> x3, local copies, waits for them, and re-layouts: 1.25 us -> 2.15 us
    pallas_call x1, Pallas kernels: 2.6 us -> 3.4 us  [score_shares(): pl.pallas_call(functools.partial(share_kernel, row_count), out_shape=jax....]
    ppermute x9 -> x6, waiting for transfers between devices: 6.38 us -> 6.32 us  [swapped(): lax.ppermute(array, axis, [(i, i ^ distance) for i in range(lax.axis_size...]
  transfers between devices with their start and end apart: 9 -> 7, of which waited for: 6 -> 6; matrix products, arithmetic and copies ran while one was open for 7% -> 4% of each run, Pallas kernels for 26% -> 16%
where the time goes in v7:
time: 61.1 us; the launch traced here: 60.9 us
  waiting for transfers between devices  17.8 us (29%)
  Pallas kernels  17.2 us (28%)
  between operations  14.1 us (23%)
  starting transfers between devices  8.19 us (13%)
  local copies, waits for them, and re-layouts  2.15 us (4%)
  other arithmetic  1.38 us (2%)
    reduce_scatter x1, waiting for transfers between devices, few_tokens(): arrived = lax.psum_scatter(shares, 'dp', scatter_dimension=0)  11.5 us
    pallas_call x1, Pallas kernels, hessian_rows(): pl.pallas_call(functools.partial(hessian_kernel, row_count, col_count), o...  10 us
    ppermute x6, starting transfers between devices, swapped(): lax.ppermute(array, axis, [(i, i ^ distance) for i in range(lax.axis_size...  8.16 us
    ppermute x6, waiting for transfers between devices, swapped(): lax.ppermute(array, axis, [(i, i ^ distance) for i in range(lax.axis_size...  6.32 us
    pallas_call x1, Pallas kernels, score_shares(): pl.pallas_call(functools.partial(share_kernel, row_count), out_shape=jax....  3.4 us
    pallas_call x1, Pallas kernels, project(): pl.pallas_call(project_kernel, in_specs=[pl.BlockSpec(memory_space=pl.ANY...  3.04 us
    unnamed x3, local copies, waits for them, and re-layouts  2.15 us
  transfers between devices with their start and end apart: 7, of which 6 were waited for; matrix products, arithmetic and copies ran while one was open for 4% of the time, Pallas kernels for 16%

profile of v7, /device:TPU:0, one launch (start us, length us, event | category | flops | bytes accessed | tf_op | source)
XLA Modules:
  0.0 60.9 jit_solution(12158885499955290509)
XLA Ops:
  7.2 0.0 reduce-scatter.2.cloned.1.call-start
  7.2 3.0 %shard_map.86 = (f32[64,256]{1,0:T(8,128)S(1)}, f32[64,256]{1,0:T(8,128)S(1)}) custom-call(bf16[256,1024]{1,0:T(8,128)(2,1)} %act.1, bf16[256,3584]{1,0:T(8,128)(2,1)} %grad.1, bf16[64,1024]{1,0:T(8,128)(2,1)} %bitcast.10, bf16[64,3584]{1,0:T(8,128)(2,1)} %bitcast.9), custom_call_target="tpu_custom_call" | custom-call | tf_op jit(solution)/shard_map/pallas_call | solution.py:144
  10.3 0.5 collective-permute-start
  10.8 0.7 %convert_element_type.5 = f32[2]{0:T(128)S(1)} convert(s32[2]{0:T(128)} %param.13) | non-fusion elementwise | flops 2 | bytes 16 | tf_op jit(solution)/shard_map/convert_element_type | solution.py:359
  11.4 0.2 collective-permute-done.other_ref
  11.7 2.9 %collective-permute-start.1 = (f32[64,256]{1,0:T(8,128)S(1)}, f32[64,256]{1,0:T(8,128)S(1)}, u32[]{:S(2)}, u32[]{:S(2)}) collective-permute-start(f32[64,256]{1,0:T(8,128)S(1)} %shard_map.87.one_ref), channel_id=1, source_target_pairs={{0,2},{1,3},{2,0},{3,1},{4,6},{5,7},{6,4},{7,5},{8,10},{9,11},{10,... | collective-permute-start | bytes 196616 | tf_op jit(solution)/shard_map/ppermute | solution.py:348
  14.6 0.7 %compare_select_fusion = f32[2,128]{1,0:T(2,128)S(1)} fusion(f32[2]{0:T(128)S(1)} %convert_element_type.5, s32[2]{0:T(128)} %param.12), kind=kLoop, calls=%fused_computation | loop fusion | flops 512 | bytes 1040 | tf_op jit(solution)/shard_map/mul | solution.py:359
  15.3 1.7 %collective-permute-done.1.other_ref = f32[64,256]{1,0:T(8,128)S(1)} collective-permute-done((f32[64,256]{1,0:T(8,128)S(1)}, f32[64,256]{1,0:T(8,128)S(1)}, u32[]{:S(2)}, u32[]{:S(2)}) %collective-permute-start.1) | collective-permute-done | bytes 65568 | tf_op jit(solution)/shard_map/ppermute | solution.py:348
  17.0 4.0 %collective-permute-start.4 = (bf16[80,256]{1,0:T(8,128)(2,1)S(1)}, bf16[80,256]{1,0:T(8,128)(2,1)S(1)}, u32[]{:S(2)}, u32[]{:S(2)}) collective-permute-start(bf16[80,256]{1,0:T(8,128)(2,1)S(1)} %shard_map.88.refs_0_), channel_id=1, source_target_pairs={{0,12},{4,8},{8,4},{12,0},{1,13},{5,9},{9,5},{13,1},{2,14},{6,10},... | collective-permute-start | bytes 122888 | tf_op jit(solution)/shard_map/ppermute | solution.py:348
  21.1 0.0 collective-permute-start.3
  21.1 0.6 %collective-permute-start.2 = (bf16[80,256]{1,0:T(8,128)(2,1)S(1)}, bf16[80,256]{1,0:T(8,128)(2,1)S(1)}, u32[]{:S(2)}, u32[]{:S(2)}) collective-permute-start(bf16[80,256]{1,0:T(8,128)(2,1)S(1)} %shard_map.88.refs_0_), channel_id=1, source_target_pairs={{0,4},{4,0},{8,12},{12,8},{1,5},{5,1},{9,13},{13,9},{2,6},{6,2},{1... | collective-permute-start | bytes 122888 | tf_op jit(solution)/shard_map/ppermute | solution.py:348
  21.7 1.6 %collective-permute-done.4.refs_3_ = bf16[80,256]{1,0:T(8,128)(2,1)S(1)} collective-permute-done((bf16[80,256]{1,0:T(8,128)(2,1)S(1)}, bf16[80,256]{1,0:T(8,128)(2,1)S(1)}, u32[]{:S(2)}, u32[]{:S(2)}) %collective-permute-start.4) | collective-permute-done | bytes 40992 | tf_op jit(solution)/shard_map/ppermute | solution.py:348
  23.3 2.7 %collective-permute-done.3.refs_2_ = bf16[80,256]{1,0:T(8,128)(2,1)S(1)} collective-permute-done((bf16[80,256]{1,0:T(8,128)(2,1)S(1)}, bf16[80,256]{1,0:T(8,128)(2,1)S(1)}, u32[]{:S(2)}, u32[]{:S(2)}) %collective-permute-start.3) | collective-permute-done | bytes 40992 | tf_op jit(solution)/shard_map/ppermute | solution.py:348
  26.0 0.0 collective-permute-done.2.refs_1_
  26.0 0.1 collective-permute-start.5
  26.1 1.2 %copy.9 = bf16[1024,256]{0,1:T(8,128)(2,1)S(1)} copy(bf16[1024,256]{1,0:T(8,128)(2,1)} %param.11) | data formatting | bytes 1048576 | tf_op args[4]
  27.3 0.1 collective-permute-done.5.other
  27.4 3.4 %shard_map.91 = bf16[4,256,256]{2,1,0:T(8,128)(2,1)} custom-call(bf16[4,80,256]{2,1,0:T(8,128)(2,1)S(1)} %shard_map.89.mine, bf16[4,80,256]{2,1,0:T(8,128)(2,1)S(1)} %collective-permute-done.5.other, bf16[256,1024]{1,0:T(8,128)(2,1)S(1)} %bitcast.5), custom_call_target="tpu_custom_call" | custom-call | tf_op jit(solution)/shard_map/pallas_call | solution.py:255
  30.8 0.0 reduce-scatter.2.cloned.1.call-update
  30.9 10.0 %shard_map.90 = f32[1024,4096]{1,0:T(8,128)} custom-call(bf16[4,80,256]{2,1,0:T(8,128)(2,1)S(1)} %shard_map.89.mine, bf16[4,80,256]{2,1,0:T(8,128)(2,1)S(1)} %collective-permute-done.5.other), custom_call_target="tpu_custom_call" | custom-call | tf_op jit(solution)/shard_map/pallas_call | solution.py:312
  40.9 11.5 %reduce-scatter.2.cloned.1.call-done = bf16[1,256,256]{2,1,0:T(8,128)(2,1)} async-done(((bf16[4,256,256]{2,1,0:T(8,128)(2,1)}), bf16[1,256,256]{2,1,0:T(8,128)(2,1)}) %reduce-scatter.2.cloned.1.call-update) | async-done | bytes 131088 | tf_op jit(solution)/shard_map/reduce_scatter | solution.py:372
  52.4 0.0 copy-start
  52.4 0.9 %copy-done = bf16[1,256,256]{2,1,0:T(8,128)(2,1)S(1)} copy-done((bf16[1,256,256]{2,1,0:T(8,128)(2,1)S(1)}, bf16[1,256,256]{2,1,0:T(8,128)(2,1)}, u32[]{:S(2)}) %copy-start) | copy-done | bytes 131096
  53.3 0.8 %shard_map.92 = bf16[256,256]{1,0:T(8,128)(2,1)} custom-call(bf16[256,256]{1,0:T(8,128)(2,1)S(1)} %bitcast.6, f32[1,256]{1,0:T(1,128)S(1)} %bitcast.8), custom_call_target="tpu_custom_call" | custom-call | tf_op jit(solution)/shard_map/pallas_call | solution.py:340
  (3 shorter events, 0.0 us)
Async XLA Ops:
  7.2 45.2 %reduce-scatter.2.cloned.1.call-start = ((), (), s32[]{:S(2)}) async-start(), calls=%async_computation.1 | async-start | bytes 655360 | tf_op jit(solution)/shard_map/reduce_scatter | solution.py:372
  10.3 1.4 %collective-permute-start = (f32[64,256]{1,0:T(8,128)S(1)}, f32[64,256]{1,0:T(8,128)S(1)}, u32[]{:S(2)}, u32[]{:S(2)}) collective-permute-start(f32[64,256]{1,0:T(8,128)S(1)} %get-tuple-element.5), channel_id=1, source_target_pairs={{0,1},{1,0},{2,3},{3,2},{4,5},{5,4},{6,7},{7,6},{8,9},{9,8},{10,11... | collective-permute-start | bytes 196616 | tf_op jit(solution)/shard_map/ppermute | solution.py:348
  11.7 5.3 %collective-permute-start.1 = (f32[64,256]{1,0:T(8,128)S(1)}, f32[64,256]{1,0:T(8,128)S(1)}, u32[]{:S(2)}, u32[]{:S(2)}) collective-permute-start(f32[64,256]{1,0:T(8,128)S(1)} %shard_map.87.one_ref), channel_id=1, source_target_pairs={{0,2},{1,3},{2,0},{3,1},{4,6},{5,7},{6,4},{7,5},{8,10},{9,11},{10,... | collective-permute-start | bytes 196616 | tf_op jit(solution)/shard_map/ppermute | solution.py:348
  17.0 6.2 %collective-permute-start.4 = (bf16[80,256]{1,0:T(8,128)(2,1)S(1)}, bf16[80,256]{1,0:T(8,128)(2,1)S(1)}, u32[]{:S(2)}, u32[]{:S(2)}) collective-permute-start(bf16[80,256]{1,0:T(8,128)(2,1)S(1)} %shard_map.88.refs_0_), channel_id=1, source_target_pairs={{0,12},{4,8},{8,4},{12,0},{1,13},{5,9},{9,5},{13,1},{2,14},{6,10},... | collective-permute-start | bytes 122888 | tf_op jit(solution)/shard_map/ppermute | solution.py:348
  21.1 4.9 %collective-permute-start.3 = (bf16[80,256]{1,0:T(8,128)(2,1)S(1)}, bf16[80,256]{1,0:T(8,128)(2,1)S(1)}, u32[]{:S(2)}, u32[]{:S(2)}) collective-permute-start(bf16[80,256]{1,0:T(8,128)(2,1)S(1)} %shard_map.88.refs_0_), channel_id=1, source_target_pairs={{0,8},{4,12},{8,0},{12,4},{1,9},{5,13},{9,1},{13,5},{2,10},{6,14},... | collective-permute-start | bytes 122888 | tf_op jit(solution)/shard_map/ppermute | solution.py:348
  21.1 4.9 %collective-permute-start.2 = (bf16[80,256]{1,0:T(8,128)(2,1)S(1)}, bf16[80,256]{1,0:T(8,128)(2,1)S(1)}, u32[]{:S(2)}, u32[]{:S(2)}) collective-permute-start(bf16[80,256]{1,0:T(8,128)(2,1)S(1)} %shard_map.88.refs_0_), channel_id=1, source_target_pairs={{0,4},{4,0},{8,12},{12,8},{1,5},{5,1},{9,13},{13,9},{2,6},{6,2},{1... | collective-permute-start | bytes 122888 | tf_op jit(solution)/shard_map/ppermute | solution.py:348
  26.0 1.5 %collective-permute-start.5 = (bf16[4,80,256]{2,1,0:T(8,128)(2,1)S(1)}, bf16[4,80,256]{2,1,0:T(8,128)(2,1)S(1)}, u32[]{:S(2)}, u32[]{:S(2)}) collective-permute-start(bf16[4,80,256]{2,1,0:T(8,128)(2,1)S(1)} %shard_map.89.mine), channel_id=1, source_target_pairs={{0,1},{1,0},{2,3},{3,2},{4,5},{5,4},{6,7},{7,6},{8,9},{9,8},{10,11... | collective-permute-start | bytes 491528 | tf_op jit(solution)/shard_map/ppermute | solution.py:348
  52.4 0.9 %copy-start = (bf16[1,256,256]{2,1,0:T(8,128)(2,1)S(1)}, bf16[1,256,256]{2,1,0:T(8,128)(2,1)}, u32[]{:S(2)}) copy-start(bf16[1,256,256]{2,1,0:T(8,128)(2,1)} %reduce-scatter.2.cloned.1.call-done) | copy-start | bytes 393220
Sparse Core Ops, SparseCore 0:
  31.0 21.3 reduce-scatter.1

commit v8 on v6

--- a/solution.py
+++ b/solution.py
@@ -109,24 +109,31 @@
     return pltpu.CompilerParams(vmem_limit_bytes=int(mib * MIB))
 
 
-def project_kernel(act, grad, pin, pout, keep_ref, send_ref, act_v, grad_v, pin_v, pout_v, sems):
+def project_kernel(
+    act, grad, pin, pout, query, keep_ref, send_ref, keep_query_ref, send_query_ref, *scratch
+):
+    act_v, grad_v, pin_v, pout_v, query_v, sems = scratch
     chunk = act.shape[1]
     while grad.shape[1] % chunk:
         chunk //= 2
     spans = [pl.ds(c, chunk) for c in range(0, grad.shape[1], chunk)]
-    copies = [pltpu.make_async_copy(s, d, sems.at[n]) for n, (s, d) in enumerate(((pin, pin_v), (act, act_v), (pout, pout_v)))]
-    copies += [
-        pltpu.make_async_copy(grad.at[:, span], grad_v.at[:, span], sems.at[3 + n])
-        for n, span in enumerate(spans)
-    ]
+    pairs = [(pin, pin_v), (act, act_v), (query, query_v), (pout, pout_v)]
+    pairs += [(grad.at[:, span], grad_v.at[:, span]) for span in spans]
+    copies = [pltpu.make_async_copy(s, d, sems.at[n]) for n, (s, d) in enumerate(pairs)]
     for copy in copies:
         copy.start()
     copies[0].wait()
     copies[1].wait()
     part_act = lax.dot_general(pin_v[...], act_v[...], NT, preferred_element_type=jnp.float32)
     copies[2].wait()
+    query_t = query_v[...].T
+    half = query_t.shape[0] // 2
+    even = lax.rem(lax.axis_index("dp"), 2) == 0
+    keep_query_ref[...] = jnp.where(even, query_t[:half], query_t[half:])
+    send_query_ref[...] = jnp.where(even, query_t[half:], query_t[:half])
+    copies[3].wait()
     part_grad = jnp.zeros_like(part_act)
-    for copy, span in zip(copies[3:], spans):
+    for copy, span in zip(copies[4:], spans):
         copy.wait()
         part_grad += lax.dot_general(
             pout_v[:, span], grad_v[:, span], NT, preferred_element_type=jnp.float32
@@ -136,24 +143,27 @@
     send_ref[...] = jnp.where(even, part_grad, part_act)
 
 
-def project(activations, out_grads, proj_in_t, proj_out_t):
+def project(activations, out_grads, proj_in_t, proj_out_t, queries):
     tok, d_here = activations.shape
     f_here = out_grads.shape[1]
     rank = proj_in_t.shape[0]
+    rows, count = queries.shape
     out = jax.ShapeDtypeStruct((rank, tok), jnp.float32)
+    out_query = jax.ShapeDtypeStruct((count // 2, rows), queries.dtype)
     return pl.pallas_call(
         project_kernel,
-        in_specs=[pl.BlockSpec(memory_space=pl.ANY)] * 4,
-        out_shape=[out, out],
+        in_specs=[pl.BlockSpec(memory_space=pl.ANY)] * 5,
+        out_shape=[out, out, out_query, out_query],
         scratch_shapes=[
             pltpu.VMEM((tok, d_here), jnp.bfloat16),
             pltpu.VMEM((tok, f_here), jnp.bfloat16),
             pltpu.VMEM((rank, d_here), jnp.bfloat16),
             pltpu.VMEM((rank, f_here), jnp.bfloat16),
-            pltpu.SemaphoreType.DMA((3 + f_here // 128,)),
+            pltpu.VMEM((rows, count), queries.dtype),
+            pltpu.SemaphoreType.DMA((4 + f_here // 128,)),
         ],
         compiler_params=params(53.75),
-    )(activations, out_grads, proj_in_t, proj_out_t)
+    )(activations, out_grads, proj_in_t, proj_out_t, queries)
 
 
 def add_kernel(one_ref, other_ref, out_ref):
@@ -217,19 +227,21 @@
     return scale
 
 
-def share_kernel(row_count, mine, other, query_ref, *refs):
+def share_kernel(row_count, mine, other, query_ref, near_query_ref, *refs):
     factors, weights, features = refs[-3:]
     out_refs = refs[:-3]
     lay_out_factors(mine, other, factors, weights)
     rank = factors.shape[0] // 2
     tokens = factors.shape[1]
     tok = tokens // len(out_refs)
-    first = rank + lax.axis_index("dp") * row_count
     act = factors[:rank, :]
-    for i in range(row_count):
-        row = factors[pl.ds(first + i, 1), :]
-        features[i * rank : (i + 1) * rank, :] = (row * act).astype(jnp.bfloat16)
-    plain = jnp.dot(query_ref[...], features[...], preferred_element_type=jnp.float32)
+    plain = 0.0
+    for near, queries in ((0, query_ref), (1, near_query_ref)):
+        first = rank + (lax.axis_index("dp") ^ near) * row_count
+        for i in range(row_count):
+            row = factors[pl.ds(first + i, 1), :]
+            features[near, i * rank : (i + 1) * rank, :] = (row * act).astype(jnp.bfloat16)
+        plain += jnp.dot(queries[...], features[near], preferred_element_type=jnp.float32)
     weight = weights[...]
     live = weight > 0.0
     act = jnp.where(live, act, 0.0)
@@ -251,7 +263,7 @@
         out_ref[...] = share[:, k * tok : (k + 1) * tok].astype(jnp.bfloat16)
 
 
-def score_shares(mine, other, queries_t, rank, row_count):
+def score_shares(mine, other, queries_t, near_queries_t, rank, row_count):
     blocks, _, tok = mine.shape
     count, rows = queries_t.shape
     out = jax.ShapeDtypeStruct((count, tok), jnp.bfloat16)
@@ -261,10 +273,10 @@
         scratch_shapes=[
             pltpu.VMEM((2 * rank, tok * blocks), jnp.float32),
             pltpu.VMEM((1, tok * blocks), jnp.float32),
-            pltpu.VMEM((rows, tok * blocks), jnp.bfloat16),
+            pltpu.VMEM((2, rows, tok * blocks), jnp.bfloat16),
         ],
         compiler_params=params(40),
-    )(mine, other, queries_t)
+    )(mine, other, queries_t, near_queries_t)
 
 
 def hessian_kernel(row_count, col_count, mine, other, out, factors, weights, weighted, *scratch):
@@ -329,22 +341,28 @@
     )(mine, other)
 
 
-def finish_kernel(*refs):
-    weight_ref, out_ref = refs[-2], refs[-1]
-    total = refs[0][...].astype(jnp.float32)
-    for ref in refs[1:-2]:
-        total = total + ref[...].astype(jnp.float32)
-    total = jnp.where(weight_ref[...] > 0.0, total, 0.0)
-    out_ref[...] = total.T.astype(out_ref.dtype)
-
-
-def finish_scores(shares, weight):
-    count, tok = shares[0].shape
+def finish_kernel(payload_ref, *refs):
+    shares, out_ref = refs[:-1], refs[-1]
+    weight = payload_ref[...].astype(jnp.float32)[-1:]
+    totals = []
+    for near in range(2):
+        total = shares[near][...].astype(jnp.float32)
+        for ref in shares[near + 2 :: 2]:
+            total = total + ref[...].astype(jnp.float32)
+        totals.append(jnp.where(weight > 0.0, total, 0.0).T.astype(out_ref.dtype))
+    even = lax.rem(lax.axis_index("dp"), 2) == 0
+    half = totals[0].shape[1]
+    out_ref[:, :half] = jnp.where(even, totals[0], totals[1])
+    out_ref[:, half:] = jnp.where(even, totals[1], totals[0])
+
+
+def finish_scores(payload, shares):
+    half, tok = shares[0].shape
     return pl.pallas_call(
         finish_kernel,
-        out_shape=jax.ShapeDtypeStruct((tok, count), jnp.bfloat16),
-        compiler_params=params(40),
-    )(*shares, weight)
+        out_shape=jax.ShapeDtypeStruct((tok, 2 * half), jnp.bfloat16),
+        compiler_params=params(40),
+    )(payload, *shares)
 
 
 def swapped(array, axis, distance):
@@ -352,16 +370,18 @@
 
 
 def few_tokens(activations, out_grads, proj_in, proj_out, queries, lengths, credit):
-    tok_rows = activations.shape[0]
-    seq_len = tok_rows // lengths.shape[0]
     dp_count = lax.axis_size("dp")
     query_count = lax.axis_size("query")
     rank = proj_in.shape[1]
     row_count = rank // dp_count
+    seq_len = activations.shape[0] // lengths.shape[0]
     live = jnp.arange(seq_len, dtype=jnp.int32)[None, :] < lengths[:, None]
-    weight = (credit[:, None].astype(jnp.float32) * live.astype(jnp.float32)).reshape(1, -1)
-    keep, send = project(activations, out_grads, proj_in.T, proj_out.T)
+    weight = jnp.where(live, credit[:, None], 0).astype(jnp.float32).reshape(1, -1)
+    keep, send, queries_t, send_queries = project(
+        activations, out_grads, proj_in.T, proj_out.T, queries
+    )
     other = swapped(send, "query", 1)
+    near_queries_t = swapped(send_queries, "dp", 1)
     distance = 2
     while distance < query_count:
         keep = add(keep, other)
@@ -371,10 +391,10 @@
     others = [swapped(payload, "dp", k) for k in reversed(range(1, dp_count))]
     mine = stack([payload] + others[::-1])
     other = swapped(mine, "query", 1)
-    shares = score_shares(mine, other, queries.T, rank, row_count)
+    shares = score_shares(mine, other, queries_t, near_queries_t, rank, row_count)
     arrived = [swapped(shares[k], "dp", k) for k in reversed(range(1, dp_count))]
     hessian = hessian_rows(mine, other, rank, row_count)
-    return hessian, finish_scores([shares[0]] + arrived, weight)
+    return hessian, finish_scores(payload, [shares[0]] + arrived[::-1])
 
 
 def power_of_two(count):
@@ -384,7 +404,7 @@
 def per_device(activations, *others):
     rank = others[1].shape[1]
     dp_count, query_count = lax.axis_size("dp"), lax.axis_size("query")
-    pairs = query_count > 1 and power_of_two(query_count) and power_of_two(dp_count)
+    pairs = min(dp_count, query_count) > 1 and power_of_two(dp_count) and power_of_two(query_count)
     if pairs and activations.shape[0] * dp_count <= rank * rank:
         return few_tokens(activations, *others)
     return many_tokens(activations, *others)

time: 39 us -> 40.5 us (1.038)
  starting transfers between devices: 12.6 us -> 13.7 us
  waiting for transfers between devices: 6.38 us -> 7.25 us
  other arithmetic: 1.38 us -> 0.74 us
  Pallas kernels: 16.5 us -> 17 us
    ppermute x9 -> x10, starting transfers between devices: 12.6 us -> 13.7 us  [swapped(): lax.ppermute(array, axis, [(i, i ^ distance) for i in range(lax.axis_size...]
    ppermute x9 -> x10, waiting for transfers between devices: 6.38 us -> 7.25 us  [swapped(): lax.ppermute(array, axis, [(i, i ^ distance) for i in range(lax.axis_size...]
    pallas_call x1, Pallas kernels: 3.04 us -> 3.78 us  [project(): pl.pallas_call(project_kernel, in_specs=[pl.BlockSpec(memory_space=pl.ANY...]
    mul x1 -> x0, other arithmetic: 0.72 us -> none  [few_tokens(): credit[:, None].astype(jnp.float32) * live.astype(jnp.float32)]
    unnamed x1 -> x2, local copies, waits for them, and re-layouts: 1.25 us -> 0.95 us
  transfers between devices with their start and end apart: 9 -> 10, of which waited for: 6 -> 4; matrix products, arithmetic and copies ran while one was open for 7% -> 2% of each run, Pallas kernels for 26% -> 25%
where the time goes in v8:
time: 40.5 us; the launch traced here: 40.4 us
  Pallas kernels  17 us (42%)
  starting transfers between devices  13.7 us (34%)
  waiting for transfers between devices  7.25 us (18%)
  local copies, waits for them, and re-layouts  0.95 us (2%)
  other arithmetic  0.74 us (2%)
  between operations  0.72 us (2%)
    ppermute x10, starting transfers between devices, swapped(): lax.ppermute(array, axis, [(i, i ^ distance) for i in range(lax.axis_size...  13.7 us
    pallas_call x1, Pallas kernels, hessian_rows(): pl.pallas_call(functools.partial(hessian_kernel, row_count, col_count), o...  10 us
    ppermute x10, waiting for transfers between devices, swapped(): lax.ppermute(array, axis, [(i, i ^ distance) for i in range(lax.axis_size...  7.25 us
    pallas_call x1, Pallas kernels, project(): pl.pallas_call(project_kernel, in_specs=[pl.BlockSpec(memory_space=pl.ANY...  3.78 us
    pallas_call x1, Pallas kernels, score_shares(): pl.pallas_call(functools.partial(share_kernel, row_count), out_shape=[out...  2.42 us
    unnamed x2, local copies, waits for them, and re-layouts  0.95 us
  transfers between devices with their start and end apart: 10, of which 4 were waited for; matrix products, arithmetic and copies ran while one was open for 2% of the time, Pallas kernels for 25%

profile of v8, /device:TPU:0, one launch (start us, length us, event | category | flops | bytes accessed | tf_op | source)
XLA Modules:
  0.0 40.4 jit_solution(1635264949690794960)
XLA Ops:
  0.6 3.8 %shard_map.86 = (f32[64,256]{1,0:T(8,128)S(1)}, f32[64,256]{1,0:T(8,128)S(1)}, bf16[128,1024]{1,0:T(8,128)(2,1)}, bf16[128,1024]{1,0:T(8,128)(2,1)}) custom-call(bf16[256,1024]{1,0:T(8,128)(2,1)} %act.1, bf16[256,3584]{1,0:T(8,128)(2,1)} %grad.1, bf16[64,1024]{1,0:T(8,128)(2,1)} %bitcast.5, bf16[64,3584]{1,0:T(8,128)(2,1)} %bitcast.4, bf16[1024,256]{1,0:T(8,128)(2,1)} %query.1), custom_call_target="tpu_custom_call" | custom-call | tf_op jit(solution)/shard_map/pallas_call | solution.py:153
  4.4 0.5 %collective-permute-start = (f32[64,256]{1,0:T(8,128)S(1)}, f32[64,256]{1,0:T(8,128)S(1)}, u32[]{:S(2)}, u32[]{:S(2)}) collective-permute-start(f32[64,256]{1,0:T(8,128)S(1)} %get-tuple-element.11), channel_id=1, source_target_pairs={{0,1},{1,0},{2,3},{3,2},{4,5},{5,4},{6,7},{7,6},{8,9},{9,8},{10,11... | collective-permute-start | bytes 196616 | tf_op jit(solution)/shard_map/ppermute | solution.py:369
  4.9 2.6 %collective-permute-start.6 = (bf16[128,1024]{1,0:T(8,128)(2,1)}, bf16[128,1024]{1,0:T(8,128)(2,1)S(1)}, u32[]{:S(2)}, u32[]{:S(2)}) collective-permute-start(bf16[128,1024]{1,0:T(8,128)(2,1)} %get-tuple-element.13), channel_id=1, source_target_pairs={{0,4},{4,0},{8,12},{12,8},{1,5},{5,1},{9,13},{13,9},{2,6},{6,2},{1... | collective-permute-start | bytes 786440 | tf_op jit(solution)/shard_map/ppermute | solution.py:369
  7.6 0.0 collective-permute-done.other_ref
  7.6 1.6 %collective-permute-start.1 = (f32[64,256]{1,0:T(8,128)S(1)}, f32[64,256]{1,0:T(8,128)S(1)}, u32[]{:S(2)}, u32[]{:S(2)}) collective-permute-start(f32[64,256]{1,0:T(8,128)S(1)} %shard_map.87.one_ref), channel_id=1, source_target_pairs={{0,2},{1,3},{2,0},{3,1},{4,6},{5,7},{6,4},{7,5},{8,10},{9,11},{10,... | collective-permute-start | bytes 196616 | tf_op jit(solution)/shard_map/ppermute | solution.py:369
  9.2 0.7 %fusion = f32[2,128]{1,0:T(2,128)S(1)} fusion(s32[2]{0:T(128)} %param.13, s32[2]{0:T(128)} %param.12), kind=kLoop, calls=%fused_computation.1 | loop fusion | flops 768 | bytes 1040 | tf_op jit(solution)/shard_map/convert_element_type | solution.py:379
  9.9 2.0 %collective-permute-done.1.other_ref = f32[64,256]{1,0:T(8,128)S(1)} collective-permute-done((f32[64,256]{1,0:T(8,128)S(1)}, f32[64,256]{1,0:T(8,128)S(1)}, u32[]{:S(2)}, u32[]{:S(2)}) %collective-permute-start.1) | collective-permute-done | bytes 65568 | tf_op jit(solution)/shard_map/ppermute | solution.py:369
  12.0 3.3 %collective-permute-start.4 = (bf16[80,256]{1,0:T(8,128)(2,1)S(1)}, bf16[80,256]{1,0:T(8,128)(2,1)S(1)}, u32[]{:S(2)}, u32[]{:S(2)}) collective-permute-start(bf16[80,256]{1,0:T(8,128)(2,1)S(1)} %shard_map.88.refs_0_.payload_ref), channel_id=1, source_target_pairs={{0,12},{4,8},{8,4},{12,0},{1,13},{5,9},{9,5},{13,1},{2,14},{6,10},... | collective-permute-start | bytes 122888 | tf_op jit(solution)/shard_map/ppermute | solution.py:369
  15.2 0.0 collective-permute-start.3
  15.2 1.2 %collective-permute-start.2 = (bf16[80,256]{1,0:T(8,128)(2,1)S(1)}, bf16[80,256]{1,0:T(8,128)(2,1)S(1)}, u32[]{:S(2)}, u32[]{:S(2)}) collective-permute-start(bf16[80,256]{1,0:T(8,128)(2,1)S(1)} %shard_map.88.refs_0_.payload_ref), channel_id=1, source_target_pairs={{0,4},{4,0},{8,12},{12,8},{1,5},{5,1},{9,13},{13,9},{2,6},{6,2},{1... | collective-permute-start | bytes 122888 | tf_op jit(solution)/shard_map/ppermute | solution.py:369
  16.4 1.9 %collective-permute-done.4.refs_3_ = bf16[80,256]{1,0:T(8,128)(2,1)S(1)} collective-permute-done((bf16[80,256]{1,0:T(8,128)(2,1)S(1)}, bf16[80,256]{1,0:T(8,128)(2,1)S(1)}, u32[]{:S(2)}, u32[]{:S(2)}) %collective-permute-start.4) | collective-permute-done | bytes 40992 | tf_op jit(solution)/shard_map/ppermute | solution.py:369
  18.3 2.0 %collective-permute-done.3.refs_2_ = bf16[80,256]{1,0:T(8,128)(2,1)S(1)} collective-permute-done((bf16[80,256]{1,0:T(8,128)(2,1)S(1)}, bf16[80,256]{1,0:T(8,128)(2,1)S(1)}, u32[]{:S(2)}, u32[]{:S(2)}) %collective-permute-start.3) | collective-permute-done | bytes 40992 | tf_op jit(solution)/shard_map/ppermute | solution.py:369
  20.2 0.0 collective-permute-done.2.refs_1_
  20.3 0.1 collective-permute-start.5
  20.3 0.0 collective-permute-done.6.near_query_ref
  20.3 1.4 %collective-permute-done.5.other = bf16[4,80,256]{2,1,0:T(8,128)(2,1)S(1)} collective-permute-done((bf16[4,80,256]{2,1,0:T(8,128)(2,1)S(1)}, bf16[4,80,256]{2,1,0:T(8,128)(2,1)S(1)}, u32[]{:S(2)}, u32[]{:S(2)}) %collective-permute-start.5) | collective-permute-done | bytes 163872 | tf_op jit(solution)/shard_map/ppermute | solution.py:369
  21.7 0.0 copy-start
  21.7 0.9 %copy-done = bf16[128,1024]{1,0:T(8,128)(2,1)S(1)} copy-done((bf16[128,1024]{1,0:T(8,128)(2,1)S(1)}, bf16[128,1024]{1,0:T(8,128)(2,1)}, u32[]{:S(2)}) %copy-start) | copy-done | bytes 262168
  22.7 2.4 %shard_map.91 = (bf16[128,256]{1,0:T(8,128)(2,1)S(1)}, bf16[128,256]{1,0:T(8,128)(2,1)S(1)}, bf16[128,256]{1,0:T(8,128)(2,1)S(1)}, bf16[128,256]{1,0:T(8,128)(2,1)S(1)}) custom-call(bf16[4,80,256]{2,1,0:T(8,128)(2,1)S(1)} %shard_map.89.mine, bf16[4,80,256]{2,1,0:T(8,128)(2,1)S(1)} %collective-permute-done.5.other, bf16[128,1024]{1,0:T(8,128)(2,1)S(1)} %copy-done, ...), custom_call_target="tpu_custom_call" | custom-call | tf_op jit(solution)/shard_map/pallas_call | solution.py:270
  25.1 0.2 collective-permute-start.7
  25.3 1.8 %collective-permute-start.8 = (bf16[128,256]{1,0:T(8,128)(2,1)S(1)}, bf16[128,256]{1,0:T(8,128)(2,1)S(1)}, u32[]{:S(2)}, u32[]{:S(2)}) collective-permute-start(bf16[128,256]{1,0:T(8,128)(2,1)S(1)} %get-tuple-element.16), channel_id=1, source_target_pairs={{0,8},{4,12},{8,0},{12,4},{1,9},{5,13},{9,1},{13,5},{2,10},{6,14},... | collective-permute-start | bytes 196616 | tf_op jit(solution)/shard_map/ppermute | solution.py:369
  27.1 2.4 %collective-permute-start.9 = (bf16[128,256]{1,0:T(8,128)(2,1)S(1)}, bf16[128,256]{1,0:T(8,128)(2,1)S(1)}, u32[]{:S(2)}, u32[]{:S(2)}) collective-permute-start(bf16[128,256]{1,0:T(8,128)(2,1)S(1)} %get-tuple-element.17), channel_id=1, source_target_pairs={{0,12},{4,8},{8,4},{12,0},{1,13},{5,9},{9,5},{13,1},{2,14},{6,10},... | collective-permute-start | bytes 196616 | tf_op jit(solution)/shard_map/ppermute | solution.py:369
  29.5 10.0 %shard_map.90 = f32[1024,4096]{1,0:T(8,128)} custom-call(bf16[4,80,256]{2,1,0:T(8,128)(2,1)S(1)} %shard_map.89.mine, bf16[4,80,256]{2,1,0:T(8,128)(2,1)S(1)} %collective-permute-done.5.other), custom_call_target="tpu_custom_call" | custom-call | tf_op jit(solution)/shard_map/pallas_call | solution.py:327
  39.6 0.0 collective-permute-done.7.refs_1_
  39.6 0.0 collective-permute-done.8.refs_2_
  39.6 0.0 collective-permute-done.9.refs_3_
  39.6 0.8 %shard_map.92 = bf16[256,256]{1,0:T(8,128)(2,1)} custom-call(bf16[80,256]{1,0:T(8,128)(2,1)S(1)} %shard_map.88.refs_0_.payload_ref, bf16[128,256]{1,0:T(8,128)(2,1)S(1)} %get-tuple-element.14.refs_0_, bf16[128,256]{1,0:T(8,128)(2,1)S(1)} %collective-permute-done.7.refs_1_, bf16[128,256]{1,0:T(8,128)(2,1)S(1)} %collective-permute-done.8.refs_2_, ...), custom_call_target="tpu_custom_call" | custom-call | tf_op jit(solution)/shard_map/pallas_call | solution.py:361
  (3 shorter events, 0.0 us)
Async XLA Ops:
  4.4 3.2 %collective-permute-start = (f32[64,256]{1,0:T(8,128)S(1)}, f32[64,256]{1,0:T(8,128)S(1)}, u32[]{:S(2)}, u32[]{:S(2)}) collective-permute-start(f32[64,256]{1,0:T(8,128)S(1)} %get-tuple-element.11), channel_id=1, source_target_pairs={{0,1},{1,0},{2,3},{3,2},{4,5},{5,4},{6,7},{7,6},{8,9},{9,8},{10,11... | collective-permute-start | bytes 196616 | tf_op jit(solution)/shard_map/ppermute | solution.py:369
  4.9 15.4 %collective-permute-start.6 = (bf16[128,1024]{1,0:T(8,128)(2,1)}, bf16[128,1024]{1,0:T(8,128)(2,1)S(1)}, u32[]{:S(2)}, u32[]{:S(2)}) collective-permute-start(bf16[128,1024]{1,0:T(8,128)(2,1)} %get-tuple-element.13), channel_id=1, source_target_pairs={{0,4},{4,0},{8,12},{12,8},{1,5},{5,1},{9,13},{13,9},{2,6},{6,2},{1... | collective-permute-start | bytes 786440 | tf_op jit(solution)/shard_map/ppermute | solution.py:369
  7.6 4.3 %collective-permute-start.1 = (f32[64,256]{1,0:T(8,128)S(1)}, f32[64,256]{1,0:T(8,128)S(1)}, u32[]{:S(2)}, u32[]{:S(2)}) collective-permute-start(f32[64,256]{1,0:T(8,128)S(1)} %shard_map.87.one_ref), channel_id=1, source_target_pairs={{0,2},{1,3},{2,0},{3,1},{4,6},{5,7},{6,4},{7,5},{8,10},{9,11},{10,... | collective-permute-start | bytes 196616 | tf_op jit(solution)/shard_map/ppermute | solution.py:369
  12.0 6.3 %collective-permute-start.4 = (bf16[80,256]{1,0:T(8,128)(2,1)S(1)}, bf16[80,256]{1,0:T(8,128)(2,1)S(1)}, u32[]{:S(2)}, u32[]{:S(2)}) collective-permute-start(bf16[80,256]{1,0:T(8,128)(2,1)S(1)} %shard_map.88.refs_0_.payload_ref), channel_id=1, source_target_pairs={{0,12},{4,8},{8,4},{12,0},{1,13},{5,9},{9,5},{13,1},{2,14},{6,10},... | collective-permute-start | bytes 122888 | tf_op jit(solution)/shard_map/ppermute | solution.py:369
  15.2 5.0 %collective-permute-start.3 = (bf16[80,256]{1,0:T(8,128)(2,1)S(1)}, bf16[80,256]{1,0:T(8,128)(2,1)S(1)}, u32[]{:S(2)}, u32[]{:S(2)}) collective-permute-start(bf16[80,256]{1,0:T(8,128)(2,1)S(1)} %shard_map.88.refs_0_.payload_ref), channel_id=1, source_target_pairs={{0,8},{4,12},{8,0},{12,4},{1,9},{5,13},{9,1},{13,5},{2,10},{6,14},... | collective-permute-start | bytes 122888 | tf_op jit(solution)/shard_map/ppermute | solution.py:369
  15.2 5.0 %collective-permute-start.2 = (bf16[80,256]{1,0:T(8,128)(2,1)S(1)}, bf16[80,256]{1,0:T(8,128)(2,1)S(1)}, u32[]{:S(2)}, u32[]{:S(2)}) collective-permute-start(bf16[80,256]{1,0:T(8,128)(2,1)S(1)} %shard_map.88.refs_0_.payload_ref), channel_id=1, source_target_pairs={{0,4},{4,0},{8,12},{12,8},{1,5},{5,1},{9,13},{13,9},{2,6},{6,2},{1... | collective-permute-start | bytes 122888 | tf_op jit(solution)/shard_map/ppermute | solution.py:369
  20.3 1.5 %collective-permute-start.5 = (bf16[4,80,256]{2,1,0:T(8,128)(2,1)S(1)}, bf16[4,80,256]{2,1,0:T(8,128)(2,1)S(1)}, u32[]{:S(2)}, u32[]{:S(2)}) collective-permute-start(bf16[4,80,256]{2,1,0:T(8,128)(2,1)S(1)} %shard_map.89.mine), channel_id=1, source_target_pairs={{0,1},{1,0},{2,3},{3,2},{4,5},{5,4},{6,7},{7,6},{8,9},{9,8},{10,11... | collective-permute-start | bytes 491528 | tf_op jit(solution)/shard_map/ppermute | solution.py:369
  21.7 1.0 %copy-start = (bf16[128,1024]{1,0:T(8,128)(2,1)S(1)}, bf16[128,1024]{1,0:T(8,128)(2,1)}, u32[]{:S(2)}) copy-start(bf16[128,1024]{1,0:T(8,128)(2,1)} %get-tuple-element.12.query_ref) | copy-start | bytes 786436
  25.1 14.5 %collective-permute-start.7 = (bf16[128,256]{1,0:T(8,128)(2,1)S(1)}, bf16[128,256]{1,0:T(8,128)(2,1)S(1)}, u32[]{:S(2)}, u32[]{:S(2)}) collective-permute-start(bf16[128,256]{1,0:T(8,128)(2,1)S(1)} %get-tuple-element.15), channel_id=1, source_target_pairs={{0,4},{4,0},{8,12},{12,8},{1,5},{5,1},{9,13},{13,9},{2,6},{6,2},{1... | collective-permute-start | bytes 196616 | tf_op jit(solution)/shard_map/ppermute | solution.py:369
  25.3 14.2 %collective-permute-start.8 = (bf16[128,256]{1,0:T(8,128)(2,1)S(1)}, bf16[128,256]{1,0:T(8,128)(2,1)S(1)}, u32[]{:S(2)}, u32[]{:S(2)}) collective-permute-start(bf16[128,256]{1,0:T(8,128)(2,1)S(1)} %get-tuple-element.16), channel_id=1, source_target_pairs={{0,8},{4,12},{8,0},{12,4},{1,9},{5,13},{9,1},{13,5},{2,10},{6,14},... | collective-permute-start | bytes 196616 | tf_op jit(solution)/shard_map/ppermute | solution.py:369
  27.1 12.4 %collective-permute-start.9 = (bf16[128,256]{1,0:T(8,128)(2,1)S(1)}, bf16[128,256]{1,0:T(8,128)(2,1)S(1)}, u32[]{:S(2)}, u32[]{:S(2)}) collective-permute-start(bf16[128,256]{1,0:T(8,128)(2,1)S(1)} %get-tuple-element.17), channel_id=1, source_target_pairs={{0,12},{4,8},{8,4},{12,0},{1,13},{5,9},{9,5},{13,1},{2,14},{6,10},... | collective-permute-start | bytes 196616 | tf_op jit(solution)/shard_map/ppermute | solution.py:369

commit v9 on v8

--- a/solution.py
+++ b/solution.py
@@ -109,31 +109,24 @@
     return pltpu.CompilerParams(vmem_limit_bytes=int(mib * MIB))
 
 
-def project_kernel(
-    act, grad, pin, pout, query, keep_ref, send_ref, keep_query_ref, send_query_ref, *scratch
-):
-    act_v, grad_v, pin_v, pout_v, query_v, sems = scratch
+def project_kernel(act, grad, pin, pout, keep_ref, send_ref, act_v, grad_v, pin_v, pout_v, sems):
     chunk = act.shape[1]
     while grad.shape[1] % chunk:
         chunk //= 2
     spans = [pl.ds(c, chunk) for c in range(0, grad.shape[1], chunk)]
-    pairs = [(pin, pin_v), (act, act_v), (query, query_v), (pout, pout_v)]
-    pairs += [(grad.at[:, span], grad_v.at[:, span]) for span in spans]
-    copies = [pltpu.make_async_copy(s, d, sems.at[n]) for n, (s, d) in enumerate(pairs)]
+    copies = [pltpu.make_async_copy(s, d, sems.at[n]) for n, (s, d) in enumerate(((pin, pin_v), (act, act_v), (pout, pout_v)))]
+    copies += [
+        pltpu.make_async_copy(grad.at[:, span], grad_v.at[:, span], sems.at[3 + n])
+        for n, span in enumerate(spans)
+    ]
     for copy in copies:
         copy.start()
     copies[0].wait()
     copies[1].wait()
     part_act = lax.dot_general(pin_v[...], act_v[...], NT, preferred_element_type=jnp.float32)
     copies[2].wait()
-    query_t = query_v[...].T
-    half = query_t.shape[0] // 2
-    even = lax.rem(lax.axis_index("dp"), 2) == 0
-    keep_query_ref[...] = jnp.where(even, query_t[:half], query_t[half:])
-    send_query_ref[...] = jnp.where(even, query_t[half:], query_t[:half])
-    copies[3].wait()
     part_grad = jnp.zeros_like(part_act)
-    for copy, span in zip(copies[4:], spans):
+    for copy, span in zip(copies[3:], spans):
         copy.wait()
         part_grad += lax.dot_general(
             pout_v[:, span], grad_v[:, span], NT, preferred_element_type=jnp.float32
@@ -143,27 +136,47 @@
     send_ref[...] = jnp.where(even, part_grad, part_act)
 
 
-def project(activations, out_grads, proj_in_t, proj_out_t, queries):
+def project(activations, out_grads, proj_in_t, proj_out_t):
     tok, d_here = activations.shape
     f_here = out_grads.shape[1]
     rank = proj_in_t.shape[0]
-    rows, count = queries.shape
     out = jax.ShapeDtypeStruct((rank, tok), jnp.float32)
-    out_query = jax.ShapeDtypeStruct((count // 2, rows), queries.dtype)
     return pl.pallas_call(
         project_kernel,
-        in_specs=[pl.BlockSpec(memory_space=pl.ANY)] * 5,
-        out_shape=[out, out, out_query, out_query],
+        in_specs=[pl.BlockSpec(memory_space=pl.ANY)] * 4,
+        out_shape=[out, out],
         scratch_shapes=[
             pltpu.VMEM((tok, d_here), jnp.bfloat16),
             pltpu.VMEM((tok, f_here), jnp.bfloat16),
             pltpu.VMEM((rank, d_here), jnp.bfloat16),
             pltpu.VMEM((rank, f_here), jnp.bfloat16),
-            pltpu.VMEM((rows, count), queries.dtype),
-            pltpu.SemaphoreType.DMA((4 + f_here // 128,)),
+            pltpu.SemaphoreType.DMA((3 + f_here // 128,)),
         ],
         compiler_params=params(53.75),
-    )(activations, out_grads, proj_in_t, proj_out_t, queries)
+    )(activations, out_grads, proj_in_t, proj_out_t)
+
+
+def split_kernel(query, _, keep_ref, send_ref, query_v, sem):
+    fetch = pltpu.make_async_copy(query, query_v, sem)
+    fetch.start()
+    fetch.wait()
+    query_t = query_v[...].T
+    half = keep_ref.shape[0]
+    even = lax.rem(lax.axis_index("dp"), 2) == 0
+    keep_ref[...] = jnp.where(even, query_t[:half], query_t[half:])
+    send_ref[...] = jnp.where(even, query_t[half:], query_t[:half])
+
+
+def split_queries(queries, after):
+    rows, count = queries.shape
+    out = jax.ShapeDtypeStruct((count // 2, rows), queries.dtype)
+    return pl.pallas_call(
+        split_kernel,
+        in_specs=[pl.BlockSpec(memory_space=pl.ANY)] * 2,
+        out_shape=[out, out],
+        scratch_shapes=[pltpu.VMEM(queries.shape, queries.dtype), pltpu.SemaphoreType.DMA],
+        compiler_params=params(53),
+    )(queries, after)
 
 
 def add_kernel(one_ref, other_ref, out_ref):
@@ -193,29 +206,44 @@
     )(one, other, weight)
 
 
-def stack_kernel(*refs):
+def stack_kernel(_, *refs):
     for k, ref in enumerate(refs[:-1]):
         refs[-1][k] = ref[...]
 
 
-def stack(parts):
+def stack(parts, after):
+    whole = pl.BlockSpec(memory_space=pltpu.VMEM)
     return pl.pallas_call(
         stack_kernel,
+        in_specs=[pl.BlockSpec(memory_space=pl.ANY)] + [whole] * len(parts),
         out_shape=jax.ShapeDtypeStruct((len(parts),) + parts[0].shape, parts[0].dtype),
-        compiler_params=params(40),
-    )(*parts)
-
-
-def lay_out_factors(mine, other, factors, weights):
-    blocks, _, tok = mine.shape
+        compiler_params=params(30),
+    )(after, *parts)
+
+
+def lay_out_factors(blocks, factors, weights):
     rank = factors.shape[0] // 2
     here = pl.multiple_of(lax.rem(lax.axis_index("query"), 2) * rank, rank)
     there = pl.multiple_of(rank - here, rank)
-    for k in range(blocks):
-        span = slice(k * tok, (k + 1) * tok)
-        factors[pl.ds(here, rank), span] = mine[k, :rank].astype(jnp.float32)
-        factors[pl.ds(there, rank), span] = other[k, :rank].astype(jnp.float32)
-        weights[:, span] = mine[k, rank:].astype(jnp.float32)[:1]
+    for k, (mine, other) in enumerate(blocks):
+        span = slice(k * mine.shape[1], (k + 1) * mine.shape[1])
+        factors[pl.ds(here, rank), span] = mine[:rank].astype(jnp.float32)
+        factors[pl.ds(there, rank), span] = other[:rank].astype(jnp.float32)
+        weights[:, span] = mine[rank:].astype(jnp.float32)[:1]
+
+
+def block_pairs(mine, other):
+    return [(mine.at[k], other.at[k]) for k in range(mine.shape[0])]
+
+
+def weigh_rows(row_count, factors, weights, weighted):
+    rank = factors.shape[0] // 2
+    act, weight = factors[:rank, :], weights[...]
+    first = rank + lax.axis_index("dp") * row_count
+    for i in range(row_count):
+        left = (factors[pl.ds(first + i, 1), :] * act).astype(jnp.bfloat16)
+        left = (weight * left.astype(jnp.float32)).astype(jnp.bfloat16)
+        weighted[i * rank : (i + 1) * rank, :] = left
 
 
 def range_scale(values):
@@ -227,10 +255,10 @@
     return scale
 
 
-def share_kernel(row_count, mine, other, query_ref, near_query_ref, *refs):
+def share_kernel(row_count, own, own_other, mine, other, query_ref, near_query_ref, *refs):
     factors, weights, features = refs[-3:]
     out_refs = refs[:-3]
-    lay_out_factors(mine, other, factors, weights)
+    lay_out_factors([(own, own_other)] + block_pairs(mine, other), factors, weights)
     rank = factors.shape[0] // 2
     tokens = factors.shape[1]
     tok = tokens // len(out_refs)
@@ -263,8 +291,8 @@
         out_ref[...] = share[:, k * tok : (k + 1) * tok].astype(jnp.bfloat16)
 
 
-def score_shares(mine, other, queries_t, near_queries_t, rank, row_count):
-    blocks, _, tok = mine.shape
+def score_shares(own, own_other, mine, other, queries_t, near_queries_t, rank, row_count):
+    blocks, tok = mine.shape[0] + 1, mine.shape[2]
     count, rows = queries_t.shape
     out = jax.ShapeDtypeStruct((count, tok), jnp.bfloat16)
     return pl.pallas_call(
@@ -275,35 +303,64 @@
             pltpu.VMEM((1, tok * blocks), jnp.float32),
             pltpu.VMEM((2, rows, tok * blocks), jnp.bfloat16),
         ],
-        compiler_params=params(40),
-    )(mine, other, queries_t, near_queries_t)
-
-
-def hessian_kernel(row_count, col_count, mine, other, out, factors, weights, weighted, *scratch):
-    rights, result, sems = scratch[:2], scratch[2], scratch[3]
+        compiler_params=params(30),
+    )(own, own_other, mine, other, queries_t, near_queries_t)
+
+
+def build_columns(first, act, factors, right):
+    rank = act.shape[0]
+    for i in range(right.shape[0] // rank):
+        row = rank + first + i
+        right[i * rank : (i + 1) * rank, :] = (factors[row : row + 1, :] * act).astype(jnp.bfloat16)
+
+
+def own_kernel(row_count, col_count, own, own_other, out, factors, weights, weighted, *rights):
     rank = factors.shape[0] // 2
-    tokens = factors.shape[1]
+    cols = col_count * rank
+    lay_out_factors([(own, own_other)], factors, weights)
+    weigh_rows(row_count, factors, weights, weighted)
+    act = factors[:rank, :]
+    build_columns(0, act, factors, rights[0])
+    for step in range(rank // col_count):
+        if (step + 1) * col_count < rank:
+            build_columns((step + 1) * col_count, act, factors, rights[(step + 1) % 2])
+        out[:, step * cols : (step + 1) * cols] = lax.dot_general(
+            weighted[...], rights[step % 2][...], NT, preferred_element_type=jnp.float32
+        )
+
+
+def own_tokens_sum(own, own_other, rank, row_count, col_count=8):
+    tok = own.shape[1]
     rows, cols = row_count * rank, col_count * rank
-    steps = rank // col_count
-    lay_out_factors(mine, other, factors, weights)
-    act, weight = factors[:rank, :], weights[...]
-    first = rank + lax.axis_index("dp") * row_count
-    for i in range(row_count):
-        left = (factors[pl.ds(first + i, 1), :] * act).astype(jnp.bfloat16)
-        left = (weight * left.astype(jnp.float32)).astype(jnp.bfloat16)
-        weighted[i * rank : (i + 1) * rank, :] = left
-
-    def build(step):
-        for i in range(col_count):
-            row = rank + step * col_count + i
-            right = (factors[row : row + 1, :] * act).astype(jnp.bfloat16)
-            rights[step % 2][i * rank : (i + 1) * rank, :] = right
-
+    return pl.pallas_call(
+        functools.partial(own_kernel, row_count, col_count),
+        out_shape=jax.ShapeDtypeStruct((rows, rank * rank), jnp.float32),
+        scratch_shapes=[
+            pltpu.VMEM((2 * rank, tok), jnp.float32),
+            pltpu.VMEM((1, tok), jnp.float32),
+            pltpu.VMEM((rows, tok), jnp.bfloat16),
+            pltpu.VMEM((cols, tok), jnp.bfloat16),
+            pltpu.VMEM((cols, tok), jnp.bfloat16),
+        ],
+        compiler_params=params(16),
+    )(own, own_other)
+
+
+def hessian_kernel(row_count, col_count, mine, other, own_sum, out, *scratch):
+    factors, weights, weighted, rights = *scratch[:3], scratch[3:5]
+    result, sems = scratch[5:]
+    rank = factors.shape[0] // 2
+    blocks = mine.shape[0]
+    tokens = factors.shape[1] // blocks * (blocks + 1)
+    rows, cols = row_count * rank, col_count * rank
+    lay_out_factors(block_pairs(mine, other), factors, weights)
+    weigh_rows(row_count, factors, weights, weighted)
+    act = factors[:rank, :]
     copies = []
-    build(0)
-    for step in range(steps):
-        if step + 1 < steps:
-            build(step + 1)
+    build_columns(0, act, factors, rights[0])
+    for step in range(rank // col_count):
+        if (step + 1) * col_count < rank:
+            build_columns((step + 1) * col_count, act, factors, rights[(step + 1) % 2])
         for row in range(0, rows, TILE):
             here = pl.ds(row, TILE), pl.ds(step * cols, cols)
             tile = lax.dot_general(
@@ -312,7 +369,7 @@
                 NT,
                 preferred_element_type=jnp.float32,
             )
-            result[here] = tile * (1.0 / tokens)
+            result[here] = (own_sum[here] + tile) * (1.0 / tokens)
             copy = pltpu.make_async_copy(result.at[here], out.at[here], sems.at[len(copies)])
             copy.start()
             copies.append(copy)
@@ -320,7 +377,7 @@
         copy.wait()
 
 
-def hessian_rows(mine, other, rank, row_count, col_count=8):
+def hessian_rows(mine, other, own_sum, rank, row_count, col_count=8):
     blocks, _, tok = mine.shape
     feat = rank * rank
     rows, cols = row_count * rank, col_count * rank
@@ -337,8 +394,8 @@
             pltpu.VMEM((rows, feat), jnp.float32),
             pltpu.SemaphoreType.DMA((feat // cols * (rows // TILE),)),
         ],
-        compiler_params=params(40),
-    )(mine, other)
+        compiler_params=params(30),
+    )(mine, other, own_sum)
 
 
 def finish_kernel(payload_ref, *refs):
@@ -377,24 +434,27 @@
     seq_len = activations.shape[0] // lengths.shape[0]
     live = jnp.arange(seq_len, dtype=jnp.int32)[None, :] < lengths[:, None]
     weight = jnp.where(live, credit[:, None], 0).astype(jnp.float32).reshape(1, -1)
-    keep, send, queries_t, send_queries = project(
-        activations, out_grads, proj_in.T, proj_out.T, queries
-    )
+    keep, send = project(activations, out_grads, proj_in.T, proj_out.T)
     other = swapped(send, "query", 1)
-    near_queries_t = swapped(send_queries, "dp", 1)
     distance = 2
     while distance < query_count:
         keep = add(keep, other)
         other = swapped(keep, "query", distance)
         distance *= 2
-    payload = add_to_payload(keep, other, weight)
-    others = [swapped(payload, "dp", k) for k in reversed(range(1, dp_count))]
-    mine = stack([payload] + others[::-1])
+    queries_t, send_queries = split_queries(queries, keep)
+    near_queries_t = swapped(send_queries, "dp", 1)
+    own = add_to_payload(keep, other, weight)
+    others = [swapped(own, "dp", k) for k in reversed(range(1, dp_count))]
+    own_other = swapped(own, "query", 1)
+    own_sum = own_tokens_sum(own, own_other, rank, row_count)
+    mine = stack(others[::-1], own_sum)
     other = swapped(mine, "query", 1)
-    shares = score_shares(mine, other, queries_t, near_queries_t, rank, row_count)
+    shares = score_shares(
+        own, own_other, mine, other, queries_t, near_queries_t, rank, row_count
+    )
     arrived = [swapped(shares[k], "dp", k) for k in reversed(range(1, dp_count))]
-    hessian = hessian_rows(mine, other, rank, row_count)
-    return hessian, finish_scores(payload, [shares[0]] + arrived[::-1])
+    hessian = hessian_rows(mine, other, own_sum, rank, row_count)
+    return hessian, finish_scores(own, [shares[0]] + arrived[::-1])
 
 
 def power_of_two(count):

time: 40.5 us -> 39.3 us (0.970)
  waiting for transfers between devices: 7.25 us -> 5.71 us
  local copies, waits for them, and re-layouts: 0.95 us -> 0 us
  Pallas kernels: 17 us -> 17.8 us
    pallas_call x1 -> x3, Pallas kernels: 0.01 us -> 3.66 us  [the longest x1 2.41 us: own_tokens_sum(): pl.pallas_call(functools.partial(own_kernel, row_count, col_count), out_s...]
    pallas_call x1, Pallas kernels: 10 us -> 7.87 us  [hessian_rows(): pl.pallas_call(functools.partial(hessian_kernel, row_count, col_count), o...]
    ppermute x10 -> x11, waiting for transfers between devices: 7.25 us -> 5.71 us  [swapped(): lax.ppermute(array, axis, [(i, i ^ distance) for i in range(lax.axis_size...]
    unnamed x2 -> x0, local copies, waits for them, and re-layouts: 0.95 us -> none
    pallas_call x1, Pallas kernels: 3.78 us -> 3.04 us  [project(): pl.pallas_call(project_kernel, in_specs=[pl.BlockSpec(memory_space=pl.ANY...]
    ppermute x10 -> x11, starting transfers between devices: 13.7 us -> 14.1 us  [swapped(): lax.ppermute(array, axis, [(i, i ^ distance) for i in range(lax.axis_size...]
  transfers between devices with their start and end apart: 10 -> 11, of which waited for: 4 -> 4; matrix products, arithmetic and copies ran while one was open for 2% -> 2% of each run, Pallas kernels for 25% -> 30%
where the time goes in v9:
time: 39.3 us; the launch traced here: 39.1 us
  Pallas kernels  17.8 us (45%)
  starting transfers between devices  14.1 us (36%)
  waiting for transfers between devices  5.71 us (15%)
  other arithmetic  0.74 us (2%)
  between operations  0.73 us (2%)
    ppermute x11, starting transfers between devices, swapped(): lax.ppermute(array, axis, [(i, i ^ distance) for i in range(lax.axis_size...  14.1 us
    pallas_call x1, Pallas kernels, hessian_rows(): pl.pallas_call(functools.partial(hessian_kernel, row_count, col_count), o...  7.87 us
    ppermute x11, waiting for transfers between devices, swapped(): lax.ppermute(array, axis, [(i, i ^ distance) for i in range(lax.axis_size...  5.71 us
    pallas_call x1, Pallas kernels, project(): pl.pallas_call(project_kernel, in_specs=[pl.BlockSpec(memory_space=pl.ANY...  3.04 us
    pallas_call x1, Pallas kernels, score_shares(): pl.pallas_call(functools.partial(share_kernel, row_count), out_shape=[out...  2.42 us
    pallas_call x1, Pallas kernels, own_tokens_sum(): pl.pallas_call(functools.partial(own_kernel, row_count, col_count), out_s...  2.41 us
    pallas_call x1, Pallas kernels, split_queries(): pl.pallas_call(split_kernel, in_specs=[pl.BlockSpec(memory_space=pl.ANY)]...  1.25 us
  transfers between devices with their start and end apart: 11, of which 4 were waited for; matrix products, arithmetic and copies ran while one was open for 2% of the time, Pallas kernels for 30%

profile of v9, /device:TPU:0, one launch (start us, length us, event | category | flops | bytes accessed | tf_op | source)
XLA Modules:
  0.0 39.1 jit_solution(16359818477319142031)
XLA Ops:
  0.6 3.0 %shard_map.86 = (f32[64,256]{1,0:T(8,128)S(1)}, f32[64,256]{1,0:T(8,128)S(1)}) custom-call(bf16[256,1024]{1,0:T(8,128)(2,1)} %act.1, bf16[256,3584]{1,0:T(8,128)(2,1)} %grad.1, bf16[64,1024]{1,0:T(8,128)(2,1)} %bitcast.5, bf16[64,3584]{1,0:T(8,128)(2,1)} %bitcast.4), custom_call_target="tpu_custom_call" | custom-call | tf_op jit(solution)/shard_map/pallas_call | solution.py:144
  3.7 0.5 %collective-permute-start = (f32[64,256]{1,0:T(8,128)S(1)}, f32[64,256]{1,0:T(8,128)S(1)}, u32[]{:S(2)}, u32[]{:S(2)}) collective-permute-start(f32[64,256]{1,0:T(8,128)S(1)} %get-tuple-element.11), channel_id=1, source_target_pairs={{0,1},{1,0},{2,3},{3,2},{4,5},{5,4},{6,7},{7,6},{8,9},{9,8},{10,11... | collective-permute-start | bytes 196616 | tf_op jit(solution)/shard_map/ppermute | solution.py:426
  4.2 0.9 %collective-permute-done.other_ref = f32[64,256]{1,0:T(8,128)S(1)} collective-permute-done((f32[64,256]{1,0:T(8,128)S(1)}, f32[64,256]{1,0:T(8,128)S(1)}, u32[]{:S(2)}, u32[]{:S(2)}) %collective-permute-start) | collective-permute-done | bytes 65568 | tf_op jit(solution)/shard_map/ppermute | solution.py:426
  5.1 2.9 %collective-permute-start.1 = (f32[64,256]{1,0:T(8,128)S(1)}, f32[64,256]{1,0:T(8,128)S(1)}, u32[]{:S(2)}, u32[]{:S(2)}) collective-permute-start(f32[64,256]{1,0:T(8,128)S(1)} %shard_map.87.one_ref._), channel_id=1, source_target_pairs={{0,2},{1,3},{2,0},{3,1},{4,6},{5,7},{6,4},{7,5},{8,10},{9,11},{10,... | collective-permute-start | bytes 196616 | tf_op jit(solution)/shard_map/ppermute | solution.py:426
  8.0 1.2 %shard_map.92 = (bf16[128,1024]{1,0:T(8,128)(2,1)S(1)}, bf16[128,1024]{1,0:T(8,128)(2,1)S(1)}) custom-call(bf16[1024,256]{1,0:T(8,128)(2,1)} %query.1, f32[64,256]{1,0:T(8,128)S(1)} %shard_map.87.one_ref._), custom_call_target="tpu_custom_call" | custom-call | tf_op jit(solution)/shard_map/pallas_call | solution.py:173
  9.3 1.6 %collective-permute-start.7 = (bf16[128,1024]{1,0:T(8,128)(2,1)S(1)}, bf16[128,1024]{1,0:T(8,128)(2,1)S(1)}, u32[]{:S(2)}, u32[]{:S(2)}) collective-permute-start(bf16[128,1024]{1,0:T(8,128)(2,1)S(1)} %get-tuple-element.13), channel_id=1, source_target_pairs={{0,4},{4,0},{8,12},{12,8},{1,5},{5,1},{9,13},{13,9},{2,6},{6,2},{1... | collective-permute-start | bytes 786440 | tf_op jit(solution)/shard_map/ppermute | solution.py:426
  10.9 0.7 %fusion = f32[2,128]{1,0:T(2,128)S(1)} fusion(s32[2]{0:T(128)} %param.13, s32[2]{0:T(128)} %param.12), kind=kLoop, calls=%fused_computation.1 | loop fusion | flops 768 | bytes 1040 | tf_op jit(solution)/shard_map/convert_element_type | solution.py:436
  11.7 0.0 collective-permute-done.1.other_ref
  11.7 0.1 collective-permute-start.2
  11.8 0.8 %collective-permute-start.3 = (bf16[80,256]{1,0:T(8,128)(2,1)S(1)}, bf16[80,256]{1,0:T(8,128)(2,1)S(1)}, u32[]{:S(2)}, u32[]{:S(2)}) collective-permute-start(bf16[80,256]{1,0:T(8,128)(2,1)S(1)} %shard_map.88.own.payload_ref), channel_id=1, source_target_pairs={{0,4},{4,0},{8,12},{12,8},{1,5},{5,1},{9,13},{13,9},{2,6},{6,2},{1... | collective-permute-start | bytes 122888 | tf_op jit(solution)/shard_map/ppermute | solution.py:426
  12.5 2.6 %collective-permute-start.4 = (bf16[80,256]{1,0:T(8,128)(2,1)S(1)}, bf16[80,256]{1,0:T(8,128)(2,1)S(1)}, u32[]{:S(2)}, u32[]{:S(2)}) collective-permute-start(bf16[80,256]{1,0:T(8,128)(2,1)S(1)} %shard_map.88.own.payload_ref), channel_id=1, source_target_pairs={{0,8},{4,12},{8,0},{12,4},{1,9},{5,13},{9,1},{13,5},{2,10},{6,14},... | collective-permute-start | bytes 122888 | tf_op jit(solution)/shard_map/ppermute | solution.py:426
  15.1 1.1 %collective-permute-start.5 = (bf16[80,256]{1,0:T(8,128)(2,1)S(1)}, bf16[80,256]{1,0:T(8,128)(2,1)S(1)}, u32[]{:S(2)}, u32[]{:S(2)}) collective-permute-start(bf16[80,256]{1,0:T(8,128)(2,1)S(1)} %shard_map.88.own.payload_ref), channel_id=1, source_target_pairs={{0,12},{4,8},{8,4},{12,0},{1,13},{5,9},{9,5},{13,1},{2,14},{6,10},... | collective-permute-start | bytes 122888 | tf_op jit(solution)/shard_map/ppermute | solution.py:426
  16.2 0.0 collective-permute-done.2.own_other
  16.2 2.4 %shard_map.89._.own_sum = f32[1024,4096]{1,0:T(8,128)S(1)} custom-call(bf16[80,256]{1,0:T(8,128)(2,1)S(1)} %shard_map.88.own.payload_ref, bf16[80,256]{1,0:T(8,128)(2,1)S(1)} %collective-permute-done.2.own_other), custom_call_target="tpu_custom_call" | custom-call | tf_op jit(solution)/shard_map/pallas_call | solution.py:335
  18.6 0.6 %collective-permute-done.3.refs_0_ = bf16[80,256]{1,0:T(8,128)(2,1)S(1)} collective-permute-done((bf16[80,256]{1,0:T(8,128)(2,1)S(1)}, bf16[80,256]{1,0:T(8,128)(2,1)S(1)}, u32[]{:S(2)}, u32[]{:S(2)}) %collective-permute-start.3) | collective-permute-done | bytes 40992 | tf_op jit(solution)/shard_map/ppermute | solution.py:426
  19.2 0.0 collective-permute-done.4.refs_1_
  19.2 2.9 %collective-permute-done.5.refs_2_ = bf16[80,256]{1,0:T(8,128)(2,1)S(1)} collective-permute-done((bf16[80,256]{1,0:T(8,128)(2,1)S(1)}, bf16[80,256]{1,0:T(8,128)(2,1)S(1)}, u32[]{:S(2)}, u32[]{:S(2)}) %collective-permute-start.5) | collective-permute-done | bytes 40992 | tf_op jit(solution)/shard_map/ppermute | solution.py:426
  22.1 0.1 collective-permute-start.6
  22.2 1.3 %collective-permute-done.6.other = bf16[3,80,256]{2,1,0:T(8,128)(2,1)S(1)} collective-permute-done((bf16[3,80,256]{2,1,0:T(8,128)(2,1)S(1)}, bf16[3,80,256]{2,1,0:T(8,128)(2,1)S(1)}, u32[]{:S(2)}, u32[]{:S(2)}) %collective-permute-start.6) | collective-permute-done | bytes 122912 | tf_op jit(solution)/shard_map/ppermute | solution.py:426
  23.5 0.0 collective-permute-done.7.near_query_ref
  23.5 2.4 %shard_map.93 = (bf16[128,256]{1,0:T(8,128)(2,1)S(1)}, bf16[128,256]{1,0:T(8,128)(2,1)S(1)}, bf16[128,256]{1,0:T(8,128)(2,1)S(1)}, bf16[128,256]{1,0:T(8,128)(2,1)S(1)}) custom-call(bf16[80,256]{1,0:T(8,128)(2,1)S(1)} %shard_map.88.own.payload_ref, bf16[80,256]{1,0:T(8,128)(2,1)S(1)} %collective-permute-done.2.own_other, ...), custom_call_target="tpu_custom_call" | custom-call | tf_op jit(solution)/shard_map/pallas_call | solution.py:298
  25.9 1.6 %collective-permute-start.10 = (bf16[128,256]{1,0:T(8,128)(2,1)S(1)}, bf16[128,256]{1,0:T(8,128)(2,1)S(1)}, u32[]{:S(2)}, u32[]{:S(2)}) collective-permute-start(bf16[128,256]{1,0:T(8,128)(2,1)S(1)} %get-tuple-element.17), channel_id=1, source_target_pairs={{0,12},{4,8},{8,4},{12,0},{1,13},{5,9},{9,5},{13,1},{2,14},{6,10},... | collective-permute-start | bytes 196616 | tf_op jit(solution)/shard_map/ppermute | solution.py:426
  27.6 0.0 collective-permute-start.8
  27.6 2.8 %collective-permute-start.9 = (bf16[128,256]{1,0:T(8,128)(2,1)S(1)}, bf16[128,256]{1,0:T(8,128)(2,1)S(1)}, u32[]{:S(2)}, u32[]{:S(2)}) collective-permute-start(bf16[128,256]{1,0:T(8,128)(2,1)S(1)} %get-tuple-element.16), channel_id=1, source_target_pairs={{0,8},{4,12},{8,0},{12,4},{1,9},{5,13},{9,1},{13,5},{2,10},{6,14},... | collective-permute-start | bytes 196616 | tf_op jit(solution)/shard_map/ppermute | solution.py:426
  30.4 7.9 %shard_map.91 = f32[1024,4096]{1,0:T(8,128)} custom-call(bf16[3,80,256]{2,1,0:T(8,128)(2,1)S(1)} %shard_map.90.mine, bf16[3,80,256]{2,1,0:T(8,128)(2,1)S(1)} %collective-permute-done.6.other, f32[1024,4096]{1,0:T(8,128)S(1)} %shard_map.89._.own_sum), custom_call_target="tpu_custom_call" | custom-call | tf_op jit(solution)/shard_map/pallas_call | solution.py:384
  38.3 0.0 collective-permute-done.10.refs_3_
  38.3 0.0 collective-permute-done.8.refs_1_
  38.3 0.0 collective-permute-done.9.refs_2_
  38.3 0.8 %shard_map.94 = bf16[256,256]{1,0:T(8,128)(2,1)} custom-call(bf16[80,256]{1,0:T(8,128)(2,1)S(1)} %shard_map.88.own.payload_ref, bf16[128,256]{1,0:T(8,128)(2,1)S(1)} %get-tuple-element.14.refs_0_, bf16[128,256]{1,0:T(8,128)(2,1)S(1)} %collective-permute-done.8.refs_1_, bf16[128,256]{1,0:T(8,128)(2,1)S(1)} %collective-permute-done.9.refs_2_, ...), custom_call_target="tpu_custom_call" | custom-call | tf_op jit(solution)/shard_map/pallas_call | solution.py:418
  (3 shorter events, 0.0 us)
Async XLA Ops:
  3.7 1.4 %collective-permute-start = (f32[64,256]{1,0:T(8,128)S(1)}, f32[64,256]{1,0:T(8,128)S(1)}, u32[]{:S(2)}, u32[]{:S(2)}) collective-permute-start(f32[64,256]{1,0:T(8,128)S(1)} %get-tuple-element.11), channel_id=1, source_target_pairs={{0,1},{1,0},{2,3},{3,2},{4,5},{5,4},{6,7},{7,6},{8,9},{9,8},{10,11... | collective-permute-start | bytes 196616 | tf_op jit(solution)/shard_map/ppermute | solution.py:426
  5.1 6.5 %collective-permute-start.1 = (f32[64,256]{1,0:T(8,128)S(1)}, f32[64,256]{1,0:T(8,128)S(1)}, u32[]{:S(2)}, u32[]{:S(2)}) collective-permute-start(f32[64,256]{1,0:T(8,128)S(1)} %shard_map.87.one_ref._), channel_id=1, source_target_pairs={{0,2},{1,3},{2,0},{3,1},{4,6},{5,7},{6,4},{7,5},{8,10},{9,11},{10,... | collective-permute-start | bytes 196616 | tf_op jit(solution)/shard_map/ppermute | solution.py:426
  9.3 14.2 %collective-permute-start.7 = (bf16[128,1024]{1,0:T(8,128)(2,1)S(1)}, bf16[128,1024]{1,0:T(8,128)(2,1)S(1)}, u32[]{:S(2)}, u32[]{:S(2)}) collective-permute-start(bf16[128,1024]{1,0:T(8,128)(2,1)S(1)} %get-tuple-element.13), channel_id=1, source_target_pairs={{0,4},{4,0},{8,12},{12,8},{1,5},{5,1},{9,13},{13,9},{2,6},{6,2},{1... | collective-permute-start | bytes 786440 | tf_op jit(solution)/shard_map/ppermute | solution.py:426
  11.7 4.5 %collective-permute-start.2 = (bf16[80,256]{1,0:T(8,128)(2,1)S(1)}, bf16[80,256]{1,0:T(8,128)(2,1)S(1)}, u32[]{:S(2)}, u32[]{:S(2)}) collective-permute-start(bf16[80,256]{1,0:T(8,128)(2,1)S(1)} %shard_map.88.own.payload_ref), channel_id=1, source_target_pairs={{0,1},{1,0},{2,3},{3,2},{4,5},{5,4},{6,7},{7,6},{8,9},{9,8},{10,11... | collective-permute-start | bytes 122888 | tf_op jit(solution)/shard_map/ppermute | solution.py:426
  11.8 7.4 %collective-permute-start.3 = (bf16[80,256]{1,0:T(8,128)(2,1)S(1)}, bf16[80,256]{1,0:T(8,128)(2,1)S(1)}, u32[]{:S(2)}, u32[]{:S(2)}) collective-permute-start(bf16[80,256]{1,0:T(8,128)(2,1)S(1)} %shard_map.88.own.payload_ref), channel_id=1, source_target_pairs={{0,4},{4,0},{8,12},{12,8},{1,5},{5,1},{9,13},{13,9},{2,6},{6,2},{1... | collective-permute-start | bytes 122888 | tf_op jit(solution)/shard_map/ppermute | solution.py:426
  12.5 6.7 %collective-permute-start.4 = (bf16[80,256]{1,0:T(8,128)(2,1)S(1)}, bf16[80,256]{1,0:T(8,128)(2,1)S(1)}, u32[]{:S(2)}, u32[]{:S(2)}) collective-permute-start(bf16[80,256]{1,0:T(8,128)(2,1)S(1)} %shard_map.88.own.payload_ref), channel_id=1, source_target_pairs={{0,8},{4,12},{8,0},{12,4},{1,9},{5,13},{9,1},{13,5},{2,10},{6,14},... | collective-permute-start | bytes 122888 | tf_op jit(solution)/shard_map/ppermute | solution.py:426
  15.1 7.0 %collective-permute-start.5 = (bf16[80,256]{1,0:T(8,128)(2,1)S(1)}, bf16[80,256]{1,0:T(8,128)(2,1)S(1)}, u32[]{:S(2)}, u32[]{:S(2)}) collective-permute-start(bf16[80,256]{1,0:T(8,128)(2,1)S(1)} %shard_map.88.own.payload_ref), channel_id=1, source_target_pairs={{0,12},{4,8},{8,4},{12,0},{1,13},{5,9},{9,5},{13,1},{2,14},{6,10},... | collective-permute-start | bytes 122888 | tf_op jit(solution)/shard_map/ppermute | solution.py:426
  22.1 1.4 %collective-permute-start.6 = (bf16[3,80,256]{2,1,0:T(8,128)(2,1)S(1)}, bf16[3,80,256]{2,1,0:T(8,128)(2,1)S(1)}, u32[]{:S(2)}, u32[]{:S(2)}) collective-permute-start(bf16[3,80,256]{2,1,0:T(8,128)(2,1)S(1)} %shard_map.90.mine), channel_id=1, source_target_pairs={{0,1},{1,0},{2,3},{3,2},{4,5},{5,4},{6,7},{7,6},{8,9},{9,8},{10,11... | collective-permute-start | bytes 368648 | tf_op jit(solution)/shard_map/ppermute | solution.py:426
  25.9 12.3 %collective-permute-start.10 = (bf16[128,256]{1,0:T(8,128)(2,1)S(1)}, bf16[128,256]{1,0:T(8,128)(2,1)S(1)}, u32[]{:S(2)}, u32[]{:S(2)}) collective-permute-start(bf16[128,256]{1,0:T(8,128)(2,1)S(1)} %get-tuple-element.17), channel_id=1, source_target_pairs={{0,12},{4,8},{8,4},{12,0},{1,13},{5,9},{9,5},{13,1},{2,14},{6,10},... | collective-permute-start | bytes 196616 | tf_op jit(solution)/shard_map/ppermute | solution.py:426
  27.6 10.7 %collective-permute-start.8 = (bf16[128,256]{1,0:T(8,128)(2,1)S(1)}, bf16[128,256]{1,0:T(8,128)(2,1)S(1)}, u32[]{:S(2)}, u32[]{:S(2)}) collective-permute-start(bf16[128,256]{1,0:T(8,128)(2,1)S(1)} %get-tuple-element.15), channel_id=1, source_target_pairs={{0,4},{4,0},{8,12},{12,8},{1,5},{5,1},{9,13},{13,9},{2,6},{6,2},{1... | collective-permute-start | bytes 196616 | tf_op jit(solution)/shard_map/ppermute | solution.py:426
  27.6 10.7 %collective-permute-start.9 = (bf16[128,256]{1,0:T(8,128)(2,1)S(1)}, bf16[128,256]{1,0:T(8,128)(2,1)S(1)}, u32[]{:S(2)}, u32[]{:S(2)}) collective-permute-start(bf16[128,256]{1,0:T(8,128)(2,1)S(1)} %get-tuple-element.16), channel_id=1, source_target_pairs={{0,8},{4,12},{8,0},{12,4},{1,9},{5,13},{9,1},{13,5},{2,10},{6,14},... | collective-permute-start | bytes 196616 | tf_op jit(solution)/shard_map/ppermute | solution.py:426

commit v10 on v9

--- a/solution.py
+++ b/solution.py
@@ -109,7 +109,9 @@
     return pltpu.CompilerParams(vmem_limit_bytes=int(mib * MIB))
 
 
-def project_kernel(act, grad, pin, pout, keep_ref, send_ref, act_v, grad_v, pin_v, pout_v, sems):
+def project_kernel(
+    act, grad, pin, pout, query, keep_ref, send_ref, send_query, act_v, grad_v, pin_v, pout_v, sems
+):
     chunk = act.shape[1]
     while grad.shape[1] % chunk:
         chunk //= 2
@@ -119,6 +121,10 @@
         pltpu.make_async_copy(grad.at[:, span], grad_v.at[:, span], sems.at[3 + n])
         for n, span in enumerate(spans)
     ]
+    half = send_query.shape[1]
+    even = lax.rem(lax.axis_index("dp"), 2) == 0
+    span = pl.ds(pl.multiple_of(jnp.where(even, half, 0), half), half)
+    copies.append(pltpu.make_async_copy(query.at[:, span], send_query, sems.at[len(copies)]))
     for copy in copies:
         copy.start()
     copies[0].wait()
@@ -126,7 +132,7 @@
     part_act = lax.dot_general(pin_v[...], act_v[...], NT, preferred_element_type=jnp.float32)
     copies[2].wait()
     part_grad = jnp.zeros_like(part_act)
-    for copy, span in zip(copies[3:], spans):
+    for copy, span in zip(copies[3:-1], spans):
         copy.wait()
         part_grad += lax.dot_general(
             pout_v[:, span], grad_v[:, span], NT, preferred_element_type=jnp.float32
@@ -134,49 +140,53 @@
     even = lax.rem(lax.axis_index("query"), 2) == 0
     keep_ref[...] = jnp.where(even, part_act, part_grad)
     send_ref[...] = jnp.where(even, part_grad, part_act)
-
-
-def project(activations, out_grads, proj_in_t, proj_out_t):
+    copies[-1].wait()
+
+
+def project(activations, out_grads, proj_in_t, proj_out_t, queries):
     tok, d_here = activations.shape
     f_here = out_grads.shape[1]
     rank = proj_in_t.shape[0]
     out = jax.ShapeDtypeStruct((rank, tok), jnp.float32)
+    out_query = jax.ShapeDtypeStruct((queries.shape[0], queries.shape[1] // 2), queries.dtype)
+    whole = pl.BlockSpec(memory_space=pltpu.VMEM)
     return pl.pallas_call(
         project_kernel,
-        in_specs=[pl.BlockSpec(memory_space=pl.ANY)] * 4,
-        out_shape=[out, out],
+        in_specs=[pl.BlockSpec(memory_space=pl.ANY)] * 5,
+        out_specs=[whole, whole, pl.BlockSpec(memory_space=pl.ANY)],
+        out_shape=[out, out, out_query],
         scratch_shapes=[
             pltpu.VMEM((tok, d_here), jnp.bfloat16),
             pltpu.VMEM((tok, f_here), jnp.bfloat16),
             pltpu.VMEM((rank, d_here), jnp.bfloat16),
             pltpu.VMEM((rank, f_here), jnp.bfloat16),
-            pltpu.SemaphoreType.DMA((3 + f_here // 128,)),
+            pltpu.SemaphoreType.DMA((4 + f_here // 128,)),
         ],
         compiler_params=params(53.75),
-    )(activations, out_grads, proj_in_t, proj_out_t)
-
-
-def split_kernel(query, _, keep_ref, send_ref, query_v, sem):
-    fetch = pltpu.make_async_copy(query, query_v, sem)
+    )(activations, out_grads, proj_in_t, proj_out_t, queries)
+
+
+def turn_kernel(query, near_query, out_ref, near_out_ref, query_v, sem):
+    half = query_v.shape[1]
+    odd = lax.rem(lax.axis_index("dp"), 2)
+    span = pl.ds(pl.multiple_of(odd * half, half), half)
+    fetch = pltpu.make_async_copy(query.at[:, span], query_v, sem)
     fetch.start()
+    near_out_ref[...] = near_query[...].T
     fetch.wait()
-    query_t = query_v[...].T
-    half = keep_ref.shape[0]
-    even = lax.rem(lax.axis_index("dp"), 2) == 0
-    keep_ref[...] = jnp.where(even, query_t[:half], query_t[half:])
-    send_ref[...] = jnp.where(even, query_t[half:], query_t[:half])
-
-
-def split_queries(queries, after):
-    rows, count = queries.shape
-    out = jax.ShapeDtypeStruct((count // 2, rows), queries.dtype)
-    return pl.pallas_call(
-        split_kernel,
-        in_specs=[pl.BlockSpec(memory_space=pl.ANY)] * 2,
+    out_ref[...] = query_v[...].T
+
+
+def turn_queries(queries, near_queries):
+    rows, half = near_queries.shape
+    out = jax.ShapeDtypeStruct((half, rows), queries.dtype)
+    return pl.pallas_call(
+        turn_kernel,
+        in_specs=[pl.BlockSpec(memory_space=pl.ANY), pl.BlockSpec(memory_space=pltpu.VMEM)],
         out_shape=[out, out],
-        scratch_shapes=[pltpu.VMEM(queries.shape, queries.dtype), pltpu.SemaphoreType.DMA],
-        compiler_params=params(53),
-    )(queries, after)
+        scratch_shapes=[pltpu.VMEM((rows, half), queries.dtype), pltpu.SemaphoreType.DMA],
+        compiler_params=params(30),
+    )(queries, near_queries)
 
 
 def add_kernel(one_ref, other_ref, out_ref):
@@ -206,7 +216,7 @@
     )(one, other, weight)
 
 
-def stack_kernel(_, *refs):
+def stack_kernel(_, __, *refs):
     for k, ref in enumerate(refs[:-1]):
         refs[-1][k] = ref[...]
 
@@ -215,10 +225,10 @@
     whole = pl.BlockSpec(memory_space=pltpu.VMEM)
     return pl.pallas_call(
         stack_kernel,
-        in_specs=[pl.BlockSpec(memory_space=pl.ANY)] + [whole] * len(parts),
+        in_specs=[pl.BlockSpec(memory_space=pl.ANY)] * 2 + [whole] * len(parts),
         out_shape=jax.ShapeDtypeStruct((len(parts),) + parts[0].shape, parts[0].dtype),
         compiler_params=params(30),
-    )(after, *parts)
+    )(*after, *parts)
 
 
 def lay_out_factors(blocks, factors, weights):
@@ -434,20 +444,22 @@
     seq_len = activations.shape[0] // lengths.shape[0]
     live = jnp.arange(seq_len, dtype=jnp.int32)[None, :] < lengths[:, None]
     weight = jnp.where(live, credit[:, None], 0).astype(jnp.float32).reshape(1, -1)
-    keep, send = project(activations, out_grads, proj_in.T, proj_out.T)
+    keep, send, send_queries = project(
+        activations, out_grads, proj_in.T, proj_out.T, queries
+    )
     other = swapped(send, "query", 1)
+    near_queries = swapped(send_queries, "dp", 1)
     distance = 2
     while distance < query_count:
         keep = add(keep, other)
         other = swapped(keep, "query", distance)
         distance *= 2
-    queries_t, send_queries = split_queries(queries, keep)
-    near_queries_t = swapped(send_queries, "dp", 1)
     own = add_to_payload(keep, other, weight)
+    own_other = swapped(own, "query", 1)
     others = [swapped(own, "dp", k) for k in reversed(range(1, dp_count))]
-    own_other = swapped(own, "query", 1)
     own_sum = own_tokens_sum(own, own_other, rank, row_count)
-    mine = stack(others[::-1], own_sum)
+    queries_t, near_queries_t = turn_queries(queries, near_queries)
+    mine = stack(others[::-1], (own_sum, queries_t))
     other = swapped(mine, "query", 1)
     shares = score_shares(
         own, own_other, mine, other, queries_t, near_queries_t, rank, row_count

time: 39.3 us -> 44.4 us (1.13)
  Pallas kernels: 17.8 us -> 23.2 us
    pallas_call x1, Pallas kernels: 3.04 us -> 9.35 us  [project(): pl.pallas_call(project_kernel, in_specs=[pl.BlockSpec(memory_space=pl.ANY...]
    pallas_call x1, Pallas kernels: 1.25 us -> 0.31 us  [turn_queries(): pl.pallas_call(turn_kernel, in_specs=[pl.BlockSpec(memory_space=pl.ANY),...]
  transfers between devices with their start and end apart: 11 -> 11, of which waited for: 4 -> 3; matrix products, arithmetic and copies ran while one was open for 2% -> 2% of each run, Pallas kernels for 30% -> 24%
where the time goes in v10:
time: 44.4 us; the launch traced here: 44.2 us
  Pallas kernels  23.2 us (52%)
  starting transfers between devices  13.8 us (31%)
  waiting for transfers between devices  5.77 us (13%)
  between operations  0.76 us (2%)
  other arithmetic  0.74 us (2%)
    ppermute x11, starting transfers between devices, swapped(): lax.ppermute(array, axis, [(i, i ^ distance) for i in range(lax.axis_size...  13.8 us
    pallas_call x1, Pallas kernels, project(): pl.pallas_call(project_kernel, in_specs=[pl.BlockSpec(memory_space=pl.ANY...  9.35 us
    pallas_call x1, Pallas kernels, hessian_rows(): pl.pallas_call(functools.partial(hessian_kernel, row_count, col_count), o...  7.87 us
    ppermute x11, waiting for transfers between devices, swapped(): lax.ppermute(array, axis, [(i, i ^ distance) for i in range(lax.axis_size...  5.77 us
    pallas_call x1, Pallas kernels, score_shares(): pl.pallas_call(functools.partial(share_kernel, row_count), out_shape=[out...  2.42 us
    pallas_call x1, Pallas kernels, own_tokens_sum(): pl.pallas_call(functools.partial(own_kernel, row_count, col_count), out_s...  2.41 us
  transfers between devices with their start and end apart: 11, of which 3 were waited for; matrix products, arithmetic and copies ran while one was open for 2% of the time, Pallas kernels for 24%

profile of v10, /device:TPU:0, one launch (start us, length us, event | category | flops | bytes accessed | tf_op | source)
XLA Modules:
  0.0 44.2 jit_solution(12611816932599215512)
XLA Ops:
  0.6 0.0 copy-start
  0.6 9.4 %shard_map.86 = (f32[64,256]{1,0:T(8,128)S(1)}, f32[64,256]{1,0:T(8,128)S(1)}, bf16[1024,128]{1,0:T(8,128)(2,1)}) custom-call(bf16[256,1024]{1,0:T(8,128)(2,1)} %act.1, bf16[256,3584]{1,0:T(8,128)(2,1)} %grad.1, bf16[64,1024]{1,0:T(8,128)(2,1)} %bitcast.5, bf16[64,3584]{1,0:T(8,128)(2,1)} %bitcast.4, bf16[1024,256]{1,0:T(8,128)(2,1)} %query.3), custom_call_target="tpu_custom_call" | custom-call | tf_op jit(solution)/shard_map/pallas_call | solution.py:153
  10.0 0.5 %collective-permute-start = (f32[64,256]{1,0:T(8,128)S(1)}, f32[64,256]{1,0:T(8,128)S(1)}, u32[]{:S(2)}, u32[]{:S(2)}) collective-permute-start(f32[64,256]{1,0:T(8,128)S(1)} %get-tuple-element.12), channel_id=1, source_target_pairs={{0,1},{1,0},{2,3},{3,2},{4,5},{5,4},{6,7},{7,6},{8,9},{9,8},{10,11... | collective-permute-start | bytes 196616 | tf_op jit(solution)/shard_map/ppermute | solution.py:436
  10.5 2.6 %collective-permute-start.3 = (bf16[1024,128]{1,0:T(8,128)(2,1)}, bf16[1024,128]{1,0:T(8,128)(2,1)S(1)}, u32[]{:S(2)}, u32[]{:S(2)}) collective-permute-start(bf16[1024,128]{1,0:T(8,128)(2,1)} %get-tuple-element.13), channel_id=1, source_target_pairs={{0,4},{4,0},{8,12},{12,8},{1,5},{5,1},{9,13},{13,9},{2,6},{6,2},{1... | collective-permute-start | bytes 786440 | tf_op jit(solution)/shard_map/ppermute | solution.py:436
  13.2 0.0 collective-permute-done.other_ref
  13.2 1.6 %collective-permute-start.1 = (f32[64,256]{1,0:T(8,128)S(1)}, f32[64,256]{1,0:T(8,128)S(1)}, u32[]{:S(2)}, u32[]{:S(2)}) collective-permute-start(f32[64,256]{1,0:T(8,128)S(1)} %shard_map.87.one_ref), channel_id=1, source_target_pairs={{0,2},{1,3},{2,0},{3,1},{4,6},{5,7},{6,4},{7,5},{8,10},{9,11},{10,... | collective-permute-start | bytes 196616 | tf_op jit(solution)/shard_map/ppermute | solution.py:436
  14.7 0.7 %fusion = f32[2,128]{1,0:T(2,128)S(1)} fusion(s32[2]{0:T(128)} %param.13, s32[2]{0:T(128)} %param.12), kind=kLoop, calls=%fused_computation.1 | loop fusion | flops 768 | bytes 1040 | tf_op jit(solution)/shard_map/convert_element_type | solution.py:446
  15.5 2.0 %collective-permute-done.1.other_ref = f32[64,256]{1,0:T(8,128)S(1)} collective-permute-done((f32[64,256]{1,0:T(8,128)S(1)}, f32[64,256]{1,0:T(8,128)S(1)}, u32[]{:S(2)}, u32[]{:S(2)}) %collective-permute-start.1) | collective-permute-done | bytes 65568 | tf_op jit(solution)/shard_map/ppermute | solution.py:436
  17.5 0.1 collective-permute-start.2
  17.6 1.2 %collective-permute-start.4 = (bf16[80,256]{1,0:T(8,128)(2,1)S(1)}, bf16[80,256]{1,0:T(8,128)(2,1)S(1)}, u32[]{:S(2)}, u32[]{:S(2)}) collective-permute-start(bf16[80,256]{1,0:T(8,128)(2,1)S(1)} %shard_map.88.own.payload_ref), channel_id=1, source_target_pairs={{0,4},{4,0},{8,12},{12,8},{1,5},{5,1},{9,13},{13,9},{2,6},{6,2},{1... | collective-permute-start | bytes 122888 | tf_op jit(solution)/shard_map/ppermute | solution.py:436
  18.8 2.6 %collective-permute-start.5 = (bf16[80,256]{1,0:T(8,128)(2,1)S(1)}, bf16[80,256]{1,0:T(8,128)(2,1)S(1)}, u32[]{:S(2)}, u32[]{:S(2)}) collective-permute-start(bf16[80,256]{1,0:T(8,128)(2,1)S(1)} %shard_map.88.own.payload_ref), channel_id=1, source_target_pairs={{0,8},{4,12},{8,0},{12,4},{1,9},{5,13},{9,1},{13,5},{2,10},{6,14},... | collective-permute-start | bytes 122888 | tf_op jit(solution)/shard_map/ppermute | solution.py:436
  21.4 0.6 %collective-permute-start.6 = (bf16[80,256]{1,0:T(8,128)(2,1)S(1)}, bf16[80,256]{1,0:T(8,128)(2,1)S(1)}, u32[]{:S(2)}, u32[]{:S(2)}) collective-permute-start(bf16[80,256]{1,0:T(8,128)(2,1)S(1)} %shard_map.88.own.payload_ref), channel_id=1, source_target_pairs={{0,12},{4,8},{8,4},{12,0},{1,13},{5,9},{9,5},{13,1},{2,14},{6,10},... | collective-permute-start | bytes 122888 | tf_op jit(solution)/shard_map/ppermute | solution.py:436
  22.1 0.0 collective-permute-done.2.own_other
  22.1 2.4 %shard_map.89._.own_sum = f32[1024,4096]{1,0:T(8,128)S(1)} custom-call(bf16[80,256]{1,0:T(8,128)(2,1)S(1)} %shard_map.88.own.payload_ref, bf16[80,256]{1,0:T(8,128)(2,1)S(1)} %collective-permute-done.2.own_other), custom_call_target="tpu_custom_call" | custom-call | tf_op jit(solution)/shard_map/pallas_call | solution.py:345
  24.5 0.0 collective-permute-done.3.near_query
  24.5 0.0 copy-done
  24.5 0.3 shard_map.90
  24.8 0.0 collective-permute-done.4.refs_0_
  24.8 0.0 collective-permute-done.5.refs_1_
  24.8 2.4 %collective-permute-done.6.refs_2_ = bf16[80,256]{1,0:T(8,128)(2,1)S(1)} collective-permute-done((bf16[80,256]{1,0:T(8,128)(2,1)S(1)}, bf16[80,256]{1,0:T(8,128)(2,1)S(1)}, u32[]{:S(2)}, u32[]{:S(2)}) %collective-permute-start.6) | collective-permute-done | bytes 40992 | tf_op jit(solution)/shard_map/ppermute | solution.py:436
  27.3 0.1 collective-permute-start.7
  27.3 1.3 %collective-permute-done.7.other = bf16[3,80,256]{2,1,0:T(8,128)(2,1)S(1)} collective-permute-done((bf16[3,80,256]{2,1,0:T(8,128)(2,1)S(1)}, bf16[3,80,256]{2,1,0:T(8,128)(2,1)S(1)}, u32[]{:S(2)}, u32[]{:S(2)}) %collective-permute-start.7) | collective-permute-done | bytes 122912 | tf_op jit(solution)/shard_map/ppermute | solution.py:436
  28.7 2.4 %shard_map.93 = (bf16[128,256]{1,0:T(8,128)(2,1)S(1)}, bf16[128,256]{1,0:T(8,128)(2,1)S(1)}, bf16[128,256]{1,0:T(8,128)(2,1)S(1)}, bf16[128,256]{1,0:T(8,128)(2,1)S(1)}) custom-call(bf16[80,256]{1,0:T(8,128)(2,1)S(1)} %shard_map.88.own.payload_ref, bf16[80,256]{1,0:T(8,128)(2,1)S(1)} %collective-permute-done.2.own_other, ...), custom_call_target="tpu_custom_call" | custom-call | tf_op jit(solution)/shard_map/pallas_call | solution.py:308
  31.1 1.3 %collective-permute-start.10 = (bf16[128,256]{1,0:T(8,128)(2,1)S(1)}, bf16[128,256]{1,0:T(8,128)(2,1)S(1)}, u32[]{:S(2)}, u32[]{:S(2)}) collective-permute-start(bf16[128,256]{1,0:T(8,128)(2,1)S(1)} %get-tuple-element.19), channel_id=1, source_target_pairs={{0,12},{4,8},{8,4},{12,0},{1,13},{5,9},{9,5},{13,1},{2,14},{6,10},... | collective-permute-start | bytes 196616 | tf_op jit(solution)/shard_map/ppermute | solution.py:436
  32.4 0.1 collective-permute-start.8
  32.5 3.1 %collective-permute-start.9 = (bf16[128,256]{1,0:T(8,128)(2,1)S(1)}, bf16[128,256]{1,0:T(8,128)(2,1)S(1)}, u32[]{:S(2)}, u32[]{:S(2)}) collective-permute-start(bf16[128,256]{1,0:T(8,128)(2,1)S(1)} %get-tuple-element.18), channel_id=1, source_target_pairs={{0,8},{4,12},{8,0},{12,4},{1,9},{5,13},{9,1},{13,5},{2,10},{6,14},... | collective-permute-start | bytes 196616 | tf_op jit(solution)/shard_map/ppermute | solution.py:436
  35.5 7.9 %shard_map.92 = f32[1024,4096]{1,0:T(8,128)} custom-call(bf16[3,80,256]{2,1,0:T(8,128)(2,1)S(1)} %shard_map.91.mine, bf16[3,80,256]{2,1,0:T(8,128)(2,1)S(1)} %collective-permute-done.7.other, f32[1024,4096]{1,0:T(8,128)S(1)} %shard_map.89._.own_sum), custom_call_target="tpu_custom_call" | custom-call | tf_op jit(solution)/shard_map/pallas_call | solution.py:394
  43.4 0.0 collective-permute-done.10.refs_3_
  43.4 0.0 collective-permute-done.8.refs_1_
  43.4 0.0 collective-permute-done.9.refs_2_
  43.4 0.8 %shard_map.94 = bf16[256,256]{1,0:T(8,128)(2,1)} custom-call(bf16[80,256]{1,0:T(8,128)(2,1)S(1)} %shard_map.88.own.payload_ref, bf16[128,256]{1,0:T(8,128)(2,1)S(1)} %get-tuple-element.16.refs_0_, bf16[128,256]{1,0:T(8,128)(2,1)S(1)} %collective-permute-done.8.refs_1_, bf16[128,256]{1,0:T(8,128)(2,1)S(1)} %collective-permute-done.9.refs_2_, ...), custom_call_target="tpu_custom_call" | custom-call | tf_op jit(solution)/shard_map/pallas_call | solution.py:428
  (3 shorter events, 0.0 us)
Async XLA Ops:
  0.6 23.9 %copy-start = (bf16[1024,256]{1,0:T(8,128)(2,1)S(1)}, bf16[1024,256]{1,0:T(8,128)(2,1)}, u32[]{:S(2)}) copy-start(bf16[1024,256]{1,0:T(8,128)(2,1)} %query.3) | copy-start | bytes 1572868
  10.0 3.2 %collective-permute-start = (f32[64,256]{1,0:T(8,128)S(1)}, f32[64,256]{1,0:T(8,128)S(1)}, u32[]{:S(2)}, u32[]{:S(2)}) collective-permute-start(f32[64,256]{1,0:T(8,128)S(1)} %get-tuple-element.12), channel_id=1, source_target_pairs={{0,1},{1,0},{2,3},{3,2},{4,5},{5,4},{6,7},{7,6},{8,9},{9,8},{10,11... | collective-permute-start | bytes 196616 | tf_op jit(solution)/shard_map/ppermute | solution.py:436
  10.5 14.0 %collective-permute-start.3 = (bf16[1024,128]{1,0:T(8,128)(2,1)}, bf16[1024,128]{1,0:T(8,128)(2,1)S(1)}, u32[]{:S(2)}, u32[]{:S(2)}) collective-permute-start(bf16[1024,128]{1,0:T(8,128)(2,1)} %get-tuple-element.13), channel_id=1, source_target_pairs={{0,4},{4,0},{8,12},{12,8},{1,5},{5,1},{9,13},{13,9},{2,6},{6,2},{1... | collective-permute-start | bytes 786440 | tf_op jit(solution)/shard_map/ppermute | solution.py:436
  13.2 4.3 %collective-permute-start.1 = (f32[64,256]{1,0:T(8,128)S(1)}, f32[64,256]{1,0:T(8,128)S(1)}, u32[]{:S(2)}, u32[]{:S(2)}) collective-permute-start(f32[64,256]{1,0:T(8,128)S(1)} %shard_map.87.one_ref), channel_id=1, source_target_pairs={{0,2},{1,3},{2,0},{3,1},{4,6},{5,7},{6,4},{7,5},{8,10},{9,11},{10,... | collective-permute-start | bytes 196616 | tf_op jit(solution)/shard_map/ppermute | solution.py:436
  17.5 4.5 %collective-permute-start.2 = (bf16[80,256]{1,0:T(8,128)(2,1)S(1)}, bf16[80,256]{1,0:T(8,128)(2,1)S(1)}, u32[]{:S(2)}, u32[]{:S(2)}) collective-permute-start(bf16[80,256]{1,0:T(8,128)(2,1)S(1)} %shard_map.88.own.payload_ref), channel_id=1, source_target_pairs={{0,1},{1,0},{2,3},{3,2},{4,5},{5,4},{6,7},{7,6},{8,9},{9,8},{10,11... | collective-permute-start | bytes 122888 | tf_op jit(solution)/shard_map/ppermute | solution.py:436
  17.6 7.2 %collective-permute-start.4 = (bf16[80,256]{1,0:T(8,128)(2,1)S(1)}, bf16[80,256]{1,0:T(8,128)(2,1)S(1)}, u32[]{:S(2)}, u32[]{:S(2)}) collective-permute-start(bf16[80,256]{1,0:T(8,128)(2,1)S(1)} %shard_map.88.own.payload_ref), channel_id=1, source_target_pairs={{0,4},{4,0},{8,12},{12,8},{1,5},{5,1},{9,13},{13,9},{2,6},{6,2},{1... | collective-permute-start | bytes 122888 | tf_op jit(solution)/shard_map/ppermute | solution.py:436
  18.8 6.0 %collective-permute-start.5 = (bf16[80,256]{1,0:T(8,128)(2,1)S(1)}, bf16[80,256]{1,0:T(8,128)(2,1)S(1)}, u32[]{:S(2)}, u32[]{:S(2)}) collective-permute-start(bf16[80,256]{1,0:T(8,128)(2,1)S(1)} %shard_map.88.own.payload_ref), channel_id=1, source_target_pairs={{0,8},{4,12},{8,0},{12,4},{1,9},{5,13},{9,1},{13,5},{2,10},{6,14},... | collective-permute-start | bytes 122888 | tf_op jit(solution)/shard_map/ppermute | solution.py:436
  21.4 5.8 %collective-permute-start.6 = (bf16[80,256]{1,0:T(8,128)(2,1)S(1)}, bf16[80,256]{1,0:T(8,128)(2,1)S(1)}, u32[]{:S(2)}, u32[]{:S(2)}) collective-permute-start(bf16[80,256]{1,0:T(8,128)(2,1)S(1)} %shard_map.88.own.payload_ref), channel_id=1, source_target_pairs={{0,12},{4,8},{8,4},{12,0},{1,13},{5,9},{9,5},{13,1},{2,14},{6,10},... | collective-permute-start | bytes 122888 | tf_op jit(solution)/shard_map/ppermute | solution.py:436
  27.3 1.4 %collective-permute-start.7 = (bf16[3,80,256]{2,1,0:T(8,128)(2,1)S(1)}, bf16[3,80,256]{2,1,0:T(8,128)(2,1)S(1)}, u32[]{:S(2)}, u32[]{:S(2)}) collective-permute-start(bf16[3,80,256]{2,1,0:T(8,128)(2,1)S(1)} %shard_map.91.mine), channel_id=1, source_target_pairs={{0,1},{1,0},{2,3},{3,2},{4,5},{5,4},{6,7},{7,6},{8,9},{9,8},{10,11... | collective-permute-start | bytes 368648 | tf_op jit(solution)/shard_map/ppermute | solution.py:436
  31.1 12.3 %collective-permute-start.10 = (bf16[128,256]{1,0:T(8,128)(2,1)S(1)}, bf16[128,256]{1,0:T(8,128)(2,1)S(1)}, u32[]{:S(2)}, u32[]{:S(2)}) collective-permute-start(bf16[128,256]{1,0:T(8,128)(2,1)S(1)} %get-tuple-element.19), channel_id=1, source_target_pairs={{0,12},{4,8},{8,4},{12,0},{1,13},{5,9},{9,5},{13,1},{2,14},{6,10},... | collective-permute-start | bytes 196616 | tf_op jit(solution)/shard_map/ppermute | solution.py:436
  32.4 11.1 %collective-permute-start.8 = (bf16[128,256]{1,0:T(8,128)(2,1)S(1)}, bf16[128,256]{1,0:T(8,128)(2,1)S(1)}, u32[]{:S(2)}, u32[]{:S(2)}) collective-permute-start(bf16[128,256]{1,0:T(8,128)(2,1)S(1)} %get-tuple-element.17), channel_id=1, source_target_pairs={{0,4},{4,0},{8,12},{12,8},{1,5},{5,1},{9,13},{13,9},{2,6},{6,2},{1... | collective-permute-start | bytes 196616 | tf_op jit(solution)/shard_map/ppermute | solution.py:436
  32.5 11.0 %collective-permute-start.9 = (bf16[128,256]{1,0:T(8,128)(2,1)S(1)}, bf16[128,256]{1,0:T(8,128)(2,1)S(1)}, u32[]{:S(2)}, u32[]{:S(2)}) collective-permute-start(bf16[128,256]{1,0:T(8,128)(2,1)S(1)} %get-tuple-element.18), channel_id=1, source_target_pairs={{0,8},{4,12},{8,0},{12,4},{1,9},{5,13},{9,1},{13,5},{2,10},{6,14},... | collective-permute-start | bytes 196616 | tf_op jit(solution)/shard_map/ppermute | solution.py:436

commit v11 on v10

--- a/solution.py
+++ b/solution.py
@@ -110,7 +110,7 @@
 
 
 def project_kernel(
-    act, grad, pin, pout, query, keep_ref, send_ref, send_query, act_v, grad_v, pin_v, pout_v, sems
+    act, grad, pin, pout, query, keep_ref, send_ref, send_query, act_v, grad_v, pin_v, pout_v, query_v, sems
 ):
     chunk = act.shape[1]
     while grad.shape[1] % chunk:
@@ -124,15 +124,19 @@
     half = send_query.shape[1]
     even = lax.rem(lax.axis_index("dp"), 2) == 0
     span = pl.ds(pl.multiple_of(jnp.where(even, half, 0), half), half)
-    copies.append(pltpu.make_async_copy(query.at[:, span], send_query, sems.at[len(copies)]))
+    fetch = pltpu.make_async_copy(query.at[:, span], query_v, sems.at[len(copies)])
+    fetch.start()
     for copy in copies:
         copy.start()
     copies[0].wait()
     copies[1].wait()
     part_act = lax.dot_general(pin_v[...], act_v[...], NT, preferred_element_type=jnp.float32)
+    fetch.wait()
+    hand_out = pltpu.make_async_copy(query_v, send_query, sems.at[len(copies)])
+    hand_out.start()
     copies[2].wait()
     part_grad = jnp.zeros_like(part_act)
-    for copy, span in zip(copies[3:-1], spans):
+    for copy, span in zip(copies[3:], spans):
         copy.wait()
         part_grad += lax.dot_general(
             pout_v[:, span], grad_v[:, span], NT, preferred_element_type=jnp.float32
@@ -140,7 +144,7 @@
     even = lax.rem(lax.axis_index("query"), 2) == 0
     keep_ref[...] = jnp.where(even, part_act, part_grad)
     send_ref[...] = jnp.where(even, part_grad, part_act)
-    copies[-1].wait()
+    hand_out.wait()
 
 
 def project(activations, out_grads, proj_in_t, proj_out_t, queries):
@@ -160,6 +164,7 @@
             pltpu.VMEM((tok, f_here), jnp.bfloat16),
             pltpu.VMEM((rank, d_here), jnp.bfloat16),
             pltpu.VMEM((rank, f_here), jnp.bfloat16),
+            pltpu.VMEM(out_query.shape, out_query.dtype),
             pltpu.SemaphoreType.DMA((4 + f_here // 128,)),
         ],
         compiler_params=params(53.75),
@@ -217,16 +222,22 @@
 
 
 def stack_kernel(_, __, *refs):
-    for k, ref in enumerate(refs[:-1]):
-        refs[-1][k] = ref[...]
-
-
-def stack(parts, after):
+    parts, (out_ref, factors_ref) = refs[:-2], refs[-2:]
+    for k, ref in enumerate(parts):
+        out_ref[k] = ref[...]
+        factors_ref[k] = ref[: factors_ref.shape[1]]
+
+
+def stack(parts, rank, after):
+    rows, tok = parts[0].shape
     whole = pl.BlockSpec(memory_space=pltpu.VMEM)
     return pl.pallas_call(
         stack_kernel,
         in_specs=[pl.BlockSpec(memory_space=pl.ANY)] * 2 + [whole] * len(parts),
-        out_shape=jax.ShapeDtypeStruct((len(parts),) + parts[0].shape, parts[0].dtype),
+        out_shape=[
+            jax.ShapeDtypeStruct((len(parts), rows, tok), parts[0].dtype),
+            jax.ShapeDtypeStruct((len(parts), rank, tok), parts[0].dtype),
+        ],
         compiler_params=params(30),
     )(*after, *parts)
 
@@ -243,14 +254,14 @@
 
 
 def block_pairs(mine, other):
-    return [(mine.at[k], other.at[k]) for k in range(mine.shape[0])]
-
-
-def weigh_rows(row_count, factors, weights, weighted):
+    return [(mine.at[k], other.at[k]) for k in reversed(range(mine.shape[0]))]
+
+
+def weigh_rows(first_row, end_row, row_count, factors, weights, weighted):
     rank = factors.shape[0] // 2
     act, weight = factors[:rank, :], weights[...]
     first = rank + lax.axis_index("dp") * row_count
-    for i in range(row_count):
+    for i in range(first_row // rank, end_row // rank):
         left = (factors[pl.ds(first + i, 1), :] * act).astype(jnp.bfloat16)
         left = (weight * left.astype(jnp.float32)).astype(jnp.bfloat16)
         weighted[i * rank : (i + 1) * rank, :] = left
@@ -293,8 +304,8 @@
     gram = jnp.dot(act.T.astype(jnp.bfloat16), act_b, preferred_element_type=jnp.float32) * jnp.dot(
         grad.T.astype(jnp.bfloat16), grad_b, preferred_element_type=jnp.float32
     )
-    gram = (gram * (1.0 / (tokens * step))).astype(jnp.bfloat16)
-    image = jnp.dot((plain * weight).astype(jnp.bfloat16), gram, preferred_element_type=jnp.float32)
+    weighted = (plain * (weight * (1.0 / (tokens * step)))).astype(jnp.bfloat16)
+    image = jnp.dot(weighted, gram.astype(jnp.bfloat16), preferred_element_type=jnp.float32)
     scale = act_scale * grad_scale
     share = ((2.0 - 0.1 / 1.1) * plain - image) * scale * (scale / step)
     for k, out_ref in enumerate(out_refs):
@@ -328,7 +339,7 @@
     rank = factors.shape[0] // 2
     cols = col_count * rank
     lay_out_factors([(own, own_other)], factors, weights)
-    weigh_rows(row_count, factors, weights, weighted)
+    weigh_rows(0, weighted.shape[0], row_count, factors, weights, weighted)
     act = factors[:rank, :]
     build_columns(0, act, factors, rights[0])
     for step in range(rank // col_count):
@@ -364,7 +375,6 @@
     tokens = factors.shape[1] // blocks * (blocks + 1)
     rows, cols = row_count * rank, col_count * rank
     lay_out_factors(block_pairs(mine, other), factors, weights)
-    weigh_rows(row_count, factors, weights, weighted)
     act = factors[:rank, :]
     copies = []
     build_columns(0, act, factors, rights[0])
@@ -372,6 +382,8 @@
         if (step + 1) * col_count < rank:
             build_columns((step + 1) * col_count, act, factors, rights[(step + 1) % 2])
         for row in range(0, rows, TILE):
+            if step == 0:
+                weigh_rows(row, row + TILE, row_count, factors, weights, weighted)
             here = pl.ds(row, TILE), pl.ds(step * cols, cols)
             tile = lax.dot_general(
                 weighted[row : row + TILE, :],
@@ -459,8 +471,8 @@
     others = [swapped(own, "dp", k) for k in reversed(range(1, dp_count))]
     own_sum = own_tokens_sum(own, own_other, rank, row_count)
     queries_t, near_queries_t = turn_queries(queries, near_queries)
-    mine = stack(others[::-1], (own_sum, queries_t))
-    other = swapped(mine, "query", 1)
+    mine, factors = stack(others, rank, (own_sum, queries_t))
+    other = swapped(factors, "query", 1)
     shares = score_shares(
         own, own_other, mine, other, queries_t, near_queries_t, rank, row_count
     )

time: 44.4 us -> 36.8 us (0.83)
  Pallas kernels: 23.2 us -> 17 us
  waiting for transfers between devices: 5.77 us -> 4.36 us
    pallas_call x1, Pallas kernels: 9.35 us -> 3.19 us  [project(): pl.pallas_call(project_kernel, in_specs=[pl.BlockSpec(memory_space=pl.ANY...]
    ppermute x11, waiting for transfers between devices: 5.77 us -> 4.36 us  [swapped(): lax.ppermute(array, axis, [(i, i ^ distance) for i in range(lax.axis_size...]
  transfers between devices with their start and end apart: 11 -> 11, of which waited for: 3 -> 3; matrix products, arithmetic and copies ran while one was open for 2% -> 2% of each run, Pallas kernels for 24% -> 29%
where the time goes in v11:
time: 36.8 us; the launch traced here: 36.6 us
  Pallas kernels  17 us (46%)
  starting transfers between devices  13.8 us (38%)
  waiting for transfers between devices  4.36 us (12%)
  between operations  0.76 us (2%)
  other arithmetic  0.74 us (2%)
    ppermute x11, starting transfers between devices, swapped(): lax.ppermute(array, axis, [(i, i ^ distance) for i in range(lax.axis_size...  13.8 us
    pallas_call x1, Pallas kernels, hessian_rows(): pl.pallas_call(functools.partial(hessian_kernel, row_count, col_count), o...  7.88 us
    ppermute x11, waiting for transfers between devices, swapped(): lax.ppermute(array, axis, [(i, i ^ distance) for i in range(lax.axis_size...  4.36 us
    pallas_call x1, Pallas kernels, project(): pl.pallas_call(project_kernel, in_specs=[pl.BlockSpec(memory_space=pl.ANY...  3.19 us
    pallas_call x1, Pallas kernels, own_tokens_sum(): pl.pallas_call(functools.partial(own_kernel, row_count, col_count), out_s...  2.4 us
    pallas_call x1, Pallas kernels, score_shares(): pl.pallas_call(functools.partial(share_kernel, row_count), out_shape=[out...  2.39 us
    pallas_call x1, Pallas kernels, finish_scores(): pl.pallas_call(finish_kernel, out_shape=jax.ShapeDtypeStruct((tok, 2 * ha...  0.77 us
    convert_element_type x1, other arithmetic, few_tokens(): jnp.where(live, credit[:, None], 0).astype(jnp.float32).reshape(1, -1)  0.74 us
  transfers between devices with their start and end apart: 11, of which 3 were waited for; matrix products, arithmetic and copies ran while one was open for 2% of the time, Pallas kernels for 29%

profile of v11, /device:TPU:0, one launch (start us, length us, event | category | flops | bytes accessed | tf_op | source)
XLA Modules:
  0.0 36.6 jit_solution(11848379538629912141)
XLA Ops:
  0.6 0.0 copy-start
  0.6 3.2 %shard_map.86 = (f32[64,256]{1,0:T(8,128)S(1)}, f32[64,256]{1,0:T(8,128)S(1)}, bf16[1024,128]{1,0:T(8,128)(2,1)}) custom-call(bf16[256,1024]{1,0:T(8,128)(2,1)} %act.1, bf16[256,3584]{1,0:T(8,128)(2,1)} %grad.1, bf16[64,1024]{1,0:T(8,128)(2,1)} %bitcast.5, bf16[64,3584]{1,0:T(8,128)(2,1)} %bitcast.4, bf16[1024,256]{1,0:T(8,128)(2,1)} %query.3), custom_call_target="tpu_custom_call" | custom-call | tf_op jit(solution)/shard_map/pallas_call | solution.py:157
  3.8 0.5 %collective-permute-start = (f32[64,256]{1,0:T(8,128)S(1)}, f32[64,256]{1,0:T(8,128)S(1)}, u32[]{:S(2)}, u32[]{:S(2)}) collective-permute-start(f32[64,256]{1,0:T(8,128)S(1)} %get-tuple-element.14), channel_id=1, source_target_pairs={{0,1},{1,0},{2,3},{3,2},{4,5},{5,4},{6,7},{7,6},{8,9},{9,8},{10,11... | collective-permute-start | bytes 196616 | tf_op jit(solution)/shard_map/ppermute | solution.py:448
  4.4 2.7 %collective-permute-start.3 = (bf16[1024,128]{1,0:T(8,128)(2,1)}, bf16[1024,128]{1,0:T(8,128)(2,1)S(1)}, u32[]{:S(2)}, u32[]{:S(2)}) collective-permute-start(bf16[1024,128]{1,0:T(8,128)(2,1)} %get-tuple-element.15), channel_id=1, source_target_pairs={{0,4},{4,0},{8,12},{12,8},{1,5},{5,1},{9,13},{13,9},{2,6},{6,2},{1... | collective-permute-start | bytes 786440 | tf_op jit(solution)/shard_map/ppermute | solution.py:448
  7.0 0.0 collective-permute-done.other_ref
  7.0 1.6 %collective-permute-start.1 = (f32[64,256]{1,0:T(8,128)S(1)}, f32[64,256]{1,0:T(8,128)S(1)}, u32[]{:S(2)}, u32[]{:S(2)}) collective-permute-start(f32[64,256]{1,0:T(8,128)S(1)} %shard_map.87.one_ref), channel_id=1, source_target_pairs={{0,2},{1,3},{2,0},{3,1},{4,6},{5,7},{6,4},{7,5},{8,10},{9,11},{10,... | collective-permute-start | bytes 196616 | tf_op jit(solution)/shard_map/ppermute | solution.py:448
  8.6 0.7 %fusion = f32[2,128]{1,0:T(2,128)S(1)} fusion(s32[2]{0:T(128)} %param.13, s32[2]{0:T(128)} %param.12), kind=kLoop, calls=%fused_computation.1 | loop fusion | flops 768 | bytes 1040 | tf_op jit(solution)/shard_map/convert_element_type | solution.py:458
  9.3 2.0 %collective-permute-done.1.other_ref = f32[64,256]{1,0:T(8,128)S(1)} collective-permute-done((f32[64,256]{1,0:T(8,128)S(1)}, f32[64,256]{1,0:T(8,128)S(1)}, u32[]{:S(2)}, u32[]{:S(2)}) %collective-permute-start.1) | collective-permute-done | bytes 65568 | tf_op jit(solution)/shard_map/ppermute | solution.py:448
  11.4 0.1 collective-permute-start.2
  11.4 3.3 %collective-permute-start.4 = (bf16[80,256]{1,0:T(8,128)(2,1)S(1)}, bf16[80,256]{1,0:T(8,128)(2,1)S(1)}, u32[]{:S(2)}, u32[]{:S(2)}) collective-permute-start(bf16[80,256]{1,0:T(8,128)(2,1)S(1)} %shard_map.88.own.payload_ref), channel_id=1, source_target_pairs={{0,12},{4,8},{8,4},{12,0},{1,13},{5,9},{9,5},{13,1},{2,14},{6,10},... | collective-permute-start | bytes 122888 | tf_op jit(solution)/shard_map/ppermute | solution.py:448
  14.7 0.0 collective-permute-start.5
  14.7 1.2 %collective-permute-start.6 = (bf16[80,256]{1,0:T(8,128)(2,1)S(1)}, bf16[80,256]{1,0:T(8,128)(2,1)S(1)}, u32[]{:S(2)}, u32[]{:S(2)}) collective-permute-start(bf16[80,256]{1,0:T(8,128)(2,1)S(1)} %shard_map.88.own.payload_ref), channel_id=1, source_target_pairs={{0,4},{4,0},{8,12},{12,8},{1,5},{5,1},{9,13},{13,9},{2,6},{6,2},{1... | collective-permute-start | bytes 122888 | tf_op jit(solution)/shard_map/ppermute | solution.py:448
  15.9 0.0 collective-permute-done.2.own_other
  15.9 2.4 %shard_map.89._.own_sum = f32[1024,4096]{1,0:T(8,128)S(1)} custom-call(bf16[80,256]{1,0:T(8,128)(2,1)S(1)} %shard_map.88.own.payload_ref, bf16[80,256]{1,0:T(8,128)(2,1)S(1)} %collective-permute-done.2.own_other), custom_call_target="tpu_custom_call" | custom-call | tf_op jit(solution)/shard_map/pallas_call | solution.py:356
  18.3 0.0 collective-permute-done.3.near_query
  18.3 0.0 copy-done
  18.3 0.3 shard_map.90
  18.7 0.0 collective-permute-done.4.refs_0_
  18.7 1.0 %collective-permute-done.5.refs_1_ = bf16[80,256]{1,0:T(8,128)(2,1)S(1)} collective-permute-done((bf16[80,256]{1,0:T(8,128)(2,1)S(1)}, bf16[80,256]{1,0:T(8,128)(2,1)S(1)}, u32[]{:S(2)}, u32[]{:S(2)}) %collective-permute-start.5) | collective-permute-done | bytes 40992 | tf_op jit(solution)/shard_map/ppermute | solution.py:448
  19.7 0.0 collective-permute-done.6.refs_2_
  19.7 0.1 collective-permute-start.7
  19.8 1.3 %collective-permute-done.7.other = bf16[3,64,256]{2,1,0:T(8,128)(2,1)S(1)} collective-permute-done((bf16[3,64,256]{2,1,0:T(8,128)(2,1)S(1)}, bf16[3,64,256]{2,1,0:T(8,128)(2,1)S(1)}, u32[]{:S(2)}, u32[]{:S(2)}) %collective-permute-start.7) | collective-permute-done | bytes 98336 | tf_op jit(solution)/shard_map/ppermute | solution.py:448
  21.1 2.4 %shard_map.93 = (bf16[128,256]{1,0:T(8,128)(2,1)S(1)}, bf16[128,256]{1,0:T(8,128)(2,1)S(1)}, bf16[128,256]{1,0:T(8,128)(2,1)S(1)}, bf16[128,256]{1,0:T(8,128)(2,1)S(1)}) custom-call(bf16[80,256]{1,0:T(8,128)(2,1)S(1)} %shard_map.88.own.payload_ref, bf16[80,256]{1,0:T(8,128)(2,1)S(1)} %collective-permute-done.2.own_other, ...), custom_call_target="tpu_custom_call" | custom-call | tf_op jit(solution)/shard_map/pallas_call | solution.py:319
  23.5 2.3 %collective-permute-start.10 = (bf16[128,256]{1,0:T(8,128)(2,1)S(1)}, bf16[128,256]{1,0:T(8,128)(2,1)S(1)}, u32[]{:S(2)}, u32[]{:S(2)}) collective-permute-start(bf16[128,256]{1,0:T(8,128)(2,1)S(1)} %get-tuple-element.23), channel_id=1, source_target_pairs={{0,12},{4,8},{8,4},{12,0},{1,13},{5,9},{9,5},{13,1},{2,14},{6,10},... | collective-permute-start | bytes 196616 | tf_op jit(solution)/shard_map/ppermute | solution.py:448
  25.7 0.3 collective-permute-start.8
  26.0 1.9 %collective-permute-start.9 = (bf16[128,256]{1,0:T(8,128)(2,1)S(1)}, bf16[128,256]{1,0:T(8,128)(2,1)S(1)}, u32[]{:S(2)}, u32[]{:S(2)}) collective-permute-start(bf16[128,256]{1,0:T(8,128)(2,1)S(1)} %get-tuple-element.22), channel_id=1, source_target_pairs={{0,8},{4,12},{8,0},{12,4},{1,9},{5,13},{9,1},{13,5},{2,10},{6,14},... | collective-permute-start | bytes 196616 | tf_op jit(solution)/shard_map/ppermute | solution.py:448
  27.9 7.9 %shard_map.92 = f32[1024,4096]{1,0:T(8,128)} custom-call(bf16[3,80,256]{2,1,0:T(8,128)(2,1)S(1)} %get-tuple-element.17.mine, bf16[3,64,256]{2,1,0:T(8,128)(2,1)S(1)} %collective-permute-done.7.other, f32[1024,4096]{1,0:T(8,128)S(1)} %shard_map.89._.own_sum), custom_call_target="tpu_custom_call" | custom-call | tf_op jit(solution)/shard_map/pallas_call | solution.py:406
  35.8 0.0 collective-permute-done.10.refs_3_
  35.8 0.0 collective-permute-done.8.refs_1_
  35.8 0.0 collective-permute-done.9.refs_2_
  35.8 0.8 %shard_map.94 = bf16[256,256]{1,0:T(8,128)(2,1)} custom-call(bf16[80,256]{1,0:T(8,128)(2,1)S(1)} %shard_map.88.own.payload_ref, bf16[128,256]{1,0:T(8,128)(2,1)S(1)} %get-tuple-element.20.refs_0_, bf16[128,256]{1,0:T(8,128)(2,1)S(1)} %collective-permute-done.8.refs_1_, bf16[128,256]{1,0:T(8,128)(2,1)S(1)} %collective-permute-done.9.refs_2_, ...), custom_call_target="tpu_custom_call" | custom-call | tf_op jit(solution)/shard_map/pallas_call | solution.py:440
  (3 shorter events, 0.0 us)
Async XLA Ops:
  0.6 17.7 %copy-start = (bf16[1024,256]{1,0:T(8,128)(2,1)S(1)}, bf16[1024,256]{1,0:T(8,128)(2,1)}, u32[]{:S(2)}) copy-start(bf16[1024,256]{1,0:T(8,128)(2,1)} %query.3) | copy-start | bytes 1572868
  3.8 3.2 %collective-permute-start = (f32[64,256]{1,0:T(8,128)S(1)}, f32[64,256]{1,0:T(8,128)S(1)}, u32[]{:S(2)}, u32[]{:S(2)}) collective-permute-start(f32[64,256]{1,0:T(8,128)S(1)} %get-tuple-element.14), channel_id=1, source_target_pairs={{0,1},{1,0},{2,3},{3,2},{4,5},{5,4},{6,7},{7,6},{8,9},{9,8},{10,11... | collective-permute-start | bytes 196616 | tf_op jit(solution)/shard_map/ppermute | solution.py:448
  4.4 14.0 %collective-permute-start.3 = (bf16[1024,128]{1,0:T(8,128)(2,1)}, bf16[1024,128]{1,0:T(8,128)(2,1)S(1)}, u32[]{:S(2)}, u32[]{:S(2)}) collective-permute-start(bf16[1024,128]{1,0:T(8,128)(2,1)} %get-tuple-element.15), channel_id=1, source_target_pairs={{0,4},{4,0},{8,12},{12,8},{1,5},{5,1},{9,13},{13,9},{2,6},{6,2},{1... | collective-permute-start | bytes 786440 | tf_op jit(solution)/shard_map/ppermute | solution.py:448
  7.0 4.3 %collective-permute-start.1 = (f32[64,256]{1,0:T(8,128)S(1)}, f32[64,256]{1,0:T(8,128)S(1)}, u32[]{:S(2)}, u32[]{:S(2)}) collective-permute-start(f32[64,256]{1,0:T(8,128)S(1)} %shard_map.87.one_ref), channel_id=1, source_target_pairs={{0,2},{1,3},{2,0},{3,1},{4,6},{5,7},{6,4},{7,5},{8,10},{9,11},{10,... | collective-permute-start | bytes 196616 | tf_op jit(solution)/shard_map/ppermute | solution.py:448
  11.4 4.5 %collective-permute-start.2 = (bf16[80,256]{1,0:T(8,128)(2,1)S(1)}, bf16[80,256]{1,0:T(8,128)(2,1)S(1)}, u32[]{:S(2)}, u32[]{:S(2)}) collective-permute-start(bf16[80,256]{1,0:T(8,128)(2,1)S(1)} %shard_map.88.own.payload_ref), channel_id=1, source_target_pairs={{0,1},{1,0},{2,3},{3,2},{4,5},{5,4},{6,7},{7,6},{8,9},{9,8},{10,11... | collective-permute-start | bytes 122888 | tf_op jit(solution)/shard_map/ppermute | solution.py:448
  11.4 7.2 %collective-permute-start.4 = (bf16[80,256]{1,0:T(8,128)(2,1)S(1)}, bf16[80,256]{1,0:T(8,128)(2,1)S(1)}, u32[]{:S(2)}, u32[]{:S(2)}) collective-permute-start(bf16[80,256]{1,0:T(8,128)(2,1)S(1)} %shard_map.88.own.payload_ref), channel_id=1, source_target_pairs={{0,12},{4,8},{8,4},{12,0},{1,13},{5,9},{9,5},{13,1},{2,14},{6,10},... | collective-permute-start | bytes 122888 | tf_op jit(solution)/shard_map/ppermute | solution.py:448
  14.7 5.0 %collective-permute-start.5 = (bf16[80,256]{1,0:T(8,128)(2,1)S(1)}, bf16[80,256]{1,0:T(8,128)(2,1)S(1)}, u32[]{:S(2)}, u32[]{:S(2)}) collective-permute-start(bf16[80,256]{1,0:T(8,128)(2,1)S(1)} %shard_map.88.own.payload_ref), channel_id=1, source_target_pairs={{0,8},{4,12},{8,0},{12,4},{1,9},{5,13},{9,1},{13,5},{2,10},{6,14},... | collective-permute-start | bytes 122888 | tf_op jit(solution)/shard_map/ppermute | solution.py:448
  14.7 5.0 %collective-permute-start.6 = (bf16[80,256]{1,0:T(8,128)(2,1)S(1)}, bf16[80,256]{1,0:T(8,128)(2,1)S(1)}, u32[]{:S(2)}, u32[]{:S(2)}) collective-permute-start(bf16[80,256]{1,0:T(8,128)(2,1)S(1)} %shard_map.88.own.payload_ref), channel_id=1, source_target_pairs={{0,4},{4,0},{8,12},{12,8},{1,5},{5,1},{9,13},{13,9},{2,6},{6,2},{1... | collective-permute-start | bytes 122888 | tf_op jit(solution)/shard_map/ppermute | solution.py:448
  19.7 1.4 %collective-permute-start.7 = (bf16[3,64,256]{2,1,0:T(8,128)(2,1)S(1)}, bf16[3,64,256]{2,1,0:T(8,128)(2,1)S(1)}, u32[]{:S(2)}, u32[]{:S(2)}) collective-permute-start(bf16[3,64,256]{2,1,0:T(8,128)(2,1)S(1)} %get-tuple-element.18), channel_id=1, source_target_pairs={{0,1},{1,0},{2,3},{3,2},{4,5},{5,4},{6,7},{7,6},{8,9},{9,8},{10,11... | collective-permute-start | bytes 294920 | tf_op jit(solution)/shard_map/ppermute | solution.py:448
  23.5 12.3 %collective-permute-start.10 = (bf16[128,256]{1,0:T(8,128)(2,1)S(1)}, bf16[128,256]{1,0:T(8,128)(2,1)S(1)}, u32[]{:S(2)}, u32[]{:S(2)}) collective-permute-start(bf16[128,256]{1,0:T(8,128)(2,1)S(1)} %get-tuple-element.23), channel_id=1, source_target_pairs={{0,12},{4,8},{8,4},{12,0},{1,13},{5,9},{9,5},{13,1},{2,14},{6,10},... | collective-permute-start | bytes 196616 | tf_op jit(solution)/shard_map/ppermute | solution.py:448
  25.7 10.1 %collective-permute-start.8 = (bf16[128,256]{1,0:T(8,128)(2,1)S(1)}, bf16[128,256]{1,0:T(8,128)(2,1)S(1)}, u32[]{:S(2)}, u32[]{:S(2)}) collective-permute-start(bf16[128,256]{1,0:T(8,128)(2,1)S(1)} %get-tuple-element.21), channel_id=1, source_target_pairs={{0,4},{4,0},{8,12},{12,8},{1,5},{5,1},{9,13},{13,9},{2,6},{6,2},{1... | collective-permute-start | bytes 196616 | tf_op jit(solution)/shard_map/ppermute | solution.py:448
  26.0 9.8 %collective-permute-start.9 = (bf16[128,256]{1,0:T(8,128)(2,1)S(1)}, bf16[128,256]{1,0:T(8,128)(2,1)S(1)}, u32[]{:S(2)}, u32[]{:S(2)}) collective-permute-start(bf16[128,256]{1,0:T(8,128)(2,1)S(1)} %get-tuple-element.22), channel_id=1, source_target_pairs={{0,8},{4,12},{8,0},{12,4},{1,9},{5,13},{9,1},{13,5},{2,10},{6,14},... | collective-permute-start | bytes 196616 | tf_op jit(solution)/shard_map/ppermute | solution.py:448

commit v12 on v11

--- a/solution.py
+++ b/solution.py
@@ -130,7 +130,7 @@
         copy.start()
     copies[0].wait()
     copies[1].wait()
-    part_act = lax.dot_general(pin_v[...], act_v[...], NT, preferred_element_type=jnp.float32)
+    part_act = lax.dot_general(act_v[...], pin_v[...], NT, preferred_element_type=jnp.float32)
     fetch.wait()
     hand_out = pltpu.make_async_copy(query_v, send_query, sems.at[len(copies)])
     hand_out.start()
@@ -139,11 +139,11 @@
     for copy, span in zip(copies[3:], spans):
         copy.wait()
         part_grad += lax.dot_general(
-            pout_v[:, span], grad_v[:, span], NT, preferred_element_type=jnp.float32
+            grad_v[:, span], pout_v[:, span], NT, preferred_element_type=jnp.float32
         )
     even = lax.rem(lax.axis_index("query"), 2) == 0
-    keep_ref[...] = jnp.where(even, part_act, part_grad)
-    send_ref[...] = jnp.where(even, part_grad, part_act)
+    keep_ref[...] = jnp.where(even, part_act, part_grad).T
+    send_ref[...] = jnp.where(even, part_grad, part_act).T
     hand_out.wait()
 
 
@@ -301,11 +301,26 @@
     level = jnp.sum(weight * norms, axis=1, keepdims=True) / (tokens * rank * rank)
     step = 1.1 * level
     act_b, grad_b = act.astype(jnp.bfloat16), grad.astype(jnp.bfloat16)
-    gram = jnp.dot(act.T.astype(jnp.bfloat16), act_b, preferred_element_type=jnp.float32) * jnp.dot(
-        grad.T.astype(jnp.bfloat16), grad_b, preferred_element_type=jnp.float32
-    )
+    act_rows, grad_rows = act.T.astype(jnp.bfloat16), grad.T.astype(jnp.bfloat16)
     weighted = (plain * (weight * (1.0 / (tokens * step)))).astype(jnp.bfloat16)
-    image = jnp.dot(weighted, gram.astype(jnp.bfloat16), preferred_element_type=jnp.float32)
+    images = [0.0] * (tokens // TILE)
+    for p in range(tokens // TILE):
+        here = slice(p * TILE, (p + 1) * TILE)
+        gram = jnp.dot(
+            act_rows[here], act_b[:, p * TILE :], preferred_element_type=jnp.float32
+        ) * jnp.dot(grad_rows[here], grad_b[:, p * TILE :], preferred_element_type=jnp.float32)
+        gram = gram.astype(jnp.bfloat16)
+        forward = jnp.dot(weighted[:, here], gram, preferred_element_type=jnp.float32)
+        for q in range(p, tokens // TILE):
+            images[q] += forward[:, (q - p) * TILE : (q - p + 1) * TILE]
+        if p + 1 < tokens // TILE:
+            images[p] += lax.dot_general(
+                weighted[:, (p + 1) * TILE :],
+                gram[:, TILE:],
+                NT,
+                preferred_element_type=jnp.float32,
+            )
+    image = jnp.concatenate(images, axis=1)
     scale = act_scale * grad_scale
     share = ((2.0 - 0.1 / 1.1) * plain - image) * scale * (scale / step)
     for k, out_ref in enumerate(out_refs):

time: 36.8 us -> 37 us (level)
  no operation moved by 1% of the time
where the time goes in v12:
time: 37 us; the launch traced here: 36.8 us
  Pallas kernels  17.2 us (46%)
  starting transfers between devices  13.8 us (37%)
  waiting for transfers between devices  4.36 us (12%)
  between operations  0.76 us (2%)
  other arithmetic  0.74 us (2%)
    ppermute x11, starting transfers between devices, swapped(): lax.ppermute(array, axis, [(i, i ^ distance) for i in range(lax.axis_size...  13.8 us
    pallas_call x1, Pallas kernels, hessian_rows(): pl.pallas_call(functools.partial(hessian_kernel, row_count, col_count), o...  7.88 us
    ppermute x11, waiting for transfers between devices, swapped(): lax.ppermute(array, axis, [(i, i ^ distance) for i in range(lax.axis_size...  4.36 us
    pallas_call x1, Pallas kernels, project(): pl.pallas_call(project_kernel, in_specs=[pl.BlockSpec(memory_space=pl.ANY...  3.26 us
    pallas_call x1, Pallas kernels, score_shares(): pl.pallas_call(functools.partial(share_kernel, row_count), out_shape=[out...  2.52 us
    pallas_call x1, Pallas kernels, own_tokens_sum(): pl.pallas_call(functools.partial(own_kernel, row_count, col_count), out_s...  2.4 us
    pallas_call x1, Pallas kernels, finish_scores(): pl.pallas_call(finish_kernel, out_shape=jax.ShapeDtypeStruct((tok, 2 * ha...  0.77 us
    convert_element_type x1, other arithmetic, few_tokens(): jnp.where(live, credit[:, None], 0).astype(jnp.float32).reshape(1, -1)  0.74 us
  transfers between devices with their start and end apart: 11, of which 3 were waited for; matrix products, arithmetic and copies ran while one was open for 2% of the time, Pallas kernels for 29%

profile of v12, /device:TPU:0, one launch (start us, length us, event | category | flops | bytes accessed | tf_op | source)
XLA Modules:
  0.0 36.8 jit_solution(13827470275245559431)
XLA Ops:
  0.6 0.0 copy-start
  0.6 3.3 %shard_map.86 = (f32[64,256]{1,0:T(8,128)S(1)}, f32[64,256]{1,0:T(8,128)S(1)}, bf16[1024,128]{1,0:T(8,128)(2,1)}) custom-call(bf16[256,1024]{1,0:T(8,128)(2,1)} %act.1, bf16[256,3584]{1,0:T(8,128)(2,1)} %grad.1, bf16[64,1024]{1,0:T(8,128)(2,1)} %bitcast.5, bf16[64,3584]{1,0:T(8,128)(2,1)} %bitcast.4, bf16[1024,256]{1,0:T(8,128)(2,1)} %query.3), custom_call_target="tpu_custom_call" | custom-call | tf_op jit(solution)/shard_map/pallas_call | solution.py:157
  3.9 0.5 %collective-permute-start = (f32[64,256]{1,0:T(8,128)S(1)}, f32[64,256]{1,0:T(8,128)S(1)}, u32[]{:S(2)}, u32[]{:S(2)}) collective-permute-start(f32[64,256]{1,0:T(8,128)S(1)} %get-tuple-element.14), channel_id=1, source_target_pairs={{0,1},{1,0},{2,3},{3,2},{4,5},{5,4},{6,7},{7,6},{8,9},{9,8},{10,11... | collective-permute-start | bytes 196616 | tf_op jit(solution)/shard_map/ppermute | solution.py:463
  4.4 2.6 %collective-permute-start.3 = (bf16[1024,128]{1,0:T(8,128)(2,1)}, bf16[1024,128]{1,0:T(8,128)(2,1)S(1)}, u32[]{:S(2)}, u32[]{:S(2)}) collective-permute-start(bf16[1024,128]{1,0:T(8,128)(2,1)} %get-tuple-element.15), channel_id=1, source_target_pairs={{0,4},{4,0},{8,12},{12,8},{1,5},{5,1},{9,13},{13,9},{2,6},{6,2},{1... | collective-permute-start | bytes 786440 | tf_op jit(solution)/shard_map/ppermute | solution.py:463
  7.1 0.0 collective-permute-done.other_ref
  7.1 1.6 %collective-permute-start.1 = (f32[64,256]{1,0:T(8,128)S(1)}, f32[64,256]{1,0:T(8,128)S(1)}, u32[]{:S(2)}, u32[]{:S(2)}) collective-permute-start(f32[64,256]{1,0:T(8,128)S(1)} %shard_map.87.one_ref), channel_id=1, source_target_pairs={{0,2},{1,3},{2,0},{3,1},{4,6},{5,7},{6,4},{7,5},{8,10},{9,11},{10,... | collective-permute-start | bytes 196616 | tf_op jit(solution)/shard_map/ppermute | solution.py:463
  8.6 0.7 %fusion = f32[2,128]{1,0:T(2,128)S(1)} fusion(s32[2]{0:T(128)} %param.13, s32[2]{0:T(128)} %param.12), kind=kLoop, calls=%fused_computation.1 | loop fusion | flops 768 | bytes 1040 | tf_op jit(solution)/shard_map/convert_element_type | solution.py:473
  9.4 2.0 %collective-permute-done.1.other_ref = f32[64,256]{1,0:T(8,128)S(1)} collective-permute-done((f32[64,256]{1,0:T(8,128)S(1)}, f32[64,256]{1,0:T(8,128)S(1)}, u32[]{:S(2)}, u32[]{:S(2)}) %collective-permute-start.1) | collective-permute-done | bytes 65568 | tf_op jit(solution)/shard_map/ppermute | solution.py:463
  11.4 0.1 collective-permute-start.2
  11.5 3.3 %collective-permute-start.4 = (bf16[80,256]{1,0:T(8,128)(2,1)S(1)}, bf16[80,256]{1,0:T(8,128)(2,1)S(1)}, u32[]{:S(2)}, u32[]{:S(2)}) collective-permute-start(bf16[80,256]{1,0:T(8,128)(2,1)S(1)} %shard_map.88.own.payload_ref), channel_id=1, source_target_pairs={{0,12},{4,8},{8,4},{12,0},{1,13},{5,9},{9,5},{13,1},{2,14},{6,10},... | collective-permute-start | bytes 122888 | tf_op jit(solution)/shard_map/ppermute | solution.py:463
  14.8 0.0 collective-permute-start.5
  14.8 1.2 %collective-permute-start.6 = (bf16[80,256]{1,0:T(8,128)(2,1)S(1)}, bf16[80,256]{1,0:T(8,128)(2,1)S(1)}, u32[]{:S(2)}, u32[]{:S(2)}) collective-permute-start(bf16[80,256]{1,0:T(8,128)(2,1)S(1)} %shard_map.88.own.payload_ref), channel_id=1, source_target_pairs={{0,4},{4,0},{8,12},{12,8},{1,5},{5,1},{9,13},{13,9},{2,6},{6,2},{1... | collective-permute-start | bytes 122888 | tf_op jit(solution)/shard_map/ppermute | solution.py:463
  16.0 0.0 collective-permute-done.2.own_other
  16.0 2.4 %shard_map.89._.own_sum = f32[1024,4096]{1,0:T(8,128)S(1)} custom-call(bf16[80,256]{1,0:T(8,128)(2,1)S(1)} %shard_map.88.own.payload_ref, bf16[80,256]{1,0:T(8,128)(2,1)S(1)} %collective-permute-done.2.own_other), custom_call_target="tpu_custom_call" | custom-call | tf_op jit(solution)/shard_map/pallas_call | solution.py:371
  18.4 0.0 collective-permute-done.3.near_query
  18.4 0.0 copy-done
  18.4 0.3 shard_map.90
  18.7 0.0 collective-permute-done.4.refs_0_
  18.7 1.0 %collective-permute-done.5.refs_1_ = bf16[80,256]{1,0:T(8,128)(2,1)S(1)} collective-permute-done((bf16[80,256]{1,0:T(8,128)(2,1)S(1)}, bf16[80,256]{1,0:T(8,128)(2,1)S(1)}, u32[]{:S(2)}, u32[]{:S(2)}) %collective-permute-start.5) | collective-permute-done | bytes 40992 | tf_op jit(solution)/shard_map/ppermute | solution.py:463
  19.8 0.0 collective-permute-done.6.refs_2_
  19.8 0.1 collective-permute-start.7
  19.9 1.3 %collective-permute-done.7.other = bf16[3,64,256]{2,1,0:T(8,128)(2,1)S(1)} collective-permute-done((bf16[3,64,256]{2,1,0:T(8,128)(2,1)S(1)}, bf16[3,64,256]{2,1,0:T(8,128)(2,1)S(1)}, u32[]{:S(2)}, u32[]{:S(2)}) %collective-permute-start.7) | collective-permute-done | bytes 98336 | tf_op jit(solution)/shard_map/ppermute | solution.py:463
  21.1 2.5 %shard_map.93 = (bf16[128,256]{1,0:T(8,128)(2,1)S(1)}, bf16[128,256]{1,0:T(8,128)(2,1)S(1)}, bf16[128,256]{1,0:T(8,128)(2,1)S(1)}, bf16[128,256]{1,0:T(8,128)(2,1)S(1)}) custom-call(bf16[80,256]{1,0:T(8,128)(2,1)S(1)} %shard_map.88.own.payload_ref, bf16[80,256]{1,0:T(8,128)(2,1)S(1)} %collective-permute-done.2.own_other, ...), custom_call_target="tpu_custom_call" | custom-call | tf_op jit(solution)/shard_map/pallas_call | solution.py:334
  23.7 2.3 %collective-permute-start.10 = (bf16[128,256]{1,0:T(8,128)(2,1)S(1)}, bf16[128,256]{1,0:T(8,128)(2,1)S(1)}, u32[]{:S(2)}, u32[]{:S(2)}) collective-permute-start(bf16[128,256]{1,0:T(8,128)(2,1)S(1)} %get-tuple-element.23), channel_id=1, source_target_pairs={{0,12},{4,8},{8,4},{12,0},{1,13},{5,9},{9,5},{13,1},{2,14},{6,10},... | collective-permute-start | bytes 196616 | tf_op jit(solution)/shard_map/ppermute | solution.py:463
  25.9 0.3 collective-permute-start.8
  26.2 1.9 %collective-permute-start.9 = (bf16[128,256]{1,0:T(8,128)(2,1)S(1)}, bf16[128,256]{1,0:T(8,128)(2,1)S(1)}, u32[]{:S(2)}, u32[]{:S(2)}) collective-permute-start(bf16[128,256]{1,0:T(8,128)(2,1)S(1)} %get-tuple-element.22), channel_id=1, source_target_pairs={{0,8},{4,12},{8,0},{12,4},{1,9},{5,13},{9,1},{13,5},{2,10},{6,14},... | collective-permute-start | bytes 196616 | tf_op jit(solution)/shard_map/ppermute | solution.py:463
  28.1 7.9 %shard_map.92 = f32[1024,4096]{1,0:T(8,128)} custom-call(bf16[3,80,256]{2,1,0:T(8,128)(2,1)S(1)} %get-tuple-element.17.mine, bf16[3,64,256]{2,1,0:T(8,128)(2,1)S(1)} %collective-permute-done.7.other, f32[1024,4096]{1,0:T(8,128)S(1)} %shard_map.89._.own_sum), custom_call_target="tpu_custom_call" | custom-call | tf_op jit(solution)/shard_map/pallas_call | solution.py:421
  36.0 0.0 collective-permute-done.10.refs_3_
  36.0 0.0 collective-permute-done.8.refs_1_
  36.0 0.0 collective-permute-done.9.refs_2_
  36.0 0.8 %shard_map.94 = bf16[256,256]{1,0:T(8,128)(2,1)} custom-call(bf16[80,256]{1,0:T(8,128)(2,1)S(1)} %shard_map.88.own.payload_ref, bf16[128,256]{1,0:T(8,128)(2,1)S(1)} %get-tuple-element.20.refs_0_, bf16[128,256]{1,0:T(8,128)(2,1)S(1)} %collective-permute-done.8.refs_1_, bf16[128,256]{1,0:T(8,128)(2,1)S(1)} %collective-permute-done.9.refs_2_, ...), custom_call_target="tpu_custom_call" | custom-call | tf_op jit(solution)/shard_map/pallas_call | solution.py:455
  (3 shorter events, 0.0 us)
Async XLA Ops:
  0.6 17.8 %copy-start = (bf16[1024,256]{1,0:T(8,128)(2,1)S(1)}, bf16[1024,256]{1,0:T(8,128)(2,1)}, u32[]{:S(2)}) copy-start(bf16[1024,256]{1,0:T(8,128)(2,1)} %query.3) | copy-start | bytes 1572868
  3.9 3.2 %collective-permute-start = (f32[64,256]{1,0:T(8,128)S(1)}, f32[64,256]{1,0:T(8,128)S(1)}, u32[]{:S(2)}, u32[]{:S(2)}) collective-permute-start(f32[64,256]{1,0:T(8,128)S(1)} %get-tuple-element.14), channel_id=1, source_target_pairs={{0,1},{1,0},{2,3},{3,2},{4,5},{5,4},{6,7},{7,6},{8,9},{9,8},{10,11... | collective-permute-start | bytes 196616 | tf_op jit(solution)/shard_map/ppermute | solution.py:463
  4.4 14.0 %collective-permute-start.3 = (bf16[1024,128]{1,0:T(8,128)(2,1)}, bf16[1024,128]{1,0:T(8,128)(2,1)S(1)}, u32[]{:S(2)}, u32[]{:S(2)}) collective-permute-start(bf16[1024,128]{1,0:T(8,128)(2,1)} %get-tuple-element.15), channel_id=1, source_target_pairs={{0,4},{4,0},{8,12},{12,8},{1,5},{5,1},{9,13},{13,9},{2,6},{6,2},{1... | collective-permute-start | bytes 786440 | tf_op jit(solution)/shard_map/ppermute | solution.py:463
  7.1 4.3 %collective-permute-start.1 = (f32[64,256]{1,0:T(8,128)S(1)}, f32[64,256]{1,0:T(8,128)S(1)}, u32[]{:S(2)}, u32[]{:S(2)}) collective-permute-start(f32[64,256]{1,0:T(8,128)S(1)} %shard_map.87.one_ref), channel_id=1, source_target_pairs={{0,2},{1,3},{2,0},{3,1},{4,6},{5,7},{6,4},{7,5},{8,10},{9,11},{10,... | collective-permute-start | bytes 196616 | tf_op jit(solution)/shard_map/ppermute | solution.py:463
  11.4 4.5 %collective-permute-start.2 = (bf16[80,256]{1,0:T(8,128)(2,1)S(1)}, bf16[80,256]{1,0:T(8,128)(2,1)S(1)}, u32[]{:S(2)}, u32[]{:S(2)}) collective-permute-start(bf16[80,256]{1,0:T(8,128)(2,1)S(1)} %shard_map.88.own.payload_ref), channel_id=1, source_target_pairs={{0,1},{1,0},{2,3},{3,2},{4,5},{5,4},{6,7},{7,6},{8,9},{9,8},{10,11... | collective-permute-start | bytes 122888 | tf_op jit(solution)/shard_map/ppermute | solution.py:463
  11.5 7.2 %collective-permute-start.4 = (bf16[80,256]{1,0:T(8,128)(2,1)S(1)}, bf16[80,256]{1,0:T(8,128)(2,1)S(1)}, u32[]{:S(2)}, u32[]{:S(2)}) collective-permute-start(bf16[80,256]{1,0:T(8,128)(2,1)S(1)} %shard_map.88.own.payload_ref), channel_id=1, source_target_pairs={{0,12},{4,8},{8,4},{12,0},{1,13},{5,9},{9,5},{13,1},{2,14},{6,10},... | collective-permute-start | bytes 122888 | tf_op jit(solution)/shard_map/ppermute | solution.py:463
  14.8 5.0 %collective-permute-start.5 = (bf16[80,256]{1,0:T(8,128)(2,1)S(1)}, bf16[80,256]{1,0:T(8,128)(2,1)S(1)}, u32[]{:S(2)}, u32[]{:S(2)}) collective-permute-start(bf16[80,256]{1,0:T(8,128)(2,1)S(1)} %shard_map.88.own.payload_ref), channel_id=1, source_target_pairs={{0,8},{4,12},{8,0},{12,4},{1,9},{5,13},{9,1},{13,5},{2,10},{6,14},... | collective-permute-start | bytes 122888 | tf_op jit(solution)/shard_map/ppermute | solution.py:463
  14.8 5.0 %collective-permute-start.6 = (bf16[80,256]{1,0:T(8,128)(2,1)S(1)}, bf16[80,256]{1,0:T(8,128)(2,1)S(1)}, u32[]{:S(2)}, u32[]{:S(2)}) collective-permute-start(bf16[80,256]{1,0:T(8,128)(2,1)S(1)} %shard_map.88.own.payload_ref), channel_id=1, source_target_pairs={{0,4},{4,0},{8,12},{12,8},{1,5},{5,1},{9,13},{13,9},{2,6},{6,2},{1... | collective-permute-start | bytes 122888 | tf_op jit(solution)/shard_map/ppermute | solution.py:463
  19.8 1.4 %collective-permute-start.7 = (bf16[3,64,256]{2,1,0:T(8,128)(2,1)S(1)}, bf16[3,64,256]{2,1,0:T(8,128)(2,1)S(1)}, u32[]{:S(2)}, u32[]{:S(2)}) collective-permute-start(bf16[3,64,256]{2,1,0:T(8,128)(2,1)S(1)} %get-tuple-element.18), channel_id=1, source_target_pairs={{0,1},{1,0},{2,3},{3,2},{4,5},{5,4},{6,7},{7,6},{8,9},{9,8},{10,11... | collective-permute-start | bytes 294920 | tf_op jit(solution)/shard_map/ppermute | solution.py:463
  23.7 12.3 %collective-permute-start.10 = (bf16[128,256]{1,0:T(8,128)(2,1)S(1)}, bf16[128,256]{1,0:T(8,128)(2,1)S(1)}, u32[]{:S(2)}, u32[]{:S(2)}) collective-permute-start(bf16[128,256]{1,0:T(8,128)(2,1)S(1)} %get-tuple-element.23), channel_id=1, source_target_pairs={{0,12},{4,8},{8,4},{12,0},{1,13},{5,9},{9,5},{13,1},{2,14},{6,10},... | collective-permute-start | bytes 196616 | tf_op jit(solution)/shard_map/ppermute | solution.py:463
  25.9 10.1 %collective-permute-start.8 = (bf16[128,256]{1,0:T(8,128)(2,1)S(1)}, bf16[128,256]{1,0:T(8,128)(2,1)S(1)}, u32[]{:S(2)}, u32[]{:S(2)}) collective-permute-start(bf16[128,256]{1,0:T(8,128)(2,1)S(1)} %get-tuple-element.21), channel_id=1, source_target_pairs={{0,4},{4,0},{8,12},{12,8},{1,5},{5,1},{9,13},{13,9},{2,6},{6,2},{1... | collective-permute-start | bytes 196616 | tf_op jit(solution)/shard_map/ppermute | solution.py:463
  26.2 9.8 %collective-permute-start.9 = (bf16[128,256]{1,0:T(8,128)(2,1)S(1)}, bf16[128,256]{1,0:T(8,128)(2,1)S(1)}, u32[]{:S(2)}, u32[]{:S(2)}) collective-permute-start(bf16[128,256]{1,0:T(8,128)(2,1)S(1)} %get-tuple-element.22), channel_id=1, source_target_pairs={{0,8},{4,12},{8,0},{12,4},{1,9},{5,13},{9,1},{13,5},{2,10},{6,14},... | collective-permute-start | bytes 196616 | tf_op jit(solution)/shard_map/ppermute | solution.py:463

commit v13 on v11

--- a/solution.py
+++ b/solution.py
@@ -109,9 +109,7 @@
     return pltpu.CompilerParams(vmem_limit_bytes=int(mib * MIB))
 
 
-def project_kernel(
-    act, grad, pin, pout, query, keep_ref, send_ref, send_query, act_v, grad_v, pin_v, pout_v, query_v, sems
-):
+def project_kernel(act, grad, pin, pout, keep_ref, send_ref, act_v, grad_v, pin_v, pout_v, sems):
     chunk = act.shape[1]
     while grad.shape[1] % chunk:
         chunk //= 2
@@ -121,19 +119,11 @@
         pltpu.make_async_copy(grad.at[:, span], grad_v.at[:, span], sems.at[3 + n])
         for n, span in enumerate(spans)
     ]
-    half = send_query.shape[1]
-    even = lax.rem(lax.axis_index("dp"), 2) == 0
-    span = pl.ds(pl.multiple_of(jnp.where(even, half, 0), half), half)
-    fetch = pltpu.make_async_copy(query.at[:, span], query_v, sems.at[len(copies)])
-    fetch.start()
     for copy in copies:
         copy.start()
     copies[0].wait()
     copies[1].wait()
     part_act = lax.dot_general(pin_v[...], act_v[...], NT, preferred_element_type=jnp.float32)
-    fetch.wait()
-    hand_out = pltpu.make_async_copy(query_v, send_query, sems.at[len(copies)])
-    hand_out.start()
     copies[2].wait()
     part_grad = jnp.zeros_like(part_act)
     for copy, span in zip(copies[3:], spans):
@@ -144,52 +134,38 @@
     even = lax.rem(lax.axis_index("query"), 2) == 0
     keep_ref[...] = jnp.where(even, part_act, part_grad)
     send_ref[...] = jnp.where(even, part_grad, part_act)
-    hand_out.wait()
-
-
-def project(activations, out_grads, proj_in_t, proj_out_t, queries):
+
+
+def project(activations, out_grads, proj_in_t, proj_out_t):
     tok, d_here = activations.shape
     f_here = out_grads.shape[1]
     rank = proj_in_t.shape[0]
     out = jax.ShapeDtypeStruct((rank, tok), jnp.float32)
-    out_query = jax.ShapeDtypeStruct((queries.shape[0], queries.shape[1] // 2), queries.dtype)
-    whole = pl.BlockSpec(memory_space=pltpu.VMEM)
     return pl.pallas_call(
         project_kernel,
-        in_specs=[pl.BlockSpec(memory_space=pl.ANY)] * 5,
-        out_specs=[whole, whole, pl.BlockSpec(memory_space=pl.ANY)],
-        out_shape=[out, out, out_query],
+        in_specs=[pl.BlockSpec(memory_space=pl.ANY)] * 4,
+        out_shape=[out, out],
         scratch_shapes=[
             pltpu.VMEM((tok, d_here), jnp.bfloat16),
             pltpu.VMEM((tok, f_here), jnp.bfloat16),
             pltpu.VMEM((rank, d_here), jnp.bfloat16),
             pltpu.VMEM((rank, f_here), jnp.bfloat16),
-            pltpu.VMEM(out_query.shape, out_query.dtype),
-            pltpu.SemaphoreType.DMA((4 + f_here // 128,)),
+            pltpu.SemaphoreType.DMA((3 + f_here // 128,)),
         ],
         compiler_params=params(53.75),
-    )(activations, out_grads, proj_in_t, proj_out_t, queries)
-
-
-def turn_kernel(query, near_query, out_ref, near_out_ref, query_v, sem):
-    half = query_v.shape[1]
-    odd = lax.rem(lax.axis_index("dp"), 2)
-    span = pl.ds(pl.multiple_of(odd * half, half), half)
-    fetch = pltpu.make_async_copy(query.at[:, span], query_v, sem)
-    fetch.start()
+    )(activations, out_grads, proj_in_t, proj_out_t)
+
+
+def turn_kernel(query, near_query, out_ref, near_out_ref):
+    out_ref[...] = query[...].T
     near_out_ref[...] = near_query[...].T
-    fetch.wait()
-    out_ref[...] = query_v[...].T
 
 
 def turn_queries(queries, near_queries):
-    rows, half = near_queries.shape
-    out = jax.ShapeDtypeStruct((half, rows), queries.dtype)
+    out = jax.ShapeDtypeStruct(queries.shape[::-1], queries.dtype)
     return pl.pallas_call(
         turn_kernel,
-        in_specs=[pl.BlockSpec(memory_space=pl.ANY), pl.BlockSpec(memory_space=pltpu.VMEM)],
         out_shape=[out, out],
-        scratch_shapes=[pltpu.VMEM((rows, half), queries.dtype), pltpu.SemaphoreType.DMA],
         compiler_params=params(30),
     )(queries, near_queries)
 
@@ -277,15 +253,15 @@
 
 
 def share_kernel(row_count, own, own_other, mine, other, query_ref, near_query_ref, *refs):
-    factors, weights, features = refs[-3:]
-    out_refs = refs[:-3]
+    factors, weights, features, gram = refs[-4:]
+    out_refs = refs[:-4]
     lay_out_factors([(own, own_other)] + block_pairs(mine, other), factors, weights)
     rank = factors.shape[0] // 2
     tokens = factors.shape[1]
-    tok = tokens // len(out_refs)
+    tok = own.shape[1]
     act = factors[:rank, :]
     plain = 0.0
-    for near, queries in ((0, query_ref), (1, near_query_ref)):
+    for near, queries in enumerate((query_ref, near_query_ref)):
         first = rank + (lax.axis_index("dp") ^ near) * row_count
         for i in range(row_count):
             row = factors[pl.ds(first + i, 1), :]
@@ -301,28 +277,35 @@
     level = jnp.sum(weight * norms, axis=1, keepdims=True) / (tokens * rank * rank)
     step = 1.1 * level
     act_b, grad_b = act.astype(jnp.bfloat16), grad.astype(jnp.bfloat16)
-    gram = jnp.dot(act.T.astype(jnp.bfloat16), act_b, preferred_element_type=jnp.float32) * jnp.dot(
-        grad.T.astype(jnp.bfloat16), grad_b, preferred_element_type=jnp.float32
-    )
+    act_rows, grad_rows = act.T.astype(jnp.bfloat16), grad.T.astype(jnp.bfloat16)
     weighted = (plain * (weight * (1.0 / (tokens * step)))).astype(jnp.bfloat16)
-    image = jnp.dot(weighted, gram.astype(jnp.bfloat16), preferred_element_type=jnp.float32)
     scale = act_scale * grad_scale
-    share = ((2.0 - 0.1 / 1.1) * plain - image) * scale * (scale / step)
-    for k, out_ref in enumerate(out_refs):
-        out_ref[...] = share[:, k * tok : (k + 1) * tok].astype(jnp.bfloat16)
+    for n, out_ref in enumerate(out_refs):
+        block = slice(2 * n * tok, (2 * n + 1) * tok)
+        for row in range(0, tokens, TILE // 2):
+            here = slice(row, row + TILE // 2)
+            tile = jnp.dot(act_rows[here], act_b[:, block], preferred_element_type=jnp.float32)
+            tile *= jnp.dot(grad_rows[here], grad_b[:, block], preferred_element_type=jnp.float32)
+            gram[n, here, :] = tile.astype(jnp.bfloat16)
+        image = jnp.dot(weighted, gram[n], preferred_element_type=jnp.float32)
+        share = ((2.0 - 0.1 / 1.1) * plain[:, block] - image) * scale * (scale / step)
+        out_ref[...] = share.astype(out_ref.dtype)
 
 
 def score_shares(own, own_other, mine, other, queries_t, near_queries_t, rank, row_count):
     blocks, tok = mine.shape[0] + 1, mine.shape[2]
     count, rows = queries_t.shape
-    out = jax.ShapeDtypeStruct((count, tok), jnp.bfloat16)
     return pl.pallas_call(
         functools.partial(share_kernel, row_count),
-        out_shape=[out] * blocks,
+        out_shape=[
+            jax.ShapeDtypeStruct((count, tok), jnp.bfloat16 if k else jnp.float32)
+            for k in range(0, blocks, 2)
+        ],
         scratch_shapes=[
             pltpu.VMEM((2 * rank, tok * blocks), jnp.float32),
             pltpu.VMEM((1, tok * blocks), jnp.float32),
             pltpu.VMEM((2, rows, tok * blocks), jnp.bfloat16),
+            pltpu.VMEM((blocks // 2, tok * blocks, tok), jnp.bfloat16),
         ],
         compiler_params=params(30),
     )(own, own_other, mine, other, queries_t, near_queries_t)
@@ -422,24 +405,18 @@
 
 def finish_kernel(payload_ref, *refs):
     shares, out_ref = refs[:-1], refs[-1]
+    total = shares[0][...]
+    for ref in shares[1:]:
+        total = total + ref[...].astype(jnp.float32)
     weight = payload_ref[...].astype(jnp.float32)[-1:]
-    totals = []
-    for near in range(2):
-        total = shares[near][...].astype(jnp.float32)
-        for ref in shares[near + 2 :: 2]:
-            total = total + ref[...].astype(jnp.float32)
-        totals.append(jnp.where(weight > 0.0, total, 0.0).T.astype(out_ref.dtype))
-    even = lax.rem(lax.axis_index("dp"), 2) == 0
-    half = totals[0].shape[1]
-    out_ref[:, :half] = jnp.where(even, totals[0], totals[1])
-    out_ref[:, half:] = jnp.where(even, totals[1], totals[0])
+    out_ref[...] = jnp.where(weight > 0.0, total, 0.0).T.astype(out_ref.dtype)
 
 
 def finish_scores(payload, shares):
-    half, tok = shares[0].shape
+    count, tok = shares[0].shape
     return pl.pallas_call(
         finish_kernel,
-        out_shape=jax.ShapeDtypeStruct((tok, 2 * half), jnp.bfloat16),
+        out_shape=jax.ShapeDtypeStruct((tok, count), jnp.bfloat16),
         compiler_params=params(40),
     )(payload, *shares)
 
@@ -456,11 +433,9 @@
     seq_len = activations.shape[0] // lengths.shape[0]
     live = jnp.arange(seq_len, dtype=jnp.int32)[None, :] < lengths[:, None]
     weight = jnp.where(live, credit[:, None], 0).astype(jnp.float32).reshape(1, -1)
-    keep, send, send_queries = project(
-        activations, out_grads, proj_in.T, proj_out.T, queries
-    )
+    near_queries = swapped(queries, "dp", 1)
+    keep, send = project(activations, out_grads, proj_in.T, proj_out.T)
     other = swapped(send, "query", 1)
-    near_queries = swapped(send_queries, "dp", 1)
     distance = 2
     while distance < query_count:
         keep = add(keep, other)
@@ -476,9 +451,9 @@
     shares = score_shares(
         own, own_other, mine, other, queries_t, near_queries_t, rank, row_count
     )
-    arrived = [swapped(shares[k], "dp", k) for k in reversed(range(1, dp_count))]
+    arrived = [swapped(share, "dp", 2 * n) for n, share in enumerate(shares) if n]
     hessian = hessian_rows(mine, other, own_sum, rank, row_count)
-    return hessian, finish_scores(own, [shares[0]] + arrived[::-1])
+    return hessian, finish_scores(own, [shares[0]] + arrived)
 
 
 def power_of_two(count):

time: 36.8 us -> 34.7 us (0.943)
  starting transfers between devices: 13.8 us -> 10.7 us
  waiting for transfers between devices: 4.36 us -> 5.49 us
    ppermute x11 -> x9, starting transfers between devices: 13.8 us -> 10.7 us  [swapped(): lax.ppermute(array, axis, [(i, i ^ distance) for i in range(lax.axis_size...]
    ppermute x11 -> x9, waiting for transfers between devices: 4.36 us -> 5.49 us  [swapped(): lax.ppermute(array, axis, [(i, i ^ distance) for i in range(lax.axis_size...]
  transfers between devices with their start and end apart: 11 -> 9, of which waited for: 3 -> 4; matrix products, arithmetic and copies ran while one was open for 2% -> 2% of each run, Pallas kernels for 29% -> 40%
where the time goes in v13:
time: 34.7 us; the launch traced here: 34.5 us
  Pallas kernels  16.8 us (48%)
  starting transfers between devices  10.7 us (31%)
  waiting for transfers between devices  5.49 us (16%)
  between operations  0.75 us (2%)
  other arithmetic  0.74 us (2%)
    ppermute x9, starting transfers between devices, swapped(): lax.ppermute(array, axis, [(i, i ^ distance) for i in range(lax.axis_size...  10.7 us
    pallas_call x1, Pallas kernels, hessian_rows(): pl.pallas_call(functools.partial(hessian_kernel, row_count, col_count), o...  7.88 us
    ppermute x9, waiting for transfers between devices, swapped(): lax.ppermute(array, axis, [(i, i ^ distance) for i in range(lax.axis_size...  5.49 us
    pallas_call x1, Pallas kernels, project(): pl.pallas_call(project_kernel, in_specs=[pl.BlockSpec(memory_space=pl.ANY...  3.04 us
    pallas_call x1, Pallas kernels, own_tokens_sum(): pl.pallas_call(functools.partial(own_kernel, row_count, col_count), out_s...  2.41 us
    pallas_call x1, Pallas kernels, score_shares(): pl.pallas_call(functools.partial(share_kernel, row_count), out_shape=[jax...  2.36 us
    pallas_call x1, Pallas kernels, finish_scores(): pl.pallas_call(finish_kernel, out_shape=jax.ShapeDtypeStruct((tok, count)...  0.77 us
    convert_element_type x1, other arithmetic, few_tokens(): jnp.where(live, credit[:, None], 0).astype(jnp.float32).reshape(1, -1)  0.74 us
  transfers between devices with their start and end apart: 9, of which 4 were waited for; matrix products, arithmetic and copies ran while one was open for 2% of the time, Pallas kernels for 40%

profile of v13, /device:TPU:0, one launch (start us, length us, event | category | flops | bytes accessed | tf_op | source)
XLA Modules:
  0.0 34.5 jit_solution(13482889350288055236)
XLA Ops:
  0.6 0.0 copy-start
  0.6 3.1 %collective-permute-start.3 = (bf16[1024,256]{1,0:T(8,128)(2,1)}, bf16[1024,256]{1,0:T(8,128)(2,1)S(1)}, u32[]{:S(2)}, u32[]{:S(2)}) collective-permute-start(bf16[1024,256]{1,0:T(8,128)(2,1)} %query.1), channel_id=1, source_target_pairs={{0,4},{4,0},{8,12},{12,8},{1,5},{5,1},{9,13},{13,9},{2,6},{6,2},{1... | collective-permute-start | bytes 1572872 | tf_op jit(solution)/shard_map/ppermute | solution.py:425
  3.7 3.0 %shard_map.86 = (f32[64,256]{1,0:T(8,128)S(1)}, f32[64,256]{1,0:T(8,128)S(1)}) custom-call(bf16[256,1024]{1,0:T(8,128)(2,1)} %act.1, bf16[256,3584]{1,0:T(8,128)(2,1)} %grad.1, bf16[64,1024]{1,0:T(8,128)(2,1)} %bitcast.5, bf16[64,3584]{1,0:T(8,128)(2,1)} %bitcast.4), custom_call_target="tpu_custom_call" | custom-call | tf_op jit(solution)/shard_map/pallas_call | solution.py:144
  6.8 0.1 collective-permute-start
  6.9 1.2 %collective-permute-done.other_ref = f32[64,256]{1,0:T(8,128)S(1)} collective-permute-done((f32[64,256]{1,0:T(8,128)S(1)}, f32[64,256]{1,0:T(8,128)S(1)}, u32[]{:S(2)}, u32[]{:S(2)}) %collective-permute-start) | collective-permute-done | bytes 65568 | tf_op jit(solution)/shard_map/ppermute | solution.py:425
  8.1 1.6 %collective-permute-start.1 = (f32[64,256]{1,0:T(8,128)S(1)}, f32[64,256]{1,0:T(8,128)S(1)}, u32[]{:S(2)}, u32[]{:S(2)}) collective-permute-start(f32[64,256]{1,0:T(8,128)S(1)} %shard_map.87.one_ref), channel_id=1, source_target_pairs={{0,2},{1,3},{2,0},{3,1},{4,6},{5,7},{6,4},{7,5},{8,10},{9,11},{10,... | collective-permute-start | bytes 196616 | tf_op jit(solution)/shard_map/ppermute | solution.py:425
  9.7 0.7 %fusion = f32[2,128]{1,0:T(2,128)S(1)} fusion(s32[2]{0:T(128)} %param.13, s32[2]{0:T(128)} %param.12), kind=kLoop, calls=%fused_computation.1 | loop fusion | flops 768 | bytes 1040 | tf_op jit(solution)/shard_map/convert_element_type | solution.py:435
  10.4 2.0 %collective-permute-done.1.other_ref = f32[64,256]{1,0:T(8,128)S(1)} collective-permute-done((f32[64,256]{1,0:T(8,128)S(1)}, f32[64,256]{1,0:T(8,128)S(1)}, u32[]{:S(2)}, u32[]{:S(2)}) %collective-permute-start.1) | collective-permute-done | bytes 65568 | tf_op jit(solution)/shard_map/ppermute | solution.py:425
  12.5 0.1 collective-permute-start.2
  12.5 2.5 %collective-permute-start.4 = (bf16[80,256]{1,0:T(8,128)(2,1)S(1)}, bf16[80,256]{1,0:T(8,128)(2,1)S(1)}, u32[]{:S(2)}, u32[]{:S(2)}) collective-permute-start(bf16[80,256]{1,0:T(8,128)(2,1)S(1)} %shard_map.88.own.payload_ref), channel_id=1, source_target_pairs={{0,12},{4,8},{8,4},{12,0},{1,13},{5,9},{9,5},{13,1},{2,14},{6,10},... | collective-permute-start | bytes 122888 | tf_op jit(solution)/shard_map/ppermute | solution.py:425
  15.1 0.2 collective-permute-start.5
  15.3 1.7 %collective-permute-start.6 = (bf16[80,256]{1,0:T(8,128)(2,1)S(1)}, bf16[80,256]{1,0:T(8,128)(2,1)S(1)}, u32[]{:S(2)}, u32[]{:S(2)}) collective-permute-start(bf16[80,256]{1,0:T(8,128)(2,1)S(1)} %shard_map.88.own.payload_ref), channel_id=1, source_target_pairs={{0,4},{4,0},{8,12},{12,8},{1,5},{5,1},{9,13},{13,9},{2,6},{6,2},{1... | collective-permute-start | bytes 122888 | tf_op jit(solution)/shard_map/ppermute | solution.py:425
  17.0 0.0 collective-permute-done.2.own_other
  17.0 2.4 %shard_map.89._.own_sum = f32[1024,4096]{1,0:T(8,128)S(1)} custom-call(bf16[80,256]{1,0:T(8,128)(2,1)S(1)} %shard_map.88.own.payload_ref, bf16[80,256]{1,0:T(8,128)(2,1)S(1)} %collective-permute-done.2.own_other), custom_call_target="tpu_custom_call" | custom-call | tf_op jit(solution)/shard_map/pallas_call | solution.py:339
  19.4 0.0 collective-permute-done.3.near_query
  19.4 0.0 copy-done
  19.4 0.3 shard_map.90
  19.8 0.0 collective-permute-done.4.refs_0_
  19.8 0.9 %collective-permute-done.5.refs_1_ = bf16[80,256]{1,0:T(8,128)(2,1)S(1)} collective-permute-done((bf16[80,256]{1,0:T(8,128)(2,1)S(1)}, bf16[80,256]{1,0:T(8,128)(2,1)S(1)}, u32[]{:S(2)}, u32[]{:S(2)}) %collective-permute-start.5) | collective-permute-done | bytes 40992 | tf_op jit(solution)/shard_map/ppermute | solution.py:425
  20.7 0.0 collective-permute-done.6.refs_2_
  20.7 0.1 collective-permute-start.7
  20.8 1.3 %collective-permute-done.7.other = bf16[3,64,256]{2,1,0:T(8,128)(2,1)S(1)} collective-permute-done((bf16[3,64,256]{2,1,0:T(8,128)(2,1)S(1)}, bf16[3,64,256]{2,1,0:T(8,128)(2,1)S(1)}, u32[]{:S(2)}, u32[]{:S(2)}) %collective-permute-start.7) | collective-permute-done | bytes 98336 | tf_op jit(solution)/shard_map/ppermute | solution.py:425
  22.1 2.4 %shard_map.93 = (f32[256,256]{1,0:T(8,128)S(1)}, bf16[256,256]{1,0:T(8,128)(2,1)S(1)}) custom-call(bf16[80,256]{1,0:T(8,128)(2,1)S(1)} %shard_map.88.own.payload_ref, bf16[80,256]{1,0:T(8,128)(2,1)S(1)} %collective-permute-done.2.own_other, bf16[3,80,256]{2,1,0:T(8,128)(2,1)S(1)} %get-tuple-element.13.mine, ...), custom_call_target="tpu_custom_call" | custom-call | tf_op jit(solution)/shard_map/pallas_call | solution.py:298
  24.4 1.4 %collective-permute-start.8 = (bf16[256,256]{1,0:T(8,128)(2,1)S(1)}, bf16[256,256]{1,0:T(8,128)(2,1)S(1)}, u32[]{:S(2)}, u32[]{:S(2)}) collective-permute-start(bf16[256,256]{1,0:T(8,128)(2,1)S(1)} %get-tuple-element.17), channel_id=1, source_target_pairs={{0,8},{4,12},{8,0},{12,4},{1,9},{5,13},{9,1},{13,5},{2,10},{6,14},... | collective-permute-start | bytes 393224 | tf_op jit(solution)/shard_map/ppermute | solution.py:425
  25.8 7.9 %shard_map.92 = f32[1024,4096]{1,0:T(8,128)} custom-call(bf16[3,80,256]{2,1,0:T(8,128)(2,1)S(1)} %get-tuple-element.13.mine, bf16[3,64,256]{2,1,0:T(8,128)(2,1)S(1)} %collective-permute-done.7.other, f32[1024,4096]{1,0:T(8,128)S(1)} %shard_map.89._.own_sum), custom_call_target="tpu_custom_call" | custom-call | tf_op jit(solution)/shard_map/pallas_call | solution.py:389
  33.7 0.0 collective-permute-done.8.refs_1_
  33.7 0.8 %shard_map.94 = bf16[256,256]{1,0:T(8,128)(2,1)} custom-call(bf16[80,256]{1,0:T(8,128)(2,1)S(1)} %shard_map.88.own.payload_ref, f32[256,256]{1,0:T(8,128)S(1)} %get-tuple-element.16.refs_0_, bf16[256,256]{1,0:T(8,128)(2,1)S(1)} %collective-permute-done.8.refs_1_), custom_call_target="tpu_custom_call" | custom-call | tf_op jit(solution)/shard_map/pallas_call | solution.py:417
  (3 shorter events, 0.0 us)
Async XLA Ops:
  0.6 18.8 %copy-start = (bf16[1024,256]{1,0:T(8,128)(2,1)S(1)}, bf16[1024,256]{1,0:T(8,128)(2,1)}, u32[]{:S(2)}) copy-start(bf16[1024,256]{1,0:T(8,128)(2,1)} %query.1) | copy-start | bytes 1572868
  0.6 18.8 %collective-permute-start.3 = (bf16[1024,256]{1,0:T(8,128)(2,1)}, bf16[1024,256]{1,0:T(8,128)(2,1)S(1)}, u32[]{:S(2)}, u32[]{:S(2)}) collective-permute-start(bf16[1024,256]{1,0:T(8,128)(2,1)} %query.1), channel_id=1, source_target_pairs={{0,4},{4,0},{8,12},{12,8},{1,5},{5,1},{9,13},{13,9},{2,6},{6,2},{1... | collective-permute-start | bytes 1572872 | tf_op jit(solution)/shard_map/ppermute | solution.py:425
  6.8 1.3 %collective-permute-start = (f32[64,256]{1,0:T(8,128)S(1)}, f32[64,256]{1,0:T(8,128)S(1)}, u32[]{:S(2)}, u32[]{:S(2)}) collective-permute-start(f32[64,256]{1,0:T(8,128)S(1)} %get-tuple-element.11), channel_id=1, source_target_pairs={{0,1},{1,0},{2,3},{3,2},{4,5},{5,4},{6,7},{7,6},{8,9},{9,8},{10,11... | collective-permute-start | bytes 196616 | tf_op jit(solution)/shard_map/ppermute | solution.py:425
  8.1 4.3 %collective-permute-start.1 = (f32[64,256]{1,0:T(8,128)S(1)}, f32[64,256]{1,0:T(8,128)S(1)}, u32[]{:S(2)}, u32[]{:S(2)}) collective-permute-start(f32[64,256]{1,0:T(8,128)S(1)} %shard_map.87.one_ref), channel_id=1, source_target_pairs={{0,2},{1,3},{2,0},{3,1},{4,6},{5,7},{6,4},{7,5},{8,10},{9,11},{10,... | collective-permute-start | bytes 196616 | tf_op jit(solution)/shard_map/ppermute | solution.py:425
  12.5 4.5 %collective-permute-start.2 = (bf16[80,256]{1,0:T(8,128)(2,1)S(1)}, bf16[80,256]{1,0:T(8,128)(2,1)S(1)}, u32[]{:S(2)}, u32[]{:S(2)}) collective-permute-start(bf16[80,256]{1,0:T(8,128)(2,1)S(1)} %shard_map.88.own.payload_ref), channel_id=1, source_target_pairs={{0,1},{1,0},{2,3},{3,2},{4,5},{5,4},{6,7},{7,6},{8,9},{9,8},{10,11... | collective-permute-start | bytes 122888 | tf_op jit(solution)/shard_map/ppermute | solution.py:425
  12.5 7.2 %collective-permute-start.4 = (bf16[80,256]{1,0:T(8,128)(2,1)S(1)}, bf16[80,256]{1,0:T(8,128)(2,1)S(1)}, u32[]{:S(2)}, u32[]{:S(2)}) collective-permute-start(bf16[80,256]{1,0:T(8,128)(2,1)S(1)} %shard_map.88.own.payload_ref), channel_id=1, source_target_pairs={{0,12},{4,8},{8,4},{12,0},{1,13},{5,9},{9,5},{13,1},{2,14},{6,10},... | collective-permute-start | bytes 122888 | tf_op jit(solution)/shard_map/ppermute | solution.py:425
  15.1 5.6 %collective-permute-start.5 = (bf16[80,256]{1,0:T(8,128)(2,1)S(1)}, bf16[80,256]{1,0:T(8,128)(2,1)S(1)}, u32[]{:S(2)}, u32[]{:S(2)}) collective-permute-start(bf16[80,256]{1,0:T(8,128)(2,1)S(1)} %shard_map.88.own.payload_ref), channel_id=1, source_target_pairs={{0,8},{4,12},{8,0},{12,4},{1,9},{5,13},{9,1},{13,5},{2,10},{6,14},... | collective-permute-start | bytes 122888 | tf_op jit(solution)/shard_map/ppermute | solution.py:425
  15.3 5.4 %collective-permute-start.6 = (bf16[80,256]{1,0:T(8,128)(2,1)S(1)}, bf16[80,256]{1,0:T(8,128)(2,1)S(1)}, u32[]{:S(2)}, u32[]{:S(2)}) collective-permute-start(bf16[80,256]{1,0:T(8,128)(2,1)S(1)} %shard_map.88.own.payload_ref), channel_id=1, source_target_pairs={{0,4},{4,0},{8,12},{12,8},{1,5},{5,1},{9,13},{13,9},{2,6},{6,2},{1... | collective-permute-start | bytes 122888 | tf_op jit(solution)/shard_map/ppermute | solution.py:425
  20.7 1.4 %collective-permute-start.7 = (bf16[3,64,256]{2,1,0:T(8,128)(2,1)S(1)}, bf16[3,64,256]{2,1,0:T(8,128)(2,1)S(1)}, u32[]{:S(2)}, u32[]{:S(2)}) collective-permute-start(bf16[3,64,256]{2,1,0:T(8,128)(2,1)S(1)} %get-tuple-element.14), channel_id=1, source_target_pairs={{0,1},{1,0},{2,3},{3,2},{4,5},{5,4},{6,7},{7,6},{8,9},{9,8},{10,11... | collective-permute-start | bytes 294920 | tf_op jit(solution)/shard_map/ppermute | solution.py:425
  24.4 9.3 %collective-permute-start.8 = (bf16[256,256]{1,0:T(8,128)(2,1)S(1)}, bf16[256,256]{1,0:T(8,128)(2,1)S(1)}, u32[]{:S(2)}, u32[]{:S(2)}) collective-permute-start(bf16[256,256]{1,0:T(8,128)(2,1)S(1)} %get-tuple-element.17), channel_id=1, source_target_pairs={{0,8},{4,12},{8,0},{12,4},{1,9},{5,13},{9,1},{13,5},{2,10},{6,14},... | collective-permute-start | bytes 393224 | tf_op jit(solution)/shard_map/ppermute | solution.py:425

commit v14 on v13

--- a/solution.py
+++ b/solution.py
@@ -119,15 +119,17 @@
         pltpu.make_async_copy(grad.at[:, span], grad_v.at[:, span], sems.at[3 + n])
         for n, span in enumerate(spans)
     ]
-    for copy in copies:
+    for copy in copies[:6]:
         copy.start()
     copies[0].wait()
     copies[1].wait()
     part_act = lax.dot_general(pin_v[...], act_v[...], NT, preferred_element_type=jnp.float32)
     copies[2].wait()
     part_grad = jnp.zeros_like(part_act)
-    for copy, span in zip(copies[3:], spans):
-        copy.wait()
+    for n, span in enumerate(spans):
+        copies[3 + n].wait()
+        if n + 3 < len(spans):
+            copies[6 + n].start()
         part_grad += lax.dot_general(
             pout_v[:, span], grad_v[:, span], NT, preferred_element_type=jnp.float32
         )
@@ -156,20 +158,6 @@
     )(activations, out_grads, proj_in_t, proj_out_t)
 
 
-def turn_kernel(query, near_query, out_ref, near_out_ref):
-    out_ref[...] = query[...].T
-    near_out_ref[...] = near_query[...].T
-
-
-def turn_queries(queries, near_queries):
-    out = jax.ShapeDtypeStruct(queries.shape[::-1], queries.dtype)
-    return pl.pallas_call(
-        turn_kernel,
-        out_shape=[out, out],
-        compiler_params=params(30),
-    )(queries, near_queries)
-
-
 def add_kernel(one_ref, other_ref, out_ref):
     out_ref[...] = one_ref[...] + other_ref[...]
 
@@ -252,21 +240,57 @@
     return scale
 
 
-def share_kernel(row_count, own, own_other, mine, other, query_ref, near_query_ref, *refs):
+def project_queries(row_count, factors, features, queries):
+    rank = factors.shape[0] // 2
+    act = factors[:rank, :]
+    total = 0.0
+    for near, query_ref in enumerate(queries):
+        first = rank + (lax.axis_index("dp") ^ near) * row_count
+        for i in range(row_count):
+            row = factors[pl.ds(first + i, 1), :]
+            features[near, i * rank : (i + 1) * rank, :] = (row * act).astype(jnp.bfloat16)
+        total += jnp.dot(query_ref[...], features[near], preferred_element_type=jnp.float32)
+    return total
+
+
+def turn_kernel(row_count, query, near_query, own, own_other, *refs):
+    out_ref, near_out_ref, plain_ref, factors, weights, features = refs
+    out_ref[...] = query[...].T
+    near_out_ref[...] = near_query[...].T
+    lay_out_factors([(own, own_other)], factors, weights)
+    plain_ref[...] = project_queries(row_count, factors, features, (out_ref, near_out_ref))
+
+
+def turn_queries(queries, near_queries, own, own_other, rank, row_count):
+    rows, count = queries.shape
+    tok = own.shape[1]
+    out = jax.ShapeDtypeStruct((count, rows), queries.dtype)
+    return pl.pallas_call(
+        functools.partial(turn_kernel, row_count),
+        out_shape=[out, out, jax.ShapeDtypeStruct((count, tok), jnp.float32)],
+        scratch_shapes=[
+            pltpu.VMEM((2 * rank, tok), jnp.float32),
+            pltpu.VMEM((1, tok), jnp.float32),
+            pltpu.VMEM((2, rows, tok), jnp.bfloat16),
+        ],
+        compiler_params=params(30),
+    )(queries, near_queries, own, own_other)
+
+
+def share_kernel(
+    row_count, own, own_other, mine, other, query_ref, near_query_ref, own_plain_ref, *refs
+):
     factors, weights, features, gram = refs[-4:]
     out_refs = refs[:-4]
     lay_out_factors([(own, own_other)] + block_pairs(mine, other), factors, weights)
     rank = factors.shape[0] // 2
     tokens = factors.shape[1]
     tok = own.shape[1]
+    plain = project_queries(
+        row_count, factors.at[:, tok:], features, (query_ref, near_query_ref)
+    )
+    plain = jnp.concatenate([own_plain_ref[...], plain], axis=1)
     act = factors[:rank, :]
-    plain = 0.0
-    for near, queries in enumerate((query_ref, near_query_ref)):
-        first = rank + (lax.axis_index("dp") ^ near) * row_count
-        for i in range(row_count):
-            row = factors[pl.ds(first + i, 1), :]
-            features[near, i * rank : (i + 1) * rank, :] = (row * act).astype(jnp.bfloat16)
-        plain += jnp.dot(queries[...], features[near], preferred_element_type=jnp.float32)
     weight = weights[...]
     live = weight > 0.0
     act = jnp.where(live, act, 0.0)
@@ -292,7 +316,9 @@
         out_ref[...] = share.astype(out_ref.dtype)
 
 
-def score_shares(own, own_other, mine, other, queries_t, near_queries_t, rank, row_count):
+def score_shares(
+    own, own_other, mine, other, queries_t, near_queries_t, own_plain, rank, row_count
+):
     blocks, tok = mine.shape[0] + 1, mine.shape[2]
     count, rows = queries_t.shape
     return pl.pallas_call(
@@ -304,11 +330,11 @@
         scratch_shapes=[
             pltpu.VMEM((2 * rank, tok * blocks), jnp.float32),
             pltpu.VMEM((1, tok * blocks), jnp.float32),
-            pltpu.VMEM((2, rows, tok * blocks), jnp.bfloat16),
+            pltpu.VMEM((2, rows, tok * (blocks - 1)), jnp.bfloat16),
             pltpu.VMEM((blocks // 2, tok * blocks, tok), jnp.bfloat16),
         ],
         compiler_params=params(30),
-    )(own, own_other, mine, other, queries_t, near_queries_t)
+    )(own, own_other, mine, other, queries_t, near_queries_t, own_plain)
 
 
 def build_columns(first, act, factors, right):
@@ -445,11 +471,13 @@
     own_other = swapped(own, "query", 1)
     others = [swapped(own, "dp", k) for k in reversed(range(1, dp_count))]
     own_sum = own_tokens_sum(own, own_other, rank, row_count)
-    queries_t, near_queries_t = turn_queries(queries, near_queries)
+    queries_t, near_queries_t, own_plain = turn_queries(
+        queries, near_queries, own, own_other, rank, row_count
+    )
     mine, factors = stack(others, rank, (own_sum, queries_t))
     other = swapped(factors, "query", 1)
     shares = score_shares(
-        own, own_other, mine, other, queries_t, near_queries_t, rank, row_count
+        own, own_other, mine, other, queries_t, near_queries_t, own_plain, rank, row_count
     )
     arrived = [swapped(share, "dp", 2 * n) for n, share in enumerate(shares) if n]
     hessian = hessian_rows(mine, other, own_sum, rank, row_count)

time: 34.7 us -> 35.4 us (1.020)
  Pallas kernels: 16.8 us -> 17.7 us
  waiting for transfers between devices: 5.49 us -> 5.13 us
    pallas_call x1, Pallas kernels: 3.04 us -> 4 us  [project(): pl.pallas_call(project_kernel, in_specs=[pl.BlockSpec(memory_space=pl.ANY...]
    ppermute x9, waiting for transfers between devices: 5.49 us -> 5.13 us  [swapped(): lax.ppermute(array, axis, [(i, i ^ distance) for i in range(lax.axis_size...]
  transfers between devices with their start and end apart: 9 -> 9, of which waited for: 4 -> 4; matrix products, arithmetic and copies ran while one was open for 2% -> 2% of each run, Pallas kernels for 40% -> 42%
where the time goes in v14:
time: 35.4 us; the launch traced here: 35.2 us
  Pallas kernels  17.7 us (50%)
  starting transfers between devices  10.9 us (31%)
  waiting for transfers between devices  5.13 us (14%)
  between operations  0.75 us (2%)
  other arithmetic  0.74 us (2%)
    ppermute x9, starting transfers between devices, swapped(): lax.ppermute(array, axis, [(i, i ^ distance) for i in range(lax.axis_size...  10.9 us
    pallas_call x1, Pallas kernels, hessian_rows(): pl.pallas_call(functools.partial(hessian_kernel, row_count, col_count), o...  7.88 us
    ppermute x9, waiting for transfers between devices, swapped(): lax.ppermute(array, axis, [(i, i ^ distance) for i in range(lax.axis_size...  5.13 us
    pallas_call x1, Pallas kernels, project(): pl.pallas_call(project_kernel, in_specs=[pl.BlockSpec(memory_space=pl.ANY...  4 us
    pallas_call x1, Pallas kernels, own_tokens_sum(): pl.pallas_call(functools.partial(own_kernel, row_count, col_count), out_s...  2.41 us
    pallas_call x1, Pallas kernels, score_shares(): pl.pallas_call(functools.partial(share_kernel, row_count), out_shape=[jax...  2.08 us
    pallas_call x1, Pallas kernels, finish_scores(): pl.pallas_call(finish_kernel, out_shape=jax.ShapeDtypeStruct((tok, count)...  0.77 us
    convert_element_type x1, other arithmetic, few_tokens(): jnp.where(live, credit[:, None], 0).astype(jnp.float32).reshape(1, -1)  0.74 us
  transfers between devices with their start and end apart: 9, of which 4 were waited for; matrix products, arithmetic and copies ran while one was open for 2% of the time, Pallas kernels for 42%

profile of v14, /device:TPU:0, one launch (start us, length us, event | category | flops | bytes accessed | tf_op | source)
XLA Modules:
  0.0 35.2 jit_solution(3698974158116661816)
XLA Ops:
  0.6 0.0 copy-start
  0.6 3.1 %collective-permute-start.3 = (bf16[1024,256]{1,0:T(8,128)(2,1)}, bf16[1024,256]{1,0:T(8,128)(2,1)S(1)}, u32[]{:S(2)}, u32[]{:S(2)}) collective-permute-start(bf16[1024,256]{1,0:T(8,128)(2,1)} %query.1), channel_id=1, source_target_pairs={{0,4},{4,0},{8,12},{12,8},{1,5},{5,1},{9,13},{13,9},{2,6},{6,2},{1... | collective-permute-start | bytes 1572872 | tf_op jit(solution)/shard_map/ppermute | solution.py:451
  3.7 4.0 %shard_map.86 = (f32[64,256]{1,0:T(8,128)S(1)}, f32[64,256]{1,0:T(8,128)S(1)}) custom-call(bf16[256,1024]{1,0:T(8,128)(2,1)} %act.1, bf16[256,3584]{1,0:T(8,128)(2,1)} %grad.1, bf16[64,1024]{1,0:T(8,128)(2,1)} %bitcast.5, bf16[64,3584]{1,0:T(8,128)(2,1)} %bitcast.4), custom_call_target="tpu_custom_call" | custom-call | tf_op jit(solution)/shard_map/pallas_call | solution.py:146
  7.7 0.1 collective-permute-start
  7.8 1.2 %collective-permute-done.other_ref = f32[64,256]{1,0:T(8,128)S(1)} collective-permute-done((f32[64,256]{1,0:T(8,128)S(1)}, f32[64,256]{1,0:T(8,128)S(1)}, u32[]{:S(2)}, u32[]{:S(2)}) %collective-permute-start) | collective-permute-done | bytes 65568 | tf_op jit(solution)/shard_map/ppermute | solution.py:451
  9.1 1.6 %collective-permute-start.1 = (f32[64,256]{1,0:T(8,128)S(1)}, f32[64,256]{1,0:T(8,128)S(1)}, u32[]{:S(2)}, u32[]{:S(2)}) collective-permute-start(f32[64,256]{1,0:T(8,128)S(1)} %shard_map.87.one_ref), channel_id=1, source_target_pairs={{0,2},{1,3},{2,0},{3,1},{4,6},{5,7},{6,4},{7,5},{8,10},{9,11},{10,... | collective-permute-start | bytes 196616 | tf_op jit(solution)/shard_map/ppermute | solution.py:451
  10.6 0.7 %fusion = f32[2,128]{1,0:T(2,128)S(1)} fusion(s32[2]{0:T(128)} %param.13, s32[2]{0:T(128)} %param.12), kind=kLoop, calls=%fused_computation.1 | loop fusion | flops 768 | bytes 1040 | tf_op jit(solution)/shard_map/convert_element_type | solution.py:461
  11.4 2.0 %collective-permute-done.1.other_ref = f32[64,256]{1,0:T(8,128)S(1)} collective-permute-done((f32[64,256]{1,0:T(8,128)S(1)}, f32[64,256]{1,0:T(8,128)S(1)}, u32[]{:S(2)}, u32[]{:S(2)}) %collective-permute-start.1) | collective-permute-done | bytes 65568 | tf_op jit(solution)/shard_map/ppermute | solution.py:451
  13.4 0.1 collective-permute-start.2
  13.5 2.5 %collective-permute-start.4 = (bf16[80,256]{1,0:T(8,128)(2,1)S(1)}, bf16[80,256]{1,0:T(8,128)(2,1)S(1)}, u32[]{:S(2)}, u32[]{:S(2)}) collective-permute-start(bf16[80,256]{1,0:T(8,128)(2,1)S(1)} %shard_map.88.own.payload_ref), channel_id=1, source_target_pairs={{0,12},{4,8},{8,4},{12,0},{1,13},{5,9},{9,5},{13,1},{2,14},{6,10},... | collective-permute-start | bytes 122888 | tf_op jit(solution)/shard_map/ppermute | solution.py:451
  16.0 0.2 collective-permute-start.5
  16.2 1.7 %collective-permute-start.6 = (bf16[80,256]{1,0:T(8,128)(2,1)S(1)}, bf16[80,256]{1,0:T(8,128)(2,1)S(1)}, u32[]{:S(2)}, u32[]{:S(2)}) collective-permute-start(bf16[80,256]{1,0:T(8,128)(2,1)S(1)} %shard_map.88.own.payload_ref), channel_id=1, source_target_pairs={{0,4},{4,0},{8,12},{12,8},{1,5},{5,1},{9,13},{13,9},{2,6},{6,2},{1... | collective-permute-start | bytes 122888 | tf_op jit(solution)/shard_map/ppermute | solution.py:451
  17.9 0.0 collective-permute-done.2.own_other
  18.0 2.4 %shard_map.89._.own_sum = f32[1024,4096]{1,0:T(8,128)S(1)} custom-call(bf16[80,256]{1,0:T(8,128)(2,1)S(1)} %shard_map.88.own.payload_ref, bf16[80,256]{1,0:T(8,128)(2,1)S(1)} %collective-permute-done.2.own_other), custom_call_target="tpu_custom_call" | custom-call | tf_op jit(solution)/shard_map/pallas_call | solution.py:365
  20.4 0.0 collective-permute-done.3.near_query
  20.4 0.0 copy-done
  20.4 0.5 %shard_map.90 = (bf16[256,1024]{1,0:T(8,128)(2,1)S(1)}, bf16[256,1024]{1,0:T(8,128)(2,1)S(1)}, f32[256,256]{1,0:T(8,128)S(1)}) custom-call(bf16[1024,256]{1,0:T(8,128)(2,1)S(1)} %copy-done, bf16[1024,256]{1,0:T(8,128)(2,1)S(1)} %collective-permute-done.3.near_query, bf16[80,256]{1,0:T(8,128)(2,1)S(1)} %shard_map.88.own.payload_ref, ...), custom_call_target="tpu_custom_call" | custom-call | tf_op jit(solution)/shard_map/pallas_call | solution.py:268
  20.9 0.0 collective-permute-done.4.refs_0_
  20.9 0.6 %collective-permute-done.5.refs_1_ = bf16[80,256]{1,0:T(8,128)(2,1)S(1)} collective-permute-done((bf16[80,256]{1,0:T(8,128)(2,1)S(1)}, bf16[80,256]{1,0:T(8,128)(2,1)S(1)}, u32[]{:S(2)}, u32[]{:S(2)}) %collective-permute-start.5) | collective-permute-done | bytes 40992 | tf_op jit(solution)/shard_map/ppermute | solution.py:451
  21.4 0.0 collective-permute-done.6.refs_2_
  21.5 0.1 collective-permute-start.7
  21.6 1.3 %collective-permute-done.7.other = bf16[3,64,256]{2,1,0:T(8,128)(2,1)S(1)} collective-permute-done((bf16[3,64,256]{2,1,0:T(8,128)(2,1)S(1)}, bf16[3,64,256]{2,1,0:T(8,128)(2,1)S(1)}, u32[]{:S(2)}, u32[]{:S(2)}) %collective-permute-start.7) | collective-permute-done | bytes 98336 | tf_op jit(solution)/shard_map/ppermute | solution.py:451
  22.8 2.1 %shard_map.93 = (f32[256,256]{1,0:T(8,128)S(1)}, bf16[256,256]{1,0:T(8,128)(2,1)S(1)}) custom-call(bf16[80,256]{1,0:T(8,128)(2,1)S(1)} %shard_map.88.own.payload_ref, bf16[80,256]{1,0:T(8,128)(2,1)S(1)} %collective-permute-done.2.own_other, bf16[3,80,256]{2,1,0:T(8,128)(2,1)S(1)} %get-tuple-element.14.mine, ...), custom_call_target="tpu_custom_call" | custom-call | tf_op jit(solution)/shard_map/pallas_call | solution.py:324
  24.9 1.6 %collective-permute-start.8 = (bf16[256,256]{1,0:T(8,128)(2,1)S(1)}, bf16[256,256]{1,0:T(8,128)(2,1)S(1)}, u32[]{:S(2)}, u32[]{:S(2)}) collective-permute-start(bf16[256,256]{1,0:T(8,128)(2,1)S(1)} %get-tuple-element.19), channel_id=1, source_target_pairs={{0,8},{4,12},{8,0},{12,4},{1,9},{5,13},{9,1},{13,5},{2,10},{6,14},... | collective-permute-start | bytes 393224 | tf_op jit(solution)/shard_map/ppermute | solution.py:451
  26.5 7.9 %shard_map.92 = f32[1024,4096]{1,0:T(8,128)} custom-call(bf16[3,80,256]{2,1,0:T(8,128)(2,1)S(1)} %get-tuple-element.14.mine, bf16[3,64,256]{2,1,0:T(8,128)(2,1)S(1)} %collective-permute-done.7.other, f32[1024,4096]{1,0:T(8,128)S(1)} %shard_map.89._.own_sum), custom_call_target="tpu_custom_call" | custom-call | tf_op jit(solution)/shard_map/pallas_call | solution.py:415
  34.4 0.0 collective-permute-done.8.refs_1_
  34.4 0.8 %shard_map.94 = bf16[256,256]{1,0:T(8,128)(2,1)} custom-call(bf16[80,256]{1,0:T(8,128)(2,1)S(1)} %shard_map.88.own.payload_ref, f32[256,256]{1,0:T(8,128)S(1)} %get-tuple-element.18.refs_0_, bf16[256,256]{1,0:T(8,128)(2,1)S(1)} %collective-permute-done.8.refs_1_), custom_call_target="tpu_custom_call" | custom-call | tf_op jit(solution)/shard_map/pallas_call | solution.py:443
  (3 shorter events, 0.0 us)
Async XLA Ops:
  0.6 19.7 %copy-start = (bf16[1024,256]{1,0:T(8,128)(2,1)S(1)}, bf16[1024,256]{1,0:T(8,128)(2,1)}, u32[]{:S(2)}) copy-start(bf16[1024,256]{1,0:T(8,128)(2,1)} %query.1) | copy-start | bytes 1572868
  0.6 19.7 %collective-permute-start.3 = (bf16[1024,256]{1,0:T(8,128)(2,1)}, bf16[1024,256]{1,0:T(8,128)(2,1)S(1)}, u32[]{:S(2)}, u32[]{:S(2)}) collective-permute-start(bf16[1024,256]{1,0:T(8,128)(2,1)} %query.1), channel_id=1, source_target_pairs={{0,4},{4,0},{8,12},{12,8},{1,5},{5,1},{9,13},{13,9},{2,6},{6,2},{1... | collective-permute-start | bytes 1572872 | tf_op jit(solution)/shard_map/ppermute | solution.py:451
  7.7 1.3 %collective-permute-start = (f32[64,256]{1,0:T(8,128)S(1)}, f32[64,256]{1,0:T(8,128)S(1)}, u32[]{:S(2)}, u32[]{:S(2)}) collective-permute-start(f32[64,256]{1,0:T(8,128)S(1)} %get-tuple-element.12), channel_id=1, source_target_pairs={{0,1},{1,0},{2,3},{3,2},{4,5},{5,4},{6,7},{7,6},{8,9},{9,8},{10,11... | collective-permute-start | bytes 196616 | tf_op jit(solution)/shard_map/ppermute | solution.py:451
  9.1 4.3 %collective-permute-start.1 = (f32[64,256]{1,0:T(8,128)S(1)}, f32[64,256]{1,0:T(8,128)S(1)}, u32[]{:S(2)}, u32[]{:S(2)}) collective-permute-start(f32[64,256]{1,0:T(8,128)S(1)} %shard_map.87.one_ref), channel_id=1, source_target_pairs={{0,2},{1,3},{2,0},{3,1},{4,6},{5,7},{6,4},{7,5},{8,10},{9,11},{10,... | collective-permute-start | bytes 196616 | tf_op jit(solution)/shard_map/ppermute | solution.py:451
  13.4 4.5 %collective-permute-start.2 = (bf16[80,256]{1,0:T(8,128)(2,1)S(1)}, bf16[80,256]{1,0:T(8,128)(2,1)S(1)}, u32[]{:S(2)}, u32[]{:S(2)}) collective-permute-start(bf16[80,256]{1,0:T(8,128)(2,1)S(1)} %shard_map.88.own.payload_ref), channel_id=1, source_target_pairs={{0,1},{1,0},{2,3},{3,2},{4,5},{5,4},{6,7},{7,6},{8,9},{9,8},{10,11... | collective-permute-start | bytes 122888 | tf_op jit(solution)/shard_map/ppermute | solution.py:451
  13.5 7.4 %collective-permute-start.4 = (bf16[80,256]{1,0:T(8,128)(2,1)S(1)}, bf16[80,256]{1,0:T(8,128)(2,1)S(1)}, u32[]{:S(2)}, u32[]{:S(2)}) collective-permute-start(bf16[80,256]{1,0:T(8,128)(2,1)S(1)} %shard_map.88.own.payload_ref), channel_id=1, source_target_pairs={{0,12},{4,8},{8,4},{12,0},{1,13},{5,9},{9,5},{13,1},{2,14},{6,10},... | collective-permute-start | bytes 122888 | tf_op jit(solution)/shard_map/ppermute | solution.py:451
  16.0 5.4 %collective-permute-start.5 = (bf16[80,256]{1,0:T(8,128)(2,1)S(1)}, bf16[80,256]{1,0:T(8,128)(2,1)S(1)}, u32[]{:S(2)}, u32[]{:S(2)}) collective-permute-start(bf16[80,256]{1,0:T(8,128)(2,1)S(1)} %shard_map.88.own.payload_ref), channel_id=1, source_target_pairs={{0,8},{4,12},{8,0},{12,4},{1,9},{5,13},{9,1},{13,5},{2,10},{6,14},... | collective-permute-start | bytes 122888 | tf_op jit(solution)/shard_map/ppermute | solution.py:451
  16.2 5.2 %collective-permute-start.6 = (bf16[80,256]{1,0:T(8,128)(2,1)S(1)}, bf16[80,256]{1,0:T(8,128)(2,1)S(1)}, u32[]{:S(2)}, u32[]{:S(2)}) collective-permute-start(bf16[80,256]{1,0:T(8,128)(2,1)S(1)} %shard_map.88.own.payload_ref), channel_id=1, source_target_pairs={{0,4},{4,0},{8,12},{12,8},{1,5},{5,1},{9,13},{13,9},{2,6},{6,2},{1... | collective-permute-start | bytes 122888 | tf_op jit(solution)/shard_map/ppermute | solution.py:451
  21.5 1.4 %collective-permute-start.7 = (bf16[3,64,256]{2,1,0:T(8,128)(2,1)S(1)}, bf16[3,64,256]{2,1,0:T(8,128)(2,1)S(1)}, u32[]{:S(2)}, u32[]{:S(2)}) collective-permute-start(bf16[3,64,256]{2,1,0:T(8,128)(2,1)S(1)} %get-tuple-element.15), channel_id=1, source_target_pairs={{0,1},{1,0},{2,3},{3,2},{4,5},{5,4},{6,7},{7,6},{8,9},{9,8},{10,11... | collective-permute-start | bytes 294920 | tf_op jit(solution)/shard_map/ppermute | solution.py:451
  24.9 9.5 %collective-permute-start.8 = (bf16[256,256]{1,0:T(8,128)(2,1)S(1)}, bf16[256,256]{1,0:T(8,128)(2,1)S(1)}, u32[]{:S(2)}, u32[]{:S(2)}) collective-permute-start(bf16[256,256]{1,0:T(8,128)(2,1)S(1)} %get-tuple-element.19), channel_id=1, source_target_pairs={{0,8},{4,12},{8,0},{12,4},{1,9},{5,13},{9,1},{13,5},{2,10},{6,14},... | collective-permute-start | bytes 393224 | tf_op jit(solution)/shard_map/ppermute | solution.py:451

commit v15 on v14

--- a/solution.py
+++ b/solution.py
@@ -110,26 +110,20 @@
 
 
 def project_kernel(act, grad, pin, pout, keep_ref, send_ref, act_v, grad_v, pin_v, pout_v, sems):
-    chunk = act.shape[1]
-    while grad.shape[1] % chunk:
-        chunk //= 2
-    spans = [pl.ds(c, chunk) for c in range(0, grad.shape[1], chunk)]
-    copies = [pltpu.make_async_copy(s, d, sems.at[n]) for n, (s, d) in enumerate(((pin, pin_v), (act, act_v), (pout, pout_v)))]
-    copies += [
-        pltpu.make_async_copy(grad.at[:, span], grad_v.at[:, span], sems.at[3 + n])
-        for n, span in enumerate(spans)
-    ]
-    for copy in copies[:6]:
+    chunk = grad.shape[1] // 2
+    spans = [pl.ds(0, chunk), pl.ds(chunk, chunk)]
+    pairs = [(pin, pin_v), (act, act_v), (pout, pout_v)]
+    pairs += [(grad.at[:, span], grad_v.at[:, span]) for span in spans]
+    copies = [pltpu.make_async_copy(s, d, sems.at[n]) for n, (s, d) in enumerate(pairs)]
+    for copy in copies:
         copy.start()
     copies[0].wait()
     copies[1].wait()
     part_act = lax.dot_general(pin_v[...], act_v[...], NT, preferred_element_type=jnp.float32)
     copies[2].wait()
     part_grad = jnp.zeros_like(part_act)
-    for n, span in enumerate(spans):
-        copies[3 + n].wait()
-        if n + 3 < len(spans):
-            copies[6 + n].start()
+    for copy, span in zip(copies[3:], spans):
+        copy.wait()
         part_grad += lax.dot_general(
             pout_v[:, span], grad_v[:, span], NT, preferred_element_type=jnp.float32
         )
@@ -152,7 +146,7 @@
             pltpu.VMEM((tok, f_here), jnp.bfloat16),
             pltpu.VMEM((rank, d_here), jnp.bfloat16),
             pltpu.VMEM((rank, f_here), jnp.bfloat16),
-            pltpu.SemaphoreType.DMA((3 + f_here // 128,)),
+            pltpu.SemaphoreType.DMA((5,)),
         ],
         compiler_params=params(53.75),
     )(activations, out_grads, proj_in_t, proj_out_t)
@@ -202,7 +196,7 @@
             jax.ShapeDtypeStruct((len(parts), rows, tok), parts[0].dtype),
             jax.ShapeDtypeStruct((len(parts), rank, tok), parts[0].dtype),
         ],
-        compiler_params=params(30),
+        compiler_params=params(26),
     )(*after, *parts)
 
 
@@ -218,7 +212,7 @@
 
 
 def block_pairs(mine, other):
-    return [(mine.at[k], other.at[k]) for k in reversed(range(mine.shape[0]))]
+    return [(mine.at[k], other.at[k]) for k in range(mine.shape[0])]
 
 
 def weigh_rows(first_row, end_row, row_count, factors, weights, weighted):
@@ -273,15 +267,26 @@
             pltpu.VMEM((1, tok), jnp.float32),
             pltpu.VMEM((2, rows, tok), jnp.bfloat16),
         ],
-        compiler_params=params(30),
+        compiler_params=params(26),
     )(queries, near_queries, own, own_other)
+
+
+def block_share(plain, weighted, act_rows, grad_rows, act, grad, scales, gram):
+    for row in range(0, gram.shape[0], TILE // 2):
+        here = slice(row, row + TILE // 2)
+        tile = jnp.dot(act_rows[here], act, preferred_element_type=jnp.float32)
+        tile *= jnp.dot(grad_rows[here], grad, preferred_element_type=jnp.float32)
+        gram[here, :] = tile.astype(jnp.bfloat16)
+    image = jnp.dot(weighted, gram[...], preferred_element_type=jnp.float32)
+    return ((2.0 - 0.1 / 1.1) * plain - image) * scales[:1, :1] * scales[1:2, :1]
 
 
 def share_kernel(
     row_count, own, own_other, mine, other, query_ref, near_query_ref, own_plain_ref, *refs
 ):
+    weighted_ref, act_rows, grad_rows, act_own, grad_own, scales = refs[:6]
+    out_refs = refs[6:-4]
     factors, weights, features, gram = refs[-4:]
-    out_refs = refs[:-4]
     lay_out_factors([(own, own_other)] + block_pairs(mine, other), factors, weights)
     rank = factors.shape[0] // 2
     tokens = factors.shape[1]
@@ -290,29 +295,36 @@
         row_count, factors.at[:, tok:], features, (query_ref, near_query_ref)
     )
     plain = jnp.concatenate([own_plain_ref[...], plain], axis=1)
-    act = factors[:rank, :]
     weight = weights[...]
     live = weight > 0.0
-    act = jnp.where(live, act, 0.0)
+    act = jnp.where(live, factors[:rank, :], 0.0)
     grad = jnp.where(live, factors[rank:, :], 0.0)
     act_scale, grad_scale = range_scale(act), range_scale(grad)
     act, grad = act * act_scale, grad * grad_scale
     norms = jnp.sum(act * act, axis=0, keepdims=True) * jnp.sum(grad * grad, axis=0, keepdims=True)
     level = jnp.sum(weight * norms, axis=1, keepdims=True) / (tokens * rank * rank)
     step = 1.1 * level
+    scale = act_scale * grad_scale
+    scales[:1, :] = jnp.broadcast_to(scale, (1, scales.shape[1]))
+    scales[1:2, :] = jnp.broadcast_to(scale / step, (1, scales.shape[1]))
     act_b, grad_b = act.astype(jnp.bfloat16), grad.astype(jnp.bfloat16)
-    act_rows, grad_rows = act.T.astype(jnp.bfloat16), grad.T.astype(jnp.bfloat16)
-    weighted = (plain * (weight * (1.0 / (tokens * step)))).astype(jnp.bfloat16)
-    scale = act_scale * grad_scale
+    act_rows[...] = act.T.astype(jnp.bfloat16)
+    grad_rows[...] = grad.T.astype(jnp.bfloat16)
+    act_own[...] = act_b[:, :tok]
+    grad_own[...] = grad_b[:, :tok]
+    weighted_ref[...] = (plain * (weight * (1.0 / (tokens * step)))).astype(jnp.bfloat16)
     for n, out_ref in enumerate(out_refs):
-        block = slice(2 * n * tok, (2 * n + 1) * tok)
-        for row in range(0, tokens, TILE // 2):
-            here = slice(row, row + TILE // 2)
-            tile = jnp.dot(act_rows[here], act_b[:, block], preferred_element_type=jnp.float32)
-            tile *= jnp.dot(grad_rows[here], grad_b[:, block], preferred_element_type=jnp.float32)
-            gram[n, here, :] = tile.astype(jnp.bfloat16)
-        image = jnp.dot(weighted, gram[n], preferred_element_type=jnp.float32)
-        share = ((2.0 - 0.1 / 1.1) * plain[:, block] - image) * scale * (scale / step)
+        block = slice(2 * (n + 1) * tok, (2 * (n + 1) + 1) * tok)
+        share = block_share(
+            plain[:, block],
+            weighted_ref[...],
+            act_rows,
+            grad_rows,
+            act_b[:, block],
+            grad_b[:, block],
+            scales,
+            gram,
+        )
         out_ref[...] = share.astype(out_ref.dtype)
 
 
@@ -321,19 +333,25 @@
 ):
     blocks, tok = mine.shape[0] + 1, mine.shape[2]
     count, rows = queries_t.shape
+    tokens = tok * blocks
     return pl.pallas_call(
         functools.partial(share_kernel, row_count),
         out_shape=[
-            jax.ShapeDtypeStruct((count, tok), jnp.bfloat16 if k else jnp.float32)
-            for k in range(0, blocks, 2)
-        ],
+            jax.ShapeDtypeStruct((count, tokens), jnp.bfloat16),
+            jax.ShapeDtypeStruct((tokens, rank), jnp.bfloat16),
+            jax.ShapeDtypeStruct((tokens, rank), jnp.bfloat16),
+            jax.ShapeDtypeStruct((rank, tok), jnp.bfloat16),
+            jax.ShapeDtypeStruct((rank, tok), jnp.bfloat16),
+            jax.ShapeDtypeStruct((8, 128), jnp.float32),
+        ]
+        + [jax.ShapeDtypeStruct((count, tok), jnp.bfloat16)] * (blocks // 2 - 1),
         scratch_shapes=[
-            pltpu.VMEM((2 * rank, tok * blocks), jnp.float32),
-            pltpu.VMEM((1, tok * blocks), jnp.float32),
-            pltpu.VMEM((2, rows, tok * (blocks - 1)), jnp.bfloat16),
-            pltpu.VMEM((blocks // 2, tok * blocks, tok), jnp.bfloat16),
-        ],
-        compiler_params=params(30),
+            pltpu.VMEM((2 * rank, tokens), jnp.float32),
+            pltpu.VMEM((1, tokens), jnp.float32),
+            pltpu.VMEM((2, rows, tokens - tok), jnp.bfloat16),
+            pltpu.VMEM((tokens, tok), jnp.bfloat16),
+        ],
+        compiler_params=params(26),
     )(own, own_other, mine, other, queries_t, near_queries_t, own_plain)
 
 
@@ -376,9 +394,10 @@
     )(own, own_other)
 
 
-def hessian_kernel(row_count, col_count, mine, other, own_sum, out, *scratch):
-    factors, weights, weighted, rights = *scratch[:3], scratch[3:5]
-    result, sems = scratch[5:]
+def hessian_kernel(row_count, col_count, mine, other, own_sum, own_plain, *refs):
+    share_parts, out, share_ref = refs[:6], refs[6], refs[7]
+    factors, weights, weighted, rights = *refs[8:11], refs[11:13]
+    result, gram, sems = refs[13:]
     rank = factors.shape[0] // 2
     blocks = mine.shape[0]
     tokens = factors.shape[1] // blocks * (blocks + 1)
@@ -404,18 +423,35 @@
             copy = pltpu.make_async_copy(result.at[here], out.at[here], sems.at[len(copies)])
             copy.start()
             copies.append(copy)
+    share_weighted, act_rows, grad_rows, act_own, grad_own, scales = share_parts
+    share_ref[...] = block_share(
+        own_plain[...],
+        share_weighted[...],
+        act_rows,
+        grad_rows,
+        act_own[...],
+        grad_own[...],
+        scales,
+        gram,
+    )
     for copy in copies:
         copy.wait()
 
 
-def hessian_rows(mine, other, own_sum, rank, row_count, col_count=8):
+def hessian_rows(mine, other, own_sum, own_plain, share_parts, rank, row_count, col_count=8):
     blocks, _, tok = mine.shape
     feat = rank * rank
     rows, cols = row_count * rank, col_count * rank
     return pl.pallas_call(
         functools.partial(hessian_kernel, row_count, col_count),
-        out_specs=pl.BlockSpec(memory_space=pl.ANY),
-        out_shape=jax.ShapeDtypeStruct((rows, feat), jnp.float32),
+        out_specs=[
+            pl.BlockSpec(memory_space=pl.ANY),
+            pl.BlockSpec(memory_space=pltpu.VMEM),
+        ],
+        out_shape=[
+            jax.ShapeDtypeStruct((rows, feat), jnp.float32),
+            jax.ShapeDtypeStruct(own_plain.shape, jnp.float32),
+        ],
         scratch_shapes=[
             pltpu.VMEM((2 * rank, tok * blocks), jnp.float32),
             pltpu.VMEM((1, tok * blocks), jnp.float32),
@@ -423,10 +459,11 @@
             pltpu.VMEM((cols, tok * blocks), jnp.bfloat16),
             pltpu.VMEM((cols, tok * blocks), jnp.bfloat16),
             pltpu.VMEM((rows, feat), jnp.float32),
+            pltpu.VMEM((tok * (blocks + 1), tok), jnp.bfloat16),
             pltpu.SemaphoreType.DMA((feat // cols * (rows // TILE),)),
         ],
-        compiler_params=params(30),
-    )(mine, other, own_sum)
+        compiler_params=params(26),
+    )(mine, other, own_sum, own_plain, *share_parts)
 
 
 def finish_kernel(payload_ref, *refs):
@@ -474,14 +511,16 @@
     queries_t, near_queries_t, own_plain = turn_queries(
         queries, near_queries, own, own_other, rank, row_count
     )
-    mine, factors = stack(others, rank, (own_sum, queries_t))
+    mine, factors = stack(others[::-1], rank, (own_sum, queries_t))
     other = swapped(factors, "query", 1)
-    shares = score_shares(
+    parts = score_shares(
         own, own_other, mine, other, queries_t, near_queries_t, own_plain, rank, row_count
     )
-    arrived = [swapped(share, "dp", 2 * n) for n, share in enumerate(shares) if n]
-    hessian = hessian_rows(mine, other, own_sum, rank, row_count)
-    return hessian, finish_scores(own, [shares[0]] + arrived)
+    arrived = [swapped(share, "dp", 2 * (n + 1)) for n, share in enumerate(parts[6:])]
+    hessian, share = hessian_rows(
+        mine, other, own_sum, own_plain, parts[:6], rank, row_count
+    )
+    return hessian, finish_scores(own, [share] + arrived)
 
 
 def power_of_two(count):

time: 35.4 us -> 35 us (0.989)
  starting transfers between devices: 10.9 us -> 10.4 us
  waiting for transfers between devices: 5.13 us -> 5.57 us
    pallas_call x1, Pallas kernels: 7.88 us -> 9.29 us  [hessian_rows(): pl.pallas_call(functools.partial(hessian_kernel, row_count, col_count), o...]
    pallas_call x1, Pallas kernels: 4 us -> 2.66 us  [project(): pl.pallas_call(project_kernel, in_specs=[pl.BlockSpec(memory_space=pl.ANY...]
    ppermute x9, starting transfers between devices: 10.9 us -> 10.4 us  [swapped(): lax.ppermute(array, axis, [(i, i ^ distance) for i in range(lax.axis_size...]
    ppermute x9, waiting for transfers between devices: 5.13 us -> 5.57 us  [swapped(): lax.ppermute(array, axis, [(i, i ^ distance) for i in range(lax.axis_size...]
    pallas_call x1, Pallas kernels: 2.08 us -> 1.71 us  [score_shares(): pl.pallas_call(functools.partial(share_kernel, row_count), out_shape=[jax...]
  transfers between devices with their start and end apart: 9 -> 9, of which waited for: 4 -> 4; matrix products, arithmetic and copies ran while one was open for 2% -> 2% of each run, Pallas kernels for 42% -> 43%
where the time goes in v15:
time: 35 us; the launch traced here: 34.9 us
  Pallas kernels  17.4 us (50%)
  starting transfers between devices  10.4 us (30%)
  waiting for transfers between devices  5.57 us (16%)
  between operations  0.75 us (2%)
  other arithmetic  0.74 us (2%)
    ppermute x9, starting transfers between devices, swapped(): lax.ppermute(array, axis, [(i, i ^ distance) for i in range(lax.axis_size...  10.4 us
    pallas_call x1, Pallas kernels, hessian_rows(): pl.pallas_call(functools.partial(hessian_kernel, row_count, col_count), o...  9.29 us
    ppermute x9, waiting for transfers between devices, swapped(): lax.ppermute(array, axis, [(i, i ^ distance) for i in range(lax.axis_size...  5.57 us
    pallas_call x1, Pallas kernels, project(): pl.pallas_call(project_kernel, in_specs=[pl.BlockSpec(memory_space=pl.ANY...  2.66 us
    pallas_call x1, Pallas kernels, own_tokens_sum(): pl.pallas_call(functools.partial(own_kernel, row_count, col_count), out_s...  2.4 us
    pallas_call x1, Pallas kernels, score_shares(): pl.pallas_call(functools.partial(share_kernel, row_count), out_shape=[jax...  1.71 us
    pallas_call x1, Pallas kernels, finish_scores(): pl.pallas_call(finish_kernel, out_shape=jax.ShapeDtypeStruct((tok, count)...  0.77 us
    convert_element_type x1, other arithmetic, few_tokens(): jnp.where(live, credit[:, None], 0).astype(jnp.float32).reshape(1, -1)  0.74 us
  transfers between devices with their start and end apart: 9, of which 4 were waited for; matrix products, arithmetic and copies ran while one was open for 2% of the time, Pallas kernels for 43%

profile of v15, /device:TPU:0, one launch (start us, length us, event | category | flops | bytes accessed | tf_op | source)
XLA Modules:
  0.0 34.9 jit_solution(3273829112618231829)
XLA Ops:
  0.6 0.0 copy-start
  0.6 3.1 %collective-permute-start.3 = (bf16[1024,256]{1,0:T(8,128)(2,1)}, bf16[1024,256]{1,0:T(8,128)(2,1)S(1)}, u32[]{:S(2)}, u32[]{:S(2)}) collective-permute-start(bf16[1024,256]{1,0:T(8,128)(2,1)} %query.1), channel_id=1, source_target_pairs={{0,4},{4,0},{8,12},{12,8},{1,5},{5,1},{9,13},{13,9},{2,6},{6,2},{1... | collective-permute-start | bytes 1572872 | tf_op jit(solution)/shard_map/ppermute | solution.py:488
  3.7 2.7 %shard_map.86 = (f32[64,256]{1,0:T(8,128)S(1)}, f32[64,256]{1,0:T(8,128)S(1)}) custom-call(bf16[256,1024]{1,0:T(8,128)(2,1)} %act.1, bf16[256,3584]{1,0:T(8,128)(2,1)} %grad.1, bf16[64,1024]{1,0:T(8,128)(2,1)} %bitcast.5, bf16[64,3584]{1,0:T(8,128)(2,1)} %bitcast.4), custom_call_target="tpu_custom_call" | custom-call | tf_op jit(solution)/shard_map/pallas_call | solution.py:140
  6.4 0.1 collective-permute-start
  6.5 1.2 %collective-permute-done.other_ref = f32[64,256]{1,0:T(8,128)S(1)} collective-permute-done((f32[64,256]{1,0:T(8,128)S(1)}, f32[64,256]{1,0:T(8,128)S(1)}, u32[]{:S(2)}, u32[]{:S(2)}) %collective-permute-start) | collective-permute-done | bytes 65568 | tf_op jit(solution)/shard_map/ppermute | solution.py:488
  7.7 1.6 %collective-permute-start.1 = (f32[64,256]{1,0:T(8,128)S(1)}, f32[64,256]{1,0:T(8,128)S(1)}, u32[]{:S(2)}, u32[]{:S(2)}) collective-permute-start(f32[64,256]{1,0:T(8,128)S(1)} %shard_map.87.one_ref), channel_id=1, source_target_pairs={{0,2},{1,3},{2,0},{3,1},{4,6},{5,7},{6,4},{7,5},{8,10},{9,11},{10,... | collective-permute-start | bytes 196616 | tf_op jit(solution)/shard_map/ppermute | solution.py:488
  9.3 0.7 %fusion = f32[2,128]{1,0:T(2,128)S(1)} fusion(s32[2]{0:T(128)} %param.13, s32[2]{0:T(128)} %param.12), kind=kLoop, calls=%fused_computation.1 | loop fusion | flops 768 | bytes 1040 | tf_op jit(solution)/shard_map/convert_element_type | solution.py:498
  10.0 2.0 %collective-permute-done.1.other_ref = f32[64,256]{1,0:T(8,128)S(1)} collective-permute-done((f32[64,256]{1,0:T(8,128)S(1)}, f32[64,256]{1,0:T(8,128)S(1)}, u32[]{:S(2)}, u32[]{:S(2)}) %collective-permute-start.1) | collective-permute-done | bytes 65568 | tf_op jit(solution)/shard_map/ppermute | solution.py:488
  12.1 0.1 collective-permute-start.2
  12.2 2.5 %collective-permute-start.6 = (bf16[80,256]{1,0:T(8,128)(2,1)S(1)}, bf16[80,256]{1,0:T(8,128)(2,1)S(1)}, u32[]{:S(2)}, u32[]{:S(2)}) collective-permute-start(bf16[80,256]{1,0:T(8,128)(2,1)S(1)} %shard_map.88.own.payload_ref), channel_id=1, source_target_pairs={{0,12},{4,8},{8,4},{12,0},{1,13},{5,9},{9,5},{13,1},{2,14},{6,10},... | collective-permute-start | bytes 122888 | tf_op jit(solution)/shard_map/ppermute | solution.py:488
  14.7 0.2 collective-permute-start.5
  14.9 1.7 %collective-permute-start.4 = (bf16[80,256]{1,0:T(8,128)(2,1)S(1)}, bf16[80,256]{1,0:T(8,128)(2,1)S(1)}, u32[]{:S(2)}, u32[]{:S(2)}) collective-permute-start(bf16[80,256]{1,0:T(8,128)(2,1)S(1)} %shard_map.88.own.payload_ref), channel_id=1, source_target_pairs={{0,4},{4,0},{8,12},{12,8},{1,5},{5,1},{9,13},{13,9},{2,6},{6,2},{1... | collective-permute-start | bytes 122888 | tf_op jit(solution)/shard_map/ppermute | solution.py:488
  16.6 0.0 collective-permute-done.2.own_other
  16.6 2.4 %shard_map.89._.own_sum = f32[1024,4096]{1,0:T(8,128)S(1)} custom-call(bf16[80,256]{1,0:T(8,128)(2,1)S(1)} %shard_map.88.own.payload_ref, bf16[80,256]{1,0:T(8,128)(2,1)S(1)} %collective-permute-done.2.own_other), custom_call_target="tpu_custom_call" | custom-call | tf_op jit(solution)/shard_map/pallas_call | solution.py:383
  19.0 0.0 collective-permute-done.3.near_query
  19.0 0.0 copy-done
  19.0 0.5 %shard_map.90 = (bf16[256,1024]{1,0:T(8,128)(2,1)S(1)}, bf16[256,1024]{1,0:T(8,128)(2,1)S(1)}, f32[256,256]{1,0:T(8,128)S(1)}) custom-call(bf16[1024,256]{1,0:T(8,128)(2,1)S(1)} %copy-done, bf16[1024,256]{1,0:T(8,128)(2,1)S(1)} %collective-permute-done.3.near_query, bf16[80,256]{1,0:T(8,128)(2,1)S(1)} %shard_map.88.own.payload_ref, ...), custom_call_target="tpu_custom_call" | custom-call | tf_op jit(solution)/shard_map/pallas_call | solution.py:262
  19.6 0.0 collective-permute-done.6.refs_2_
  19.6 1.0 %collective-permute-done.5.refs_1_ = bf16[80,256]{1,0:T(8,128)(2,1)S(1)} collective-permute-done((bf16[80,256]{1,0:T(8,128)(2,1)S(1)}, bf16[80,256]{1,0:T(8,128)(2,1)S(1)}, u32[]{:S(2)}, u32[]{:S(2)}) %collective-permute-start.5) | collective-permute-done | bytes 40992 | tf_op jit(solution)/shard_map/ppermute | solution.py:488
  20.6 0.0 collective-permute-done.4.refs_0_
  20.6 0.1 collective-permute-start.7
  20.7 1.3 %collective-permute-done.7.other = bf16[3,64,256]{2,1,0:T(8,128)(2,1)S(1)} collective-permute-done((bf16[3,64,256]{2,1,0:T(8,128)(2,1)S(1)}, bf16[3,64,256]{2,1,0:T(8,128)(2,1)S(1)}, u32[]{:S(2)}, u32[]{:S(2)}) %collective-permute-start.7) | collective-permute-done | bytes 98336 | tf_op jit(solution)/shard_map/ppermute | solution.py:488
  21.9 1.7 %shard_map.92 = (bf16[256,1024]{1,0:T(8,128)(2,1)S(1)}, bf16[1024,64]{1,0:T(8,128)(2,1)S(1)}, bf16[1024,64]{1,0:T(8,128)(2,1)S(1)}, bf16[64,256]{1,0:T(8,128)(2,...) custom-call(bf16[80,256]{1,0:T(8,128)(2,1)S(1)} %shard_map.88.own.payload_ref, ...), custom_call_target="tpu_custom_call" | custom-call | tf_op jit(solution)/shard_map/pallas_call | solution.py:337
  23.7 1.1 %collective-permute-start.8 = (bf16[256,256]{1,0:T(8,128)(2,1)S(1)}, bf16[256,256]{1,0:T(8,128)(2,1)S(1)}, u32[]{:S(2)}, u32[]{:S(2)}) collective-permute-start(bf16[256,256]{1,0:T(8,128)(2,1)S(1)} %get-tuple-element.33), channel_id=1, source_target_pairs={{0,8},{4,12},{8,0},{12,4},{1,9},{5,13},{9,1},{13,5},{2,10},{6,14},... | collective-permute-start | bytes 393224 | tf_op jit(solution)/shard_map/ppermute | solution.py:488
  24.8 9.3 %shard_map.93 = (f32[1024,4096]{1,0:T(8,128)}, f32[256,256]{1,0:T(8,128)S(1)}) custom-call(bf16[3,80,256]{2,1,0:T(8,128)(2,1)S(1)} %get-tuple-element.21.mine, bf16[3,64,256]{2,1,0:T(8,128)(2,1)S(1)} %collective-permute-done.7.other, f32[1024,4096]{1,0:T(8,128)S(1)} %shard_map.89._.own_sum, f32[256,256]{1,0:T(8,128)S(1)} %get-tuple-element.23.own_plain_ref.own_plain, ...), custom_call_target="tpu_custom_call" | custom-call | tf_op jit(solution)/shard_map/pallas_call | solution.py:445
  34.1 0.0 collective-permute-done.8.refs_1_
  34.1 0.8 %shard_map.94 = bf16[256,256]{1,0:T(8,128)(2,1)} custom-call(bf16[80,256]{1,0:T(8,128)(2,1)S(1)} %shard_map.88.own.payload_ref, f32[256,256]{1,0:T(8,128)S(1)} %get-tuple-element.32.refs_0_, bf16[256,256]{1,0:T(8,128)(2,1)S(1)} %collective-permute-done.8.refs_1_), custom_call_target="tpu_custom_call" | custom-call | tf_op jit(solution)/shard_map/pallas_call | solution.py:480
  (3 shorter events, 0.0 us)
Async XLA Ops:
  0.6 18.4 %copy-start = (bf16[1024,256]{1,0:T(8,128)(2,1)S(1)}, bf16[1024,256]{1,0:T(8,128)(2,1)}, u32[]{:S(2)}) copy-start(bf16[1024,256]{1,0:T(8,128)(2,1)} %query.1) | copy-start | bytes 1572868
  0.6 18.4 %collective-permute-start.3 = (bf16[1024,256]{1,0:T(8,128)(2,1)}, bf16[1024,256]{1,0:T(8,128)(2,1)S(1)}, u32[]{:S(2)}, u32[]{:S(2)}) collective-permute-start(bf16[1024,256]{1,0:T(8,128)(2,1)} %query.1), channel_id=1, source_target_pairs={{0,4},{4,0},{8,12},{12,8},{1,5},{5,1},{9,13},{13,9},{2,6},{6,2},{1... | collective-permute-start | bytes 1572872 | tf_op jit(solution)/shard_map/ppermute | solution.py:488
  6.4 1.3 %collective-permute-start = (f32[64,256]{1,0:T(8,128)S(1)}, f32[64,256]{1,0:T(8,128)S(1)}, u32[]{:S(2)}, u32[]{:S(2)}) collective-permute-start(f32[64,256]{1,0:T(8,128)S(1)} %get-tuple-element.19), channel_id=1, source_target_pairs={{0,1},{1,0},{2,3},{3,2},{4,5},{5,4},{6,7},{7,6},{8,9},{9,8},{10,11... | collective-permute-start | bytes 196616 | tf_op jit(solution)/shard_map/ppermute | solution.py:488
  7.7 4.3 %collective-permute-start.1 = (f32[64,256]{1,0:T(8,128)S(1)}, f32[64,256]{1,0:T(8,128)S(1)}, u32[]{:S(2)}, u32[]{:S(2)}) collective-permute-start(f32[64,256]{1,0:T(8,128)S(1)} %shard_map.87.one_ref), channel_id=1, source_target_pairs={{0,2},{1,3},{2,0},{3,1},{4,6},{5,7},{6,4},{7,5},{8,10},{9,11},{10,... | collective-permute-start | bytes 196616 | tf_op jit(solution)/shard_map/ppermute | solution.py:488
  12.1 4.5 %collective-permute-start.2 = (bf16[80,256]{1,0:T(8,128)(2,1)S(1)}, bf16[80,256]{1,0:T(8,128)(2,1)S(1)}, u32[]{:S(2)}, u32[]{:S(2)}) collective-permute-start(bf16[80,256]{1,0:T(8,128)(2,1)S(1)} %shard_map.88.own.payload_ref), channel_id=1, source_target_pairs={{0,1},{1,0},{2,3},{3,2},{4,5},{5,4},{6,7},{7,6},{8,9},{9,8},{10,11... | collective-permute-start | bytes 122888 | tf_op jit(solution)/shard_map/ppermute | solution.py:488
  12.2 7.4 %collective-permute-start.6 = (bf16[80,256]{1,0:T(8,128)(2,1)S(1)}, bf16[80,256]{1,0:T(8,128)(2,1)S(1)}, u32[]{:S(2)}, u32[]{:S(2)}) collective-permute-start(bf16[80,256]{1,0:T(8,128)(2,1)S(1)} %shard_map.88.own.payload_ref), channel_id=1, source_target_pairs={{0,12},{4,8},{8,4},{12,0},{1,13},{5,9},{9,5},{13,1},{2,14},{6,10},... | collective-permute-start | bytes 122888 | tf_op jit(solution)/shard_map/ppermute | solution.py:488
  14.7 5.9 %collective-permute-start.5 = (bf16[80,256]{1,0:T(8,128)(2,1)S(1)}, bf16[80,256]{1,0:T(8,128)(2,1)S(1)}, u32[]{:S(2)}, u32[]{:S(2)}) collective-permute-start(bf16[80,256]{1,0:T(8,128)(2,1)S(1)} %shard_map.88.own.payload_ref), channel_id=1, source_target_pairs={{0,8},{4,12},{8,0},{12,4},{1,9},{5,13},{9,1},{13,5},{2,10},{6,14},... | collective-permute-start | bytes 122888 | tf_op jit(solution)/shard_map/ppermute | solution.py:488
  14.9 5.7 %collective-permute-start.4 = (bf16[80,256]{1,0:T(8,128)(2,1)S(1)}, bf16[80,256]{1,0:T(8,128)(2,1)S(1)}, u32[]{:S(2)}, u32[]{:S(2)}) collective-permute-start(bf16[80,256]{1,0:T(8,128)(2,1)S(1)} %shard_map.88.own.payload_ref), channel_id=1, source_target_pairs={{0,4},{4,0},{8,12},{12,8},{1,5},{5,1},{9,13},{13,9},{2,6},{6,2},{1... | collective-permute-start | bytes 122888 | tf_op jit(solution)/shard_map/ppermute | solution.py:488
  20.6 1.4 %collective-permute-start.7 = (bf16[3,64,256]{2,1,0:T(8,128)(2,1)S(1)}, bf16[3,64,256]{2,1,0:T(8,128)(2,1)S(1)}, u32[]{:S(2)}, u32[]{:S(2)}) collective-permute-start(bf16[3,64,256]{2,1,0:T(8,128)(2,1)S(1)} %get-tuple-element.22), channel_id=1, source_target_pairs={{0,1},{1,0},{2,3},{3,2},{4,5},{5,4},{6,7},{7,6},{8,9},{9,8},{10,11... | collective-permute-start | bytes 294920 | tf_op jit(solution)/shard_map/ppermute | solution.py:488
  23.7 10.4 %collective-permute-start.8 = (bf16[256,256]{1,0:T(8,128)(2,1)S(1)}, bf16[256,256]{1,0:T(8,128)(2,1)S(1)}, u32[]{:S(2)}, u32[]{:S(2)}) collective-permute-start(bf16[256,256]{1,0:T(8,128)(2,1)S(1)} %get-tuple-element.33), channel_id=1, source_target_pairs={{0,8},{4,12},{8,0},{12,4},{1,9},{5,13},{9,1},{13,5},{2,10},{6,14},... | collective-permute-start | bytes 393224 | tf_op jit(solution)/shard_map/ppermute | solution.py:488

commit v16 on v14

--- a/solution.py
+++ b/solution.py
@@ -110,26 +110,20 @@
 
 
 def project_kernel(act, grad, pin, pout, keep_ref, send_ref, act_v, grad_v, pin_v, pout_v, sems):
-    chunk = act.shape[1]
-    while grad.shape[1] % chunk:
-        chunk //= 2
-    spans = [pl.ds(c, chunk) for c in range(0, grad.shape[1], chunk)]
-    copies = [pltpu.make_async_copy(s, d, sems.at[n]) for n, (s, d) in enumerate(((pin, pin_v), (act, act_v), (pout, pout_v)))]
-    copies += [
-        pltpu.make_async_copy(grad.at[:, span], grad_v.at[:, span], sems.at[3 + n])
-        for n, span in enumerate(spans)
-    ]
-    for copy in copies[:6]:
+    chunk = grad.shape[1] // 2
+    spans = [pl.ds(0, chunk), pl.ds(chunk, chunk)]
+    pairs = [(pin, pin_v), (act, act_v), (pout, pout_v)]
+    pairs += [(grad.at[:, span], grad_v.at[:, span]) for span in spans]
+    copies = [pltpu.make_async_copy(s, d, sems.at[n]) for n, (s, d) in enumerate(pairs)]
+    for copy in copies:
         copy.start()
     copies[0].wait()
     copies[1].wait()
     part_act = lax.dot_general(pin_v[...], act_v[...], NT, preferred_element_type=jnp.float32)
     copies[2].wait()
     part_grad = jnp.zeros_like(part_act)
-    for n, span in enumerate(spans):
-        copies[3 + n].wait()
-        if n + 3 < len(spans):
-            copies[6 + n].start()
+    for copy, span in zip(copies[3:], spans):
+        copy.wait()
         part_grad += lax.dot_general(
             pout_v[:, span], grad_v[:, span], NT, preferred_element_type=jnp.float32
         )
@@ -152,7 +146,7 @@
             pltpu.VMEM((tok, f_here), jnp.bfloat16),
             pltpu.VMEM((rank, d_here), jnp.bfloat16),
             pltpu.VMEM((rank, f_here), jnp.bfloat16),
-            pltpu.SemaphoreType.DMA((3 + f_here // 128,)),
+            pltpu.SemaphoreType.DMA((5,)),
         ],
         compiler_params=params(53.75),
     )(activations, out_grads, proj_in_t, proj_out_t)
@@ -202,7 +196,7 @@
             jax.ShapeDtypeStruct((len(parts), rows, tok), parts[0].dtype),
             jax.ShapeDtypeStruct((len(parts), rank, tok), parts[0].dtype),
         ],
-        compiler_params=params(30),
+        compiler_params=params(26),
     )(*after, *parts)
 
 
@@ -273,7 +267,7 @@
             pltpu.VMEM((1, tok), jnp.float32),
             pltpu.VMEM((2, rows, tok), jnp.bfloat16),
         ],
-        compiler_params=params(30),
+        compiler_params=params(26),
     )(queries, near_queries, own, own_other)
 
 
@@ -333,7 +327,7 @@
             pltpu.VMEM((2, rows, tok * (blocks - 1)), jnp.bfloat16),
             pltpu.VMEM((blocks // 2, tok * blocks, tok), jnp.bfloat16),
         ],
-        compiler_params=params(30),
+        compiler_params=params(26),
     )(own, own_other, mine, other, queries_t, near_queries_t, own_plain)
 
 
@@ -390,12 +384,13 @@
     for step in range(rank // col_count):
         if (step + 1) * col_count < rank:
             build_columns((step + 1) * col_count, act, factors, rights[(step + 1) % 2])
-        for row in range(0, rows, TILE):
+        height = 2 * TILE if step and rows % (2 * TILE) == 0 else TILE
+        for row in range(0, rows, height):
             if step == 0:
-                weigh_rows(row, row + TILE, row_count, factors, weights, weighted)
-            here = pl.ds(row, TILE), pl.ds(step * cols, cols)
+                weigh_rows(row, row + height, row_count, factors, weights, weighted)
+            here = pl.ds(row, height), pl.ds(step * cols, cols)
             tile = lax.dot_general(
-                weighted[row : row + TILE, :],
+                weighted[row : row + height, :],
                 rights[step % 2][...],
                 NT,
                 preferred_element_type=jnp.float32,
@@ -425,7 +420,7 @@
             pltpu.VMEM((rows, feat), jnp.float32),
             pltpu.SemaphoreType.DMA((feat // cols * (rows // TILE),)),
         ],
-        compiler_params=params(30),
+        compiler_params=params(26),
     )(mine, other, own_sum)
 
 

time: 35.4 us -> 34.2 us (0.966)
  Pallas kernels: 17.7 us -> 16.5 us
  starting transfers between devices: 10.9 us -> 10.4 us
  waiting for transfers between devices: 5.13 us -> 5.58 us
    pallas_call x1, Pallas kernels: 4 us -> 2.66 us  [project(): pl.pallas_call(project_kernel, in_specs=[pl.BlockSpec(memory_space=pl.ANY...]
    ppermute x9, waiting for transfers between devices: 5.13 us -> 5.58 us  [swapped(): lax.ppermute(array, axis, [(i, i ^ distance) for i in range(lax.axis_size...]
    ppermute x9, starting transfers between devices: 10.9 us -> 10.4 us  [swapped(): lax.ppermute(array, axis, [(i, i ^ distance) for i in range(lax.axis_size...]
  transfers between devices with their start and end apart: 9 -> 9, of which waited for: 4 -> 4; matrix products, arithmetic and copies ran while one was open for 2% -> 2% of each run, Pallas kernels for 42% -> 40%
where the time goes in v16:
time: 34.2 us; the launch traced here: 34 us
  Pallas kernels  16.5 us (48%)
  starting transfers between devices  10.4 us (30%)
  waiting for transfers between devices  5.58 us (16%)
  between operations  0.75 us (2%)
  other arithmetic  0.74 us (2%)
    ppermute x9, starting transfers between devices, swapped(): lax.ppermute(array, axis, [(i, i ^ distance) for i in range(lax.axis_size...  10.4 us
    pallas_call x1, Pallas kernels, hessian_rows(): pl.pallas_call(functools.partial(hessian_kernel, row_count, col_count), o...  8.06 us
    ppermute x9, waiting for transfers between devices, swapped(): lax.ppermute(array, axis, [(i, i ^ distance) for i in range(lax.axis_size...  5.58 us
    pallas_call x1, Pallas kernels, project(): pl.pallas_call(project_kernel, in_specs=[pl.BlockSpec(memory_space=pl.ANY...  2.66 us
    pallas_call x1, Pallas kernels, own_tokens_sum(): pl.pallas_call(functools.partial(own_kernel, row_count, col_count), out_s...  2.4 us
    pallas_call x1, Pallas kernels, score_shares(): pl.pallas_call(functools.partial(share_kernel, row_count), out_shape=[jax...  2.09 us
    pallas_call x1, Pallas kernels, finish_scores(): pl.pallas_call(finish_kernel, out_shape=jax.ShapeDtypeStruct((tok, count)...  0.77 us
    convert_element_type x1, other arithmetic, few_tokens(): jnp.where(live, credit[:, None], 0).astype(jnp.float32).reshape(1, -1)  0.74 us
  transfers between devices with their start and end apart: 9, of which 4 were waited for; matrix products, arithmetic and copies ran while one was open for 2% of the time, Pallas kernels for 40%

profile of v16, /device:TPU:0, one launch (start us, length us, event | category | flops | bytes accessed | tf_op | source)
XLA Modules:
  0.0 34.0 jit_solution(8927814700132652555)
XLA Ops:
  0.6 0.0 copy-start
  0.6 3.1 %collective-permute-start.3 = (bf16[1024,256]{1,0:T(8,128)(2,1)}, bf16[1024,256]{1,0:T(8,128)(2,1)S(1)}, u32[]{:S(2)}, u32[]{:S(2)}) collective-permute-start(bf16[1024,256]{1,0:T(8,128)(2,1)} %query.1), channel_id=1, source_target_pairs={{0,4},{4,0},{8,12},{12,8},{1,5},{5,1},{9,13},{13,9},{2,6},{6,2},{1... | collective-permute-start | bytes 1572872 | tf_op jit(solution)/shard_map/ppermute | solution.py:446
  3.7 2.7 %shard_map.86 = (f32[64,256]{1,0:T(8,128)S(1)}, f32[64,256]{1,0:T(8,128)S(1)}) custom-call(bf16[256,1024]{1,0:T(8,128)(2,1)} %act.1, bf16[256,3584]{1,0:T(8,128)(2,1)} %grad.1, bf16[64,1024]{1,0:T(8,128)(2,1)} %bitcast.5, bf16[64,3584]{1,0:T(8,128)(2,1)} %bitcast.4), custom_call_target="tpu_custom_call" | custom-call | tf_op jit(solution)/shard_map/pallas_call | solution.py:140
  6.4 0.1 collective-permute-start
  6.5 1.2 %collective-permute-done.other_ref = f32[64,256]{1,0:T(8,128)S(1)} collective-permute-done((f32[64,256]{1,0:T(8,128)S(1)}, f32[64,256]{1,0:T(8,128)S(1)}, u32[]{:S(2)}, u32[]{:S(2)}) %collective-permute-start) | collective-permute-done | bytes 65568 | tf_op jit(solution)/shard_map/ppermute | solution.py:446
  7.7 1.6 %collective-permute-start.1 = (f32[64,256]{1,0:T(8,128)S(1)}, f32[64,256]{1,0:T(8,128)S(1)}, u32[]{:S(2)}, u32[]{:S(2)}) collective-permute-start(f32[64,256]{1,0:T(8,128)S(1)} %shard_map.87.one_ref), channel_id=1, source_target_pairs={{0,2},{1,3},{2,0},{3,1},{4,6},{5,7},{6,4},{7,5},{8,10},{9,11},{10,... | collective-permute-start | bytes 196616 | tf_op jit(solution)/shard_map/ppermute | solution.py:446
  9.3 0.7 %fusion = f32[2,128]{1,0:T(2,128)S(1)} fusion(s32[2]{0:T(128)} %param.13, s32[2]{0:T(128)} %param.12), kind=kLoop, calls=%fused_computation.1 | loop fusion | flops 768 | bytes 1040 | tf_op jit(solution)/shard_map/convert_element_type | solution.py:456
  10.0 2.0 %collective-permute-done.1.other_ref = f32[64,256]{1,0:T(8,128)S(1)} collective-permute-done((f32[64,256]{1,0:T(8,128)S(1)}, f32[64,256]{1,0:T(8,128)S(1)}, u32[]{:S(2)}, u32[]{:S(2)}) %collective-permute-start.1) | collective-permute-done | bytes 65568 | tf_op jit(solution)/shard_map/ppermute | solution.py:446
  12.1 0.1 collective-permute-start.2
  12.2 2.5 %collective-permute-start.4 = (bf16[80,256]{1,0:T(8,128)(2,1)S(1)}, bf16[80,256]{1,0:T(8,128)(2,1)S(1)}, u32[]{:S(2)}, u32[]{:S(2)}) collective-permute-start(bf16[80,256]{1,0:T(8,128)(2,1)S(1)} %shard_map.88.own.payload_ref), channel_id=1, source_target_pairs={{0,12},{4,8},{8,4},{12,0},{1,13},{5,9},{9,5},{13,1},{2,14},{6,10},... | collective-permute-start | bytes 122888 | tf_op jit(solution)/shard_map/ppermute | solution.py:446
  14.7 0.2 collective-permute-start.5
  14.9 1.7 %collective-permute-start.6 = (bf16[80,256]{1,0:T(8,128)(2,1)S(1)}, bf16[80,256]{1,0:T(8,128)(2,1)S(1)}, u32[]{:S(2)}, u32[]{:S(2)}) collective-permute-start(bf16[80,256]{1,0:T(8,128)(2,1)S(1)} %shard_map.88.own.payload_ref), channel_id=1, source_target_pairs={{0,4},{4,0},{8,12},{12,8},{1,5},{5,1},{9,13},{13,9},{2,6},{6,2},{1... | collective-permute-start | bytes 122888 | tf_op jit(solution)/shard_map/ppermute | solution.py:446
  16.6 0.0 collective-permute-done.2.own_other
  16.6 2.4 %shard_map.89._.own_sum = f32[1024,4096]{1,0:T(8,128)S(1)} custom-call(bf16[80,256]{1,0:T(8,128)(2,1)S(1)} %shard_map.88.own.payload_ref, bf16[80,256]{1,0:T(8,128)(2,1)S(1)} %collective-permute-done.2.own_other), custom_call_target="tpu_custom_call" | custom-call | tf_op jit(solution)/shard_map/pallas_call | solution.py:359
  19.0 0.0 collective-permute-done.3.near_query
  19.0 0.0 copy-done
  19.0 0.5 %shard_map.90 = (bf16[256,1024]{1,0:T(8,128)(2,1)S(1)}, bf16[256,1024]{1,0:T(8,128)(2,1)S(1)}, f32[256,256]{1,0:T(8,128)S(1)}) custom-call(bf16[1024,256]{1,0:T(8,128)(2,1)S(1)} %copy-done, bf16[1024,256]{1,0:T(8,128)(2,1)S(1)} %collective-permute-done.3.near_query, bf16[80,256]{1,0:T(8,128)(2,1)S(1)} %shard_map.88.own.payload_ref, ...), custom_call_target="tpu_custom_call" | custom-call | tf_op jit(solution)/shard_map/pallas_call | solution.py:262
  19.5 0.0 collective-permute-done.4.refs_0_
  19.6 1.0 %collective-permute-done.5.refs_1_ = bf16[80,256]{1,0:T(8,128)(2,1)S(1)} collective-permute-done((bf16[80,256]{1,0:T(8,128)(2,1)S(1)}, bf16[80,256]{1,0:T(8,128)(2,1)S(1)}, u32[]{:S(2)}, u32[]{:S(2)}) %collective-permute-start.5) | collective-permute-done | bytes 40992 | tf_op jit(solution)/shard_map/ppermute | solution.py:446
  20.6 0.0 collective-permute-done.6.refs_2_
  20.6 0.1 collective-permute-start.7
  20.7 1.3 %collective-permute-done.7.other = bf16[3,64,256]{2,1,0:T(8,128)(2,1)S(1)} collective-permute-done((bf16[3,64,256]{2,1,0:T(8,128)(2,1)S(1)}, bf16[3,64,256]{2,1,0:T(8,128)(2,1)S(1)}, u32[]{:S(2)}, u32[]{:S(2)}) %collective-permute-start.7) | collective-permute-done | bytes 98336 | tf_op jit(solution)/shard_map/ppermute | solution.py:446
  21.9 2.1 %shard_map.93 = (f32[256,256]{1,0:T(8,128)S(1)}, bf16[256,256]{1,0:T(8,128)(2,1)S(1)}) custom-call(bf16[80,256]{1,0:T(8,128)(2,1)S(1)} %shard_map.88.own.payload_ref, bf16[80,256]{1,0:T(8,128)(2,1)S(1)} %collective-permute-done.2.own_other, bf16[3,80,256]{2,1,0:T(8,128)(2,1)S(1)} %get-tuple-element.14.mine, ...), custom_call_target="tpu_custom_call" | custom-call | tf_op jit(solution)/shard_map/pallas_call | solution.py:318
  24.0 1.1 %collective-permute-start.8 = (bf16[256,256]{1,0:T(8,128)(2,1)S(1)}, bf16[256,256]{1,0:T(8,128)(2,1)S(1)}, u32[]{:S(2)}, u32[]{:S(2)}) collective-permute-start(bf16[256,256]{1,0:T(8,128)(2,1)S(1)} %get-tuple-element.19), channel_id=1, source_target_pairs={{0,8},{4,12},{8,0},{12,4},{1,9},{5,13},{9,1},{13,5},{2,10},{6,14},... | collective-permute-start | bytes 393224 | tf_op jit(solution)/shard_map/ppermute | solution.py:446
  25.2 8.1 %shard_map.92 = f32[1024,4096]{1,0:T(8,128)} custom-call(bf16[3,80,256]{2,1,0:T(8,128)(2,1)S(1)} %get-tuple-element.14.mine, bf16[3,64,256]{2,1,0:T(8,128)(2,1)S(1)} %collective-permute-done.7.other, f32[1024,4096]{1,0:T(8,128)S(1)} %shard_map.89._.own_sum), custom_call_target="tpu_custom_call" | custom-call | tf_op jit(solution)/shard_map/pallas_call | solution.py:410
  33.3 0.0 collective-permute-done.8.refs_1_
  33.3 0.8 %shard_map.94 = bf16[256,256]{1,0:T(8,128)(2,1)} custom-call(bf16[80,256]{1,0:T(8,128)(2,1)S(1)} %shard_map.88.own.payload_ref, f32[256,256]{1,0:T(8,128)S(1)} %get-tuple-element.18.refs_0_, bf16[256,256]{1,0:T(8,128)(2,1)S(1)} %collective-permute-done.8.refs_1_), custom_call_target="tpu_custom_call" | custom-call | tf_op jit(solution)/shard_map/pallas_call | solution.py:438
  (3 shorter events, 0.0 us)
Async XLA Ops:
  0.6 18.4 %copy-start = (bf16[1024,256]{1,0:T(8,128)(2,1)S(1)}, bf16[1024,256]{1,0:T(8,128)(2,1)}, u32[]{:S(2)}) copy-start(bf16[1024,256]{1,0:T(8,128)(2,1)} %query.1) | copy-start | bytes 1572868
  0.6 18.4 %collective-permute-start.3 = (bf16[1024,256]{1,0:T(8,128)(2,1)}, bf16[1024,256]{1,0:T(8,128)(2,1)S(1)}, u32[]{:S(2)}, u32[]{:S(2)}) collective-permute-start(bf16[1024,256]{1,0:T(8,128)(2,1)} %query.1), channel_id=1, source_target_pairs={{0,4},{4,0},{8,12},{12,8},{1,5},{5,1},{9,13},{13,9},{2,6},{6,2},{1... | collective-permute-start | bytes 1572872 | tf_op jit(solution)/shard_map/ppermute | solution.py:446
  6.4 1.3 %collective-permute-start = (f32[64,256]{1,0:T(8,128)S(1)}, f32[64,256]{1,0:T(8,128)S(1)}, u32[]{:S(2)}, u32[]{:S(2)}) collective-permute-start(f32[64,256]{1,0:T(8,128)S(1)} %get-tuple-element.12), channel_id=1, source_target_pairs={{0,1},{1,0},{2,3},{3,2},{4,5},{5,4},{6,7},{7,6},{8,9},{9,8},{10,11... | collective-permute-start | bytes 196616 | tf_op jit(solution)/shard_map/ppermute | solution.py:446
  7.7 4.3 %collective-permute-start.1 = (f32[64,256]{1,0:T(8,128)S(1)}, f32[64,256]{1,0:T(8,128)S(1)}, u32[]{:S(2)}, u32[]{:S(2)}) collective-permute-start(f32[64,256]{1,0:T(8,128)S(1)} %shard_map.87.one_ref), channel_id=1, source_target_pairs={{0,2},{1,3},{2,0},{3,1},{4,6},{5,7},{6,4},{7,5},{8,10},{9,11},{10,... | collective-permute-start | bytes 196616 | tf_op jit(solution)/shard_map/ppermute | solution.py:446
  12.1 4.5 %collective-permute-start.2 = (bf16[80,256]{1,0:T(8,128)(2,1)S(1)}, bf16[80,256]{1,0:T(8,128)(2,1)S(1)}, u32[]{:S(2)}, u32[]{:S(2)}) collective-permute-start(bf16[80,256]{1,0:T(8,128)(2,1)S(1)} %shard_map.88.own.payload_ref), channel_id=1, source_target_pairs={{0,1},{1,0},{2,3},{3,2},{4,5},{5,4},{6,7},{7,6},{8,9},{9,8},{10,11... | collective-permute-start | bytes 122888 | tf_op jit(solution)/shard_map/ppermute | solution.py:446
  12.2 7.4 %collective-permute-start.4 = (bf16[80,256]{1,0:T(8,128)(2,1)S(1)}, bf16[80,256]{1,0:T(8,128)(2,1)S(1)}, u32[]{:S(2)}, u32[]{:S(2)}) collective-permute-start(bf16[80,256]{1,0:T(8,128)(2,1)S(1)} %shard_map.88.own.payload_ref), channel_id=1, source_target_pairs={{0,12},{4,8},{8,4},{12,0},{1,13},{5,9},{9,5},{13,1},{2,14},{6,10},... | collective-permute-start | bytes 122888 | tf_op jit(solution)/shard_map/ppermute | solution.py:446
  14.7 5.9 %collective-permute-start.5 = (bf16[80,256]{1,0:T(8,128)(2,1)S(1)}, bf16[80,256]{1,0:T(8,128)(2,1)S(1)}, u32[]{:S(2)}, u32[]{:S(2)}) collective-permute-start(bf16[80,256]{1,0:T(8,128)(2,1)S(1)} %shard_map.88.own.payload_ref), channel_id=1, source_target_pairs={{0,8},{4,12},{8,0},{12,4},{1,9},{5,13},{9,1},{13,5},{2,10},{6,14},... | collective-permute-start | bytes 122888 | tf_op jit(solution)/shard_map/ppermute | solution.py:446
  14.9 5.7 %collective-permute-start.6 = (bf16[80,256]{1,0:T(8,128)(2,1)S(1)}, bf16[80,256]{1,0:T(8,128)(2,1)S(1)}, u32[]{:S(2)}, u32[]{:S(2)}) collective-permute-start(bf16[80,256]{1,0:T(8,128)(2,1)S(1)} %shard_map.88.own.payload_ref), channel_id=1, source_target_pairs={{0,4},{4,0},{8,12},{12,8},{1,5},{5,1},{9,13},{13,9},{2,6},{6,2},{1... | collective-permute-start | bytes 122888 | tf_op jit(solution)/shard_map/ppermute | solution.py:446
  20.6 1.4 %collective-permute-start.7 = (bf16[3,64,256]{2,1,0:T(8,128)(2,1)S(1)}, bf16[3,64,256]{2,1,0:T(8,128)(2,1)S(1)}, u32[]{:S(2)}, u32[]{:S(2)}) collective-permute-start(bf16[3,64,256]{2,1,0:T(8,128)(2,1)S(1)} %get-tuple-element.15), channel_id=1, source_target_pairs={{0,1},{1,0},{2,3},{3,2},{4,5},{5,4},{6,7},{7,6},{8,9},{9,8},{10,11... | collective-permute-start | bytes 294920 | tf_op jit(solution)/shard_map/ppermute | solution.py:446
  24.0 9.2 %collective-permute-start.8 = (bf16[256,256]{1,0:T(8,128)(2,1)S(1)}, bf16[256,256]{1,0:T(8,128)(2,1)S(1)}, u32[]{:S(2)}, u32[]{:S(2)}) collective-permute-start(bf16[256,256]{1,0:T(8,128)(2,1)S(1)} %get-tuple-element.19), channel_id=1, source_target_pairs={{0,8},{4,12},{8,0},{12,4},{1,9},{5,13},{9,1},{13,5},{2,10},{6,14},... | collective-permute-start | bytes 393224 | tf_op jit(solution)/shard_map/ppermute | solution.py:446

commit v17 on v16

--- a/solution.py
+++ b/solution.py
@@ -127,16 +127,18 @@
         part_grad += lax.dot_general(
             pout_v[:, span], grad_v[:, span], NT, preferred_element_type=jnp.float32
         )
+    factors = jnp.concatenate([part_act, part_grad], axis=0)
+    half = factors.shape[1] // 2
     even = lax.rem(lax.axis_index("query"), 2) == 0
-    keep_ref[...] = jnp.where(even, part_act, part_grad)
-    send_ref[...] = jnp.where(even, part_grad, part_act)
+    keep_ref[...] = jnp.where(even, factors[:, :half], factors[:, half:])
+    send_ref[...] = jnp.where(even, factors[:, half:], factors[:, :half])
 
 
 def project(activations, out_grads, proj_in_t, proj_out_t):
     tok, d_here = activations.shape
     f_here = out_grads.shape[1]
     rank = proj_in_t.shape[0]
-    out = jax.ShapeDtypeStruct((rank, tok), jnp.float32)
+    out = jax.ShapeDtypeStruct((2 * rank, tok // 2), jnp.float32)
     return pl.pallas_call(
         project_kernel,
         in_specs=[pl.BlockSpec(memory_space=pl.ANY)] * 4,
@@ -166,7 +168,10 @@
 
 def payload_kernel(one_ref, other_ref, weight_ref, out_ref):
     total = one_ref[...] + other_ref[...]
-    weight = jnp.broadcast_to(weight_ref[...], (16, weight_ref.shape[1]))
+    half = total.shape[1]
+    even = lax.rem(lax.axis_index("query"), 2) == 0
+    weight = jnp.where(even, weight_ref[:, :half], weight_ref[:, half:])
+    weight = jnp.broadcast_to(weight, (16, half))
     out_ref[...] = jnp.concatenate([total, weight], axis=0).astype(out_ref.dtype)
 
 
@@ -180,39 +185,30 @@
 
 
 def stack_kernel(_, __, *refs):
-    parts, (out_ref, factors_ref) = refs[:-2], refs[-2:]
-    for k, ref in enumerate(parts):
-        out_ref[k] = ref[...]
-        factors_ref[k] = ref[: factors_ref.shape[1]]
-
-
-def stack(parts, rank, after):
-    rows, tok = parts[0].shape
+    for k, ref in enumerate(refs[:-1]):
+        refs[-1][k] = ref[...]
+
+
+def stack(parts, after):
     whole = pl.BlockSpec(memory_space=pltpu.VMEM)
     return pl.pallas_call(
         stack_kernel,
         in_specs=[pl.BlockSpec(memory_space=pl.ANY)] * 2 + [whole] * len(parts),
-        out_shape=[
-            jax.ShapeDtypeStruct((len(parts), rows, tok), parts[0].dtype),
-            jax.ShapeDtypeStruct((len(parts), rank, tok), parts[0].dtype),
-        ],
+        out_shape=jax.ShapeDtypeStruct((len(parts),) + parts[0].shape, parts[0].dtype),
         compiler_params=params(26),
     )(*after, *parts)
 
 
-def lay_out_factors(blocks, factors, weights):
-    rank = factors.shape[0] // 2
-    here = pl.multiple_of(lax.rem(lax.axis_index("query"), 2) * rank, rank)
-    there = pl.multiple_of(rank - here, rank)
-    for k, (mine, other) in enumerate(blocks):
-        span = slice(k * mine.shape[1], (k + 1) * mine.shape[1])
-        factors[pl.ds(here, rank), span] = mine[:rank].astype(jnp.float32)
-        factors[pl.ds(there, rank), span] = other[:rank].astype(jnp.float32)
-        weights[:, span] = mine[rank:].astype(jnp.float32)[:1]
-
-
-def block_pairs(mine, other):
-    return [(mine.at[k], other.at[k]) for k in reversed(range(mine.shape[0]))]
+def lay_out_factors(parts, factors, weights):
+    rows = factors.shape[0]
+    for k, part in enumerate(parts):
+        span = slice(k * part.shape[1], (k + 1) * part.shape[1])
+        factors[:, span] = part[:rows].astype(jnp.float32)
+        weights[:, span] = part[rows:].astype(jnp.float32)[:1]
+
+
+def parts_of(stacked):
+    return [stacked.at[k] for k in reversed(range(stacked.shape[0]))]
 
 
 def weigh_rows(first_row, end_row, row_count, factors, weights, weighted):
@@ -251,13 +247,13 @@
     out_ref, near_out_ref, plain_ref, factors, weights, features = refs
     out_ref[...] = query[...].T
     near_out_ref[...] = near_query[...].T
-    lay_out_factors([(own, own_other)], factors, weights)
+    lay_out_factors([own, own_other], factors, weights)
     plain_ref[...] = project_queries(row_count, factors, features, (out_ref, near_out_ref))
 
 
 def turn_queries(queries, near_queries, own, own_other, rank, row_count):
     rows, count = queries.shape
-    tok = own.shape[1]
+    tok = 2 * own.shape[1]
     out = jax.ShapeDtypeStruct((count, rows), queries.dtype)
     return pl.pallas_call(
         functools.partial(turn_kernel, row_count),
@@ -271,23 +267,49 @@
     )(queries, near_queries, own, own_other)
 
 
-def share_kernel(
-    row_count, own, own_other, mine, other, query_ref, near_query_ref, own_plain_ref, *refs
-):
+def half_kernel(row_count, mine, query_ref, near_query_ref, plain_ref, factors, weights, features):
+    lay_out_factors(parts_of(mine), factors, weights)
+    plain_ref[...] = project_queries(row_count, factors, features, (query_ref, near_query_ref))
+
+
+def project_half(mine, queries_t, near_queries_t, rank, row_count):
+    count, rows = queries_t.shape
+    tokens = mine.shape[0] * mine.shape[2]
+    return pl.pallas_call(
+        functools.partial(half_kernel, row_count),
+        out_shape=jax.ShapeDtypeStruct((count, tokens), jnp.float32),
+        scratch_shapes=[
+            pltpu.VMEM((2 * rank, tokens), jnp.float32),
+            pltpu.VMEM((1, tokens), jnp.float32),
+            pltpu.VMEM((2, rows, tokens), jnp.bfloat16),
+        ],
+        compiler_params=params(26),
+    )(mine, queries_t, near_queries_t)
+
+
+def share_kernel(row_count, own, own_other, mine, other, query_ref, near_query_ref, *refs):
+    own_plain_ref, half_plain_ref = refs[:2]
+    out_refs = refs[2:-4]
     factors, weights, features, gram = refs[-4:]
-    out_refs = refs[:-4]
-    lay_out_factors([(own, own_other)] + block_pairs(mine, other), factors, weights)
+    half = own.shape[1]
+    blocks = mine.shape[0] + 1
+    lay_out_factors(
+        [own] + parts_of(mine) + [own_other] + parts_of(other), factors, weights
+    )
     rank = factors.shape[0] // 2
     tokens = factors.shape[1]
-    tok = own.shape[1]
     plain = project_queries(
-        row_count, factors.at[:, tok:], features, (query_ref, near_query_ref)
-    )
-    plain = jnp.concatenate([own_plain_ref[...], plain], axis=1)
-    act = factors[:rank, :]
+        row_count,
+        factors.at[:, (blocks + 1) * half :],
+        features,
+        (query_ref, near_query_ref),
+    )
+    plain = jnp.concatenate(
+        [own_plain_ref[:, :half], half_plain_ref[...], own_plain_ref[:, half:], plain], axis=1
+    )
     weight = weights[...]
     live = weight > 0.0
-    act = jnp.where(live, act, 0.0)
+    act = jnp.where(live, factors[:rank, :], 0.0)
     grad = jnp.where(live, factors[rank:, :], 0.0)
     act_scale, grad_scale = range_scale(act), range_scale(grad)
     act, grad = act * act_scale, grad * grad_scale
@@ -298,37 +320,41 @@
     act_rows, grad_rows = act.T.astype(jnp.bfloat16), grad.T.astype(jnp.bfloat16)
     weighted = (plain * (weight * (1.0 / (tokens * step)))).astype(jnp.bfloat16)
     scale = act_scale * grad_scale
+
+    def block_of(array, k):
+        starts = (k * half, (blocks + k) * half)
+        return jnp.concatenate([array[:, i : i + half] for i in starts], axis=1)
+
     for n, out_ref in enumerate(out_refs):
-        block = slice(2 * n * tok, (2 * n + 1) * tok)
+        act_block, grad_block = block_of(act_b, 2 * n), block_of(grad_b, 2 * n)
         for row in range(0, tokens, TILE // 2):
             here = slice(row, row + TILE // 2)
-            tile = jnp.dot(act_rows[here], act_b[:, block], preferred_element_type=jnp.float32)
-            tile *= jnp.dot(grad_rows[here], grad_b[:, block], preferred_element_type=jnp.float32)
+            tile = jnp.dot(act_rows[here], act_block, preferred_element_type=jnp.float32)
+            tile *= jnp.dot(grad_rows[here], grad_block, preferred_element_type=jnp.float32)
             gram[n, here, :] = tile.astype(jnp.bfloat16)
         image = jnp.dot(weighted, gram[n], preferred_element_type=jnp.float32)
-        share = ((2.0 - 0.1 / 1.1) * plain[:, block] - image) * scale * (scale / step)
+        share = ((2.0 - 0.1 / 1.1) * block_of(plain, 2 * n) - image) * scale * (scale / step)
         out_ref[...] = share.astype(out_ref.dtype)
 
 
-def score_shares(
-    own, own_other, mine, other, queries_t, near_queries_t, own_plain, rank, row_count
-):
-    blocks, tok = mine.shape[0] + 1, mine.shape[2]
+def score_shares(own, own_other, mine, other, queries_t, near_queries_t, plains, rank, row_count):
+    blocks, half = mine.shape[0] + 1, mine.shape[2]
     count, rows = queries_t.shape
+    tokens = 2 * half * blocks
     return pl.pallas_call(
         functools.partial(share_kernel, row_count),
         out_shape=[
-            jax.ShapeDtypeStruct((count, tok), jnp.bfloat16 if k else jnp.float32)
+            jax.ShapeDtypeStruct((count, 2 * half), jnp.bfloat16 if k else jnp.float32)
             for k in range(0, blocks, 2)
         ],
         scratch_shapes=[
-            pltpu.VMEM((2 * rank, tok * blocks), jnp.float32),
-            pltpu.VMEM((1, tok * blocks), jnp.float32),
-            pltpu.VMEM((2, rows, tok * (blocks - 1)), jnp.bfloat16),
-            pltpu.VMEM((blocks // 2, tok * blocks, tok), jnp.bfloat16),
+            pltpu.VMEM((2 * rank, tokens), jnp.float32),
+            pltpu.VMEM((1, tokens), jnp.float32),
+            pltpu.VMEM((2, rows, (blocks - 1) * half), jnp.bfloat16),
+            pltpu.VMEM((blocks // 2, tokens, 2 * half), jnp.bfloat16),
         ],
         compiler_params=params(26),
-    )(own, own_other, mine, other, queries_t, near_queries_t, own_plain)
+    )(own, own_other, mine, other, queries_t, near_queries_t, *plains)
 
 
 def build_columns(first, act, factors, right):
@@ -341,7 +367,7 @@
 def own_kernel(row_count, col_count, own, own_other, out, factors, weights, weighted, *rights):
     rank = factors.shape[0] // 2
     cols = col_count * rank
-    lay_out_factors([(own, own_other)], factors, weights)
+    lay_out_factors([own, own_other], factors, weights)
     weigh_rows(0, weighted.shape[0], row_count, factors, weights, weighted)
     act = factors[:rank, :]
     build_columns(0, act, factors, rights[0])
@@ -354,7 +380,7 @@
 
 
 def own_tokens_sum(own, own_other, rank, row_count, col_count=8):
-    tok = own.shape[1]
+    tok = 2 * own.shape[1]
     rows, cols = row_count * rank, col_count * rank
     return pl.pallas_call(
         functools.partial(own_kernel, row_count, col_count),
@@ -377,20 +403,19 @@
     blocks = mine.shape[0]
     tokens = factors.shape[1] // blocks * (blocks + 1)
     rows, cols = row_count * rank, col_count * rank
-    lay_out_factors(block_pairs(mine, other), factors, weights)
+    lay_out_factors(parts_of(mine) + parts_of(other), factors, weights)
     act = factors[:rank, :]
     copies = []
     build_columns(0, act, factors, rights[0])
     for step in range(rank // col_count):
         if (step + 1) * col_count < rank:
             build_columns((step + 1) * col_count, act, factors, rights[(step + 1) % 2])
-        height = 2 * TILE if step and rows % (2 * TILE) == 0 else TILE
-        for row in range(0, rows, height):
+        for row in range(0, rows, TILE):
             if step == 0:
-                weigh_rows(row, row + height, row_count, factors, weights, weighted)
-            here = pl.ds(row, height), pl.ds(step * cols, cols)
+                weigh_rows(row, row + TILE, row_count, factors, weights, weighted)
+            here = pl.ds(row, TILE), pl.ds(step * cols, cols)
             tile = lax.dot_general(
-                weighted[row : row + height, :],
+                weighted[row : row + TILE, :],
                 rights[step % 2][...],
                 NT,
                 preferred_element_type=jnp.float32,
@@ -404,7 +429,8 @@
 
 
 def hessian_rows(mine, other, own_sum, rank, row_count, col_count=8):
-    blocks, _, tok = mine.shape
+    blocks, _, half = mine.shape
+    tok = 2 * half
     feat = rank * rank
     rows, cols = row_count * rank, col_count * rank
     return pl.pallas_call(
@@ -424,22 +450,26 @@
     )(mine, other, own_sum)
 
 
-def finish_kernel(payload_ref, *refs):
+def finish_kernel(own, own_other, *refs):
     shares, out_ref = refs[:-1], refs[-1]
     total = shares[0][...]
     for ref in shares[1:]:
         total = total + ref[...].astype(jnp.float32)
-    weight = payload_ref[...].astype(jnp.float32)[-1:]
-    out_ref[...] = jnp.where(weight > 0.0, total, 0.0).T.astype(out_ref.dtype)
-
-
-def finish_scores(payload, shares):
+    weight = jnp.concatenate([part[...].astype(jnp.float32)[-1:] for part in (own, own_other)], axis=1)
+    scores = jnp.where(weight > 0.0, total, 0.0).T.astype(out_ref.dtype)
+    half = own.shape[1]
+    here = pl.multiple_of(lax.rem(lax.axis_index("query"), 2) * half, half)
+    out_ref[pl.ds(here, half), :] = scores[:half]
+    out_ref[pl.ds(pl.multiple_of(half - here, half), half), :] = scores[half:]
+
+
+def finish_scores(own, own_other, shares):
     count, tok = shares[0].shape
     return pl.pallas_call(
         finish_kernel,
         out_shape=jax.ShapeDtypeStruct((tok, count), jnp.bfloat16),
         compiler_params=params(40),
-    )(payload, *shares)
+    )(own, own_other, *shares)
 
 
 def swapped(array, axis, distance):
@@ -469,14 +499,16 @@
     queries_t, near_queries_t, own_plain = turn_queries(
         queries, near_queries, own, own_other, rank, row_count
     )
-    mine, factors = stack(others, rank, (own_sum, queries_t))
-    other = swapped(factors, "query", 1)
+    mine = stack(others, (own_sum, queries_t))
+    other = swapped(mine, "query", 1)
+    half_plain = project_half(mine, queries_t, near_queries_t, rank, row_count)
+    plains = (own_plain, half_plain)
     shares = score_shares(
-        own, own_other, mine, other, queries_t, near_queries_t, own_plain, rank, row_count
+        own, own_other, mine, other, queries_t, near_queries_t, plains, rank, row_count
     )
     arrived = [swapped(share, "dp", 2 * n) for n, share in enumerate(shares) if n]
     hessian = hessian_rows(mine, other, own_sum, rank, row_count)
-    return hessian, finish_scores(own, [shares[0]] + arrived)
+    return hessian, finish_scores(own, own_other, [shares[0]] + arrived)
 
 
 def power_of_two(count):
@@ -486,7 +518,7 @@
 def per_device(activations, *others):
     rank = others[1].shape[1]
     dp_count, query_count = lax.axis_size("dp"), lax.axis_size("query")
-    pairs = min(dp_count, query_count) > 1 and power_of_two(dp_count) and power_of_two(query_count)
+    pairs = activations.shape[0] % 256 == 0 and min(dp_count, query_count) > 1 and power_of_two(dp_count) and power_of_two(query_count)
     if pairs and activations.shape[0] * dp_count <= rank * rank:
         return few_tokens(activations, *others)
     return many_tokens(activations, *others)

time: 34.2 us -> 34.4 us (level)
  Pallas kernels: 16.5 us -> 17.5 us
  waiting for transfers between devices: 5.58 us -> 4.6 us
    ppermute x9, waiting for transfers between devices: 5.58 us -> 4.6 us  [swapped(): lax.ppermute(array, axis, [(i, i ^ distance) for i in range(lax.axis_size...]
    pallas_call x0 -> x1, Pallas kernels: none -> 0.76 us  [project_half(): pl.pallas_call(functools.partial(half_kernel, row_count), out_shape=jax.S...]
    pallas_call x1, Pallas kernels: 8.06 us -> 8.44 us  [hessian_rows(): pl.pallas_call(functools.partial(hessian_kernel, row_count, col_count), o...]
  transfers between devices with their start and end apart: 9 -> 9, of which waited for: 4 -> 4; matrix products, arithmetic and copies ran while one was open for 2% -> 2% of each run, Pallas kernels for 40% -> 43%
where the time goes in v17:
time: 34.4 us; the launch traced here: 34.2 us
  Pallas kernels  17.5 us (51%)
  starting transfers between devices  10.6 us (31%)
  waiting for transfers between devices  4.6 us (13%)
  between operations  0.75 us (2%)
  other arithmetic  0.74 us (2%)
    ppermute x9, starting transfers between devices, swapped(): lax.ppermute(array, axis, [(i, i ^ distance) for i in range(lax.axis_size...  10.6 us
    pallas_call x1, Pallas kernels, hessian_rows(): pl.pallas_call(functools.partial(hessian_kernel, row_count, col_count), o...  8.44 us
    ppermute x9, waiting for transfers between devices, swapped(): lax.ppermute(array, axis, [(i, i ^ distance) for i in range(lax.axis_size...  4.6 us
    pallas_call x1, Pallas kernels, project(): pl.pallas_call(project_kernel, in_specs=[pl.BlockSpec(memory_space=pl.ANY...  2.66 us
    pallas_call x1, Pallas kernels, own_tokens_sum(): pl.pallas_call(functools.partial(own_kernel, row_count, col_count), out_s...  2.4 us
    pallas_call x1, Pallas kernels, score_shares(): pl.pallas_call(functools.partial(share_kernel, row_count), out_shape=[jax...  1.92 us
    pallas_call x1, Pallas kernels, finish_scores(): pl.pallas_call(finish_kernel, out_shape=jax.ShapeDtypeStruct((tok, count)...  0.77 us
    pallas_call x1, Pallas kernels, project_half(): pl.pallas_call(functools.partial(half_kernel, row_count), out_shape=jax.S...  0.76 us
  transfers between devices with their start and end apart: 9, of which 4 were waited for; matrix products, arithmetic and copies ran while one was open for 2% of the time, Pallas kernels for 43%

profile of v17, /device:TPU:0, one launch (start us, length us, event | category | flops | bytes accessed | tf_op | source)
XLA Modules:
  0.0 34.2 jit_solution(17361511203605994472)
XLA Ops:
  0.6 0.0 copy-start
  0.6 3.1 %collective-permute-start.3 = (bf16[1024,256]{1,0:T(8,128)(2,1)}, bf16[1024,256]{1,0:T(8,128)(2,1)S(1)}, u32[]{:S(2)}, u32[]{:S(2)}) collective-permute-start(bf16[1024,256]{1,0:T(8,128)(2,1)} %query.1), channel_id=1, source_target_pairs={{0,4},{4,0},{8,12},{12,8},{1,5},{5,1},{9,13},{13,9},{2,6},{6,2},{1... | collective-permute-start | bytes 1572872 | tf_op jit(solution)/shard_map/ppermute | solution.py:476
  3.7 2.7 %shard_map.86 = (f32[128,128]{1,0:T(8,128)S(1)}, f32[128,128]{1,0:T(8,128)S(1)}) custom-call(bf16[256,1024]{1,0:T(8,128)(2,1)} %act.1, bf16[256,3584]{1,0:T(8,128)(2,1)} %grad.1, bf16[64,1024]{1,0:T(8,128)(2,1)} %bitcast.5, bf16[64,3584]{1,0:T(8,128)(2,1)} %bitcast.4), custom_call_target="tpu_custom_call" | custom-call | tf_op jit(solution)/shard_map/pallas_call | solution.py:142
  6.4 0.1 collective-permute-start
  6.5 1.2 %collective-permute-done.other_ref = f32[128,128]{1,0:T(8,128)S(1)} collective-permute-done((f32[128,128]{1,0:T(8,128)S(1)}, f32[128,128]{1,0:T(8,128)S(1)}, u32[]{:S(2)}, u32[]{:S(2)}) %collective-permute-start) | collective-permute-done | bytes 65568 | tf_op jit(solution)/shard_map/ppermute | solution.py:476
  7.7 1.6 %collective-permute-start.1 = (f32[128,128]{1,0:T(8,128)S(1)}, f32[128,128]{1,0:T(8,128)S(1)}, u32[]{:S(2)}, u32[]{:S(2)}) collective-permute-start(f32[128,128]{1,0:T(8,128)S(1)} %shard_map.87.one_ref), channel_id=1, source_target_pairs={{0,2},{1,3},{2,0},{3,1},{4,6},{5,7},{6,4},{7,5},{8,10},{9,11},{10,... | collective-permute-start | bytes 196616 | tf_op jit(solution)/shard_map/ppermute | solution.py:476
  9.3 0.7 %fusion = f32[2,128]{1,0:T(2,128)S(1)} fusion(s32[2]{0:T(128)} %param.13, s32[2]{0:T(128)} %param.12), kind=kLoop, calls=%fused_computation.1 | loop fusion | flops 768 | bytes 1040 | tf_op jit(solution)/shard_map/convert_element_type | solution.py:486
  10.0 2.0 %collective-permute-done.1.other_ref = f32[128,128]{1,0:T(8,128)S(1)} collective-permute-done((f32[128,128]{1,0:T(8,128)S(1)}, f32[128,128]{1,0:T(8,128)S(1)}, u32[]{:S(2)}, u32[]{:S(2)}) %collective-permute-start.1) | collective-permute-done | bytes 65568 | tf_op jit(solution)/shard_map/ppermute | solution.py:476
  12.1 0.1 collective-permute-start.2
  12.2 2.5 %collective-permute-start.4 = (bf16[144,128]{1,0:T(8,128)(2,1)S(1)}, bf16[144,128]{1,0:T(8,128)(2,1)S(1)}, u32[]{:S(2)}, u32[]{:S(2)}) collective-permute-start(bf16[144,128]{1,0:T(8,128)(2,1)S(1)} %shard_map.88.own), channel_id=1, source_target_pairs={{0,12},{4,8},{8,4},{12,0},{1,13},{5,9},{9,5},{13,1},{2,14},{6,10},... | collective-permute-start | bytes 110600 | tf_op jit(solution)/shard_map/ppermute | solution.py:476
  14.7 0.2 collective-permute-start.5
  14.9 1.7 %collective-permute-start.6 = (bf16[144,128]{1,0:T(8,128)(2,1)S(1)}, bf16[144,128]{1,0:T(8,128)(2,1)S(1)}, u32[]{:S(2)}, u32[]{:S(2)}) collective-permute-start(bf16[144,128]{1,0:T(8,128)(2,1)S(1)} %shard_map.88.own), channel_id=1, source_target_pairs={{0,4},{4,0},{8,12},{12,8},{1,5},{5,1},{9,13},{13,9},{2,6},{6,2},{1... | collective-permute-start | bytes 110600 | tf_op jit(solution)/shard_map/ppermute | solution.py:476
  16.6 0.0 collective-permute-done.2.own_other
  16.6 2.4 %shard_map.89._.own_sum = f32[1024,4096]{1,0:T(8,128)S(1)} custom-call(bf16[144,128]{1,0:T(8,128)(2,1)S(1)} %shard_map.88.own, bf16[144,128]{1,0:T(8,128)(2,1)S(1)} %collective-permute-done.2.own_other), custom_call_target="tpu_custom_call" | custom-call | tf_op jit(solution)/shard_map/pallas_call | solution.py:385
  19.0 0.0 collective-permute-done.3.near_query
  19.0 0.0 copy-done
  19.0 0.5 %shard_map.90 = (bf16[256,1024]{1,0:T(8,128)(2,1)S(1)}, bf16[256,1024]{1,0:T(8,128)(2,1)S(1)}, f32[256,256]{1,0:T(8,128)S(1)}) custom-call(bf16[1024,256]{1,0:T(8,128)(2,1)S(1)} %copy-done, bf16[1024,256]{1,0:T(8,128)(2,1)S(1)} %collective-permute-done.3.near_query, bf16[144,128]{1,0:T(8,128)(2,1)S(1)} %shard_map.88.own, ...), custom_call_target="tpu_custom_call" | custom-call | tf_op jit(solution)/shard_map/pallas_call | solution.py:258
  19.6 0.0 collective-permute-done.4.refs_0_
  19.6 0.8 %collective-permute-done.5.refs_1_ = bf16[144,128]{1,0:T(8,128)(2,1)S(1)} collective-permute-done((bf16[144,128]{1,0:T(8,128)(2,1)S(1)}, bf16[144,128]{1,0:T(8,128)(2,1)S(1)}, u32[]{:S(2)}, u32[]{:S(2)}) %collective-permute-start.5) | collective-permute-done | bytes 36896 | tf_op jit(solution)/shard_map/ppermute | solution.py:476
  20.3 0.0 collective-permute-done.6.refs_2_
  20.4 0.1 collective-permute-start.7
  20.4 0.8 %shard_map.93.refs_1_ = f32[256,384]{1,0:T(8,128)S(1)} custom-call(bf16[3,144,128]{2,1,0:T(8,128)(2,1)S(1)} %shard_map.91.mine, bf16[256,1024]{1,0:T(8,128)(2,1)S(1)} %get-tuple-element.11.__.query_ref, bf16[256,1024]{1,0:T(8,128)(2,1)S(1)} %get-tuple-element.12.near_query_ref), custom_call_target="tpu_custom_call" | custom-call | tf_op jit(solution)/shard_map/pallas_call | solution.py:278
  21.2 0.5 %collective-permute-done.7.other = bf16[3,144,128]{2,1,0:T(8,128)(2,1)S(1)} collective-permute-done((bf16[3,144,128]{2,1,0:T(8,128)(2,1)S(1)}, bf16[3,144,128]{2,1,0:T(8,128)(2,1)S(1)}, u32[]{:S(2)}, u32[]{:S(2)}) %collective-permute-start.7) | collective-permute-done | bytes 110624 | tf_op jit(solution)/shard_map/ppermute | solution.py:476
  21.7 1.9 %shard_map.94 = (f32[256,256]{1,0:T(8,128)S(1)}, bf16[256,256]{1,0:T(8,128)(2,1)S(1)}) custom-call(bf16[144,128]{1,0:T(8,128)(2,1)S(1)} %shard_map.88.own, bf16[144,128]{1,0:T(8,128)(2,1)S(1)} %collective-permute-done.2.own_other, bf16[3,144,128]{2,1,0:T(8,128)(2,1)S(1)} %shard_map.91.mine, bf16[3,144,128]{2,1,0:T(8,128)(2,1)S(1)} %collective-permute-done.7.other, ...), custom_call_target="tpu_custom_call" | custom-call | tf_op jit(solution)/shard_map/pallas_call | solution.py:344
  23.7 1.3 %collective-permute-start.8 = (bf16[256,256]{1,0:T(8,128)(2,1)S(1)}, bf16[256,256]{1,0:T(8,128)(2,1)S(1)}, u32[]{:S(2)}, u32[]{:S(2)}) collective-permute-start(bf16[256,256]{1,0:T(8,128)(2,1)S(1)} %get-tuple-element.15), channel_id=1, source_target_pairs={{0,8},{4,12},{8,0},{12,4},{1,9},{5,13},{9,1},{13,5},{2,10},{6,14},... | collective-permute-start | bytes 393224 | tf_op jit(solution)/shard_map/ppermute | solution.py:476
  25.0 8.4 %shard_map.92 = f32[1024,4096]{1,0:T(8,128)} custom-call(bf16[3,144,128]{2,1,0:T(8,128)(2,1)S(1)} %shard_map.91.mine, bf16[3,144,128]{2,1,0:T(8,128)(2,1)S(1)} %collective-permute-done.7.other, f32[1024,4096]{1,0:T(8,128)S(1)} %shard_map.89._.own_sum), custom_call_target="tpu_custom_call" | custom-call | tf_op jit(solution)/shard_map/pallas_call | solution.py:436
  33.4 0.0 collective-permute-done.8.refs_1_
  33.4 0.8 %shard_map.95 = bf16[256,256]{1,0:T(8,128)(2,1)} custom-call(bf16[144,128]{1,0:T(8,128)(2,1)S(1)} %shard_map.88.own, bf16[144,128]{1,0:T(8,128)(2,1)S(1)} %collective-permute-done.2.own_other, f32[256,256]{1,0:T(8,128)S(1)} %get-tuple-element.14.refs_0_, bf16[256,256]{1,0:T(8,128)(2,1)S(1)} %collective-permute-done.8.refs_1_), custom_call_target="tpu_custom_call" | custom-call | tf_op jit(solution)/shard_map/pallas_call | solution.py:468
  (3 shorter events, 0.0 us)
Async XLA Ops:
  0.6 18.4 %copy-start = (bf16[1024,256]{1,0:T(8,128)(2,1)S(1)}, bf16[1024,256]{1,0:T(8,128)(2,1)}, u32[]{:S(2)}) copy-start(bf16[1024,256]{1,0:T(8,128)(2,1)} %query.1) | copy-start | bytes 1572868
  0.6 18.4 %collective-permute-start.3 = (bf16[1024,256]{1,0:T(8,128)(2,1)}, bf16[1024,256]{1,0:T(8,128)(2,1)S(1)}, u32[]{:S(2)}, u32[]{:S(2)}) collective-permute-start(bf16[1024,256]{1,0:T(8,128)(2,1)} %query.1), channel_id=1, source_target_pairs={{0,4},{4,0},{8,12},{12,8},{1,5},{5,1},{9,13},{13,9},{2,6},{6,2},{1... | collective-permute-start | bytes 1572872 | tf_op jit(solution)/shard_map/ppermute | solution.py:476
  6.4 1.3 %collective-permute-start = (f32[128,128]{1,0:T(8,128)S(1)}, f32[128,128]{1,0:T(8,128)S(1)}, u32[]{:S(2)}, u32[]{:S(2)}) collective-permute-start(f32[128,128]{1,0:T(8,128)S(1)} %get-tuple-element.10), channel_id=1, source_target_pairs={{0,1},{1,0},{2,3},{3,2},{4,5},{5,4},{6,7},{7,6},{8,9},{9,8},{10,11... | collective-permute-start | bytes 196616 | tf_op jit(solution)/shard_map/ppermute | solution.py:476
  7.7 4.3 %collective-permute-start.1 = (f32[128,128]{1,0:T(8,128)S(1)}, f32[128,128]{1,0:T(8,128)S(1)}, u32[]{:S(2)}, u32[]{:S(2)}) collective-permute-start(f32[128,128]{1,0:T(8,128)S(1)} %shard_map.87.one_ref), channel_id=1, source_target_pairs={{0,2},{1,3},{2,0},{3,1},{4,6},{5,7},{6,4},{7,5},{8,10},{9,11},{10,... | collective-permute-start | bytes 196616 | tf_op jit(solution)/shard_map/ppermute | solution.py:476
  12.1 4.5 %collective-permute-start.2 = (bf16[144,128]{1,0:T(8,128)(2,1)S(1)}, bf16[144,128]{1,0:T(8,128)(2,1)S(1)}, u32[]{:S(2)}, u32[]{:S(2)}) collective-permute-start(bf16[144,128]{1,0:T(8,128)(2,1)S(1)} %shard_map.88.own), channel_id=1, source_target_pairs={{0,1},{1,0},{2,3},{3,2},{4,5},{5,4},{6,7},{7,6},{8,9},{9,8},{10,11... | collective-permute-start | bytes 110600 | tf_op jit(solution)/shard_map/ppermute | solution.py:476
  12.2 7.4 %collective-permute-start.4 = (bf16[144,128]{1,0:T(8,128)(2,1)S(1)}, bf16[144,128]{1,0:T(8,128)(2,1)S(1)}, u32[]{:S(2)}, u32[]{:S(2)}) collective-permute-start(bf16[144,128]{1,0:T(8,128)(2,1)S(1)} %shard_map.88.own), channel_id=1, source_target_pairs={{0,12},{4,8},{8,4},{12,0},{1,13},{5,9},{9,5},{13,1},{2,14},{6,10},... | collective-permute-start | bytes 110600 | tf_op jit(solution)/shard_map/ppermute | solution.py:476
  14.7 5.6 %collective-permute-start.5 = (bf16[144,128]{1,0:T(8,128)(2,1)S(1)}, bf16[144,128]{1,0:T(8,128)(2,1)S(1)}, u32[]{:S(2)}, u32[]{:S(2)}) collective-permute-start(bf16[144,128]{1,0:T(8,128)(2,1)S(1)} %shard_map.88.own), channel_id=1, source_target_pairs={{0,8},{4,12},{8,0},{12,4},{1,9},{5,13},{9,1},{13,5},{2,10},{6,14},... | collective-permute-start | bytes 110600 | tf_op jit(solution)/shard_map/ppermute | solution.py:476
  14.9 5.4 %collective-permute-start.6 = (bf16[144,128]{1,0:T(8,128)(2,1)S(1)}, bf16[144,128]{1,0:T(8,128)(2,1)S(1)}, u32[]{:S(2)}, u32[]{:S(2)}) collective-permute-start(bf16[144,128]{1,0:T(8,128)(2,1)S(1)} %shard_map.88.own), channel_id=1, source_target_pairs={{0,4},{4,0},{8,12},{12,8},{1,5},{5,1},{9,13},{13,9},{2,6},{6,2},{1... | collective-permute-start | bytes 110600 | tf_op jit(solution)/shard_map/ppermute | solution.py:476
  20.4 1.4 %collective-permute-start.7 = (bf16[3,144,128]{2,1,0:T(8,128)(2,1)S(1)}, bf16[3,144,128]{2,1,0:T(8,128)(2,1)S(1)}, u32[]{:S(2)}, u32[]{:S(2)}) collective-permute-start(bf16[3,144,128]{2,1,0:T(8,128)(2,1)S(1)} %shard_map.91.mine), channel_id=1, source_target_pairs={{0,1},{1,0},{2,3},{3,2},{4,5},{5,4},{6,7},{7,6},{8,9},{9,8},{10,11... | collective-permute-start | bytes 331784 | tf_op jit(solution)/shard_map/ppermute | solution.py:476
  23.7 9.8 %collective-permute-start.8 = (bf16[256,256]{1,0:T(8,128)(2,1)S(1)}, bf16[256,256]{1,0:T(8,128)(2,1)S(1)}, u32[]{:S(2)}, u32[]{:S(2)}) collective-permute-start(bf16[256,256]{1,0:T(8,128)(2,1)S(1)} %get-tuple-element.15), channel_id=1, source_target_pairs={{0,8},{4,12},{8,0},{12,4},{1,9},{5,13},{9,1},{13,5},{2,10},{6,14},... | collective-permute-start | bytes 393224 | tf_op jit(solution)/shard_map/ppermute | solution.py:476

commit v18 on v17

--- a/solution.py
+++ b/solution.py
@@ -446,7 +446,7 @@
             pltpu.VMEM((rows, feat), jnp.float32),
             pltpu.SemaphoreType.DMA((feat // cols * (rows // TILE),)),
         ],
-        compiler_params=params(26),
+        compiler_params=params(30),
     )(mine, other, own_sum)
 
 

time: 34.4 us -> 34.4 us (level)
  no operation moved by 1% of the time
where the time goes in v18:
time: 34.4 us; the launch traced here: 34.2 us
  Pallas kernels  17.5 us (51%)
  starting transfers between devices  10.6 us (31%)
  waiting for transfers between devices  4.6 us (13%)
  between operations  0.75 us (2%)
  other arithmetic  0.74 us (2%)
    ppermute x9, starting transfers between devices, swapped(): lax.ppermute(array, axis, [(i, i ^ distance) for i in range(lax.axis_size...  10.6 us
    pallas_call x1, Pallas kernels, hessian_rows(): pl.pallas_call(functools.partial(hessian_kernel, row_count, col_count), o...  8.43 us
    ppermute x9, waiting for transfers between devices, swapped(): lax.ppermute(array, axis, [(i, i ^ distance) for i in range(lax.axis_size...  4.6 us
    pallas_call x1, Pallas kernels, project(): pl.pallas_call(project_kernel, in_specs=[pl.BlockSpec(memory_space=pl.ANY...  2.66 us
    pallas_call x1, Pallas kernels, own_tokens_sum(): pl.pallas_call(functools.partial(own_kernel, row_count, col_count), out_s...  2.4 us
    pallas_call x1, Pallas kernels, score_shares(): pl.pallas_call(functools.partial(share_kernel, row_count), out_shape=[jax...  1.91 us
    pallas_call x1, Pallas kernels, finish_scores(): pl.pallas_call(finish_kernel, out_shape=jax.ShapeDtypeStruct((tok, count)...  0.77 us
    pallas_call x1, Pallas kernels, project_half(): pl.pallas_call(functools.partial(half_kernel, row_count), out_shape=jax.S...  0.76 us
  transfers between devices with their start and end apart: 9, of which 4 were waited for; matrix products, arithmetic and copies ran while one was open for 2% of the time, Pallas kernels for 43%

profile of v18, /device:TPU:0, one launch (start us, length us, event | category | flops | bytes accessed | tf_op | source)
XLA Modules:
  0.0 34.2 jit_solution(16999003535018129960)
XLA Ops:
  0.6 0.0 copy-start
  0.6 3.1 %collective-permute-start.3 = (bf16[1024,256]{1,0:T(8,128)(2,1)}, bf16[1024,256]{1,0:T(8,128)(2,1)S(1)}, u32[]{:S(2)}, u32[]{:S(2)}) collective-permute-start(bf16[1024,256]{1,0:T(8,128)(2,1)} %query.1), channel_id=1, source_target_pairs={{0,4},{4,0},{8,12},{12,8},{1,5},{5,1},{9,13},{13,9},{2,6},{6,2},{1... | collective-permute-start | bytes 1572872 | tf_op jit(solution)/shard_map/ppermute | solution.py:476
  3.7 2.7 %shard_map.86 = (f32[128,128]{1,0:T(8,128)S(1)}, f32[128,128]{1,0:T(8,128)S(1)}) custom-call(bf16[256,1024]{1,0:T(8,128)(2,1)} %act.1, bf16[256,3584]{1,0:T(8,128)(2,1)} %grad.1, bf16[64,1024]{1,0:T(8,128)(2,1)} %bitcast.5, bf16[64,3584]{1,0:T(8,128)(2,1)} %bitcast.4), custom_call_target="tpu_custom_call" | custom-call | tf_op jit(solution)/shard_map/pallas_call | solution.py:142
  6.4 0.1 collective-permute-start
  6.5 1.2 %collective-permute-done.other_ref = f32[128,128]{1,0:T(8,128)S(1)} collective-permute-done((f32[128,128]{1,0:T(8,128)S(1)}, f32[128,128]{1,0:T(8,128)S(1)}, u32[]{:S(2)}, u32[]{:S(2)}) %collective-permute-start) | collective-permute-done | bytes 65568 | tf_op jit(solution)/shard_map/ppermute | solution.py:476
  7.7 1.6 %collective-permute-start.1 = (f32[128,128]{1,0:T(8,128)S(1)}, f32[128,128]{1,0:T(8,128)S(1)}, u32[]{:S(2)}, u32[]{:S(2)}) collective-permute-start(f32[128,128]{1,0:T(8,128)S(1)} %shard_map.87.one_ref), channel_id=1, source_target_pairs={{0,2},{1,3},{2,0},{3,1},{4,6},{5,7},{6,4},{7,5},{8,10},{9,11},{10,... | collective-permute-start | bytes 196616 | tf_op jit(solution)/shard_map/ppermute | solution.py:476
  9.3 0.7 %fusion = f32[2,128]{1,0:T(2,128)S(1)} fusion(s32[2]{0:T(128)} %param.13, s32[2]{0:T(128)} %param.12), kind=kLoop, calls=%fused_computation.1 | loop fusion | flops 768 | bytes 1040 | tf_op jit(solution)/shard_map/convert_element_type | solution.py:486
  10.0 2.0 %collective-permute-done.1.other_ref = f32[128,128]{1,0:T(8,128)S(1)} collective-permute-done((f32[128,128]{1,0:T(8,128)S(1)}, f32[128,128]{1,0:T(8,128)S(1)}, u32[]{:S(2)}, u32[]{:S(2)}) %collective-permute-start.1) | collective-permute-done | bytes 65568 | tf_op jit(solution)/shard_map/ppermute | solution.py:476
  12.1 0.1 collective-permute-start.2
  12.2 2.5 %collective-permute-start.4 = (bf16[144,128]{1,0:T(8,128)(2,1)S(1)}, bf16[144,128]{1,0:T(8,128)(2,1)S(1)}, u32[]{:S(2)}, u32[]{:S(2)}) collective-permute-start(bf16[144,128]{1,0:T(8,128)(2,1)S(1)} %shard_map.88.own), channel_id=1, source_target_pairs={{0,12},{4,8},{8,4},{12,0},{1,13},{5,9},{9,5},{13,1},{2,14},{6,10},... | collective-permute-start | bytes 110600 | tf_op jit(solution)/shard_map/ppermute | solution.py:476
  14.7 0.2 collective-permute-start.5
  14.9 1.7 %collective-permute-start.6 = (bf16[144,128]{1,0:T(8,128)(2,1)S(1)}, bf16[144,128]{1,0:T(8,128)(2,1)S(1)}, u32[]{:S(2)}, u32[]{:S(2)}) collective-permute-start(bf16[144,128]{1,0:T(8,128)(2,1)S(1)} %shard_map.88.own), channel_id=1, source_target_pairs={{0,4},{4,0},{8,12},{12,8},{1,5},{5,1},{9,13},{13,9},{2,6},{6,2},{1... | collective-permute-start | bytes 110600 | tf_op jit(solution)/shard_map/ppermute | solution.py:476
  16.6 0.0 collective-permute-done.2.own_other
  16.6 2.4 %shard_map.89._.own_sum = f32[1024,4096]{1,0:T(8,128)S(1)} custom-call(bf16[144,128]{1,0:T(8,128)(2,1)S(1)} %shard_map.88.own, bf16[144,128]{1,0:T(8,128)(2,1)S(1)} %collective-permute-done.2.own_other), custom_call_target="tpu_custom_call" | custom-call | tf_op jit(solution)/shard_map/pallas_call | solution.py:385
  19.0 0.0 collective-permute-done.3.near_query
  19.0 0.0 copy-done
  19.0 0.5 %shard_map.90 = (bf16[256,1024]{1,0:T(8,128)(2,1)S(1)}, bf16[256,1024]{1,0:T(8,128)(2,1)S(1)}, f32[256,256]{1,0:T(8,128)S(1)}) custom-call(bf16[1024,256]{1,0:T(8,128)(2,1)S(1)} %copy-done, bf16[1024,256]{1,0:T(8,128)(2,1)S(1)} %collective-permute-done.3.near_query, bf16[144,128]{1,0:T(8,128)(2,1)S(1)} %shard_map.88.own, ...), custom_call_target="tpu_custom_call" | custom-call | tf_op jit(solution)/shard_map/pallas_call | solution.py:258
  19.6 0.0 collective-permute-done.4.refs_0_
  19.6 0.8 %collective-permute-done.5.refs_1_ = bf16[144,128]{1,0:T(8,128)(2,1)S(1)} collective-permute-done((bf16[144,128]{1,0:T(8,128)(2,1)S(1)}, bf16[144,128]{1,0:T(8,128)(2,1)S(1)}, u32[]{:S(2)}, u32[]{:S(2)}) %collective-permute-start.5) | collective-permute-done | bytes 36896 | tf_op jit(solution)/shard_map/ppermute | solution.py:476
  20.3 0.0 collective-permute-done.6.refs_2_
  20.4 0.1 collective-permute-start.7
  20.4 0.8 %shard_map.93.refs_1_ = f32[256,384]{1,0:T(8,128)S(1)} custom-call(bf16[3,144,128]{2,1,0:T(8,128)(2,1)S(1)} %shard_map.91.mine, bf16[256,1024]{1,0:T(8,128)(2,1)S(1)} %get-tuple-element.11.__.query_ref, bf16[256,1024]{1,0:T(8,128)(2,1)S(1)} %get-tuple-element.12.near_query_ref), custom_call_target="tpu_custom_call" | custom-call | tf_op jit(solution)/shard_map/pallas_call | solution.py:278
  21.2 0.5 %collective-permute-done.7.other = bf16[3,144,128]{2,1,0:T(8,128)(2,1)S(1)} collective-permute-done((bf16[3,144,128]{2,1,0:T(8,128)(2,1)S(1)}, bf16[3,144,128]{2,1,0:T(8,128)(2,1)S(1)}, u32[]{:S(2)}, u32[]{:S(2)}) %collective-permute-start.7) | collective-permute-done | bytes 110624 | tf_op jit(solution)/shard_map/ppermute | solution.py:476
  21.7 1.9 %shard_map.94 = (f32[256,256]{1,0:T(8,128)S(1)}, bf16[256,256]{1,0:T(8,128)(2,1)S(1)}) custom-call(bf16[144,128]{1,0:T(8,128)(2,1)S(1)} %shard_map.88.own, bf16[144,128]{1,0:T(8,128)(2,1)S(1)} %collective-permute-done.2.own_other, bf16[3,144,128]{2,1,0:T(8,128)(2,1)S(1)} %shard_map.91.mine, bf16[3,144,128]{2,1,0:T(8,128)(2,1)S(1)} %collective-permute-done.7.other, ...), custom_call_target="tpu_custom_call" | custom-call | tf_op jit(solution)/shard_map/pallas_call | solution.py:344
  23.7 1.3 %collective-permute-start.8 = (bf16[256,256]{1,0:T(8,128)(2,1)S(1)}, bf16[256,256]{1,0:T(8,128)(2,1)S(1)}, u32[]{:S(2)}, u32[]{:S(2)}) collective-permute-start(bf16[256,256]{1,0:T(8,128)(2,1)S(1)} %get-tuple-element.15), channel_id=1, source_target_pairs={{0,8},{4,12},{8,0},{12,4},{1,9},{5,13},{9,1},{13,5},{2,10},{6,14},... | collective-permute-start | bytes 393224 | tf_op jit(solution)/shard_map/ppermute | solution.py:476
  25.0 8.4 %shard_map.92 = f32[1024,4096]{1,0:T(8,128)} custom-call(bf16[3,144,128]{2,1,0:T(8,128)(2,1)S(1)} %shard_map.91.mine, bf16[3,144,128]{2,1,0:T(8,128)(2,1)S(1)} %collective-permute-done.7.other, f32[1024,4096]{1,0:T(8,128)S(1)} %shard_map.89._.own_sum), custom_call_target="tpu_custom_call" | custom-call | tf_op jit(solution)/shard_map/pallas_call | solution.py:436
  33.4 0.0 collective-permute-done.8.refs_1_
  33.4 0.8 %shard_map.95 = bf16[256,256]{1,0:T(8,128)(2,1)} custom-call(bf16[144,128]{1,0:T(8,128)(2,1)S(1)} %shard_map.88.own, bf16[144,128]{1,0:T(8,128)(2,1)S(1)} %collective-permute-done.2.own_other, f32[256,256]{1,0:T(8,128)S(1)} %get-tuple-element.14.refs_0_, bf16[256,256]{1,0:T(8,128)(2,1)S(1)} %collective-permute-done.8.refs_1_), custom_call_target="tpu_custom_call" | custom-call | tf_op jit(solution)/shard_map/pallas_call | solution.py:468
  (3 shorter events, 0.0 us)
Async XLA Ops:
  0.6 18.4 %copy-start = (bf16[1024,256]{1,0:T(8,128)(2,1)S(1)}, bf16[1024,256]{1,0:T(8,128)(2,1)}, u32[]{:S(2)}) copy-start(bf16[1024,256]{1,0:T(8,128)(2,1)} %query.1) | copy-start | bytes 1572868
  0.6 18.4 %collective-permute-start.3 = (bf16[1024,256]{1,0:T(8,128)(2,1)}, bf16[1024,256]{1,0:T(8,128)(2,1)S(1)}, u32[]{:S(2)}, u32[]{:S(2)}) collective-permute-start(bf16[1024,256]{1,0:T(8,128)(2,1)} %query.1), channel_id=1, source_target_pairs={{0,4},{4,0},{8,12},{12,8},{1,5},{5,1},{9,13},{13,9},{2,6},{6,2},{1... | collective-permute-start | bytes 1572872 | tf_op jit(solution)/shard_map/ppermute | solution.py:476
  6.4 1.3 %collective-permute-start = (f32[128,128]{1,0:T(8,128)S(1)}, f32[128,128]{1,0:T(8,128)S(1)}, u32[]{:S(2)}, u32[]{:S(2)}) collective-permute-start(f32[128,128]{1,0:T(8,128)S(1)} %get-tuple-element.10), channel_id=1, source_target_pairs={{0,1},{1,0},{2,3},{3,2},{4,5},{5,4},{6,7},{7,6},{8,9},{9,8},{10,11... | collective-permute-start | bytes 196616 | tf_op jit(solution)/shard_map/ppermute | solution.py:476
  7.7 4.3 %collective-permute-start.1 = (f32[128,128]{1,0:T(8,128)S(1)}, f32[128,128]{1,0:T(8,128)S(1)}, u32[]{:S(2)}, u32[]{:S(2)}) collective-permute-start(f32[128,128]{1,0:T(8,128)S(1)} %shard_map.87.one_ref), channel_id=1, source_target_pairs={{0,2},{1,3},{2,0},{3,1},{4,6},{5,7},{6,4},{7,5},{8,10},{9,11},{10,... | collective-permute-start | bytes 196616 | tf_op jit(solution)/shard_map/ppermute | solution.py:476
  12.1 4.5 %collective-permute-start.2 = (bf16[144,128]{1,0:T(8,128)(2,1)S(1)}, bf16[144,128]{1,0:T(8,128)(2,1)S(1)}, u32[]{:S(2)}, u32[]{:S(2)}) collective-permute-start(bf16[144,128]{1,0:T(8,128)(2,1)S(1)} %shard_map.88.own), channel_id=1, source_target_pairs={{0,1},{1,0},{2,3},{3,2},{4,5},{5,4},{6,7},{7,6},{8,9},{9,8},{10,11... | collective-permute-start | bytes 110600 | tf_op jit(solution)/shard_map/ppermute | solution.py:476
  12.2 7.4 %collective-permute-start.4 = (bf16[144,128]{1,0:T(8,128)(2,1)S(1)}, bf16[144,128]{1,0:T(8,128)(2,1)S(1)}, u32[]{:S(2)}, u32[]{:S(2)}) collective-permute-start(bf16[144,128]{1,0:T(8,128)(2,1)S(1)} %shard_map.88.own), channel_id=1, source_target_pairs={{0,12},{4,8},{8,4},{12,0},{1,13},{5,9},{9,5},{13,1},{2,14},{6,10},... | collective-permute-start | bytes 110600 | tf_op jit(solution)/shard_map/ppermute | solution.py:476
  14.7 5.6 %collective-permute-start.5 = (bf16[144,128]{1,0:T(8,128)(2,1)S(1)}, bf16[144,128]{1,0:T(8,128)(2,1)S(1)}, u32[]{:S(2)}, u32[]{:S(2)}) collective-permute-start(bf16[144,128]{1,0:T(8,128)(2,1)S(1)} %shard_map.88.own), channel_id=1, source_target_pairs={{0,8},{4,12},{8,0},{12,4},{1,9},{5,13},{9,1},{13,5},{2,10},{6,14},... | collective-permute-start | bytes 110600 | tf_op jit(solution)/shard_map/ppermute | solution.py:476
  14.9 5.4 %collective-permute-start.6 = (bf16[144,128]{1,0:T(8,128)(2,1)S(1)}, bf16[144,128]{1,0:T(8,128)(2,1)S(1)}, u32[]{:S(2)}, u32[]{:S(2)}) collective-permute-start(bf16[144,128]{1,0:T(8,128)(2,1)S(1)} %shard_map.88.own), channel_id=1, source_target_pairs={{0,4},{4,0},{8,12},{12,8},{1,5},{5,1},{9,13},{13,9},{2,6},{6,2},{1... | collective-permute-start | bytes 110600 | tf_op jit(solution)/shard_map/ppermute | solution.py:476
  20.4 1.4 %collective-permute-start.7 = (bf16[3,144,128]{2,1,0:T(8,128)(2,1)S(1)}, bf16[3,144,128]{2,1,0:T(8,128)(2,1)S(1)}, u32[]{:S(2)}, u32[]{:S(2)}) collective-permute-start(bf16[3,144,128]{2,1,0:T(8,128)(2,1)S(1)} %shard_map.91.mine), channel_id=1, source_target_pairs={{0,1},{1,0},{2,3},{3,2},{4,5},{5,4},{6,7},{7,6},{8,9},{9,8},{10,11... | collective-permute-start | bytes 331784 | tf_op jit(solution)/shard_map/ppermute | solution.py:476
  23.7 9.8 %collective-permute-start.8 = (bf16[256,256]{1,0:T(8,128)(2,1)S(1)}, bf16[256,256]{1,0:T(8,128)(2,1)S(1)}, u32[]{:S(2)}, u32[]{:S(2)}) collective-permute-start(bf16[256,256]{1,0:T(8,128)(2,1)S(1)} %get-tuple-element.15), channel_id=1, source_target_pairs={{0,8},{4,12},{8,0},{12,4},{1,9},{5,13},{9,1},{13,5},{2,10},{6,14},... | collective-permute-start | bytes 393224 | tf_op jit(solution)/shard_map/ppermute | solution.py:476

commit v19 on v16

--- a/solution.py
+++ b/solution.py
@@ -165,7 +165,7 @@
 
 
 def payload_kernel(one_ref, other_ref, weight_ref, out_ref):
-    total = one_ref[...] + other_ref[...]
+    total = jnp.where(weight_ref[...] > 0.0, one_ref[...] + other_ref[...], 0.0)
     weight = jnp.broadcast_to(weight_ref[...], (16, weight_ref.shape[1]))
     out_ref[...] = jnp.concatenate([total, weight], axis=0).astype(out_ref.dtype)
 
@@ -286,26 +286,28 @@
     plain = jnp.concatenate([own_plain_ref[...], plain], axis=1)
     act = factors[:rank, :]
     weight = weights[...]
-    live = weight > 0.0
-    act = jnp.where(live, act, 0.0)
-    grad = jnp.where(live, factors[rank:, :], 0.0)
+    act, grad = factors[:rank, :], factors[rank:, :]
     act_scale, grad_scale = range_scale(act), range_scale(grad)
     act, grad = act * act_scale, grad * grad_scale
     norms = jnp.sum(act * act, axis=0, keepdims=True) * jnp.sum(grad * grad, axis=0, keepdims=True)
     level = jnp.sum(weight * norms, axis=1, keepdims=True) / (tokens * rank * rank)
     step = 1.1 * level
     act_b, grad_b = act.astype(jnp.bfloat16), grad.astype(jnp.bfloat16)
-    act_rows, grad_rows = act.T.astype(jnp.bfloat16), grad.T.astype(jnp.bfloat16)
     weighted = (plain * (weight * (1.0 / (tokens * step)))).astype(jnp.bfloat16)
     scale = act_scale * grad_scale
     for n, out_ref in enumerate(out_refs):
         block = slice(2 * n * tok, (2 * n + 1) * tok)
-        for row in range(0, tokens, TILE // 2):
-            here = slice(row, row + TILE // 2)
-            tile = jnp.dot(act_rows[here], act_b[:, block], preferred_element_type=jnp.float32)
-            tile *= jnp.dot(grad_rows[here], grad_b[:, block], preferred_element_type=jnp.float32)
-            gram[n, here, :] = tile.astype(jnp.bfloat16)
-        image = jnp.dot(weighted, gram[n], preferred_element_type=jnp.float32)
+        act_rows, grad_rows = act_b[:, block].T, grad_b[:, block].T
+        for col in range(0, tokens, TILE):
+            there = slice(col, col + TILE)
+            for row in range(0, tok, TILE // 2):
+                here = slice(row, row + TILE // 2)
+                tile = jnp.dot(act_rows[here], act_b[:, there], preferred_element_type=jnp.float32)
+                tile *= jnp.dot(
+                    grad_rows[here], grad_b[:, there], preferred_element_type=jnp.float32
+                )
+                gram[n, here, there] = tile.astype(jnp.bfloat16)
+        image = lax.dot_general(weighted, gram[n], NT, preferred_element_type=jnp.float32)
         share = ((2.0 - 0.1 / 1.1) * plain[:, block] - image) * scale * (scale / step)
         out_ref[...] = share.astype(out_ref.dtype)
 
@@ -325,7 +327,7 @@
             pltpu.VMEM((2 * rank, tok * blocks), jnp.float32),
             pltpu.VMEM((1, tok * blocks), jnp.float32),
             pltpu.VMEM((2, rows, tok * (blocks - 1)), jnp.bfloat16),
-            pltpu.VMEM((blocks // 2, tok * blocks, tok), jnp.bfloat16),
+            pltpu.VMEM((blocks // 2, tok, tok * blocks), jnp.bfloat16),
         ],
         compiler_params=params(26),
     )(own, own_other, mine, other, queries_t, near_queries_t, own_plain)
@@ -384,13 +386,12 @@
     for step in range(rank // col_count):
         if (step + 1) * col_count < rank:
             build_columns((step + 1) * col_count, act, factors, rights[(step + 1) % 2])
-        height = 2 * TILE if step and rows % (2 * TILE) == 0 else TILE
-        for row in range(0, rows, height):
+        for row in range(0, rows, TILE):
             if step == 0:
-                weigh_rows(row, row + height, row_count, factors, weights, weighted)
-            here = pl.ds(row, height), pl.ds(step * cols, cols)
+                weigh_rows(row, row + TILE, row_count, factors, weights, weighted)
+            here = pl.ds(row, TILE), pl.ds(step * cols, cols)
             tile = lax.dot_general(
-                weighted[row : row + height, :],
+                weighted[row : row + TILE, :],
                 rights[step % 2][...],
                 NT,
                 preferred_element_type=jnp.float32,

time: 34.2 us -> 34.2 us (level)
  no operation moved by 1% of the time
where the time goes in v19:
time: 34.2 us; the launch traced here: 34 us
  Pallas kernels  16.5 us (48%)
  starting transfers between devices  10.4 us (30%)
  waiting for transfers between devices  5.57 us (16%)
  other arithmetic  0.74 us (2%)
  between operations  0.74 us (2%)
    ppermute x9, starting transfers between devices, swapped(): lax.ppermute(array, axis, [(i, i ^ distance) for i in range(lax.axis_size...  10.4 us
    pallas_call x1, Pallas kernels, hessian_rows(): pl.pallas_call(functools.partial(hessian_kernel, row_count, col_count), o...  7.88 us
    ppermute x9, waiting for transfers between devices, swapped(): lax.ppermute(array, axis, [(i, i ^ distance) for i in range(lax.axis_size...  5.57 us
    pallas_call x1, Pallas kernels, project(): pl.pallas_call(project_kernel, in_specs=[pl.BlockSpec(memory_space=pl.ANY...  2.66 us
    pallas_call x1, Pallas kernels, own_tokens_sum(): pl.pallas_call(functools.partial(own_kernel, row_count, col_count), out_s...  2.4 us
    pallas_call x1, Pallas kernels, score_shares(): pl.pallas_call(functools.partial(share_kernel, row_count), out_shape=[jax...  2.23 us
    pallas_call x1, Pallas kernels, finish_scores(): pl.pallas_call(finish_kernel, out_shape=jax.ShapeDtypeStruct((tok, count)...  0.77 us
    convert_element_type x1, other arithmetic, few_tokens(): jnp.where(live, credit[:, None], 0).astype(jnp.float32).reshape(1, -1)  0.74 us
  transfers between devices with their start and end apart: 9, of which 4 were waited for; matrix products, arithmetic and copies ran while one was open for 2% of the time, Pallas kernels for 40%

profile of v19, /device:TPU:0, one launch (start us, length us, event | category | flops | bytes accessed | tf_op | source)
XLA Modules:
  0.0 34.0 jit_solution(1892498782681287880)
XLA Ops:
  0.6 0.0 copy-start
  0.6 3.1 %collective-permute-start.3 = (bf16[1024,256]{1,0:T(8,128)(2,1)}, bf16[1024,256]{1,0:T(8,128)(2,1)S(1)}, u32[]{:S(2)}, u32[]{:S(2)}) collective-permute-start(bf16[1024,256]{1,0:T(8,128)(2,1)} %query.1), channel_id=1, source_target_pairs={{0,4},{4,0},{8,12},{12,8},{1,5},{5,1},{9,13},{13,9},{2,6},{6,2},{1... | collective-permute-start | bytes 1572872 | tf_op jit(solution)/shard_map/ppermute | solution.py:447
  3.7 2.7 %shard_map.86 = (f32[64,256]{1,0:T(8,128)S(1)}, f32[64,256]{1,0:T(8,128)S(1)}) custom-call(bf16[256,1024]{1,0:T(8,128)(2,1)} %act.1, bf16[256,3584]{1,0:T(8,128)(2,1)} %grad.1, bf16[64,1024]{1,0:T(8,128)(2,1)} %bitcast.5, bf16[64,3584]{1,0:T(8,128)(2,1)} %bitcast.4), custom_call_target="tpu_custom_call" | custom-call | tf_op jit(solution)/shard_map/pallas_call | solution.py:140
  6.4 0.1 collective-permute-start
  6.5 1.2 %collective-permute-done.other_ref = f32[64,256]{1,0:T(8,128)S(1)} collective-permute-done((f32[64,256]{1,0:T(8,128)S(1)}, f32[64,256]{1,0:T(8,128)S(1)}, u32[]{:S(2)}, u32[]{:S(2)}) %collective-permute-start) | collective-permute-done | bytes 65568 | tf_op jit(solution)/shard_map/ppermute | solution.py:447
  7.7 1.6 %collective-permute-start.1 = (f32[64,256]{1,0:T(8,128)S(1)}, f32[64,256]{1,0:T(8,128)S(1)}, u32[]{:S(2)}, u32[]{:S(2)}) collective-permute-start(f32[64,256]{1,0:T(8,128)S(1)} %shard_map.87.one_ref), channel_id=1, source_target_pairs={{0,2},{1,3},{2,0},{3,1},{4,6},{5,7},{6,4},{7,5},{8,10},{9,11},{10,... | collective-permute-start | bytes 196616 | tf_op jit(solution)/shard_map/ppermute | solution.py:447
  9.3 0.7 %fusion = f32[2,128]{1,0:T(2,128)S(1)} fusion(s32[2]{0:T(128)} %param.13, s32[2]{0:T(128)} %param.12), kind=kLoop, calls=%fused_computation.1 | loop fusion | flops 768 | bytes 1040 | tf_op jit(solution)/shard_map/convert_element_type | solution.py:457
  10.0 2.0 %collective-permute-done.1.other_ref = f32[64,256]{1,0:T(8,128)S(1)} collective-permute-done((f32[64,256]{1,0:T(8,128)S(1)}, f32[64,256]{1,0:T(8,128)S(1)}, u32[]{:S(2)}, u32[]{:S(2)}) %collective-permute-start.1) | collective-permute-done | bytes 65568 | tf_op jit(solution)/shard_map/ppermute | solution.py:447
  12.1 0.1 collective-permute-start.2
  12.2 2.5 %collective-permute-start.4 = (bf16[80,256]{1,0:T(8,128)(2,1)S(1)}, bf16[80,256]{1,0:T(8,128)(2,1)S(1)}, u32[]{:S(2)}, u32[]{:S(2)}) collective-permute-start(bf16[80,256]{1,0:T(8,128)(2,1)S(1)} %shard_map.88.own.payload_ref), channel_id=1, source_target_pairs={{0,12},{4,8},{8,4},{12,0},{1,13},{5,9},{9,5},{13,1},{2,14},{6,10},... | collective-permute-start | bytes 122888 | tf_op jit(solution)/shard_map/ppermute | solution.py:447
  14.7 0.2 collective-permute-start.5
  14.9 1.7 %collective-permute-start.6 = (bf16[80,256]{1,0:T(8,128)(2,1)S(1)}, bf16[80,256]{1,0:T(8,128)(2,1)S(1)}, u32[]{:S(2)}, u32[]{:S(2)}) collective-permute-start(bf16[80,256]{1,0:T(8,128)(2,1)S(1)} %shard_map.88.own.payload_ref), channel_id=1, source_target_pairs={{0,4},{4,0},{8,12},{12,8},{1,5},{5,1},{9,13},{13,9},{2,6},{6,2},{1... | collective-permute-start | bytes 122888 | tf_op jit(solution)/shard_map/ppermute | solution.py:447
  16.6 0.0 collective-permute-done.2.own_other
  16.6 2.4 %shard_map.89._.own_sum = f32[1024,4096]{1,0:T(8,128)S(1)} custom-call(bf16[80,256]{1,0:T(8,128)(2,1)S(1)} %shard_map.88.own.payload_ref, bf16[80,256]{1,0:T(8,128)(2,1)S(1)} %collective-permute-done.2.own_other), custom_call_target="tpu_custom_call" | custom-call | tf_op jit(solution)/shard_map/pallas_call | solution.py:361
  19.0 0.0 collective-permute-done.3.near_query
  19.0 0.0 copy-done
  19.0 0.5 %shard_map.90 = (bf16[256,1024]{1,0:T(8,128)(2,1)S(1)}, bf16[256,1024]{1,0:T(8,128)(2,1)S(1)}, f32[256,256]{1,0:T(8,128)S(1)}) custom-call(bf16[1024,256]{1,0:T(8,128)(2,1)S(1)} %copy-done, bf16[1024,256]{1,0:T(8,128)(2,1)S(1)} %collective-permute-done.3.near_query, bf16[80,256]{1,0:T(8,128)(2,1)S(1)} %shard_map.88.own.payload_ref, ...), custom_call_target="tpu_custom_call" | custom-call | tf_op jit(solution)/shard_map/pallas_call | solution.py:262
  19.6 0.0 collective-permute-done.4.refs_0_
  19.6 1.0 %collective-permute-done.5.refs_1_ = bf16[80,256]{1,0:T(8,128)(2,1)S(1)} collective-permute-done((bf16[80,256]{1,0:T(8,128)(2,1)S(1)}, bf16[80,256]{1,0:T(8,128)(2,1)S(1)}, u32[]{:S(2)}, u32[]{:S(2)}) %collective-permute-start.5) | collective-permute-done | bytes 40992 | tf_op jit(solution)/shard_map/ppermute | solution.py:447
  20.6 0.0 collective-permute-done.6.refs_2_
  20.6 0.1 collective-permute-start.7
  20.7 1.3 %collective-permute-done.7.other = bf16[3,64,256]{2,1,0:T(8,128)(2,1)S(1)} collective-permute-done((bf16[3,64,256]{2,1,0:T(8,128)(2,1)S(1)}, bf16[3,64,256]{2,1,0:T(8,128)(2,1)S(1)}, u32[]{:S(2)}, u32[]{:S(2)}) %collective-permute-start.7) | collective-permute-done | bytes 98336 | tf_op jit(solution)/shard_map/ppermute | solution.py:447
  21.9 2.2 %shard_map.93 = (f32[256,256]{1,0:T(8,128)S(1)}, bf16[256,256]{1,0:T(8,128)(2,1)S(1)}) custom-call(bf16[80,256]{1,0:T(8,128)(2,1)S(1)} %shard_map.88.own.payload_ref, bf16[80,256]{1,0:T(8,128)(2,1)S(1)} %collective-permute-done.2.own_other, bf16[3,80,256]{2,1,0:T(8,128)(2,1)S(1)} %get-tuple-element.14.mine, ...), custom_call_target="tpu_custom_call" | custom-call | tf_op jit(solution)/shard_map/pallas_call | solution.py:320
  24.2 1.1 %collective-permute-start.8 = (bf16[256,256]{1,0:T(8,128)(2,1)S(1)}, bf16[256,256]{1,0:T(8,128)(2,1)S(1)}, u32[]{:S(2)}, u32[]{:S(2)}) collective-permute-start(bf16[256,256]{1,0:T(8,128)(2,1)S(1)} %get-tuple-element.19), channel_id=1, source_target_pairs={{0,8},{4,12},{8,0},{12,4},{1,9},{5,13},{9,1},{13,5},{2,10},{6,14},... | collective-permute-start | bytes 393224 | tf_op jit(solution)/shard_map/ppermute | solution.py:447
  25.3 7.9 %shard_map.92 = f32[1024,4096]{1,0:T(8,128)} custom-call(bf16[3,80,256]{2,1,0:T(8,128)(2,1)S(1)} %get-tuple-element.14.mine, bf16[3,64,256]{2,1,0:T(8,128)(2,1)S(1)} %collective-permute-done.7.other, f32[1024,4096]{1,0:T(8,128)S(1)} %shard_map.89._.own_sum), custom_call_target="tpu_custom_call" | custom-call | tf_op jit(solution)/shard_map/pallas_call | solution.py:411
  33.2 0.0 collective-permute-done.8.refs_1_
  33.2 0.8 %shard_map.94 = bf16[256,256]{1,0:T(8,128)(2,1)} custom-call(bf16[80,256]{1,0:T(8,128)(2,1)S(1)} %shard_map.88.own.payload_ref, f32[256,256]{1,0:T(8,128)S(1)} %get-tuple-element.18.refs_0_, bf16[256,256]{1,0:T(8,128)(2,1)S(1)} %collective-permute-done.8.refs_1_), custom_call_target="tpu_custom_call" | custom-call | tf_op jit(solution)/shard_map/pallas_call | solution.py:439
  (3 shorter events, 0.0 us)
Async XLA Ops:
  0.6 18.4 %copy-start = (bf16[1024,256]{1,0:T(8,128)(2,1)S(1)}, bf16[1024,256]{1,0:T(8,128)(2,1)}, u32[]{:S(2)}) copy-start(bf16[1024,256]{1,0:T(8,128)(2,1)} %query.1) | copy-start | bytes 1572868
  0.6 18.4 %collective-permute-start.3 = (bf16[1024,256]{1,0:T(8,128)(2,1)}, bf16[1024,256]{1,0:T(8,128)(2,1)S(1)}, u32[]{:S(2)}, u32[]{:S(2)}) collective-permute-start(bf16[1024,256]{1,0:T(8,128)(2,1)} %query.1), channel_id=1, source_target_pairs={{0,4},{4,0},{8,12},{12,8},{1,5},{5,1},{9,13},{13,9},{2,6},{6,2},{1... | collective-permute-start | bytes 1572872 | tf_op jit(solution)/shard_map/ppermute | solution.py:447
  6.4 1.3 %collective-permute-start = (f32[64,256]{1,0:T(8,128)S(1)}, f32[64,256]{1,0:T(8,128)S(1)}, u32[]{:S(2)}, u32[]{:S(2)}) collective-permute-start(f32[64,256]{1,0:T(8,128)S(1)} %get-tuple-element.12), channel_id=1, source_target_pairs={{0,1},{1,0},{2,3},{3,2},{4,5},{5,4},{6,7},{7,6},{8,9},{9,8},{10,11... | collective-permute-start | bytes 196616 | tf_op jit(solution)/shard_map/ppermute | solution.py:447
  7.7 4.3 %collective-permute-start.1 = (f32[64,256]{1,0:T(8,128)S(1)}, f32[64,256]{1,0:T(8,128)S(1)}, u32[]{:S(2)}, u32[]{:S(2)}) collective-permute-start(f32[64,256]{1,0:T(8,128)S(1)} %shard_map.87.one_ref), channel_id=1, source_target_pairs={{0,2},{1,3},{2,0},{3,1},{4,6},{5,7},{6,4},{7,5},{8,10},{9,11},{10,... | collective-permute-start | bytes 196616 | tf_op jit(solution)/shard_map/ppermute | solution.py:447
  12.1 4.5 %collective-permute-start.2 = (bf16[80,256]{1,0:T(8,128)(2,1)S(1)}, bf16[80,256]{1,0:T(8,128)(2,1)S(1)}, u32[]{:S(2)}, u32[]{:S(2)}) collective-permute-start(bf16[80,256]{1,0:T(8,128)(2,1)S(1)} %shard_map.88.own.payload_ref), channel_id=1, source_target_pairs={{0,1},{1,0},{2,3},{3,2},{4,5},{5,4},{6,7},{7,6},{8,9},{9,8},{10,11... | collective-permute-start | bytes 122888 | tf_op jit(solution)/shard_map/ppermute | solution.py:447
  12.2 7.4 %collective-permute-start.4 = (bf16[80,256]{1,0:T(8,128)(2,1)S(1)}, bf16[80,256]{1,0:T(8,128)(2,1)S(1)}, u32[]{:S(2)}, u32[]{:S(2)}) collective-permute-start(bf16[80,256]{1,0:T(8,128)(2,1)S(1)} %shard_map.88.own.payload_ref), channel_id=1, source_target_pairs={{0,12},{4,8},{8,4},{12,0},{1,13},{5,9},{9,5},{13,1},{2,14},{6,10},... | collective-permute-start | bytes 122888 | tf_op jit(solution)/shard_map/ppermute | solution.py:447
  14.7 5.9 %collective-permute-start.5 = (bf16[80,256]{1,0:T(8,128)(2,1)S(1)}, bf16[80,256]{1,0:T(8,128)(2,1)S(1)}, u32[]{:S(2)}, u32[]{:S(2)}) collective-permute-start(bf16[80,256]{1,0:T(8,128)(2,1)S(1)} %shard_map.88.own.payload_ref), channel_id=1, source_target_pairs={{0,8},{4,12},{8,0},{12,4},{1,9},{5,13},{9,1},{13,5},{2,10},{6,14},... | collective-permute-start | bytes 122888 | tf_op jit(solution)/shard_map/ppermute | solution.py:447
  14.9 5.7 %collective-permute-start.6 = (bf16[80,256]{1,0:T(8,128)(2,1)S(1)}, bf16[80,256]{1,0:T(8,128)(2,1)S(1)}, u32[]{:S(2)}, u32[]{:S(2)}) collective-permute-start(bf16[80,256]{1,0:T(8,128)(2,1)S(1)} %shard_map.88.own.payload_ref), channel_id=1, source_target_pairs={{0,4},{4,0},{8,12},{12,8},{1,5},{5,1},{9,13},{13,9},{2,6},{6,2},{1... | collective-permute-start | bytes 122888 | tf_op jit(solution)/shard_map/ppermute | solution.py:447
  20.6 1.4 %collective-permute-start.7 = (bf16[3,64,256]{2,1,0:T(8,128)(2,1)S(1)}, bf16[3,64,256]{2,1,0:T(8,128)(2,1)S(1)}, u32[]{:S(2)}, u32[]{:S(2)}) collective-permute-start(bf16[3,64,256]{2,1,0:T(8,128)(2,1)S(1)} %get-tuple-element.15), channel_id=1, source_target_pairs={{0,1},{1,0},{2,3},{3,2},{4,5},{5,4},{6,7},{7,6},{8,9},{9,8},{10,11... | collective-permute-start | bytes 294920 | tf_op jit(solution)/shard_map/ppermute | solution.py:447
  24.2 9.0 %collective-permute-start.8 = (bf16[256,256]{1,0:T(8,128)(2,1)S(1)}, bf16[256,256]{1,0:T(8,128)(2,1)S(1)}, u32[]{:S(2)}, u32[]{:S(2)}) collective-permute-start(bf16[256,256]{1,0:T(8,128)(2,1)S(1)} %get-tuple-element.19), channel_id=1, source_target_pairs={{0,8},{4,12},{8,0},{12,4},{1,9},{5,13},{9,1},{13,5},{2,10},{6,14},... | collective-permute-start | bytes 393224 | tf_op jit(solution)/shard_map/ppermute | solution.py:447

commit v20 on v16

--- a/solution.py
+++ b/solution.py
@@ -165,7 +165,7 @@
 
 
 def payload_kernel(one_ref, other_ref, weight_ref, out_ref):
-    total = one_ref[...] + other_ref[...]
+    total = jnp.where(weight_ref[...] > 0.0, one_ref[...] + other_ref[...], 0.0)
     weight = jnp.broadcast_to(weight_ref[...], (16, weight_ref.shape[1]))
     out_ref[...] = jnp.concatenate([total, weight], axis=0).astype(out_ref.dtype)
 
@@ -234,61 +234,52 @@
     return scale
 
 
-def project_queries(row_count, factors, features, queries):
+def project_queries(row_count, factors, features, query_ref):
     rank = factors.shape[0] // 2
     act = factors[:rank, :]
-    total = 0.0
-    for near, query_ref in enumerate(queries):
+    for near in range(2):
         first = rank + (lax.axis_index("dp") ^ near) * row_count
         for i in range(row_count):
             row = factors[pl.ds(first + i, 1), :]
-            features[near, i * rank : (i + 1) * rank, :] = (row * act).astype(jnp.bfloat16)
-        total += jnp.dot(query_ref[...], features[near], preferred_element_type=jnp.float32)
-    return total
+            start = (near * row_count + i) * rank
+            features[start : start + rank, :] = (row * act).astype(jnp.bfloat16)
+    return jnp.dot(query_ref[...], features[...], preferred_element_type=jnp.float32)
 
 
 def turn_kernel(row_count, query, near_query, own, own_other, *refs):
-    out_ref, near_out_ref, plain_ref, factors, weights, features = refs
-    out_ref[...] = query[...].T
-    near_out_ref[...] = near_query[...].T
+    out_ref, plain_ref, factors, weights, features = refs
+    rows = query.shape[0]
+    out_ref[:, :rows] = query[...].T
+    out_ref[:, rows:] = near_query[...].T
     lay_out_factors([(own, own_other)], factors, weights)
-    plain_ref[...] = project_queries(row_count, factors, features, (out_ref, near_out_ref))
+    plain_ref[...] = project_queries(row_count, factors, features, out_ref)
 
 
 def turn_queries(queries, near_queries, own, own_other, rank, row_count):
     rows, count = queries.shape
     tok = own.shape[1]
-    out = jax.ShapeDtypeStruct((count, rows), queries.dtype)
+    out = jax.ShapeDtypeStruct((count, 2 * rows), queries.dtype)
     return pl.pallas_call(
         functools.partial(turn_kernel, row_count),
-        out_shape=[out, out, jax.ShapeDtypeStruct((count, tok), jnp.float32)],
+        out_shape=[out, jax.ShapeDtypeStruct((count, tok), jnp.float32)],
         scratch_shapes=[
             pltpu.VMEM((2 * rank, tok), jnp.float32),
             pltpu.VMEM((1, tok), jnp.float32),
-            pltpu.VMEM((2, rows, tok), jnp.bfloat16),
+            pltpu.VMEM((2 * rows, tok), jnp.bfloat16),
         ],
         compiler_params=params(26),
     )(queries, near_queries, own, own_other)
 
 
-def share_kernel(
-    row_count, own, own_other, mine, other, query_ref, near_query_ref, own_plain_ref, *refs
-):
-    factors, weights, features, gram = refs[-4:]
-    out_refs = refs[:-4]
+def share_kernel(row_count, own, own_other, mine, other, query_ref, own_plain_ref, *refs):
+    factors, weights, features, gram, plain, weighted = refs[-6:]
+    out_refs = refs[:-6]
     lay_out_factors([(own, own_other)] + block_pairs(mine, other), factors, weights)
     rank = factors.shape[0] // 2
     tokens = factors.shape[1]
     tok = own.shape[1]
-    plain = project_queries(
-        row_count, factors.at[:, tok:], features, (query_ref, near_query_ref)
-    )
-    plain = jnp.concatenate([own_plain_ref[...], plain], axis=1)
-    act = factors[:rank, :]
     weight = weights[...]
-    live = weight > 0.0
-    act = jnp.where(live, act, 0.0)
-    grad = jnp.where(live, factors[rank:, :], 0.0)
+    act, grad = factors[:rank, :], factors[rank:, :]
     act_scale, grad_scale = range_scale(act), range_scale(grad)
     act, grad = act * act_scale, grad * grad_scale
     norms = jnp.sum(act * act, axis=0, keepdims=True) * jnp.sum(grad * grad, axis=0, keepdims=True)
@@ -296,8 +287,17 @@
     step = 1.1 * level
     act_b, grad_b = act.astype(jnp.bfloat16), grad.astype(jnp.bfloat16)
     act_rows, grad_rows = act.T.astype(jnp.bfloat16), grad.T.astype(jnp.bfloat16)
-    weighted = (plain * (weight * (1.0 / (tokens * step)))).astype(jnp.bfloat16)
     scale = act_scale * grad_scale
+    per_token = weight * (1.0 / (tokens * step))
+    for start in range(0, tokens, tok):
+        here = slice(start, start + tok)
+        if start:
+            plain[:, here] = project_queries(
+                row_count, factors.at[:, here], features.at[start // tok - 1], query_ref
+            )
+        else:
+            plain[:, here] = own_plain_ref[...]
+        weighted[:, here] = (plain[:, here] * per_token[:, here]).astype(jnp.bfloat16)
     for n, out_ref in enumerate(out_refs):
         block = slice(2 * n * tok, (2 * n + 1) * tok)
         for row in range(0, tokens, TILE // 2):
@@ -305,16 +305,14 @@
             tile = jnp.dot(act_rows[here], act_b[:, block], preferred_element_type=jnp.float32)
             tile *= jnp.dot(grad_rows[here], grad_b[:, block], preferred_element_type=jnp.float32)
             gram[n, here, :] = tile.astype(jnp.bfloat16)
-        image = jnp.dot(weighted, gram[n], preferred_element_type=jnp.float32)
+        image = jnp.dot(weighted[...], gram[n], preferred_element_type=jnp.float32)
         share = ((2.0 - 0.1 / 1.1) * plain[:, block] - image) * scale * (scale / step)
         out_ref[...] = share.astype(out_ref.dtype)
 
 
-def score_shares(
-    own, own_other, mine, other, queries_t, near_queries_t, own_plain, rank, row_count
-):
+def score_shares(own, own_other, mine, other, queries_t, own_plain, rank, row_count):
     blocks, tok = mine.shape[0] + 1, mine.shape[2]
-    count, rows = queries_t.shape
+    count, depth = queries_t.shape
     return pl.pallas_call(
         functools.partial(share_kernel, row_count),
         out_shape=[
@@ -324,11 +322,13 @@
         scratch_shapes=[
             pltpu.VMEM((2 * rank, tok * blocks), jnp.float32),
             pltpu.VMEM((1, tok * blocks), jnp.float32),
-            pltpu.VMEM((2, rows, tok * (blocks - 1)), jnp.bfloat16),
+            pltpu.VMEM((blocks - 1, depth, tok), jnp.bfloat16),
             pltpu.VMEM((blocks // 2, tok * blocks, tok), jnp.bfloat16),
+            pltpu.VMEM((count, tok * blocks), jnp.float32),
+            pltpu.VMEM((count, tok * blocks), jnp.bfloat16),
         ],
         compiler_params=params(26),
-    )(own, own_other, mine, other, queries_t, near_queries_t, own_plain)
+    )(own, own_other, mine, other, queries_t, own_plain)
 
 
 def build_columns(first, act, factors, right):
@@ -384,13 +384,12 @@
     for step in range(rank // col_count):
         if (step + 1) * col_count < rank:
             build_columns((step + 1) * col_count, act, factors, rights[(step + 1) % 2])
-        height = 2 * TILE if step and rows % (2 * TILE) == 0 else TILE
-        for row in range(0, rows, height):
+        for row in range(0, rows, TILE):
             if step == 0:
-                weigh_rows(row, row + height, row_count, factors, weights, weighted)
-            here = pl.ds(row, height), pl.ds(step * cols, cols)
+                weigh_rows(row, row + TILE, row_count, factors, weights, weighted)
+            here = pl.ds(row, TILE), pl.ds(step * cols, cols)
             tile = lax.dot_general(
-                weighted[row : row + height, :],
+                weighted[row : row + TILE, :],
                 rights[step % 2][...],
                 NT,
                 preferred_element_type=jnp.float32,
@@ -466,14 +465,12 @@
     own_other = swapped(own, "query", 1)
     others = [swapped(own, "dp", k) for k in reversed(range(1, dp_count))]
     own_sum = own_tokens_sum(own, own_other, rank, row_count)
-    queries_t, near_queries_t, own_plain = turn_queries(
+    queries_t, own_plain = turn_queries(
         queries, near_queries, own, own_other, rank, row_count
     )
     mine, factors = stack(others, rank, (own_sum, queries_t))
     other = swapped(factors, "query", 1)
-    shares = score_shares(
-        own, own_other, mine, other, queries_t, near_queries_t, own_plain, rank, row_count
-    )
+    shares = score_shares(own, own_other, mine, other, queries_t, own_plain, rank, row_count)
     arrived = [swapped(share, "dp", 2 * n) for n, share in enumerate(shares) if n]
     hessian = hessian_rows(mine, other, own_sum, rank, row_count)
     return hessian, finish_scores(own, [shares[0]] + arrived)

time: 34.2 us -> 34.1 us (level)
  no operation moved by 1% of the time
where the time goes in v20:
time: 34.1 us; the launch traced here: 33.9 us
  Pallas kernels  16.4 us (48%)
  starting transfers between devices  10.4 us (30%)
  waiting for transfers between devices  5.57 us (16%)
  other arithmetic  0.74 us (2%)
  between operations  0.74 us (2%)
    ppermute x9, starting transfers between devices, swapped(): lax.ppermute(array, axis, [(i, i ^ distance) for i in range(lax.axis_size...  10.4 us
    pallas_call x1, Pallas kernels, hessian_rows(): pl.pallas_call(functools.partial(hessian_kernel, row_count, col_count), o...  7.88 us
    ppermute x9, waiting for transfers between devices, swapped(): lax.ppermute(array, axis, [(i, i ^ distance) for i in range(lax.axis_size...  5.57 us
    pallas_call x1, Pallas kernels, project(): pl.pallas_call(project_kernel, in_specs=[pl.BlockSpec(memory_space=pl.ANY...  2.66 us
    pallas_call x1, Pallas kernels, own_tokens_sum(): pl.pallas_call(functools.partial(own_kernel, row_count, col_count), out_s...  2.4 us
    pallas_call x1, Pallas kernels, score_shares(): pl.pallas_call(functools.partial(share_kernel, row_count), out_shape=[jax...  2.19 us
    pallas_call x1, Pallas kernels, finish_scores(): pl.pallas_call(finish_kernel, out_shape=jax.ShapeDtypeStruct((tok, count)...  0.77 us
    convert_element_type x1, other arithmetic, few_tokens(): jnp.where(live, credit[:, None], 0).astype(jnp.float32).reshape(1, -1)  0.74 us
  transfers between devices with their start and end apart: 9, of which 4 were waited for; matrix products, arithmetic and copies ran while one was open for 2% of the time, Pallas kernels for 40%

profile of v20, /device:TPU:0, one launch (start us, length us, event | category | flops | bytes accessed | tf_op | source)
XLA Modules:
  0.0 33.9 jit_solution(16611209183358187812)
XLA Ops:
  0.6 0.0 copy-start
  0.6 3.1 %collective-permute-start.3 = (bf16[1024,256]{1,0:T(8,128)(2,1)}, bf16[1024,256]{1,0:T(8,128)(2,1)S(1)}, u32[]{:S(2)}, u32[]{:S(2)}) collective-permute-start(bf16[1024,256]{1,0:T(8,128)(2,1)} %query.1), channel_id=1, source_target_pairs={{0,4},{4,0},{8,12},{12,8},{1,5},{5,1},{9,13},{13,9},{2,6},{6,2},{1... | collective-permute-start | bytes 1572872 | tf_op jit(solution)/shard_map/ppermute | solution.py:445
  3.7 2.7 %shard_map.86 = (f32[64,256]{1,0:T(8,128)S(1)}, f32[64,256]{1,0:T(8,128)S(1)}) custom-call(bf16[256,1024]{1,0:T(8,128)(2,1)} %act.1, bf16[256,3584]{1,0:T(8,128)(2,1)} %grad.1, bf16[64,1024]{1,0:T(8,128)(2,1)} %bitcast.5, bf16[64,3584]{1,0:T(8,128)(2,1)} %bitcast.4), custom_call_target="tpu_custom_call" | custom-call | tf_op jit(solution)/shard_map/pallas_call | solution.py:140
  6.4 0.1 collective-permute-start
  6.5 1.2 %collective-permute-done.other_ref = f32[64,256]{1,0:T(8,128)S(1)} collective-permute-done((f32[64,256]{1,0:T(8,128)S(1)}, f32[64,256]{1,0:T(8,128)S(1)}, u32[]{:S(2)}, u32[]{:S(2)}) %collective-permute-start) | collective-permute-done | bytes 65568 | tf_op jit(solution)/shard_map/ppermute | solution.py:445
  7.7 1.6 %collective-permute-start.1 = (f32[64,256]{1,0:T(8,128)S(1)}, f32[64,256]{1,0:T(8,128)S(1)}, u32[]{:S(2)}, u32[]{:S(2)}) collective-permute-start(f32[64,256]{1,0:T(8,128)S(1)} %shard_map.87.one_ref), channel_id=1, source_target_pairs={{0,2},{1,3},{2,0},{3,1},{4,6},{5,7},{6,4},{7,5},{8,10},{9,11},{10,... | collective-permute-start | bytes 196616 | tf_op jit(solution)/shard_map/ppermute | solution.py:445
  9.3 0.7 %fusion = f32[2,128]{1,0:T(2,128)S(1)} fusion(s32[2]{0:T(128)} %param.13, s32[2]{0:T(128)} %param.12), kind=kLoop, calls=%fused_computation.1 | loop fusion | flops 768 | bytes 1040 | tf_op jit(solution)/shard_map/convert_element_type | solution.py:455
  10.0 2.0 %collective-permute-done.1.other_ref = f32[64,256]{1,0:T(8,128)S(1)} collective-permute-done((f32[64,256]{1,0:T(8,128)S(1)}, f32[64,256]{1,0:T(8,128)S(1)}, u32[]{:S(2)}, u32[]{:S(2)}) %collective-permute-start.1) | collective-permute-done | bytes 65568 | tf_op jit(solution)/shard_map/ppermute | solution.py:445
  12.1 0.1 collective-permute-start.2
  12.2 2.5 %collective-permute-start.4 = (bf16[80,256]{1,0:T(8,128)(2,1)S(1)}, bf16[80,256]{1,0:T(8,128)(2,1)S(1)}, u32[]{:S(2)}, u32[]{:S(2)}) collective-permute-start(bf16[80,256]{1,0:T(8,128)(2,1)S(1)} %shard_map.88.own.payload_ref), channel_id=1, source_target_pairs={{0,12},{4,8},{8,4},{12,0},{1,13},{5,9},{9,5},{13,1},{2,14},{6,10},... | collective-permute-start | bytes 122888 | tf_op jit(solution)/shard_map/ppermute | solution.py:445
  14.7 0.2 collective-permute-start.5
  14.9 1.7 %collective-permute-start.6 = (bf16[80,256]{1,0:T(8,128)(2,1)S(1)}, bf16[80,256]{1,0:T(8,128)(2,1)S(1)}, u32[]{:S(2)}, u32[]{:S(2)}) collective-permute-start(bf16[80,256]{1,0:T(8,128)(2,1)S(1)} %shard_map.88.own.payload_ref), channel_id=1, source_target_pairs={{0,4},{4,0},{8,12},{12,8},{1,5},{5,1},{9,13},{13,9},{2,6},{6,2},{1... | collective-permute-start | bytes 122888 | tf_op jit(solution)/shard_map/ppermute | solution.py:445
  16.6 0.0 collective-permute-done.2.own_other
  16.6 2.4 %shard_map.89._.own_sum = f32[1024,4096]{1,0:T(8,128)S(1)} custom-call(bf16[80,256]{1,0:T(8,128)(2,1)S(1)} %shard_map.88.own.payload_ref, bf16[80,256]{1,0:T(8,128)(2,1)S(1)} %collective-permute-done.2.own_other), custom_call_target="tpu_custom_call" | custom-call | tf_op jit(solution)/shard_map/pallas_call | solution.py:359
  19.0 0.0 collective-permute-done.3.near_query
  19.0 0.0 copy-done
  19.0 0.5 %shard_map.90 = (bf16[256,2048]{1,0:T(8,128)(2,1)S(1)}, f32[256,256]{1,0:T(8,128)S(1)}) custom-call(bf16[1024,256]{1,0:T(8,128)(2,1)S(1)} %copy-done, bf16[1024,256]{1,0:T(8,128)(2,1)S(1)} %collective-permute-done.3.near_query, bf16[80,256]{1,0:T(8,128)(2,1)S(1)} %shard_map.88.own.payload_ref, bf16[80,256]{1,0:T(8,128)(2,1)S(1)} %collective-permute-done.2.own_other), custom_call_target="tpu_custom_call" | custom-call | tf_op jit(solution)/shard_map/pallas_call | solution.py:262
  19.6 0.0 collective-permute-done.4.refs_0_
  19.6 1.0 %collective-permute-done.5.refs_1_ = bf16[80,256]{1,0:T(8,128)(2,1)S(1)} collective-permute-done((bf16[80,256]{1,0:T(8,128)(2,1)S(1)}, bf16[80,256]{1,0:T(8,128)(2,1)S(1)}, u32[]{:S(2)}, u32[]{:S(2)}) %collective-permute-start.5) | collective-permute-done | bytes 40992 | tf_op jit(solution)/shard_map/ppermute | solution.py:445
  20.6 0.0 collective-permute-done.6.refs_2_
  20.6 0.1 collective-permute-start.7
  20.7 1.3 %collective-permute-done.7.other = bf16[3,64,256]{2,1,0:T(8,128)(2,1)S(1)} collective-permute-done((bf16[3,64,256]{2,1,0:T(8,128)(2,1)S(1)}, bf16[3,64,256]{2,1,0:T(8,128)(2,1)S(1)}, u32[]{:S(2)}, u32[]{:S(2)}) %collective-permute-start.7) | collective-permute-done | bytes 98336 | tf_op jit(solution)/shard_map/ppermute | solution.py:445
  21.9 2.2 %shard_map.93 = (f32[256,256]{1,0:T(8,128)S(1)}, bf16[256,256]{1,0:T(8,128)(2,1)S(1)}) custom-call(bf16[80,256]{1,0:T(8,128)(2,1)S(1)} %shard_map.88.own.payload_ref, bf16[80,256]{1,0:T(8,128)(2,1)S(1)} %collective-permute-done.2.own_other, bf16[3,80,256]{2,1,0:T(8,128)(2,1)S(1)} %get-tuple-element.13.mine, ...), custom_call_target="tpu_custom_call" | custom-call | tf_op jit(solution)/shard_map/pallas_call | solution.py:316
  24.1 1.1 %collective-permute-start.8 = (bf16[256,256]{1,0:T(8,128)(2,1)S(1)}, bf16[256,256]{1,0:T(8,128)(2,1)S(1)}, u32[]{:S(2)}, u32[]{:S(2)}) collective-permute-start(bf16[256,256]{1,0:T(8,128)(2,1)S(1)} %get-tuple-element.17), channel_id=1, source_target_pairs={{0,8},{4,12},{8,0},{12,4},{1,9},{5,13},{9,1},{13,5},{2,10},{6,14},... | collective-permute-start | bytes 393224 | tf_op jit(solution)/shard_map/ppermute | solution.py:445
  25.3 7.9 %shard_map.92 = f32[1024,4096]{1,0:T(8,128)} custom-call(bf16[3,80,256]{2,1,0:T(8,128)(2,1)S(1)} %get-tuple-element.13.mine, bf16[3,64,256]{2,1,0:T(8,128)(2,1)S(1)} %collective-permute-done.7.other, f32[1024,4096]{1,0:T(8,128)S(1)} %shard_map.89._.own_sum), custom_call_target="tpu_custom_call" | custom-call | tf_op jit(solution)/shard_map/pallas_call | solution.py:409
  33.2 0.0 collective-permute-done.8.refs_1_
  33.2 0.8 %shard_map.94 = bf16[256,256]{1,0:T(8,128)(2,1)} custom-call(bf16[80,256]{1,0:T(8,128)(2,1)S(1)} %shard_map.88.own.payload_ref, f32[256,256]{1,0:T(8,128)S(1)} %get-tuple-element.16.refs_0_, bf16[256,256]{1,0:T(8,128)(2,1)S(1)} %collective-permute-done.8.refs_1_), custom_call_target="tpu_custom_call" | custom-call | tf_op jit(solution)/shard_map/pallas_call | solution.py:437
  (3 shorter events, 0.0 us)
Async XLA Ops:
  0.6 18.4 %copy-start = (bf16[1024,256]{1,0:T(8,128)(2,1)S(1)}, bf16[1024,256]{1,0:T(8,128)(2,1)}, u32[]{:S(2)}) copy-start(bf16[1024,256]{1,0:T(8,128)(2,1)} %query.1) | copy-start | bytes 1572868
  0.6 18.4 %collective-permute-start.3 = (bf16[1024,256]{1,0:T(8,128)(2,1)}, bf16[1024,256]{1,0:T(8,128)(2,1)S(1)}, u32[]{:S(2)}, u32[]{:S(2)}) collective-permute-start(bf16[1024,256]{1,0:T(8,128)(2,1)} %query.1), channel_id=1, source_target_pairs={{0,4},{4,0},{8,12},{12,8},{1,5},{5,1},{9,13},{13,9},{2,6},{6,2},{1... | collective-permute-start | bytes 1572872 | tf_op jit(solution)/shard_map/ppermute | solution.py:445
  6.4 1.3 %collective-permute-start = (f32[64,256]{1,0:T(8,128)S(1)}, f32[64,256]{1,0:T(8,128)S(1)}, u32[]{:S(2)}, u32[]{:S(2)}) collective-permute-start(f32[64,256]{1,0:T(8,128)S(1)} %get-tuple-element.11), channel_id=1, source_target_pairs={{0,1},{1,0},{2,3},{3,2},{4,5},{5,4},{6,7},{7,6},{8,9},{9,8},{10,11... | collective-permute-start | bytes 196616 | tf_op jit(solution)/shard_map/ppermute | solution.py:445
  7.7 4.3 %collective-permute-start.1 = (f32[64,256]{1,0:T(8,128)S(1)}, f32[64,256]{1,0:T(8,128)S(1)}, u32[]{:S(2)}, u32[]{:S(2)}) collective-permute-start(f32[64,256]{1,0:T(8,128)S(1)} %shard_map.87.one_ref), channel_id=1, source_target_pairs={{0,2},{1,3},{2,0},{3,1},{4,6},{5,7},{6,4},{7,5},{8,10},{9,11},{10,... | collective-permute-start | bytes 196616 | tf_op jit(solution)/shard_map/ppermute | solution.py:445
  12.1 4.5 %collective-permute-start.2 = (bf16[80,256]{1,0:T(8,128)(2,1)S(1)}, bf16[80,256]{1,0:T(8,128)(2,1)S(1)}, u32[]{:S(2)}, u32[]{:S(2)}) collective-permute-start(bf16[80,256]{1,0:T(8,128)(2,1)S(1)} %shard_map.88.own.payload_ref), channel_id=1, source_target_pairs={{0,1},{1,0},{2,3},{3,2},{4,5},{5,4},{6,7},{7,6},{8,9},{9,8},{10,11... | collective-permute-start | bytes 122888 | tf_op jit(solution)/shard_map/ppermute | solution.py:445
  12.2 7.4 %collective-permute-start.4 = (bf16[80,256]{1,0:T(8,128)(2,1)S(1)}, bf16[80,256]{1,0:T(8,128)(2,1)S(1)}, u32[]{:S(2)}, u32[]{:S(2)}) collective-permute-start(bf16[80,256]{1,0:T(8,128)(2,1)S(1)} %shard_map.88.own.payload_ref), channel_id=1, source_target_pairs={{0,12},{4,8},{8,4},{12,0},{1,13},{5,9},{9,5},{13,1},{2,14},{6,10},... | collective-permute-start | bytes 122888 | tf_op jit(solution)/shard_map/ppermute | solution.py:445
  14.7 5.9 %collective-permute-start.5 = (bf16[80,256]{1,0:T(8,128)(2,1)S(1)}, bf16[80,256]{1,0:T(8,128)(2,1)S(1)}, u32[]{:S(2)}, u32[]{:S(2)}) collective-permute-start(bf16[80,256]{1,0:T(8,128)(2,1)S(1)} %shard_map.88.own.payload_ref), channel_id=1, source_target_pairs={{0,8},{4,12},{8,0},{12,4},{1,9},{5,13},{9,1},{13,5},{2,10},{6,14},... | collective-permute-start | bytes 122888 | tf_op jit(solution)/shard_map/ppermute | solution.py:445
  14.9 5.7 %collective-permute-start.6 = (bf16[80,256]{1,0:T(8,128)(2,1)S(1)}, bf16[80,256]{1,0:T(8,128)(2,1)S(1)}, u32[]{:S(2)}, u32[]{:S(2)}) collective-permute-start(bf16[80,256]{1,0:T(8,128)(2,1)S(1)} %shard_map.88.own.payload_ref), channel_id=1, source_target_pairs={{0,4},{4,0},{8,12},{12,8},{1,5},{5,1},{9,13},{13,9},{2,6},{6,2},{1... | collective-permute-start | bytes 122888 | tf_op jit(solution)/shard_map/ppermute | solution.py:445
  20.6 1.4 %collective-permute-start.7 = (bf16[3,64,256]{2,1,0:T(8,128)(2,1)S(1)}, bf16[3,64,256]{2,1,0:T(8,128)(2,1)S(1)}, u32[]{:S(2)}, u32[]{:S(2)}) collective-permute-start(bf16[3,64,256]{2,1,0:T(8,128)(2,1)S(1)} %get-tuple-element.14), channel_id=1, source_target_pairs={{0,1},{1,0},{2,3},{3,2},{4,5},{5,4},{6,7},{7,6},{8,9},{9,8},{10,11... | collective-permute-start | bytes 294920 | tf_op jit(solution)/shard_map/ppermute | solution.py:445
  24.1 9.0 %collective-permute-start.8 = (bf16[256,256]{1,0:T(8,128)(2,1)S(1)}, bf16[256,256]{1,0:T(8,128)(2,1)S(1)}, u32[]{:S(2)}, u32[]{:S(2)}) collective-permute-start(bf16[256,256]{1,0:T(8,128)(2,1)S(1)} %get-tuple-element.17), channel_id=1, source_target_pairs={{0,8},{4,12},{8,0},{12,4},{1,9},{5,13},{9,1},{13,5},{2,10},{6,14},... | collective-permute-start | bytes 393224 | tf_op jit(solution)/shard_map/ppermute | solution.py:445

commit v21 on v20

--- a/solution.py
+++ b/solution.py
@@ -278,26 +278,31 @@
     rank = factors.shape[0] // 2
     tokens = factors.shape[1]
     tok = own.shape[1]
+
+    def project_block(k):
+        here = slice(k * tok, (k + 1) * tok)
+        plain[:, here] = project_queries(
+            row_count, factors.at[:, here], features.at[k - 1], query_ref
+        )
+
+    plain[:, :tok] = own_plain_ref[...]
+    blocks = tokens // tok
+    for k in range(1, blocks // 2):
+        project_block(k)
     weight = weights[...]
     act, grad = factors[:rank, :], factors[rank:, :]
     act_scale, grad_scale = range_scale(act), range_scale(grad)
     act, grad = act * act_scale, grad * grad_scale
+    act_b, grad_b = act.astype(jnp.bfloat16), grad.astype(jnp.bfloat16)
     norms = jnp.sum(act * act, axis=0, keepdims=True) * jnp.sum(grad * grad, axis=0, keepdims=True)
     level = jnp.sum(weight * norms, axis=1, keepdims=True) / (tokens * rank * rank)
+    for k in range(max(blocks // 2, 1), blocks - 1):
+        project_block(k)
     step = 1.1 * level
-    act_b, grad_b = act.astype(jnp.bfloat16), grad.astype(jnp.bfloat16)
+    scale = act_scale * grad_scale
     act_rows, grad_rows = act.T.astype(jnp.bfloat16), grad.T.astype(jnp.bfloat16)
-    scale = act_scale * grad_scale
-    per_token = weight * (1.0 / (tokens * step))
-    for start in range(0, tokens, tok):
-        here = slice(start, start + tok)
-        if start:
-            plain[:, here] = project_queries(
-                row_count, factors.at[:, here], features.at[start // tok - 1], query_ref
-            )
-        else:
-            plain[:, here] = own_plain_ref[...]
-        weighted[:, here] = (plain[:, here] * per_token[:, here]).astype(jnp.bfloat16)
+    project_block(blocks - 1)
+    weighted[...] = (plain[...] * (weight * (1.0 / (tokens * step)))).astype(jnp.bfloat16)
     for n, out_ref in enumerate(out_refs):
         block = slice(2 * n * tok, (2 * n + 1) * tok)
         for row in range(0, tokens, TILE // 2):

time: 34.1 us -> 34.1 us (level)
  no operation moved by 1% of the time
where the time goes in v21:
time: 34.1 us; the launch traced here: 34 us
  Pallas kernels  16.5 us (48%)
  starting transfers between devices  10.4 us (30%)
  waiting for transfers between devices  5.57 us (16%)
  other arithmetic  0.74 us (2%)
  between operations  0.74 us (2%)
    ppermute x9, starting transfers between devices, swapped(): lax.ppermute(array, axis, [(i, i ^ distance) for i in range(lax.axis_size...  10.4 us
    pallas_call x1, Pallas kernels, hessian_rows(): pl.pallas_call(functools.partial(hessian_kernel, row_count, col_count), o...  7.88 us
    ppermute x9, waiting for transfers between devices, swapped(): lax.ppermute(array, axis, [(i, i ^ distance) for i in range(lax.axis_size...  5.57 us
    pallas_call x1, Pallas kernels, project(): pl.pallas_call(project_kernel, in_specs=[pl.BlockSpec(memory_space=pl.ANY...  2.66 us
    pallas_call x1, Pallas kernels, own_tokens_sum(): pl.pallas_call(functools.partial(own_kernel, row_count, col_count), out_s...  2.4 us
    pallas_call x1, Pallas kernels, score_shares(): pl.pallas_call(functools.partial(share_kernel, row_count), out_shape=[jax...  2.22 us
    pallas_call x1, Pallas kernels, finish_scores(): pl.pallas_call(finish_kernel, out_shape=jax.ShapeDtypeStruct((tok, count)...  0.77 us
    convert_element_type x1, other arithmetic, few_tokens(): jnp.where(live, credit[:, None], 0).astype(jnp.float32).reshape(1, -1)  0.74 us
  transfers between devices with their start and end apart: 9, of which 4 were waited for; matrix products, arithmetic and copies ran while one was open for 2% of the time, Pallas kernels for 40%

profile of v21, /device:TPU:0, one launch (start us, length us, event | category | flops | bytes accessed | tf_op | source)
XLA Modules:
  0.0 34.0 jit_solution(6269835334945583878)
XLA Ops:
  0.6 0.0 copy-start
  0.6 3.1 %collective-permute-start.3 = (bf16[1024,256]{1,0:T(8,128)(2,1)}, bf16[1024,256]{1,0:T(8,128)(2,1)S(1)}, u32[]{:S(2)}, u32[]{:S(2)}) collective-permute-start(bf16[1024,256]{1,0:T(8,128)(2,1)} %query.1), channel_id=1, source_target_pairs={{0,4},{4,0},{8,12},{12,8},{1,5},{5,1},{9,13},{13,9},{2,6},{6,2},{1... | collective-permute-start | bytes 1572872 | tf_op jit(solution)/shard_map/ppermute | solution.py:450
  3.7 2.7 %shard_map.86 = (f32[64,256]{1,0:T(8,128)S(1)}, f32[64,256]{1,0:T(8,128)S(1)}) custom-call(bf16[256,1024]{1,0:T(8,128)(2,1)} %act.1, bf16[256,3584]{1,0:T(8,128)(2,1)} %grad.1, bf16[64,1024]{1,0:T(8,128)(2,1)} %bitcast.5, bf16[64,3584]{1,0:T(8,128)(2,1)} %bitcast.4), custom_call_target="tpu_custom_call" | custom-call | tf_op jit(solution)/shard_map/pallas_call | solution.py:140
  6.4 0.1 collective-permute-start
  6.5 1.2 %collective-permute-done.other_ref = f32[64,256]{1,0:T(8,128)S(1)} collective-permute-done((f32[64,256]{1,0:T(8,128)S(1)}, f32[64,256]{1,0:T(8,128)S(1)}, u32[]{:S(2)}, u32[]{:S(2)}) %collective-permute-start) | collective-permute-done | bytes 65568 | tf_op jit(solution)/shard_map/ppermute | solution.py:450
  7.7 1.6 %collective-permute-start.1 = (f32[64,256]{1,0:T(8,128)S(1)}, f32[64,256]{1,0:T(8,128)S(1)}, u32[]{:S(2)}, u32[]{:S(2)}) collective-permute-start(f32[64,256]{1,0:T(8,128)S(1)} %shard_map.87.one_ref), channel_id=1, source_target_pairs={{0,2},{1,3},{2,0},{3,1},{4,6},{5,7},{6,4},{7,5},{8,10},{9,11},{10,... | collective-permute-start | bytes 196616 | tf_op jit(solution)/shard_map/ppermute | solution.py:450
  9.3 0.7 %fusion = f32[2,128]{1,0:T(2,128)S(1)} fusion(s32[2]{0:T(128)} %param.13, s32[2]{0:T(128)} %param.12), kind=kLoop, calls=%fused_computation.1 | loop fusion | flops 768 | bytes 1040 | tf_op jit(solution)/shard_map/convert_element_type | solution.py:460
  10.0 2.0 %collective-permute-done.1.other_ref = f32[64,256]{1,0:T(8,128)S(1)} collective-permute-done((f32[64,256]{1,0:T(8,128)S(1)}, f32[64,256]{1,0:T(8,128)S(1)}, u32[]{:S(2)}, u32[]{:S(2)}) %collective-permute-start.1) | collective-permute-done | bytes 65568 | tf_op jit(solution)/shard_map/ppermute | solution.py:450
  12.1 0.1 collective-permute-start.2
  12.2 2.5 %collective-permute-start.4 = (bf16[80,256]{1,0:T(8,128)(2,1)S(1)}, bf16[80,256]{1,0:T(8,128)(2,1)S(1)}, u32[]{:S(2)}, u32[]{:S(2)}) collective-permute-start(bf16[80,256]{1,0:T(8,128)(2,1)S(1)} %shard_map.88.own.payload_ref), channel_id=1, source_target_pairs={{0,12},{4,8},{8,4},{12,0},{1,13},{5,9},{9,5},{13,1},{2,14},{6,10},... | collective-permute-start | bytes 122888 | tf_op jit(solution)/shard_map/ppermute | solution.py:450
  14.7 0.2 collective-permute-start.5
  14.9 1.7 %collective-permute-start.6 = (bf16[80,256]{1,0:T(8,128)(2,1)S(1)}, bf16[80,256]{1,0:T(8,128)(2,1)S(1)}, u32[]{:S(2)}, u32[]{:S(2)}) collective-permute-start(bf16[80,256]{1,0:T(8,128)(2,1)S(1)} %shard_map.88.own.payload_ref), channel_id=1, source_target_pairs={{0,4},{4,0},{8,12},{12,8},{1,5},{5,1},{9,13},{13,9},{2,6},{6,2},{1... | collective-permute-start | bytes 122888 | tf_op jit(solution)/shard_map/ppermute | solution.py:450
  16.6 0.0 collective-permute-done.2.own_other
  16.6 2.4 %shard_map.89._.own_sum = f32[1024,4096]{1,0:T(8,128)S(1)} custom-call(bf16[80,256]{1,0:T(8,128)(2,1)S(1)} %shard_map.88.own.payload_ref, bf16[80,256]{1,0:T(8,128)(2,1)S(1)} %collective-permute-done.2.own_other), custom_call_target="tpu_custom_call" | custom-call | tf_op jit(solution)/shard_map/pallas_call | solution.py:364
  19.0 0.0 collective-permute-done.3.near_query
  19.0 0.0 copy-done
  19.0 0.5 %shard_map.90 = (bf16[256,2048]{1,0:T(8,128)(2,1)S(1)}, f32[256,256]{1,0:T(8,128)S(1)}) custom-call(bf16[1024,256]{1,0:T(8,128)(2,1)S(1)} %copy-done, bf16[1024,256]{1,0:T(8,128)(2,1)S(1)} %collective-permute-done.3.near_query, bf16[80,256]{1,0:T(8,128)(2,1)S(1)} %shard_map.88.own.payload_ref, bf16[80,256]{1,0:T(8,128)(2,1)S(1)} %collective-permute-done.2.own_other), custom_call_target="tpu_custom_call" | custom-call | tf_op jit(solution)/shard_map/pallas_call | solution.py:262
  19.6 0.0 collective-permute-done.4.refs_0_
  19.6 1.0 %collective-permute-done.5.refs_1_ = bf16[80,256]{1,0:T(8,128)(2,1)S(1)} collective-permute-done((bf16[80,256]{1,0:T(8,128)(2,1)S(1)}, bf16[80,256]{1,0:T(8,128)(2,1)S(1)}, u32[]{:S(2)}, u32[]{:S(2)}) %collective-permute-start.5) | collective-permute-done | bytes 40992 | tf_op jit(solution)/shard_map/ppermute | solution.py:450
  20.6 0.0 collective-permute-done.6.refs_2_
  20.6 0.1 collective-permute-start.7
  20.7 1.3 %collective-permute-done.7.other = bf16[3,64,256]{2,1,0:T(8,128)(2,1)S(1)} collective-permute-done((bf16[3,64,256]{2,1,0:T(8,128)(2,1)S(1)}, bf16[3,64,256]{2,1,0:T(8,128)(2,1)S(1)}, u32[]{:S(2)}, u32[]{:S(2)}) %collective-permute-start.7) | collective-permute-done | bytes 98336 | tf_op jit(solution)/shard_map/ppermute | solution.py:450
  21.9 2.2 %shard_map.93 = (f32[256,256]{1,0:T(8,128)S(1)}, bf16[256,256]{1,0:T(8,128)(2,1)S(1)}) custom-call(bf16[80,256]{1,0:T(8,128)(2,1)S(1)} %shard_map.88.own.payload_ref, bf16[80,256]{1,0:T(8,128)(2,1)S(1)} %collective-permute-done.2.own_other, bf16[3,80,256]{2,1,0:T(8,128)(2,1)S(1)} %get-tuple-element.13.mine, ...), custom_call_target="tpu_custom_call" | custom-call | tf_op jit(solution)/shard_map/pallas_call | solution.py:321
  24.2 1.1 %collective-permute-start.8 = (bf16[256,256]{1,0:T(8,128)(2,1)S(1)}, bf16[256,256]{1,0:T(8,128)(2,1)S(1)}, u32[]{:S(2)}, u32[]{:S(2)}) collective-permute-start(bf16[256,256]{1,0:T(8,128)(2,1)S(1)} %get-tuple-element.17), channel_id=1, source_target_pairs={{0,8},{4,12},{8,0},{12,4},{1,9},{5,13},{9,1},{13,5},{2,10},{6,14},... | collective-permute-start | bytes 393224 | tf_op jit(solution)/shard_map/ppermute | solution.py:450
  25.3 7.9 %shard_map.92 = f32[1024,4096]{1,0:T(8,128)} custom-call(bf16[3,80,256]{2,1,0:T(8,128)(2,1)S(1)} %get-tuple-element.13.mine, bf16[3,64,256]{2,1,0:T(8,128)(2,1)S(1)} %collective-permute-done.7.other, f32[1024,4096]{1,0:T(8,128)S(1)} %shard_map.89._.own_sum), custom_call_target="tpu_custom_call" | custom-call | tf_op jit(solution)/shard_map/pallas_call | solution.py:414
  33.2 0.0 collective-permute-done.8.refs_1_
  33.2 0.8 %shard_map.94 = bf16[256,256]{1,0:T(8,128)(2,1)} custom-call(bf16[80,256]{1,0:T(8,128)(2,1)S(1)} %shard_map.88.own.payload_ref, f32[256,256]{1,0:T(8,128)S(1)} %get-tuple-element.16.refs_0_, bf16[256,256]{1,0:T(8,128)(2,1)S(1)} %collective-permute-done.8.refs_1_), custom_call_target="tpu_custom_call" | custom-call | tf_op jit(solution)/shard_map/pallas_call | solution.py:442
  (3 shorter events, 0.0 us)
Async XLA Ops:
  0.6 18.4 %copy-start = (bf16[1024,256]{1,0:T(8,128)(2,1)S(1)}, bf16[1024,256]{1,0:T(8,128)(2,1)}, u32[]{:S(2)}) copy-start(bf16[1024,256]{1,0:T(8,128)(2,1)} %query.1) | copy-start | bytes 1572868
  0.6 18.4 %collective-permute-start.3 = (bf16[1024,256]{1,0:T(8,128)(2,1)}, bf16[1024,256]{1,0:T(8,128)(2,1)S(1)}, u32[]{:S(2)}, u32[]{:S(2)}) collective-permute-start(bf16[1024,256]{1,0:T(8,128)(2,1)} %query.1), channel_id=1, source_target_pairs={{0,4},{4,0},{8,12},{12,8},{1,5},{5,1},{9,13},{13,9},{2,6},{6,2},{1... | collective-permute-start | bytes 1572872 | tf_op jit(solution)/shard_map/ppermute | solution.py:450
  6.4 1.3 %collective-permute-start = (f32[64,256]{1,0:T(8,128)S(1)}, f32[64,256]{1,0:T(8,128)S(1)}, u32[]{:S(2)}, u32[]{:S(2)}) collective-permute-start(f32[64,256]{1,0:T(8,128)S(1)} %get-tuple-element.11), channel_id=1, source_target_pairs={{0,1},{1,0},{2,3},{3,2},{4,5},{5,4},{6,7},{7,6},{8,9},{9,8},{10,11... | collective-permute-start | bytes 196616 | tf_op jit(solution)/shard_map/ppermute | solution.py:450
  7.7 4.3 %collective-permute-start.1 = (f32[64,256]{1,0:T(8,128)S(1)}, f32[64,256]{1,0:T(8,128)S(1)}, u32[]{:S(2)}, u32[]{:S(2)}) collective-permute-start(f32[64,256]{1,0:T(8,128)S(1)} %shard_map.87.one_ref), channel_id=1, source_target_pairs={{0,2},{1,3},{2,0},{3,1},{4,6},{5,7},{6,4},{7,5},{8,10},{9,11},{10,... | collective-permute-start | bytes 196616 | tf_op jit(solution)/shard_map/ppermute | solution.py:450
  12.1 4.5 %collective-permute-start.2 = (bf16[80,256]{1,0:T(8,128)(2,1)S(1)}, bf16[80,256]{1,0:T(8,128)(2,1)S(1)}, u32[]{:S(2)}, u32[]{:S(2)}) collective-permute-start(bf16[80,256]{1,0:T(8,128)(2,1)S(1)} %shard_map.88.own.payload_ref), channel_id=1, source_target_pairs={{0,1},{1,0},{2,3},{3,2},{4,5},{5,4},{6,7},{7,6},{8,9},{9,8},{10,11... | collective-permute-start | bytes 122888 | tf_op jit(solution)/shard_map/ppermute | solution.py:450
  12.2 7.4 %collective-permute-start.4 = (bf16[80,256]{1,0:T(8,128)(2,1)S(1)}, bf16[80,256]{1,0:T(8,128)(2,1)S(1)}, u32[]{:S(2)}, u32[]{:S(2)}) collective-permute-start(bf16[80,256]{1,0:T(8,128)(2,1)S(1)} %shard_map.88.own.payload_ref), channel_id=1, source_target_pairs={{0,12},{4,8},{8,4},{12,0},{1,13},{5,9},{9,5},{13,1},{2,14},{6,10},... | collective-permute-start | bytes 122888 | tf_op jit(solution)/shard_map/ppermute | solution.py:450
  14.7 5.9 %collective-permute-start.5 = (bf16[80,256]{1,0:T(8,128)(2,1)S(1)}, bf16[80,256]{1,0:T(8,128)(2,1)S(1)}, u32[]{:S(2)}, u32[]{:S(2)}) collective-permute-start(bf16[80,256]{1,0:T(8,128)(2,1)S(1)} %shard_map.88.own.payload_ref), channel_id=1, source_target_pairs={{0,8},{4,12},{8,0},{12,4},{1,9},{5,13},{9,1},{13,5},{2,10},{6,14},... | collective-permute-start | bytes 122888 | tf_op jit(solution)/shard_map/ppermute | solution.py:450
  14.9 5.7 %collective-permute-start.6 = (bf16[80,256]{1,0:T(8,128)(2,1)S(1)}, bf16[80,256]{1,0:T(8,128)(2,1)S(1)}, u32[]{:S(2)}, u32[]{:S(2)}) collective-permute-start(bf16[80,256]{1,0:T(8,128)(2,1)S(1)} %shard_map.88.own.payload_ref), channel_id=1, source_target_pairs={{0,4},{4,0},{8,12},{12,8},{1,5},{5,1},{9,13},{13,9},{2,6},{6,2},{1... | collective-permute-start | bytes 122888 | tf_op jit(solution)/shard_map/ppermute | solution.py:450
  20.6 1.4 %collective-permute-start.7 = (bf16[3,64,256]{2,1,0:T(8,128)(2,1)S(1)}, bf16[3,64,256]{2,1,0:T(8,128)(2,1)S(1)}, u32[]{:S(2)}, u32[]{:S(2)}) collective-permute-start(bf16[3,64,256]{2,1,0:T(8,128)(2,1)S(1)} %get-tuple-element.14), channel_id=1, source_target_pairs={{0,1},{1,0},{2,3},{3,2},{4,5},{5,4},{6,7},{7,6},{8,9},{9,8},{10,11... | collective-permute-start | bytes 294920 | tf_op jit(solution)/shard_map/ppermute | solution.py:450
  24.2 9.0 %collective-permute-start.8 = (bf16[256,256]{1,0:T(8,128)(2,1)S(1)}, bf16[256,256]{1,0:T(8,128)(2,1)S(1)}, u32[]{:S(2)}, u32[]{:S(2)}) collective-permute-start(bf16[256,256]{1,0:T(8,128)(2,1)S(1)} %get-tuple-element.17), channel_id=1, source_target_pairs={{0,8},{4,12},{8,0},{12,4},{1,9},{5,13},{9,1},{13,5},{2,10},{6,14},... | collective-permute-start | bytes 393224 | tf_op jit(solution)/shard_map/ppermute | solution.py:450

commit v22 on v19

--- a/solution.py
+++ b/solution.py
@@ -271,9 +271,49 @@
     )(queries, near_queries, own, own_other)
 
 
+def scaled(values):
+    scale = range_scale(values)
+    return values * scale, scale
+
+
+def half_kernel(own, mine, gram_ref, norm_ref, scale_ref, values):
+    rank, tok = values.shape[0], own.shape[1]
+    for k, part in enumerate([own] + [mine.at[k] for k in reversed(range(mine.shape[0]))]):
+        values[:, k * tok : (k + 1) * tok] = part[:rank].astype(jnp.float32)
+    factor, scale = scaled(values[...])
+    scale_ref[...] = jnp.broadcast_to(scale, scale_ref.shape)
+    norm = jnp.sum(factor * factor, axis=0, keepdims=True)
+    norm_ref[...] = jnp.broadcast_to(norm, norm_ref.shape)
+    factor_b, factor_rows = factor.astype(jnp.bfloat16), factor.T.astype(jnp.bfloat16)
+    for n in range(gram_ref.shape[0]):
+        block = slice(2 * n * tok, (2 * n + 1) * tok)
+        for row in range(0, values.shape[1], TILE // 2):
+            here = slice(row, row + TILE // 2)
+            gram_ref[n, here, :] = jnp.dot(
+                factor_rows[here], factor_b[:, block], preferred_element_type=jnp.float32
+            )
+
+
+def half_gram(own, mine, rank):
+    blocks, tok = mine.shape[0] + 1, own.shape[1]
+    tokens = blocks * tok
+    return pl.pallas_call(
+        half_kernel,
+        out_shape=[
+            jax.ShapeDtypeStruct((blocks // 2, tokens, tok), jnp.float32),
+            jax.ShapeDtypeStruct((8, tokens), jnp.float32),
+            jax.ShapeDtypeStruct((8, 128), jnp.float32),
+        ],
+        scratch_shapes=[pltpu.VMEM((rank, tokens), jnp.float32)],
+        compiler_params=params(26),
+    )(own, mine)
+
+
 def share_kernel(
     row_count, own, own_other, mine, other, query_ref, near_query_ref, own_plain_ref, *refs
 ):
+    half_gram_ref, half_norm_ref, half_scale_ref = refs[:3]
+    refs = refs[3:]
     factors, weights, features, gram = refs[-4:]
     out_refs = refs[:-4]
     lay_out_factors([(own, own_other)] + block_pairs(mine, other), factors, weights)
@@ -284,36 +324,28 @@
         row_count, factors.at[:, tok:], features, (query_ref, near_query_ref)
     )
     plain = jnp.concatenate([own_plain_ref[...], plain], axis=1)
-    act = factors[:rank, :]
+    there = pl.multiple_of(rank - lax.rem(lax.axis_index("query"), 2) * rank, rank)
+    factor, scale = scaled(factors[pl.ds(there, rank), :])
     weight = weights[...]
-    act, grad = factors[:rank, :], factors[rank:, :]
-    act_scale, grad_scale = range_scale(act), range_scale(grad)
-    act, grad = act * act_scale, grad * grad_scale
-    norms = jnp.sum(act * act, axis=0, keepdims=True) * jnp.sum(grad * grad, axis=0, keepdims=True)
+    norms = half_norm_ref[:1, :] * jnp.sum(factor * factor, axis=0, keepdims=True)
     level = jnp.sum(weight * norms, axis=1, keepdims=True) / (tokens * rank * rank)
     step = 1.1 * level
-    act_b, grad_b = act.astype(jnp.bfloat16), grad.astype(jnp.bfloat16)
+    factor_b, factor_rows = factor.astype(jnp.bfloat16), factor.T.astype(jnp.bfloat16)
     weighted = (plain * (weight * (1.0 / (tokens * step)))).astype(jnp.bfloat16)
-    scale = act_scale * grad_scale
+    scale = scale * half_scale_ref[:1, :1]
     for n, out_ref in enumerate(out_refs):
         block = slice(2 * n * tok, (2 * n + 1) * tok)
-        act_rows, grad_rows = act_b[:, block].T, grad_b[:, block].T
-        for col in range(0, tokens, TILE):
-            there = slice(col, col + TILE)
-            for row in range(0, tok, TILE // 2):
-                here = slice(row, row + TILE // 2)
-                tile = jnp.dot(act_rows[here], act_b[:, there], preferred_element_type=jnp.float32)
-                tile *= jnp.dot(
-                    grad_rows[here], grad_b[:, there], preferred_element_type=jnp.float32
-                )
-                gram[n, here, there] = tile.astype(jnp.bfloat16)
-        image = lax.dot_general(weighted, gram[n], NT, preferred_element_type=jnp.float32)
+        for row in range(0, tokens, TILE // 2):
+            here = slice(row, row + TILE // 2)
+            tile = jnp.dot(factor_rows[here], factor_b[:, block], preferred_element_type=jnp.float32)
+            gram[n, here, :] = (tile * half_gram_ref[n, here, :]).astype(jnp.bfloat16)
+        image = jnp.dot(weighted, gram[n], preferred_element_type=jnp.float32)
         share = ((2.0 - 0.1 / 1.1) * plain[:, block] - image) * scale * (scale / step)
         out_ref[...] = share.astype(out_ref.dtype)
 
 
 def score_shares(
-    own, own_other, mine, other, queries_t, near_queries_t, own_plain, rank, row_count
+    own, own_other, mine, other, queries_t, near_queries_t, own_plain, half, rank, row_count
 ):
     blocks, tok = mine.shape[0] + 1, mine.shape[2]
     count, rows = queries_t.shape
@@ -327,10 +359,10 @@
             pltpu.VMEM((2 * rank, tok * blocks), jnp.float32),
             pltpu.VMEM((1, tok * blocks), jnp.float32),
             pltpu.VMEM((2, rows, tok * (blocks - 1)), jnp.bfloat16),
-            pltpu.VMEM((blocks // 2, tok, tok * blocks), jnp.bfloat16),
+            pltpu.VMEM((blocks // 2, tok * blocks, tok), jnp.bfloat16),
         ],
         compiler_params=params(26),
-    )(own, own_other, mine, other, queries_t, near_queries_t, own_plain)
+    )(own, own_other, mine, other, queries_t, near_queries_t, own_plain, *half)
 
 
 def build_columns(first, act, factors, right):
@@ -472,8 +504,9 @@
     )
     mine, factors = stack(others, rank, (own_sum, queries_t))
     other = swapped(factors, "query", 1)
+    half = half_gram(own, mine, rank)
     shares = score_shares(
-        own, own_other, mine, other, queries_t, near_queries_t, own_plain, rank, row_count
+        own, own_other, mine, other, queries_t, near_queries_t, own_plain, half, rank, row_count
     )
     arrived = [swapped(share, "dp", 2 * n) for n, share in enumerate(shares) if n]
     hessian = hessian_rows(mine, other, own_sum, rank, row_count)

time: 34.2 us -> 33.9 us (level)
  waiting for transfers between devices: 5.57 us -> 4.93 us
    ppermute x9, waiting for transfers between devices: 5.57 us -> 4.93 us  [swapped(): lax.ppermute(array, axis, [(i, i ^ distance) for i in range(lax.axis_size...]
    pallas_call x0 -> x1, Pallas kernels: none -> 0.64 us  [half_gram(): pl.pallas_call(half_kernel, out_shape=[jax.ShapeDtypeStruct((blocks // 2,...]
  transfers between devices with their start and end apart: 9 -> 9, of which waited for: 4 -> 4; matrix products, arithmetic and copies ran while one was open for 2% -> 2% of each run, Pallas kernels for 40% -> 42%
where the time goes in v22:
time: 33.9 us; the launch traced here: 33.7 us
  Pallas kernels  16.8 us (50%)
  starting transfers between devices  10.4 us (31%)
  waiting for transfers between devices  4.93 us (15%)
  between operations  0.75 us (2%)
  other arithmetic  0.74 us (2%)
    ppermute x9, starting transfers between devices, swapped(): lax.ppermute(array, axis, [(i, i ^ distance) for i in range(lax.axis_size...  10.4 us
    pallas_call x1, Pallas kernels, hessian_rows(): pl.pallas_call(functools.partial(hessian_kernel, row_count, col_count), o...  7.88 us
    ppermute x9, waiting for transfers between devices, swapped(): lax.ppermute(array, axis, [(i, i ^ distance) for i in range(lax.axis_size...  4.93 us
    pallas_call x1, Pallas kernels, project(): pl.pallas_call(project_kernel, in_specs=[pl.BlockSpec(memory_space=pl.ANY...  2.66 us
    pallas_call x1, Pallas kernels, own_tokens_sum(): pl.pallas_call(functools.partial(own_kernel, row_count, col_count), out_s...  2.4 us
    pallas_call x1, Pallas kernels, score_shares(): pl.pallas_call(functools.partial(share_kernel, row_count), out_shape=[jax...  1.94 us
    pallas_call x1, Pallas kernels, finish_scores(): pl.pallas_call(finish_kernel, out_shape=jax.ShapeDtypeStruct((tok, count)...  0.77 us
    convert_element_type x1, other arithmetic, few_tokens(): jnp.where(live, credit[:, None], 0).astype(jnp.float32).reshape(1, -1)  0.74 us
  transfers between devices with their start and end apart: 9, of which 4 were waited for; matrix products, arithmetic and copies ran while one was open for 2% of the time, Pallas kernels for 42%

profile of v22, /device:TPU:0, one launch (start us, length us, event | category | flops | bytes accessed | tf_op | source)
XLA Modules:
  0.0 33.7 jit_solution(3330119091091900829)
XLA Ops:
  0.6 0.0 copy-start
  0.6 3.1 %collective-permute-start.3 = (bf16[1024,256]{1,0:T(8,128)(2,1)}, bf16[1024,256]{1,0:T(8,128)(2,1)S(1)}, u32[]{:S(2)}, u32[]{:S(2)}) collective-permute-start(bf16[1024,256]{1,0:T(8,128)(2,1)} %query.1), channel_id=1, source_target_pairs={{0,4},{4,0},{8,12},{12,8},{1,5},{5,1},{9,13},{13,9},{2,6},{6,2},{1... | collective-permute-start | bytes 1572872 | tf_op jit(solution)/shard_map/ppermute | solution.py:479
  3.7 2.7 %shard_map.86 = (f32[64,256]{1,0:T(8,128)S(1)}, f32[64,256]{1,0:T(8,128)S(1)}) custom-call(bf16[256,1024]{1,0:T(8,128)(2,1)} %act.1, bf16[256,3584]{1,0:T(8,128)(2,1)} %grad.1, bf16[64,1024]{1,0:T(8,128)(2,1)} %bitcast.5, bf16[64,3584]{1,0:T(8,128)(2,1)} %bitcast.4), custom_call_target="tpu_custom_call" | custom-call | tf_op jit(solution)/shard_map/pallas_call | solution.py:140
  6.4 0.1 collective-permute-start
  6.5 1.2 %collective-permute-done.other_ref = f32[64,256]{1,0:T(8,128)S(1)} collective-permute-done((f32[64,256]{1,0:T(8,128)S(1)}, f32[64,256]{1,0:T(8,128)S(1)}, u32[]{:S(2)}, u32[]{:S(2)}) %collective-permute-start) | collective-permute-done | bytes 65568 | tf_op jit(solution)/shard_map/ppermute | solution.py:479
  7.7 1.6 %collective-permute-start.1 = (f32[64,256]{1,0:T(8,128)S(1)}, f32[64,256]{1,0:T(8,128)S(1)}, u32[]{:S(2)}, u32[]{:S(2)}) collective-permute-start(f32[64,256]{1,0:T(8,128)S(1)} %shard_map.87.one_ref), channel_id=1, source_target_pairs={{0,2},{1,3},{2,0},{3,1},{4,6},{5,7},{6,4},{7,5},{8,10},{9,11},{10,... | collective-permute-start | bytes 196616 | tf_op jit(solution)/shard_map/ppermute | solution.py:479
  9.3 0.7 %fusion = f32[2,128]{1,0:T(2,128)S(1)} fusion(s32[2]{0:T(128)} %param.13, s32[2]{0:T(128)} %param.12), kind=kLoop, calls=%fused_computation.1 | loop fusion | flops 768 | bytes 1040 | tf_op jit(solution)/shard_map/convert_element_type | solution.py:489
  10.0 2.0 %collective-permute-done.1.other_ref = f32[64,256]{1,0:T(8,128)S(1)} collective-permute-done((f32[64,256]{1,0:T(8,128)S(1)}, f32[64,256]{1,0:T(8,128)S(1)}, u32[]{:S(2)}, u32[]{:S(2)}) %collective-permute-start.1) | collective-permute-done | bytes 65568 | tf_op jit(solution)/shard_map/ppermute | solution.py:479
  12.1 0.1 collective-permute-start.2
  12.2 2.5 %collective-permute-start.4 = (bf16[80,256]{1,0:T(8,128)(2,1)S(1)}, bf16[80,256]{1,0:T(8,128)(2,1)S(1)}, u32[]{:S(2)}, u32[]{:S(2)}) collective-permute-start(bf16[80,256]{1,0:T(8,128)(2,1)S(1)} %shard_map.88.own.payload_ref), channel_id=1, source_target_pairs={{0,12},{4,8},{8,4},{12,0},{1,13},{5,9},{9,5},{13,1},{2,14},{6,10},... | collective-permute-start | bytes 122888 | tf_op jit(solution)/shard_map/ppermute | solution.py:479
  14.7 0.2 collective-permute-start.5
  14.9 1.7 %collective-permute-start.6 = (bf16[80,256]{1,0:T(8,128)(2,1)S(1)}, bf16[80,256]{1,0:T(8,128)(2,1)S(1)}, u32[]{:S(2)}, u32[]{:S(2)}) collective-permute-start(bf16[80,256]{1,0:T(8,128)(2,1)S(1)} %shard_map.88.own.payload_ref), channel_id=1, source_target_pairs={{0,4},{4,0},{8,12},{12,8},{1,5},{5,1},{9,13},{13,9},{2,6},{6,2},{1... | collective-permute-start | bytes 122888 | tf_op jit(solution)/shard_map/ppermute | solution.py:479
  16.6 0.0 collective-permute-done.2.own_other
  16.6 2.4 %shard_map.89._.own_sum = f32[1024,4096]{1,0:T(8,128)S(1)} custom-call(bf16[80,256]{1,0:T(8,128)(2,1)S(1)} %shard_map.88.own.payload_ref, bf16[80,256]{1,0:T(8,128)(2,1)S(1)} %collective-permute-done.2.own_other), custom_call_target="tpu_custom_call" | custom-call | tf_op jit(solution)/shard_map/pallas_call | solution.py:393
  19.0 0.0 collective-permute-done.3.near_query
  19.0 0.0 copy-done
  19.0 0.5 %shard_map.90 = (bf16[256,1024]{1,0:T(8,128)(2,1)S(1)}, bf16[256,1024]{1,0:T(8,128)(2,1)S(1)}, f32[256,256]{1,0:T(8,128)S(1)}) custom-call(bf16[1024,256]{1,0:T(8,128)(2,1)S(1)} %copy-done, bf16[1024,256]{1,0:T(8,128)(2,1)S(1)} %collective-permute-done.3.near_query, bf16[80,256]{1,0:T(8,128)(2,1)S(1)} %shard_map.88.own.payload_ref, ...), custom_call_target="tpu_custom_call" | custom-call | tf_op jit(solution)/shard_map/pallas_call | solution.py:262
  19.6 0.0 collective-permute-done.4.refs_0_
  19.6 1.0 %collective-permute-done.5.refs_1_ = bf16[80,256]{1,0:T(8,128)(2,1)S(1)} collective-permute-done((bf16[80,256]{1,0:T(8,128)(2,1)S(1)}, bf16[80,256]{1,0:T(8,128)(2,1)S(1)}, u32[]{:S(2)}, u32[]{:S(2)}) %collective-permute-start.5) | collective-permute-done | bytes 40992 | tf_op jit(solution)/shard_map/ppermute | solution.py:479
  20.6 0.0 collective-permute-done.6.refs_2_
  20.6 0.1 collective-permute-start.7
  20.7 0.6 %shard_map.93 = (f32[2,1024,256]{2,1,0:T(8,128)S(1)}, f32[8,1024]{1,0:T(8,128)S(1)}, f32[8,128]{1,0:T(8,128)S(1)}) custom-call(bf16[80,256]{1,0:T(8,128)(2,1)S(1)} %shard_map.88.own.payload_ref, bf16[3,80,256]{2,1,0:T(8,128)(2,1)S(1)} %get-tuple-element.17.mine), custom_call_target="tpu_custom_call" | custom-call | tf_op jit(solution)/shard_map/pallas_call | solution.py:300
  21.3 0.6 %collective-permute-done.7.other = bf16[3,64,256]{2,1,0:T(8,128)(2,1)S(1)} collective-permute-done((bf16[3,64,256]{2,1,0:T(8,128)(2,1)S(1)}, bf16[3,64,256]{2,1,0:T(8,128)(2,1)S(1)}, u32[]{:S(2)}, u32[]{:S(2)}) %collective-permute-start.7) | collective-permute-done | bytes 98336 | tf_op jit(solution)/shard_map/ppermute | solution.py:479
  21.9 1.9 %shard_map.94 = (f32[256,256]{1,0:T(8,128)S(1)}, bf16[256,256]{1,0:T(8,128)(2,1)S(1)}) custom-call(bf16[80,256]{1,0:T(8,128)(2,1)S(1)} %shard_map.88.own.payload_ref, bf16[80,256]{1,0:T(8,128)(2,1)S(1)} %collective-permute-done.2.own_other, bf16[3,80,256]{2,1,0:T(8,128)(2,1)S(1)} %get-tuple-element.17.mine, ...), custom_call_target="tpu_custom_call" | custom-call | tf_op jit(solution)/shard_map/pallas_call | solution.py:352
  23.9 1.1 %collective-permute-start.8 = (bf16[256,256]{1,0:T(8,128)(2,1)S(1)}, bf16[256,256]{1,0:T(8,128)(2,1)S(1)}, u32[]{:S(2)}, u32[]{:S(2)}) collective-permute-start(bf16[256,256]{1,0:T(8,128)(2,1)S(1)} %get-tuple-element.25), channel_id=1, source_target_pairs={{0,8},{4,12},{8,0},{12,4},{1,9},{5,13},{9,1},{13,5},{2,10},{6,14},... | collective-permute-start | bytes 393224 | tf_op jit(solution)/shard_map/ppermute | solution.py:479
  25.0 7.9 %shard_map.92 = f32[1024,4096]{1,0:T(8,128)} custom-call(bf16[3,80,256]{2,1,0:T(8,128)(2,1)S(1)} %get-tuple-element.17.mine, bf16[3,64,256]{2,1,0:T(8,128)(2,1)S(1)} %collective-permute-done.7.other, f32[1024,4096]{1,0:T(8,128)S(1)} %shard_map.89._.own_sum), custom_call_target="tpu_custom_call" | custom-call | tf_op jit(solution)/shard_map/pallas_call | solution.py:443
  32.9 0.0 collective-permute-done.8.refs_1_
  32.9 0.8 %shard_map.95 = bf16[256,256]{1,0:T(8,128)(2,1)} custom-call(bf16[80,256]{1,0:T(8,128)(2,1)S(1)} %shard_map.88.own.payload_ref, f32[256,256]{1,0:T(8,128)S(1)} %get-tuple-element.24.refs_0_, bf16[256,256]{1,0:T(8,128)(2,1)S(1)} %collective-permute-done.8.refs_1_), custom_call_target="tpu_custom_call" | custom-call | tf_op jit(solution)/shard_map/pallas_call | solution.py:471
  (3 shorter events, 0.0 us)
Async XLA Ops:
  0.6 18.4 %copy-start = (bf16[1024,256]{1,0:T(8,128)(2,1)S(1)}, bf16[1024,256]{1,0:T(8,128)(2,1)}, u32[]{:S(2)}) copy-start(bf16[1024,256]{1,0:T(8,128)(2,1)} %query.1) | copy-start | bytes 1572868
  0.6 18.4 %collective-permute-start.3 = (bf16[1024,256]{1,0:T(8,128)(2,1)}, bf16[1024,256]{1,0:T(8,128)(2,1)S(1)}, u32[]{:S(2)}, u32[]{:S(2)}) collective-permute-start(bf16[1024,256]{1,0:T(8,128)(2,1)} %query.1), channel_id=1, source_target_pairs={{0,4},{4,0},{8,12},{12,8},{1,5},{5,1},{9,13},{13,9},{2,6},{6,2},{1... | collective-permute-start | bytes 1572872 | tf_op jit(solution)/shard_map/ppermute | solution.py:479
  6.4 1.3 %collective-permute-start = (f32[64,256]{1,0:T(8,128)S(1)}, f32[64,256]{1,0:T(8,128)S(1)}, u32[]{:S(2)}, u32[]{:S(2)}) collective-permute-start(f32[64,256]{1,0:T(8,128)S(1)} %get-tuple-element.15), channel_id=1, source_target_pairs={{0,1},{1,0},{2,3},{3,2},{4,5},{5,4},{6,7},{7,6},{8,9},{9,8},{10,11... | collective-permute-start | bytes 196616 | tf_op jit(solution)/shard_map/ppermute | solution.py:479
  7.7 4.3 %collective-permute-start.1 = (f32[64,256]{1,0:T(8,128)S(1)}, f32[64,256]{1,0:T(8,128)S(1)}, u32[]{:S(2)}, u32[]{:S(2)}) collective-permute-start(f32[64,256]{1,0:T(8,128)S(1)} %shard_map.87.one_ref), channel_id=1, source_target_pairs={{0,2},{1,3},{2,0},{3,1},{4,6},{5,7},{6,4},{7,5},{8,10},{9,11},{10,... | collective-permute-start | bytes 196616 | tf_op jit(solution)/shard_map/ppermute | solution.py:479
  12.1 4.5 %collective-permute-start.2 = (bf16[80,256]{1,0:T(8,128)(2,1)S(1)}, bf16[80,256]{1,0:T(8,128)(2,1)S(1)}, u32[]{:S(2)}, u32[]{:S(2)}) collective-permute-start(bf16[80,256]{1,0:T(8,128)(2,1)S(1)} %shard_map.88.own.payload_ref), channel_id=1, source_target_pairs={{0,1},{1,0},{2,3},{3,2},{4,5},{5,4},{6,7},{7,6},{8,9},{9,8},{10,11... | collective-permute-start | bytes 122888 | tf_op jit(solution)/shard_map/ppermute | solution.py:479
  12.2 7.4 %collective-permute-start.4 = (bf16[80,256]{1,0:T(8,128)(2,1)S(1)}, bf16[80,256]{1,0:T(8,128)(2,1)S(1)}, u32[]{:S(2)}, u32[]{:S(2)}) collective-permute-start(bf16[80,256]{1,0:T(8,128)(2,1)S(1)} %shard_map.88.own.payload_ref), channel_id=1, source_target_pairs={{0,12},{4,8},{8,4},{12,0},{1,13},{5,9},{9,5},{13,1},{2,14},{6,10},... | collective-permute-start | bytes 122888 | tf_op jit(solution)/shard_map/ppermute | solution.py:479
  14.7 5.9 %collective-permute-start.5 = (bf16[80,256]{1,0:T(8,128)(2,1)S(1)}, bf16[80,256]{1,0:T(8,128)(2,1)S(1)}, u32[]{:S(2)}, u32[]{:S(2)}) collective-permute-start(bf16[80,256]{1,0:T(8,128)(2,1)S(1)} %shard_map.88.own.payload_ref), channel_id=1, source_target_pairs={{0,8},{4,12},{8,0},{12,4},{1,9},{5,13},{9,1},{13,5},{2,10},{6,14},... | collective-permute-start | bytes 122888 | tf_op jit(solution)/shard_map/ppermute | solution.py:479
  14.9 5.7 %collective-permute-start.6 = (bf16[80,256]{1,0:T(8,128)(2,1)S(1)}, bf16[80,256]{1,0:T(8,128)(2,1)S(1)}, u32[]{:S(2)}, u32[]{:S(2)}) collective-permute-start(bf16[80,256]{1,0:T(8,128)(2,1)S(1)} %shard_map.88.own.payload_ref), channel_id=1, source_target_pairs={{0,4},{4,0},{8,12},{12,8},{1,5},{5,1},{9,13},{13,9},{2,6},{6,2},{1... | collective-permute-start | bytes 122888 | tf_op jit(solution)/shard_map/ppermute | solution.py:479
  20.6 1.4 %collective-permute-start.7 = (bf16[3,64,256]{2,1,0:T(8,128)(2,1)S(1)}, bf16[3,64,256]{2,1,0:T(8,128)(2,1)S(1)}, u32[]{:S(2)}, u32[]{:S(2)}) collective-permute-start(bf16[3,64,256]{2,1,0:T(8,128)(2,1)S(1)} %get-tuple-element.18), channel_id=1, source_target_pairs={{0,1},{1,0},{2,3},{3,2},{4,5},{5,4},{6,7},{7,6},{8,9},{9,8},{10,11... | collective-permute-start | bytes 294920 | tf_op jit(solution)/shard_map/ppermute | solution.py:479
  23.9 9.0 %collective-permute-start.8 = (bf16[256,256]{1,0:T(8,128)(2,1)S(1)}, bf16[256,256]{1,0:T(8,128)(2,1)S(1)}, u32[]{:S(2)}, u32[]{:S(2)}) collective-permute-start(bf16[256,256]{1,0:T(8,128)(2,1)S(1)} %get-tuple-element.25), channel_id=1, source_target_pairs={{0,8},{4,12},{8,0},{12,4},{1,9},{5,13},{9,1},{13,5},{2,10},{6,14},... | collective-permute-start | bytes 393224 | tf_op jit(solution)/shard_map/ppermute | solution.py:479

commit v23 on v22

--- a/solution.py
+++ b/solution.py
@@ -110,10 +110,10 @@
 
 
 def project_kernel(act, grad, pin, pout, keep_ref, send_ref, act_v, grad_v, pin_v, pout_v, sems):
-    chunk = grad.shape[1] // 2
-    spans = [pl.ds(0, chunk), pl.ds(chunk, chunk)]
+    half = grad.shape[0] // 2
+    spans = [pl.ds(0, half), pl.ds(half, half)]
     pairs = [(pin, pin_v), (act, act_v), (pout, pout_v)]
-    pairs += [(grad.at[:, span], grad_v.at[:, span]) for span in spans]
+    pairs += [(grad.at[span], grad_v.at[span]) for span in spans]
     copies = [pltpu.make_async_copy(s, d, sems.at[n]) for n, (s, d) in enumerate(pairs)]
     for copy in copies:
         copy.start()
@@ -121,12 +121,13 @@
     copies[1].wait()
     part_act = lax.dot_general(pin_v[...], act_v[...], NT, preferred_element_type=jnp.float32)
     copies[2].wait()
-    part_grad = jnp.zeros_like(part_act)
+    parts = []
     for copy, span in zip(copies[3:], spans):
         copy.wait()
-        part_grad += lax.dot_general(
-            pout_v[:, span], grad_v[:, span], NT, preferred_element_type=jnp.float32
+        parts.append(
+            lax.dot_general(pout_v[...], grad_v[span], NT, preferred_element_type=jnp.float32)
         )
+    part_grad = jnp.concatenate(parts, axis=1)
     even = lax.rem(lax.axis_index("query"), 2) == 0
     keep_ref[...] = jnp.where(even, part_act, part_grad)
     send_ref[...] = jnp.where(even, part_grad, part_act)
@@ -234,38 +235,38 @@
     return scale
 
 
-def project_queries(row_count, factors, features, queries):
+def project_queries(row_count, factors, features, query_ref):
     rank = factors.shape[0] // 2
     act = factors[:rank, :]
-    total = 0.0
-    for near, query_ref in enumerate(queries):
+    for near in range(2):
         first = rank + (lax.axis_index("dp") ^ near) * row_count
         for i in range(row_count):
             row = factors[pl.ds(first + i, 1), :]
-            features[near, i * rank : (i + 1) * rank, :] = (row * act).astype(jnp.bfloat16)
-        total += jnp.dot(query_ref[...], features[near], preferred_element_type=jnp.float32)
-    return total
+            start = (near * row_count + i) * rank
+            features[start : start + rank, :] = (row * act).astype(jnp.bfloat16)
+    return jnp.dot(query_ref[...], features[...], preferred_element_type=jnp.float32)
 
 
 def turn_kernel(row_count, query, near_query, own, own_other, *refs):
-    out_ref, near_out_ref, plain_ref, factors, weights, features = refs
-    out_ref[...] = query[...].T
-    near_out_ref[...] = near_query[...].T
+    out_ref, plain_ref, factors, weights, features = refs
+    rows = query.shape[0]
+    out_ref[:, :rows] = query[...].T
+    out_ref[:, rows:] = near_query[...].T
     lay_out_factors([(own, own_other)], factors, weights)
-    plain_ref[...] = project_queries(row_count, factors, features, (out_ref, near_out_ref))
+    plain_ref[...] = project_queries(row_count, factors, features, out_ref)
 
 
 def turn_queries(queries, near_queries, own, own_other, rank, row_count):
     rows, count = queries.shape
     tok = own.shape[1]
-    out = jax.ShapeDtypeStruct((count, rows), queries.dtype)
+    out = jax.ShapeDtypeStruct((count, 2 * rows), queries.dtype)
     return pl.pallas_call(
         functools.partial(turn_kernel, row_count),
-        out_shape=[out, out, jax.ShapeDtypeStruct((count, tok), jnp.float32)],
+        out_shape=[out, jax.ShapeDtypeStruct((count, tok), jnp.float32)],
         scratch_shapes=[
             pltpu.VMEM((2 * rank, tok), jnp.float32),
             pltpu.VMEM((1, tok), jnp.float32),
-            pltpu.VMEM((2, rows, tok), jnp.bfloat16),
+            pltpu.VMEM((2 * rows, tok), jnp.bfloat16),
         ],
         compiler_params=params(26),
     )(queries, near_queries, own, own_other)
@@ -309,9 +310,7 @@
     )(own, mine)
 
 
-def share_kernel(
-    row_count, own, own_other, mine, other, query_ref, near_query_ref, own_plain_ref, *refs
-):
+def share_kernel(row_count, own, own_other, mine, other, query_ref, own_plain_ref, *refs):
     half_gram_ref, half_norm_ref, half_scale_ref = refs[:3]
     refs = refs[3:]
     factors, weights, features, gram = refs[-4:]
@@ -320,9 +319,7 @@
     rank = factors.shape[0] // 2
     tokens = factors.shape[1]
     tok = own.shape[1]
-    plain = project_queries(
-        row_count, factors.at[:, tok:], features, (query_ref, near_query_ref)
-    )
+    plain = project_queries(row_count, factors.at[:, tok:], features, query_ref)
     plain = jnp.concatenate([own_plain_ref[...], plain], axis=1)
     there = pl.multiple_of(rank - lax.rem(lax.axis_index("query"), 2) * rank, rank)
     factor, scale = scaled(factors[pl.ds(there, rank), :])
@@ -344,11 +341,9 @@
         out_ref[...] = share.astype(out_ref.dtype)
 
 
-def score_shares(
-    own, own_other, mine, other, queries_t, near_queries_t, own_plain, half, rank, row_count
-):
+def score_shares(own, own_other, mine, other, queries_t, own_plain, half, rank, row_count):
     blocks, tok = mine.shape[0] + 1, mine.shape[2]
-    count, rows = queries_t.shape
+    count, depth = queries_t.shape
     return pl.pallas_call(
         functools.partial(share_kernel, row_count),
         out_shape=[
@@ -358,11 +353,11 @@
         scratch_shapes=[
             pltpu.VMEM((2 * rank, tok * blocks), jnp.float32),
             pltpu.VMEM((1, tok * blocks), jnp.float32),
-            pltpu.VMEM((2, rows, tok * (blocks - 1)), jnp.bfloat16),
+            pltpu.VMEM((depth, tok * (blocks - 1)), jnp.bfloat16),
             pltpu.VMEM((blocks // 2, tok * blocks, tok), jnp.bfloat16),
         ],
         compiler_params=params(26),
-    )(own, own_other, mine, other, queries_t, near_queries_t, own_plain, *half)
+    )(own, own_other, mine, other, queries_t, own_plain, *half)
 
 
 def build_columns(first, act, factors, right):
@@ -499,14 +494,14 @@
     own_other = swapped(own, "query", 1)
     others = [swapped(own, "dp", k) for k in reversed(range(1, dp_count))]
     own_sum = own_tokens_sum(own, own_other, rank, row_count)
-    queries_t, near_queries_t, own_plain = turn_queries(
+    queries_t, own_plain = turn_queries(
         queries, near_queries, own, own_other, rank, row_count
     )
     mine, factors = stack(others, rank, (own_sum, queries_t))
     other = swapped(factors, "query", 1)
     half = half_gram(own, mine, rank)
     shares = score_shares(
-        own, own_other, mine, other, queries_t, near_queries_t, own_plain, half, rank, row_count
+        own, own_other, mine, other, queries_t, own_plain, half, rank, row_count
     )
     arrived = [swapped(share, "dp", 2 * n) for n, share in enumerate(shares) if n]
     hessian = hessian_rows(mine, other, own_sum, rank, row_count)

time: 33.9 us -> 34 us (level)
  no operation moved by 1% of the time
where the time goes in v23:
time: 34 us; the launch traced here: 33.8 us
  Pallas kernels  17 us (50%)
  starting transfers between devices  10.5 us (31%)
  waiting for transfers between devices  4.89 us (14%)
  other arithmetic  0.74 us (2%)
  between operations  0.74 us (2%)
    ppermute x9, starting transfers between devices, swapped(): lax.ppermute(array, axis, [(i, i ^ distance) for i in range(lax.axis_size...  10.5 us
    pallas_call x1, Pallas kernels, hessian_rows(): pl.pallas_call(functools.partial(hessian_kernel, row_count, col_count), o...  7.88 us
    ppermute x9, waiting for transfers between devices, swapped(): lax.ppermute(array, axis, [(i, i ^ distance) for i in range(lax.axis_size...  4.89 us
    pallas_call x1, Pallas kernels, project(): pl.pallas_call(project_kernel, in_specs=[pl.BlockSpec(memory_space=pl.ANY...  2.81 us
    pallas_call x1, Pallas kernels, own_tokens_sum(): pl.pallas_call(functools.partial(own_kernel, row_count, col_count), out_s...  2.4 us
    pallas_call x1, Pallas kernels, score_shares(): pl.pallas_call(functools.partial(share_kernel, row_count), out_shape=[jax...  1.95 us
    pallas_call x1, Pallas kernels, finish_scores(): pl.pallas_call(finish_kernel, out_shape=jax.ShapeDtypeStruct((tok, count)...  0.77 us
    convert_element_type x1, other arithmetic, few_tokens(): jnp.where(live, credit[:, None], 0).astype(jnp.float32).reshape(1, -1)  0.74 us
  transfers between devices with their start and end apart: 9, of which 4 were waited for; matrix products, arithmetic and copies ran while one was open for 2% of the time, Pallas kernels for 42%

profile of v23, /device:TPU:0, one launch (start us, length us, event | category | flops | bytes accessed | tf_op | source)
XLA Modules:
  0.0 33.8 jit_solution(10857619271683316635)
XLA Ops:
  0.6 0.0 copy-start
  0.6 3.1 %collective-permute-start.3 = (bf16[1024,256]{1,0:T(8,128)(2,1)}, bf16[1024,256]{1,0:T(8,128)(2,1)S(1)}, u32[]{:S(2)}, u32[]{:S(2)}) collective-permute-start(bf16[1024,256]{1,0:T(8,128)(2,1)} %query.1), channel_id=1, source_target_pairs={{0,4},{4,0},{8,12},{12,8},{1,5},{5,1},{9,13},{13,9},{2,6},{6,2},{1... | collective-permute-start | bytes 1572872 | tf_op jit(solution)/shard_map/ppermute | solution.py:474
  3.7 2.8 %shard_map.86 = (f32[64,256]{1,0:T(8,128)S(1)}, f32[64,256]{1,0:T(8,128)S(1)}) custom-call(bf16[256,1024]{1,0:T(8,128)(2,1)} %act.1, bf16[256,3584]{1,0:T(8,128)(2,1)} %grad.1, bf16[64,1024]{1,0:T(8,128)(2,1)} %bitcast.5, bf16[64,3584]{1,0:T(8,128)(2,1)} %bitcast.4), custom_call_target="tpu_custom_call" | custom-call | tf_op jit(solution)/shard_map/pallas_call | solution.py:141
  6.5 0.1 collective-permute-start
  6.6 1.2 %collective-permute-done.other_ref = f32[64,256]{1,0:T(8,128)S(1)} collective-permute-done((f32[64,256]{1,0:T(8,128)S(1)}, f32[64,256]{1,0:T(8,128)S(1)}, u32[]{:S(2)}, u32[]{:S(2)}) %collective-permute-start) | collective-permute-done | bytes 65568 | tf_op jit(solution)/shard_map/ppermute | solution.py:474
  7.9 1.6 %collective-permute-start.1 = (f32[64,256]{1,0:T(8,128)S(1)}, f32[64,256]{1,0:T(8,128)S(1)}, u32[]{:S(2)}, u32[]{:S(2)}) collective-permute-start(f32[64,256]{1,0:T(8,128)S(1)} %shard_map.87.one_ref), channel_id=1, source_target_pairs={{0,2},{1,3},{2,0},{3,1},{4,6},{5,7},{6,4},{7,5},{8,10},{9,11},{10,... | collective-permute-start | bytes 196616 | tf_op jit(solution)/shard_map/ppermute | solution.py:474
  9.4 0.7 %fusion = f32[2,128]{1,0:T(2,128)S(1)} fusion(s32[2]{0:T(128)} %param.13, s32[2]{0:T(128)} %param.12), kind=kLoop, calls=%fused_computation.1 | loop fusion | flops 768 | bytes 1040 | tf_op jit(solution)/shard_map/convert_element_type | solution.py:484
  10.2 2.0 %collective-permute-done.1.other_ref = f32[64,256]{1,0:T(8,128)S(1)} collective-permute-done((f32[64,256]{1,0:T(8,128)S(1)}, f32[64,256]{1,0:T(8,128)S(1)}, u32[]{:S(2)}, u32[]{:S(2)}) %collective-permute-start.1) | collective-permute-done | bytes 65568 | tf_op jit(solution)/shard_map/ppermute | solution.py:474
  12.2 0.1 collective-permute-start.2
  12.3 2.5 %collective-permute-start.4 = (bf16[80,256]{1,0:T(8,128)(2,1)S(1)}, bf16[80,256]{1,0:T(8,128)(2,1)S(1)}, u32[]{:S(2)}, u32[]{:S(2)}) collective-permute-start(bf16[80,256]{1,0:T(8,128)(2,1)S(1)} %shard_map.88.own.payload_ref), channel_id=1, source_target_pairs={{0,12},{4,8},{8,4},{12,0},{1,13},{5,9},{9,5},{13,1},{2,14},{6,10},... | collective-permute-start | bytes 122888 | tf_op jit(solution)/shard_map/ppermute | solution.py:474
  14.8 0.2 collective-permute-start.5
  15.0 1.7 %collective-permute-start.6 = (bf16[80,256]{1,0:T(8,128)(2,1)S(1)}, bf16[80,256]{1,0:T(8,128)(2,1)S(1)}, u32[]{:S(2)}, u32[]{:S(2)}) collective-permute-start(bf16[80,256]{1,0:T(8,128)(2,1)S(1)} %shard_map.88.own.payload_ref), channel_id=1, source_target_pairs={{0,4},{4,0},{8,12},{12,8},{1,5},{5,1},{9,13},{13,9},{2,6},{6,2},{1... | collective-permute-start | bytes 122888 | tf_op jit(solution)/shard_map/ppermute | solution.py:474
  16.8 0.0 collective-permute-done.2.own_other
  16.8 2.4 %shard_map.89._.own_sum = f32[1024,4096]{1,0:T(8,128)S(1)} custom-call(bf16[80,256]{1,0:T(8,128)(2,1)S(1)} %shard_map.88.own.payload_ref, bf16[80,256]{1,0:T(8,128)(2,1)S(1)} %collective-permute-done.2.own_other), custom_call_target="tpu_custom_call" | custom-call | tf_op jit(solution)/shard_map/pallas_call | solution.py:388
  19.2 0.0 collective-permute-done.3.near_query
  19.2 0.0 copy-done
  19.2 0.5 %shard_map.90 = (bf16[256,2048]{1,0:T(8,128)(2,1)S(1)}, f32[256,256]{1,0:T(8,128)S(1)}) custom-call(bf16[1024,256]{1,0:T(8,128)(2,1)S(1)} %copy-done, bf16[1024,256]{1,0:T(8,128)(2,1)S(1)} %collective-permute-done.3.near_query, bf16[80,256]{1,0:T(8,128)(2,1)S(1)} %shard_map.88.own.payload_ref, bf16[80,256]{1,0:T(8,128)(2,1)S(1)} %collective-permute-done.2.own_other), custom_call_target="tpu_custom_call" | custom-call | tf_op jit(solution)/shard_map/pallas_call | solution.py:263
  19.7 0.0 collective-permute-done.4.refs_0_
  19.7 1.0 %collective-permute-done.5.refs_1_ = bf16[80,256]{1,0:T(8,128)(2,1)S(1)} collective-permute-done((bf16[80,256]{1,0:T(8,128)(2,1)S(1)}, bf16[80,256]{1,0:T(8,128)(2,1)S(1)}, u32[]{:S(2)}, u32[]{:S(2)}) %collective-permute-start.5) | collective-permute-done | bytes 40992 | tf_op jit(solution)/shard_map/ppermute | solution.py:474
  20.7 0.0 collective-permute-done.6.refs_2_
  20.7 0.1 collective-permute-start.7
  20.8 0.6 %shard_map.93 = (f32[2,1024,256]{2,1,0:T(8,128)S(1)}, f32[8,1024]{1,0:T(8,128)S(1)}, f32[8,128]{1,0:T(8,128)S(1)}) custom-call(bf16[80,256]{1,0:T(8,128)(2,1)S(1)} %shard_map.88.own.payload_ref, bf16[3,80,256]{2,1,0:T(8,128)(2,1)S(1)} %get-tuple-element.16.mine), custom_call_target="tpu_custom_call" | custom-call | tf_op jit(solution)/shard_map/pallas_call | solution.py:301
  21.5 0.6 %collective-permute-done.7.other = bf16[3,64,256]{2,1,0:T(8,128)(2,1)S(1)} collective-permute-done((bf16[3,64,256]{2,1,0:T(8,128)(2,1)S(1)}, bf16[3,64,256]{2,1,0:T(8,128)(2,1)S(1)}, u32[]{:S(2)}, u32[]{:S(2)}) %collective-permute-start.7) | collective-permute-done | bytes 98336 | tf_op jit(solution)/shard_map/ppermute | solution.py:474
  22.1 2.0 %shard_map.94 = (f32[256,256]{1,0:T(8,128)S(1)}, bf16[256,256]{1,0:T(8,128)(2,1)S(1)}) custom-call(bf16[80,256]{1,0:T(8,128)(2,1)S(1)} %shard_map.88.own.payload_ref, bf16[80,256]{1,0:T(8,128)(2,1)S(1)} %collective-permute-done.2.own_other, bf16[3,80,256]{2,1,0:T(8,128)(2,1)S(1)} %get-tuple-element.16.mine, ...), custom_call_target="tpu_custom_call" | custom-call | tf_op jit(solution)/shard_map/pallas_call | solution.py:347
  24.0 1.1 %collective-permute-start.8 = (bf16[256,256]{1,0:T(8,128)(2,1)S(1)}, bf16[256,256]{1,0:T(8,128)(2,1)S(1)}, u32[]{:S(2)}, u32[]{:S(2)}) collective-permute-start(bf16[256,256]{1,0:T(8,128)(2,1)S(1)} %get-tuple-element.23), channel_id=1, source_target_pairs={{0,8},{4,12},{8,0},{12,4},{1,9},{5,13},{9,1},{13,5},{2,10},{6,14},... | collective-permute-start | bytes 393224 | tf_op jit(solution)/shard_map/ppermute | solution.py:474
  25.2 7.9 %shard_map.92 = f32[1024,4096]{1,0:T(8,128)} custom-call(bf16[3,80,256]{2,1,0:T(8,128)(2,1)S(1)} %get-tuple-element.16.mine, bf16[3,64,256]{2,1,0:T(8,128)(2,1)S(1)} %collective-permute-done.7.other, f32[1024,4096]{1,0:T(8,128)S(1)} %shard_map.89._.own_sum), custom_call_target="tpu_custom_call" | custom-call | tf_op jit(solution)/shard_map/pallas_call | solution.py:438
  33.1 0.0 collective-permute-done.8.refs_1_
  33.1 0.8 %shard_map.95 = bf16[256,256]{1,0:T(8,128)(2,1)} custom-call(bf16[80,256]{1,0:T(8,128)(2,1)S(1)} %shard_map.88.own.payload_ref, f32[256,256]{1,0:T(8,128)S(1)} %get-tuple-element.22.refs_0_, bf16[256,256]{1,0:T(8,128)(2,1)S(1)} %collective-permute-done.8.refs_1_), custom_call_target="tpu_custom_call" | custom-call | tf_op jit(solution)/shard_map/pallas_call | solution.py:466
  (3 shorter events, 0.0 us)
Async XLA Ops:
  0.6 18.5 %copy-start = (bf16[1024,256]{1,0:T(8,128)(2,1)S(1)}, bf16[1024,256]{1,0:T(8,128)(2,1)}, u32[]{:S(2)}) copy-start(bf16[1024,256]{1,0:T(8,128)(2,1)} %query.1) | copy-start | bytes 1572868
  0.6 18.5 %collective-permute-start.3 = (bf16[1024,256]{1,0:T(8,128)(2,1)}, bf16[1024,256]{1,0:T(8,128)(2,1)S(1)}, u32[]{:S(2)}, u32[]{:S(2)}) collective-permute-start(bf16[1024,256]{1,0:T(8,128)(2,1)} %query.1), channel_id=1, source_target_pairs={{0,4},{4,0},{8,12},{12,8},{1,5},{5,1},{9,13},{13,9},{2,6},{6,2},{1... | collective-permute-start | bytes 1572872 | tf_op jit(solution)/shard_map/ppermute | solution.py:474
  6.5 1.3 %collective-permute-start = (f32[64,256]{1,0:T(8,128)S(1)}, f32[64,256]{1,0:T(8,128)S(1)}, u32[]{:S(2)}, u32[]{:S(2)}) collective-permute-start(f32[64,256]{1,0:T(8,128)S(1)} %get-tuple-element.14), channel_id=1, source_target_pairs={{0,1},{1,0},{2,3},{3,2},{4,5},{5,4},{6,7},{7,6},{8,9},{9,8},{10,11... | collective-permute-start | bytes 196616 | tf_op jit(solution)/shard_map/ppermute | solution.py:474
  7.9 4.3 %collective-permute-start.1 = (f32[64,256]{1,0:T(8,128)S(1)}, f32[64,256]{1,0:T(8,128)S(1)}, u32[]{:S(2)}, u32[]{:S(2)}) collective-permute-start(f32[64,256]{1,0:T(8,128)S(1)} %shard_map.87.one_ref), channel_id=1, source_target_pairs={{0,2},{1,3},{2,0},{3,1},{4,6},{5,7},{6,4},{7,5},{8,10},{9,11},{10,... | collective-permute-start | bytes 196616 | tf_op jit(solution)/shard_map/ppermute | solution.py:474
  12.2 4.5 %collective-permute-start.2 = (bf16[80,256]{1,0:T(8,128)(2,1)S(1)}, bf16[80,256]{1,0:T(8,128)(2,1)S(1)}, u32[]{:S(2)}, u32[]{:S(2)}) collective-permute-start(bf16[80,256]{1,0:T(8,128)(2,1)S(1)} %shard_map.88.own.payload_ref), channel_id=1, source_target_pairs={{0,1},{1,0},{2,3},{3,2},{4,5},{5,4},{6,7},{7,6},{8,9},{9,8},{10,11... | collective-permute-start | bytes 122888 | tf_op jit(solution)/shard_map/ppermute | solution.py:474
  12.3 7.4 %collective-permute-start.4 = (bf16[80,256]{1,0:T(8,128)(2,1)S(1)}, bf16[80,256]{1,0:T(8,128)(2,1)S(1)}, u32[]{:S(2)}, u32[]{:S(2)}) collective-permute-start(bf16[80,256]{1,0:T(8,128)(2,1)S(1)} %shard_map.88.own.payload_ref), channel_id=1, source_target_pairs={{0,12},{4,8},{8,4},{12,0},{1,13},{5,9},{9,5},{13,1},{2,14},{6,10},... | collective-permute-start | bytes 122888 | tf_op jit(solution)/shard_map/ppermute | solution.py:474
  14.8 5.8 %collective-permute-start.5 = (bf16[80,256]{1,0:T(8,128)(2,1)S(1)}, bf16[80,256]{1,0:T(8,128)(2,1)S(1)}, u32[]{:S(2)}, u32[]{:S(2)}) collective-permute-start(bf16[80,256]{1,0:T(8,128)(2,1)S(1)} %shard_map.88.own.payload_ref), channel_id=1, source_target_pairs={{0,8},{4,12},{8,0},{12,4},{1,9},{5,13},{9,1},{13,5},{2,10},{6,14},... | collective-permute-start | bytes 122888 | tf_op jit(solution)/shard_map/ppermute | solution.py:474
  15.0 5.7 %collective-permute-start.6 = (bf16[80,256]{1,0:T(8,128)(2,1)S(1)}, bf16[80,256]{1,0:T(8,128)(2,1)S(1)}, u32[]{:S(2)}, u32[]{:S(2)}) collective-permute-start(bf16[80,256]{1,0:T(8,128)(2,1)S(1)} %shard_map.88.own.payload_ref), channel_id=1, source_target_pairs={{0,4},{4,0},{8,12},{12,8},{1,5},{5,1},{9,13},{13,9},{2,6},{6,2},{1... | collective-permute-start | bytes 122888 | tf_op jit(solution)/shard_map/ppermute | solution.py:474
  20.7 1.4 %collective-permute-start.7 = (bf16[3,64,256]{2,1,0:T(8,128)(2,1)S(1)}, bf16[3,64,256]{2,1,0:T(8,128)(2,1)S(1)}, u32[]{:S(2)}, u32[]{:S(2)}) collective-permute-start(bf16[3,64,256]{2,1,0:T(8,128)(2,1)S(1)} %get-tuple-element.17), channel_id=1, source_target_pairs={{0,1},{1,0},{2,3},{3,2},{4,5},{5,4},{6,7},{7,6},{8,9},{9,8},{10,11... | collective-permute-start | bytes 294920 | tf_op jit(solution)/shard_map/ppermute | solution.py:474
  24.0 9.0 %collective-permute-start.8 = (bf16[256,256]{1,0:T(8,128)(2,1)S(1)}, bf16[256,256]{1,0:T(8,128)(2,1)S(1)}, u32[]{:S(2)}, u32[]{:S(2)}) collective-permute-start(bf16[256,256]{1,0:T(8,128)(2,1)S(1)} %get-tuple-element.23), channel_id=1, source_target_pairs={{0,8},{4,12},{8,0},{12,4},{1,9},{5,13},{9,1},{13,5},{2,10},{6,14},... | collective-permute-start | bytes 393224 | tf_op jit(solution)/shard_map/ppermute | solution.py:474

commit v24 on v23

--- a/solution.py
+++ b/solution.py
@@ -110,10 +110,10 @@
 
 
 def project_kernel(act, grad, pin, pout, keep_ref, send_ref, act_v, grad_v, pin_v, pout_v, sems):
-    half = grad.shape[0] // 2
-    spans = [pl.ds(0, half), pl.ds(half, half)]
+    chunk = grad.shape[1] // 2
+    spans = [pl.ds(0, chunk), pl.ds(chunk, chunk)]
     pairs = [(pin, pin_v), (act, act_v), (pout, pout_v)]
-    pairs += [(grad.at[span], grad_v.at[span]) for span in spans]
+    pairs += [(grad.at[:, span], grad_v.at[:, span]) for span in spans]
     copies = [pltpu.make_async_copy(s, d, sems.at[n]) for n, (s, d) in enumerate(pairs)]
     for copy in copies:
         copy.start()
@@ -121,13 +121,12 @@
     copies[1].wait()
     part_act = lax.dot_general(pin_v[...], act_v[...], NT, preferred_element_type=jnp.float32)
     copies[2].wait()
-    parts = []
+    part_grad = jnp.zeros_like(part_act)
     for copy, span in zip(copies[3:], spans):
         copy.wait()
-        parts.append(
-            lax.dot_general(pout_v[...], grad_v[span], NT, preferred_element_type=jnp.float32)
+        part_grad += lax.dot_general(
+            pout_v[:, span], grad_v[:, span], NT, preferred_element_type=jnp.float32
         )
-    part_grad = jnp.concatenate(parts, axis=1)
     even = lax.rem(lax.axis_index("query"), 2) == 0
     keep_ref[...] = jnp.where(even, part_act, part_grad)
     send_ref[...] = jnp.where(even, part_grad, part_act)
@@ -180,6 +179,20 @@
     )(one, other, weight)
 
 
+def pass_kernel(_, __, part, out_ref):
+    out_ref[...] = part[: out_ref.shape[0]]
+
+
+def pass_factors(part, rank, after):
+    anywhere = pl.BlockSpec(memory_space=pl.ANY)
+    return pl.pallas_call(
+        pass_kernel,
+        in_specs=[anywhere, anywhere, pl.BlockSpec(memory_space=pltpu.VMEM)],
+        out_shape=jax.ShapeDtypeStruct((rank, part.shape[1]), part.dtype),
+        compiler_params=params(26),
+    )(*after, part)
+
+
 def stack_kernel(_, __, *refs):
     parts, (out_ref, factors_ref) = refs[:-2], refs[-2:]
     for k, ref in enumerate(parts):
@@ -212,8 +225,9 @@
         weights[:, span] = mine[rank:].astype(jnp.float32)[:1]
 
 
-def block_pairs(mine, other):
-    return [(mine.at[k], other.at[k]) for k in reversed(range(mine.shape[0]))]
+def block_pairs(far, far_other, mine, other):
+    near = [(mine.at[k], other.at[k]) for k in reversed(range(mine.shape[0]))]
+    return near + [(far, far_other)]
 
 
 def weigh_rows(first_row, end_row, row_count, factors, weights, weighted):
@@ -277,9 +291,10 @@
     return values * scale, scale
 
 
-def half_kernel(own, mine, gram_ref, norm_ref, scale_ref, values):
+def half_kernel(own, far, mine, gram_ref, norm_ref, scale_ref, values):
     rank, tok = values.shape[0], own.shape[1]
-    for k, part in enumerate([own] + [mine.at[k] for k in reversed(range(mine.shape[0]))]):
+    near = [mine.at[k] for k in reversed(range(mine.shape[0]))]
+    for k, part in enumerate([own] + near + [far]):
         values[:, k * tok : (k + 1) * tok] = part[:rank].astype(jnp.float32)
     factor, scale = scaled(values[...])
     scale_ref[...] = jnp.broadcast_to(scale, scale_ref.shape)
@@ -295,8 +310,8 @@
             )
 
 
-def half_gram(own, mine, rank):
-    blocks, tok = mine.shape[0] + 1, own.shape[1]
+def half_gram(own, far, mine, rank):
+    blocks, tok = mine.shape[0] + 2, own.shape[1]
     tokens = blocks * tok
     return pl.pallas_call(
         half_kernel,
@@ -307,15 +322,16 @@
         ],
         scratch_shapes=[pltpu.VMEM((rank, tokens), jnp.float32)],
         compiler_params=params(26),
-    )(own, mine)
-
-
-def share_kernel(row_count, own, own_other, mine, other, query_ref, own_plain_ref, *refs):
-    half_gram_ref, half_norm_ref, half_scale_ref = refs[:3]
-    refs = refs[3:]
+    )(own, far, mine)
+
+
+def share_kernel(row_count, own, own_other, far, far_other, mine, other, *refs):
+    query_ref, own_plain_ref = refs[:2]
+    half_gram_ref, half_norm_ref, half_scale_ref = refs[2:5]
+    refs = refs[5:]
     factors, weights, features, gram = refs[-4:]
     out_refs = refs[:-4]
-    lay_out_factors([(own, own_other)] + block_pairs(mine, other), factors, weights)
+    lay_out_factors([(own, own_other)] + block_pairs(far, far_other, mine, other), factors, weights)
     rank = factors.shape[0] // 2
     tokens = factors.shape[1]
     tok = own.shape[1]
@@ -341,8 +357,9 @@
         out_ref[...] = share.astype(out_ref.dtype)
 
 
-def score_shares(own, own_other, mine, other, queries_t, own_plain, half, rank, row_count):
-    blocks, tok = mine.shape[0] + 1, mine.shape[2]
+def score_shares(factors, queries_t, own_plain, half, rank, row_count):
+    mine = factors[-1]
+    blocks, tok = mine.shape[0] + 2, mine.shape[2]
     count, depth = queries_t.shape
     return pl.pallas_call(
         functools.partial(share_kernel, row_count),
@@ -357,7 +374,7 @@
             pltpu.VMEM((blocks // 2, tok * blocks, tok), jnp.bfloat16),
         ],
         compiler_params=params(26),
-    )(own, own_other, mine, other, queries_t, own_plain, *half)
+    )(*factors, queries_t, own_plain, *half)
 
 
 def build_columns(first, act, factors, right):
@@ -399,14 +416,16 @@
     )(own, own_other)
 
 
-def hessian_kernel(row_count, col_count, mine, other, own_sum, out, *scratch):
+def hessian_kernel(
+    row_count, col_count, far, far_other, mine, other, own_sum, out, *scratch
+):
     factors, weights, weighted, rights = *scratch[:3], scratch[3:5]
     result, sems = scratch[5:]
     rank = factors.shape[0] // 2
-    blocks = mine.shape[0]
+    blocks = mine.shape[0] + 1
     tokens = factors.shape[1] // blocks * (blocks + 1)
     rows, cols = row_count * rank, col_count * rank
-    lay_out_factors(block_pairs(mine, other), factors, weights)
+    lay_out_factors(block_pairs(far, far_other, mine, other), factors, weights)
     act = factors[:rank, :]
     copies = []
     build_columns(0, act, factors, rights[0])
@@ -431,8 +450,9 @@
         copy.wait()
 
 
-def hessian_rows(mine, other, own_sum, rank, row_count, col_count=8):
-    blocks, _, tok = mine.shape
+def hessian_rows(factors, own_sum, rank, row_count, col_count=8):
+    mine = factors[-1]
+    blocks, tok = mine.shape[0] + 1, mine.shape[2]
     feat = rank * rank
     rows, cols = row_count * rank, col_count * rank
     return pl.pallas_call(
@@ -449,7 +469,7 @@
             pltpu.SemaphoreType.DMA((feat // cols * (rows // TILE),)),
         ],
         compiler_params=params(26),
-    )(mine, other, own_sum)
+    )(*factors, own_sum)
 
 
 def finish_kernel(payload_ref, *refs):
@@ -497,14 +517,18 @@
     queries_t, own_plain = turn_queries(
         queries, near_queries, own, own_other, rank, row_count
     )
-    mine, factors = stack(others, rank, (own_sum, queries_t))
-    other = swapped(factors, "query", 1)
-    half = half_gram(own, mine, rank)
+    far = others[0]
+    far_send = pass_factors(far, rank, (own_sum, queries_t))
+    far_other = swapped(far_send, "query", 1)
+    mine, send = stack(others[1:], rank, (own_sum, far_other))
+    other = swapped(send, "query", 1)
+    half = half_gram(own, far, mine, rank)
+    factors = (far, far_other, mine, other)
     shares = score_shares(
-        own, own_other, mine, other, queries_t, own_plain, half, rank, row_count
+        (own, own_other) + factors, queries_t, own_plain, half, rank, row_count
     )
     arrived = [swapped(share, "dp", 2 * n) for n, share in enumerate(shares) if n]
-    hessian = hessian_rows(mine, other, own_sum, rank, row_count)
+    hessian = hessian_rows(factors, own_sum, rank, row_count)
     return hessian, finish_scores(own, [shares[0]] + arrived)
 
 
@@ -515,7 +539,7 @@
 def per_device(activations, *others):
     rank = others[1].shape[1]
     dp_count, query_count = lax.axis_size("dp"), lax.axis_size("query")
-    pairs = min(dp_count, query_count) > 1 and power_of_two(dp_count) and power_of_two(query_count)
+    pairs = dp_count > 2 and query_count > 1 and power_of_two(dp_count) and power_of_two(query_count)
     if pairs and activations.shape[0] * dp_count <= rank * rank:
         return few_tokens(activations, *others)
     return many_tokens(activations, *others)

time: 34 us -> 35.3 us (1.038)
  starting transfers between devices: 10.5 us -> 11.3 us
  Pallas kernels: 17 us -> 17.4 us
    ppermute x9 -> x10, starting transfers between devices: 10.5 us -> 11.3 us  [swapped(): lax.ppermute(array, axis, [(i, i ^ distance) for i in range(lax.axis_size...]
    pallas_call x1, Pallas kernels: 7.88 us -> 8.46 us  [hessian_rows(): pl.pallas_call(functools.partial(hessian_kernel, row_count, col_count), o...]
    ppermute x9 -> x10, waiting for transfers between devices: 4.89 us -> 4.93 us  [swapped(): lax.ppermute(array, axis, [(i, i ^ distance) for i in range(lax.axis_size...]
  transfers between devices with their start and end apart: 9 -> 10, of which waited for: 4 -> 5; matrix products, arithmetic and copies ran while one was open for 2% -> 2% of each run, Pallas kernels for 42% -> 42%
where the time goes in v24:
time: 35.3 us; the launch traced here: 35.1 us
  Pallas kernels  17.4 us (49%)
  starting transfers between devices  11.3 us (32%)
  waiting for transfers between devices  4.93 us (14%)
  between operations  0.75 us (2%)
  other arithmetic  0.74 us (2%)
    ppermute x10, starting transfers between devices, swapped(): lax.ppermute(array, axis, [(i, i ^ distance) for i in range(lax.axis_size...  11.3 us
    pallas_call x1, Pallas kernels, hessian_rows(): pl.pallas_call(functools.partial(hessian_kernel, row_count, col_count), o...  8.46 us
    ppermute x10, waiting for transfers between devices, swapped(): lax.ppermute(array, axis, [(i, i ^ distance) for i in range(lax.axis_size...  4.93 us
    pallas_call x1, Pallas kernels, project(): pl.pallas_call(project_kernel, in_specs=[pl.BlockSpec(memory_space=pl.ANY...  2.66 us
    pallas_call x1, Pallas kernels, own_tokens_sum(): pl.pallas_call(functools.partial(own_kernel, row_count, col_count), out_s...  2.4 us
    pallas_call x1, Pallas kernels, score_shares(): pl.pallas_call(functools.partial(share_kernel, row_count), out_shape=[jax...  1.96 us
    pallas_call x1, Pallas kernels, finish_scores(): pl.pallas_call(finish_kernel, out_shape=jax.ShapeDtypeStruct((tok, count)...  0.77 us
    convert_element_type x1, other arithmetic, few_tokens(): jnp.where(live, credit[:, None], 0).astype(jnp.float32).reshape(1, -1)  0.74 us
  transfers between devices with their start and end apart: 10, of which 5 were waited for; matrix products, arithmetic and copies ran while one was open for 2% of the time, Pallas kernels for 42%

profile of v24, /device:TPU:0, one launch (start us, length us, event | category | flops | bytes accessed | tf_op | source)
XLA Modules:
  0.0 35.1 jit_solution(18102413580159086149)
XLA Ops:
  0.6 0.0 copy-start
  0.6 3.1 %collective-permute-start.4 = (bf16[1024,256]{1,0:T(8,128)(2,1)}, bf16[1024,256]{1,0:T(8,128)(2,1)S(1)}, u32[]{:S(2)}, u32[]{:S(2)}) collective-permute-start(bf16[1024,256]{1,0:T(8,128)(2,1)} %query.1), channel_id=1, source_target_pairs={{0,4},{4,0},{8,12},{12,8},{1,5},{5,1},{9,13},{13,9},{2,6},{6,2},{1... | collective-permute-start | bytes 1572872 | tf_op jit(solution)/shard_map/ppermute | solution.py:494
  3.7 2.7 %shard_map.86 = (f32[64,256]{1,0:T(8,128)S(1)}, f32[64,256]{1,0:T(8,128)S(1)}) custom-call(bf16[256,1024]{1,0:T(8,128)(2,1)} %act.1, bf16[256,3584]{1,0:T(8,128)(2,1)} %grad.1, bf16[64,1024]{1,0:T(8,128)(2,1)} %bitcast.5, bf16[64,3584]{1,0:T(8,128)(2,1)} %bitcast.4), custom_call_target="tpu_custom_call" | custom-call | tf_op jit(solution)/shard_map/pallas_call | solution.py:140
  6.4 0.1 collective-permute-start
  6.5 1.2 %collective-permute-done.other_ref = f32[64,256]{1,0:T(8,128)S(1)} collective-permute-done((f32[64,256]{1,0:T(8,128)S(1)}, f32[64,256]{1,0:T(8,128)S(1)}, u32[]{:S(2)}, u32[]{:S(2)}) %collective-permute-start) | collective-permute-done | bytes 65568 | tf_op jit(solution)/shard_map/ppermute | solution.py:494
  7.7 1.6 %collective-permute-start.1 = (f32[64,256]{1,0:T(8,128)S(1)}, f32[64,256]{1,0:T(8,128)S(1)}, u32[]{:S(2)}, u32[]{:S(2)}) collective-permute-start(f32[64,256]{1,0:T(8,128)S(1)} %shard_map.87.one_ref), channel_id=1, source_target_pairs={{0,2},{1,3},{2,0},{3,1},{4,6},{5,7},{6,4},{7,5},{8,10},{9,11},{10,... | collective-permute-start | bytes 196616 | tf_op jit(solution)/shard_map/ppermute | solution.py:494
  9.3 0.7 %fusion = f32[2,128]{1,0:T(2,128)S(1)} fusion(s32[2]{0:T(128)} %param.13, s32[2]{0:T(128)} %param.12), kind=kLoop, calls=%fused_computation.1 | loop fusion | flops 768 | bytes 1040 | tf_op jit(solution)/shard_map/convert_element_type | solution.py:504
  10.0 2.0 %collective-permute-done.1.other_ref = f32[64,256]{1,0:T(8,128)S(1)} collective-permute-done((f32[64,256]{1,0:T(8,128)S(1)}, f32[64,256]{1,0:T(8,128)S(1)}, u32[]{:S(2)}, u32[]{:S(2)}) %collective-permute-start.1) | collective-permute-done | bytes 65568 | tf_op jit(solution)/shard_map/ppermute | solution.py:494
  12.1 0.1 collective-permute-start.3
  12.2 2.5 %collective-permute-start.2 = (bf16[80,256]{1,0:T(8,128)(2,1)S(1)}, bf16[80,256]{1,0:T(8,128)(2,1)S(1)}, u32[]{:S(2)}, u32[]{:S(2)}) collective-permute-start(bf16[80,256]{1,0:T(8,128)(2,1)S(1)} %shard_map.88.own.payload_ref), channel_id=1, source_target_pairs={{0,12},{4,8},{8,4},{12,0},{1,13},{5,9},{9,5},{13,1},{2,14},{6,10},... | collective-permute-start | bytes 122888 | tf_op jit(solution)/shard_map/ppermute | solution.py:494
  14.7 0.2 collective-permute-start.6
  14.9 1.7 %collective-permute-start.7 = (bf16[80,256]{1,0:T(8,128)(2,1)S(1)}, bf16[80,256]{1,0:T(8,128)(2,1)S(1)}, u32[]{:S(2)}, u32[]{:S(2)}) collective-permute-start(bf16[80,256]{1,0:T(8,128)(2,1)S(1)} %shard_map.88.own.payload_ref), channel_id=1, source_target_pairs={{0,4},{4,0},{8,12},{12,8},{1,5},{5,1},{9,13},{13,9},{2,6},{6,2},{1... | collective-permute-start | bytes 122888 | tf_op jit(solution)/shard_map/ppermute | solution.py:494
  16.6 0.0 collective-permute-done.3.own_other
  16.6 2.4 %shard_map.89._.own_sum = f32[1024,4096]{1,0:T(8,128)S(1)} custom-call(bf16[80,256]{1,0:T(8,128)(2,1)S(1)} %shard_map.88.own.payload_ref, bf16[80,256]{1,0:T(8,128)(2,1)S(1)} %collective-permute-done.3.own_other), custom_call_target="tpu_custom_call" | custom-call | tf_op jit(solution)/shard_map/pallas_call | solution.py:405
  19.0 0.0 collective-permute-done.4.near_query
  19.0 0.0 copy-done
  19.0 0.5 %shard_map.90 = (bf16[256,2048]{1,0:T(8,128)(2,1)S(1)}, f32[256,256]{1,0:T(8,128)S(1)}) custom-call(bf16[1024,256]{1,0:T(8,128)(2,1)S(1)} %copy-done, bf16[1024,256]{1,0:T(8,128)(2,1)S(1)} %collective-permute-done.4.near_query, bf16[80,256]{1,0:T(8,128)(2,1)S(1)} %shard_map.88.own.payload_ref, bf16[80,256]{1,0:T(8,128)(2,1)S(1)} %collective-permute-done.3.own_other), custom_call_target="tpu_custom_call" | custom-call | tf_op jit(solution)/shard_map/pallas_call | solution.py:277
  19.5 0.0 collective-permute-done.2.part.far
  19.6 0.1 collective-permute-start.5
  19.6 0.9 %collective-permute-done.6.refs_0_ = bf16[80,256]{1,0:T(8,128)(2,1)S(1)} collective-permute-done((bf16[80,256]{1,0:T(8,128)(2,1)S(1)}, bf16[80,256]{1,0:T(8,128)(2,1)S(1)}, u32[]{:S(2)}, u32[]{:S(2)}) %collective-permute-start.6) | collective-permute-done | bytes 40992 | tf_op jit(solution)/shard_map/ppermute | solution.py:494
  20.6 0.0 collective-permute-done.7.refs_1_
  20.6 0.3 collective-permute-done.5.__.far_other
  20.9 0.2 collective-permute-start.8
  21.1 0.6 %shard_map.94 = (f32[2,1024,256]{2,1,0:T(8,128)S(1)}, f32[8,1024]{1,0:T(8,128)S(1)}, f32[8,128]{1,0:T(8,128)S(1)}) custom-call(bf16[80,256]{1,0:T(8,128)(2,1)S(1)} %shard_map.88.own.payload_ref, bf16[80,256]{1,0:T(8,128)(2,1)S(1)} %collective-permute-done.2.part.far, bf16[2,80,256]{2,1,0:T(8,128)(2,1)S(1)} %get-tuple-element.16.mine), custom_call_target="tpu_custom_call" | custom-call | tf_op jit(solution)/shard_map/pallas_call | solution.py:316
  21.7 0.5 %collective-permute-done.8.other = bf16[2,64,256]{2,1,0:T(8,128)(2,1)S(1)} collective-permute-done((bf16[2,64,256]{2,1,0:T(8,128)(2,1)S(1)}, bf16[2,64,256]{2,1,0:T(8,128)(2,1)S(1)}, u32[]{:S(2)}, u32[]{:S(2)}) %collective-permute-start.8) | collective-permute-done | bytes 65568 | tf_op jit(solution)/shard_map/ppermute | solution.py:494
  22.2 2.0 %shard_map.95 = (f32[256,256]{1,0:T(8,128)S(1)}, bf16[256,256]{1,0:T(8,128)(2,1)S(1)}) custom-call(bf16[80,256]{1,0:T(8,128)(2,1)S(1)} %shard_map.88.own.payload_ref, bf16[80,256]{1,0:T(8,128)(2,1)S(1)} %collective-permute-done.3.own_other, bf16[80,256]{1,0:T(8,128)(2,1)S(1)} %collective-permute-done.2.part.far, ...), custom_call_target="tpu_custom_call" | custom-call | tf_op jit(solution)/shard_map/pallas_call | solution.py:364
  24.1 1.8 %collective-permute-start.9 = (bf16[256,256]{1,0:T(8,128)(2,1)S(1)}, bf16[256,256]{1,0:T(8,128)(2,1)S(1)}, u32[]{:S(2)}, u32[]{:S(2)}) collective-permute-start(bf16[256,256]{1,0:T(8,128)(2,1)S(1)} %get-tuple-element.23), channel_id=1, source_target_pairs={{0,8},{4,12},{8,0},{12,4},{1,9},{5,13},{9,1},{13,5},{2,10},{6,14},... | collective-permute-start | bytes 393224 | tf_op jit(solution)/shard_map/ppermute | solution.py:494
  25.9 8.5 %shard_map.93 = f32[1024,4096]{1,0:T(8,128)} custom-call(bf16[80,256]{1,0:T(8,128)(2,1)S(1)} %collective-permute-done.2.part.far, bf16[64,256]{1,0:T(8,128)(2,1)S(1)} %collective-permute-done.5.__.far_other, bf16[2,80,256]{2,1,0:T(8,128)(2,1)S(1)} %get-tuple-element.16.mine, bf16[2,64,256]{2,1,0:T(8,128)(2,1)S(1)} %collective-permute-done.8.other, ...), custom_call_target="tpu_custom_call" | custom-call | tf_op jit(solution)/shard_map/pallas_call | solution.py:458
  34.4 0.0 collective-permute-done.9.refs_1_
  34.4 0.8 %shard_map.96 = bf16[256,256]{1,0:T(8,128)(2,1)} custom-call(bf16[80,256]{1,0:T(8,128)(2,1)S(1)} %shard_map.88.own.payload_ref, f32[256,256]{1,0:T(8,128)S(1)} %get-tuple-element.22.refs_0_, bf16[256,256]{1,0:T(8,128)(2,1)S(1)} %collective-permute-done.9.refs_1_), custom_call_target="tpu_custom_call" | custom-call | tf_op jit(solution)/shard_map/pallas_call | solution.py:486
  (4 shorter events, 0.0 us)
Async XLA Ops:
  0.6 18.4 %copy-start = (bf16[1024,256]{1,0:T(8,128)(2,1)S(1)}, bf16[1024,256]{1,0:T(8,128)(2,1)}, u32[]{:S(2)}) copy-start(bf16[1024,256]{1,0:T(8,128)(2,1)} %query.1) | copy-start | bytes 1572868
  0.6 18.4 %collective-permute-start.4 = (bf16[1024,256]{1,0:T(8,128)(2,1)}, bf16[1024,256]{1,0:T(8,128)(2,1)S(1)}, u32[]{:S(2)}, u32[]{:S(2)}) collective-permute-start(bf16[1024,256]{1,0:T(8,128)(2,1)} %query.1), channel_id=1, source_target_pairs={{0,4},{4,0},{8,12},{12,8},{1,5},{5,1},{9,13},{13,9},{2,6},{6,2},{1... | collective-permute-start | bytes 1572872 | tf_op jit(solution)/shard_map/ppermute | solution.py:494
  6.4 1.3 %collective-permute-start = (f32[64,256]{1,0:T(8,128)S(1)}, f32[64,256]{1,0:T(8,128)S(1)}, u32[]{:S(2)}, u32[]{:S(2)}) collective-permute-start(f32[64,256]{1,0:T(8,128)S(1)} %get-tuple-element.14), channel_id=1, source_target_pairs={{0,1},{1,0},{2,3},{3,2},{4,5},{5,4},{6,7},{7,6},{8,9},{9,8},{10,11... | collective-permute-start | bytes 196616 | tf_op jit(solution)/shard_map/ppermute | solution.py:494
  7.7 4.3 %collective-permute-start.1 = (f32[64,256]{1,0:T(8,128)S(1)}, f32[64,256]{1,0:T(8,128)S(1)}, u32[]{:S(2)}, u32[]{:S(2)}) collective-permute-start(f32[64,256]{1,0:T(8,128)S(1)} %shard_map.87.one_ref), channel_id=1, source_target_pairs={{0,2},{1,3},{2,0},{3,1},{4,6},{5,7},{6,4},{7,5},{8,10},{9,11},{10,... | collective-permute-start | bytes 196616 | tf_op jit(solution)/shard_map/ppermute | solution.py:494
  12.1 4.5 %collective-permute-start.3 = (bf16[80,256]{1,0:T(8,128)(2,1)S(1)}, bf16[80,256]{1,0:T(8,128)(2,1)S(1)}, u32[]{:S(2)}, u32[]{:S(2)}) collective-permute-start(bf16[80,256]{1,0:T(8,128)(2,1)S(1)} %shard_map.88.own.payload_ref), channel_id=1, source_target_pairs={{0,1},{1,0},{2,3},{3,2},{4,5},{5,4},{6,7},{7,6},{8,9},{9,8},{10,11... | collective-permute-start | bytes 122888 | tf_op jit(solution)/shard_map/ppermute | solution.py:494
  12.2 7.4 %collective-permute-start.2 = (bf16[80,256]{1,0:T(8,128)(2,1)S(1)}, bf16[80,256]{1,0:T(8,128)(2,1)S(1)}, u32[]{:S(2)}, u32[]{:S(2)}) collective-permute-start(bf16[80,256]{1,0:T(8,128)(2,1)S(1)} %shard_map.88.own.payload_ref), channel_id=1, source_target_pairs={{0,12},{4,8},{8,4},{12,0},{1,13},{5,9},{9,5},{13,1},{2,14},{6,10},... | collective-permute-start | bytes 122888 | tf_op jit(solution)/shard_map/ppermute | solution.py:494
  14.7 5.9 %collective-permute-start.6 = (bf16[80,256]{1,0:T(8,128)(2,1)S(1)}, bf16[80,256]{1,0:T(8,128)(2,1)S(1)}, u32[]{:S(2)}, u32[]{:S(2)}) collective-permute-start(bf16[80,256]{1,0:T(8,128)(2,1)S(1)} %shard_map.88.own.payload_ref), channel_id=1, source_target_pairs={{0,8},{4,12},{8,0},{12,4},{1,9},{5,13},{9,1},{13,5},{2,10},{6,14},... | collective-permute-start | bytes 122888 | tf_op jit(solution)/shard_map/ppermute | solution.py:494
  14.9 5.7 %collective-permute-start.7 = (bf16[80,256]{1,0:T(8,128)(2,1)S(1)}, bf16[80,256]{1,0:T(8,128)(2,1)S(1)}, u32[]{:S(2)}, u32[]{:S(2)}) collective-permute-start(bf16[80,256]{1,0:T(8,128)(2,1)S(1)} %shard_map.88.own.payload_ref), channel_id=1, source_target_pairs={{0,4},{4,0},{8,12},{12,8},{1,5},{5,1},{9,13},{13,9},{2,6},{6,2},{1... | collective-permute-start | bytes 122888 | tf_op jit(solution)/shard_map/ppermute | solution.py:494
  19.6 1.3 %collective-permute-start.5 = (bf16[64,256]{1,0:T(8,128)(2,1)S(1)}, bf16[64,256]{1,0:T(8,128)(2,1)S(1)}, u32[]{:S(2)}, u32[]{:S(2)}) collective-permute-start(bf16[64,256]{1,0:T(8,128)(2,1)S(1)} %shard_map.91), channel_id=1, source_target_pairs={{0,1},{1,0},{2,3},{3,2},{4,5},{5,4},{6,7},{7,6},{8,9},{9,8},{10,11... | collective-permute-start | bytes 98312 | tf_op jit(solution)/shard_map/ppermute | solution.py:494
  20.9 1.3 %collective-permute-start.8 = (bf16[2,64,256]{2,1,0:T(8,128)(2,1)S(1)}, bf16[2,64,256]{2,1,0:T(8,128)(2,1)S(1)}, u32[]{:S(2)}, u32[]{:S(2)}) collective-permute-start(bf16[2,64,256]{2,1,0:T(8,128)(2,1)S(1)} %get-tuple-element.17), channel_id=1, source_target_pairs={{0,1},{1,0},{2,3},{3,2},{4,5},{5,4},{6,7},{7,6},{8,9},{9,8},{10,11... | collective-permute-start | bytes 196616 | tf_op jit(solution)/shard_map/ppermute | solution.py:494
  24.1 10.2 %collective-permute-start.9 = (bf16[256,256]{1,0:T(8,128)(2,1)S(1)}, bf16[256,256]{1,0:T(8,128)(2,1)S(1)}, u32[]{:S(2)}, u32[]{:S(2)}) collective-permute-start(bf16[256,256]{1,0:T(8,128)(2,1)S(1)} %get-tuple-element.23), channel_id=1, source_target_pairs={{0,8},{4,12},{8,0},{12,4},{1,9},{5,13},{9,1},{13,5},{2,10},{6,14},... | collective-permute-start | bytes 393224 | tf_op jit(solution)/shard_map/ppermute | solution.py:494

commit v25 on v23

--- a/solution.py
+++ b/solution.py
@@ -110,10 +110,12 @@
 
 
 def project_kernel(act, grad, pin, pout, keep_ref, send_ref, act_v, grad_v, pin_v, pout_v, sems):
-    half = grad.shape[0] // 2
-    spans = [pl.ds(0, half), pl.ds(half, half)]
+    unit = grad.shape[1] // 7
+    spans = [pl.ds(0, unit), pl.ds(unit, 2 * unit), pl.ds(3 * unit, 4 * unit)]
+    if grad.shape[1] % 7 or unit % 128:
+        spans = [pl.ds(0, grad.shape[1])]
     pairs = [(pin, pin_v), (act, act_v), (pout, pout_v)]
-    pairs += [(grad.at[span], grad_v.at[span]) for span in spans]
+    pairs += [(grad.at[:, span], grad_v.at[:, span]) for span in spans]
     copies = [pltpu.make_async_copy(s, d, sems.at[n]) for n, (s, d) in enumerate(pairs)]
     for copy in copies:
         copy.start()
@@ -121,13 +123,12 @@
     copies[1].wait()
     part_act = lax.dot_general(pin_v[...], act_v[...], NT, preferred_element_type=jnp.float32)
     copies[2].wait()
-    parts = []
+    part_grad = jnp.zeros_like(part_act)
     for copy, span in zip(copies[3:], spans):
         copy.wait()
-        parts.append(
-            lax.dot_general(pout_v[...], grad_v[span], NT, preferred_element_type=jnp.float32)
+        part_grad += lax.dot_general(
+            pout_v[:, span], grad_v[:, span], NT, preferred_element_type=jnp.float32
         )
-    part_grad = jnp.concatenate(parts, axis=1)
     even = lax.rem(lax.axis_index("query"), 2) == 0
     keep_ref[...] = jnp.where(even, part_act, part_grad)
     send_ref[...] = jnp.where(even, part_grad, part_act)
@@ -147,7 +148,7 @@
             pltpu.VMEM((tok, f_here), jnp.bfloat16),
             pltpu.VMEM((rank, d_here), jnp.bfloat16),
             pltpu.VMEM((rank, f_here), jnp.bfloat16),
-            pltpu.SemaphoreType.DMA((5,)),
+            pltpu.SemaphoreType.DMA((6,)),
         ],
         compiler_params=params(53.75),
     )(activations, out_grads, proj_in_t, proj_out_t)

time: 34 us -> 33.9 us (level)
  no operation moved by 1% of the time
where the time goes in v25:
time: 33.9 us; the launch traced here: 33.8 us
  Pallas kernels  16.9 us (50%)
  starting transfers between devices  10.4 us (31%)
  waiting for transfers between devices  4.93 us (15%)
  between operations  0.75 us (2%)
  other arithmetic  0.74 us (2%)
    ppermute x9, starting transfers between devices, swapped(): lax.ppermute(array, axis, [(i, i ^ distance) for i in range(lax.axis_size...  10.4 us
    pallas_call x1, Pallas kernels, hessian_rows(): pl.pallas_call(functools.partial(hessian_kernel, row_count, col_count), o...  7.88 us
    ppermute x9, waiting for transfers between devices, swapped(): lax.ppermute(array, axis, [(i, i ^ distance) for i in range(lax.axis_size...  4.93 us
    pallas_call x1, Pallas kernels, project(): pl.pallas_call(project_kernel, in_specs=[pl.BlockSpec(memory_space=pl.ANY...  2.74 us
    pallas_call x1, Pallas kernels, own_tokens_sum(): pl.pallas_call(functools.partial(own_kernel, row_count, col_count), out_s...  2.4 us
    pallas_call x1, Pallas kernels, score_shares(): pl.pallas_call(functools.partial(share_kernel, row_count), out_shape=[jax...  1.96 us
    pallas_call x1, Pallas kernels, finish_scores(): pl.pallas_call(finish_kernel, out_shape=jax.ShapeDtypeStruct((tok, count)...  0.77 us
    convert_element_type x1, other arithmetic, few_tokens(): jnp.where(live, credit[:, None], 0).astype(jnp.float32).reshape(1, -1)  0.74 us
  transfers between devices with their start and end apart: 9, of which 4 were waited for; matrix products, arithmetic and copies ran while one was open for 2% of the time, Pallas kernels for 42%

profile of v25, /device:TPU:0, one launch (start us, length us, event | category | flops | bytes accessed | tf_op | source)
XLA Modules:
  0.0 33.8 jit_solution(15291265616768262385)
XLA Ops:
  0.6 0.0 copy-start
  0.6 3.1 %collective-permute-start.3 = (bf16[1024,256]{1,0:T(8,128)(2,1)}, bf16[1024,256]{1,0:T(8,128)(2,1)S(1)}, u32[]{:S(2)}, u32[]{:S(2)}) collective-permute-start(bf16[1024,256]{1,0:T(8,128)(2,1)} %query.1), channel_id=1, source_target_pairs={{0,4},{4,0},{8,12},{12,8},{1,5},{5,1},{9,13},{13,9},{2,6},{6,2},{1... | collective-permute-start | bytes 1572872 | tf_op jit(solution)/shard_map/ppermute | solution.py:475
  3.7 2.7 %shard_map.86 = (f32[64,256]{1,0:T(8,128)S(1)}, f32[64,256]{1,0:T(8,128)S(1)}) custom-call(bf16[256,1024]{1,0:T(8,128)(2,1)} %act.1, bf16[256,3584]{1,0:T(8,128)(2,1)} %grad.1, bf16[64,1024]{1,0:T(8,128)(2,1)} %bitcast.5, bf16[64,3584]{1,0:T(8,128)(2,1)} %bitcast.4), custom_call_target="tpu_custom_call" | custom-call | tf_op jit(solution)/shard_map/pallas_call | solution.py:142
  6.5 0.1 collective-permute-start
  6.6 1.2 %collective-permute-done.other_ref = f32[64,256]{1,0:T(8,128)S(1)} collective-permute-done((f32[64,256]{1,0:T(8,128)S(1)}, f32[64,256]{1,0:T(8,128)S(1)}, u32[]{:S(2)}, u32[]{:S(2)}) %collective-permute-start) | collective-permute-done | bytes 65568 | tf_op jit(solution)/shard_map/ppermute | solution.py:475
  7.8 1.6 %collective-permute-start.1 = (f32[64,256]{1,0:T(8,128)S(1)}, f32[64,256]{1,0:T(8,128)S(1)}, u32[]{:S(2)}, u32[]{:S(2)}) collective-permute-start(f32[64,256]{1,0:T(8,128)S(1)} %shard_map.87.one_ref), channel_id=1, source_target_pairs={{0,2},{1,3},{2,0},{3,1},{4,6},{5,7},{6,4},{7,5},{8,10},{9,11},{10,... | collective-permute-start | bytes 196616 | tf_op jit(solution)/shard_map/ppermute | solution.py:475
  9.4 0.7 %fusion = f32[2,128]{1,0:T(2,128)S(1)} fusion(s32[2]{0:T(128)} %param.13, s32[2]{0:T(128)} %param.12), kind=kLoop, calls=%fused_computation.1 | loop fusion | flops 768 | bytes 1040 | tf_op jit(solution)/shard_map/convert_element_type | solution.py:485
  10.1 2.0 %collective-permute-done.1.other_ref = f32[64,256]{1,0:T(8,128)S(1)} collective-permute-done((f32[64,256]{1,0:T(8,128)S(1)}, f32[64,256]{1,0:T(8,128)S(1)}, u32[]{:S(2)}, u32[]{:S(2)}) %collective-permute-start.1) | collective-permute-done | bytes 65568 | tf_op jit(solution)/shard_map/ppermute | solution.py:475
  12.2 0.1 collective-permute-start.2
  12.2 2.5 %collective-permute-start.4 = (bf16[80,256]{1,0:T(8,128)(2,1)S(1)}, bf16[80,256]{1,0:T(8,128)(2,1)S(1)}, u32[]{:S(2)}, u32[]{:S(2)}) collective-permute-start(bf16[80,256]{1,0:T(8,128)(2,1)S(1)} %shard_map.88.own.payload_ref), channel_id=1, source_target_pairs={{0,12},{4,8},{8,4},{12,0},{1,13},{5,9},{9,5},{13,1},{2,14},{6,10},... | collective-permute-start | bytes 122888 | tf_op jit(solution)/shard_map/ppermute | solution.py:475
  14.8 0.2 collective-permute-start.5
  15.0 1.7 %collective-permute-start.6 = (bf16[80,256]{1,0:T(8,128)(2,1)S(1)}, bf16[80,256]{1,0:T(8,128)(2,1)S(1)}, u32[]{:S(2)}, u32[]{:S(2)}) collective-permute-start(bf16[80,256]{1,0:T(8,128)(2,1)S(1)} %shard_map.88.own.payload_ref), channel_id=1, source_target_pairs={{0,4},{4,0},{8,12},{12,8},{1,5},{5,1},{9,13},{13,9},{2,6},{6,2},{1... | collective-permute-start | bytes 122888 | tf_op jit(solution)/shard_map/ppermute | solution.py:475
  16.7 0.0 collective-permute-done.2.own_other
  16.7 2.4 %shard_map.89._.own_sum = f32[1024,4096]{1,0:T(8,128)S(1)} custom-call(bf16[80,256]{1,0:T(8,128)(2,1)S(1)} %shard_map.88.own.payload_ref, bf16[80,256]{1,0:T(8,128)(2,1)S(1)} %collective-permute-done.2.own_other), custom_call_target="tpu_custom_call" | custom-call | tf_op jit(solution)/shard_map/pallas_call | solution.py:389
  19.1 0.0 collective-permute-done.3.near_query
  19.1 0.0 copy-done
  19.1 0.5 %shard_map.90 = (bf16[256,2048]{1,0:T(8,128)(2,1)S(1)}, f32[256,256]{1,0:T(8,128)S(1)}) custom-call(bf16[1024,256]{1,0:T(8,128)(2,1)S(1)} %copy-done, bf16[1024,256]{1,0:T(8,128)(2,1)S(1)} %collective-permute-done.3.near_query, bf16[80,256]{1,0:T(8,128)(2,1)S(1)} %shard_map.88.own.payload_ref, bf16[80,256]{1,0:T(8,128)(2,1)S(1)} %collective-permute-done.2.own_other), custom_call_target="tpu_custom_call" | custom-call | tf_op jit(solution)/shard_map/pallas_call | solution.py:264
  19.6 0.0 collective-permute-done.4.refs_0_
  19.6 1.0 %collective-permute-done.5.refs_1_ = bf16[80,256]{1,0:T(8,128)(2,1)S(1)} collective-permute-done((bf16[80,256]{1,0:T(8,128)(2,1)S(1)}, bf16[80,256]{1,0:T(8,128)(2,1)S(1)}, u32[]{:S(2)}, u32[]{:S(2)}) %collective-permute-start.5) | collective-permute-done | bytes 40992 | tf_op jit(solution)/shard_map/ppermute | solution.py:475
  20.6 0.0 collective-permute-done.6.refs_2_
  20.7 0.1 collective-permute-start.7
  20.7 0.6 %shard_map.93 = (f32[2,1024,256]{2,1,0:T(8,128)S(1)}, f32[8,1024]{1,0:T(8,128)S(1)}, f32[8,128]{1,0:T(8,128)S(1)}) custom-call(bf16[80,256]{1,0:T(8,128)(2,1)S(1)} %shard_map.88.own.payload_ref, bf16[3,80,256]{2,1,0:T(8,128)(2,1)S(1)} %get-tuple-element.16.mine), custom_call_target="tpu_custom_call" | custom-call | tf_op jit(solution)/shard_map/pallas_call | solution.py:302
  21.4 0.6 %collective-permute-done.7.other = bf16[3,64,256]{2,1,0:T(8,128)(2,1)S(1)} collective-permute-done((bf16[3,64,256]{2,1,0:T(8,128)(2,1)S(1)}, bf16[3,64,256]{2,1,0:T(8,128)(2,1)S(1)}, u32[]{:S(2)}, u32[]{:S(2)}) %collective-permute-start.7) | collective-permute-done | bytes 98336 | tf_op jit(solution)/shard_map/ppermute | solution.py:475
  22.0 2.0 %shard_map.94 = (f32[256,256]{1,0:T(8,128)S(1)}, bf16[256,256]{1,0:T(8,128)(2,1)S(1)}) custom-call(bf16[80,256]{1,0:T(8,128)(2,1)S(1)} %shard_map.88.own.payload_ref, bf16[80,256]{1,0:T(8,128)(2,1)S(1)} %collective-permute-done.2.own_other, bf16[3,80,256]{2,1,0:T(8,128)(2,1)S(1)} %get-tuple-element.16.mine, ...), custom_call_target="tpu_custom_call" | custom-call | tf_op jit(solution)/shard_map/pallas_call | solution.py:348
  24.0 1.1 %collective-permute-start.8 = (bf16[256,256]{1,0:T(8,128)(2,1)S(1)}, bf16[256,256]{1,0:T(8,128)(2,1)S(1)}, u32[]{:S(2)}, u32[]{:S(2)}) collective-permute-start(bf16[256,256]{1,0:T(8,128)(2,1)S(1)} %get-tuple-element.23), channel_id=1, source_target_pairs={{0,8},{4,12},{8,0},{12,4},{1,9},{5,13},{9,1},{13,5},{2,10},{6,14},... | collective-permute-start | bytes 393224 | tf_op jit(solution)/shard_map/ppermute | solution.py:475
  25.1 7.9 %shard_map.92 = f32[1024,4096]{1,0:T(8,128)} custom-call(bf16[3,80,256]{2,1,0:T(8,128)(2,1)S(1)} %get-tuple-element.16.mine, bf16[3,64,256]{2,1,0:T(8,128)(2,1)S(1)} %collective-permute-done.7.other, f32[1024,4096]{1,0:T(8,128)S(1)} %shard_map.89._.own_sum), custom_call_target="tpu_custom_call" | custom-call | tf_op jit(solution)/shard_map/pallas_call | solution.py:439
  33.0 0.0 collective-permute-done.8.refs_1_
  33.0 0.8 %shard_map.95 = bf16[256,256]{1,0:T(8,128)(2,1)} custom-call(bf16[80,256]{1,0:T(8,128)(2,1)S(1)} %shard_map.88.own.payload_ref, f32[256,256]{1,0:T(8,128)S(1)} %get-tuple-element.22.refs_0_, bf16[256,256]{1,0:T(8,128)(2,1)S(1)} %collective-permute-done.8.refs_1_), custom_call_target="tpu_custom_call" | custom-call | tf_op jit(solution)/shard_map/pallas_call | solution.py:467
  (3 shorter events, 0.0 us)
Async XLA Ops:
  0.6 18.5 %copy-start = (bf16[1024,256]{1,0:T(8,128)(2,1)S(1)}, bf16[1024,256]{1,0:T(8,128)(2,1)}, u32[]{:S(2)}) copy-start(bf16[1024,256]{1,0:T(8,128)(2,1)} %query.1) | copy-start | bytes 1572868
  0.6 18.5 %collective-permute-start.3 = (bf16[1024,256]{1,0:T(8,128)(2,1)}, bf16[1024,256]{1,0:T(8,128)(2,1)S(1)}, u32[]{:S(2)}, u32[]{:S(2)}) collective-permute-start(bf16[1024,256]{1,0:T(8,128)(2,1)} %query.1), channel_id=1, source_target_pairs={{0,4},{4,0},{8,12},{12,8},{1,5},{5,1},{9,13},{13,9},{2,6},{6,2},{1... | collective-permute-start | bytes 1572872 | tf_op jit(solution)/shard_map/ppermute | solution.py:475
  6.5 1.3 %collective-permute-start = (f32[64,256]{1,0:T(8,128)S(1)}, f32[64,256]{1,0:T(8,128)S(1)}, u32[]{:S(2)}, u32[]{:S(2)}) collective-permute-start(f32[64,256]{1,0:T(8,128)S(1)} %get-tuple-element.14), channel_id=1, source_target_pairs={{0,1},{1,0},{2,3},{3,2},{4,5},{5,4},{6,7},{7,6},{8,9},{9,8},{10,11... | collective-permute-start | bytes 196616 | tf_op jit(solution)/shard_map/ppermute | solution.py:475
  7.8 4.3 %collective-permute-start.1 = (f32[64,256]{1,0:T(8,128)S(1)}, f32[64,256]{1,0:T(8,128)S(1)}, u32[]{:S(2)}, u32[]{:S(2)}) collective-permute-start(f32[64,256]{1,0:T(8,128)S(1)} %shard_map.87.one_ref), channel_id=1, source_target_pairs={{0,2},{1,3},{2,0},{3,1},{4,6},{5,7},{6,4},{7,5},{8,10},{9,11},{10,... | collective-permute-start | bytes 196616 | tf_op jit(solution)/shard_map/ppermute | solution.py:475
  12.2 4.5 %collective-permute-start.2 = (bf16[80,256]{1,0:T(8,128)(2,1)S(1)}, bf16[80,256]{1,0:T(8,128)(2,1)S(1)}, u32[]{:S(2)}, u32[]{:S(2)}) collective-permute-start(bf16[80,256]{1,0:T(8,128)(2,1)S(1)} %shard_map.88.own.payload_ref), channel_id=1, source_target_pairs={{0,1},{1,0},{2,3},{3,2},{4,5},{5,4},{6,7},{7,6},{8,9},{9,8},{10,11... | collective-permute-start | bytes 122888 | tf_op jit(solution)/shard_map/ppermute | solution.py:475
  12.2 7.4 %collective-permute-start.4 = (bf16[80,256]{1,0:T(8,128)(2,1)S(1)}, bf16[80,256]{1,0:T(8,128)(2,1)S(1)}, u32[]{:S(2)}, u32[]{:S(2)}) collective-permute-start(bf16[80,256]{1,0:T(8,128)(2,1)S(1)} %shard_map.88.own.payload_ref), channel_id=1, source_target_pairs={{0,12},{4,8},{8,4},{12,0},{1,13},{5,9},{9,5},{13,1},{2,14},{6,10},... | collective-permute-start | bytes 122888 | tf_op jit(solution)/shard_map/ppermute | solution.py:475
  14.8 5.9 %collective-permute-start.5 = (bf16[80,256]{1,0:T(8,128)(2,1)S(1)}, bf16[80,256]{1,0:T(8,128)(2,1)S(1)}, u32[]{:S(2)}, u32[]{:S(2)}) collective-permute-start(bf16[80,256]{1,0:T(8,128)(2,1)S(1)} %shard_map.88.own.payload_ref), channel_id=1, source_target_pairs={{0,8},{4,12},{8,0},{12,4},{1,9},{5,13},{9,1},{13,5},{2,10},{6,14},... | collective-permute-start | bytes 122888 | tf_op jit(solution)/shard_map/ppermute | solution.py:475
  15.0 5.7 %collective-permute-start.6 = (bf16[80,256]{1,0:T(8,128)(2,1)S(1)}, bf16[80,256]{1,0:T(8,128)(2,1)S(1)}, u32[]{:S(2)}, u32[]{:S(2)}) collective-permute-start(bf16[80,256]{1,0:T(8,128)(2,1)S(1)} %shard_map.88.own.payload_ref), channel_id=1, source_target_pairs={{0,4},{4,0},{8,12},{12,8},{1,5},{5,1},{9,13},{13,9},{2,6},{6,2},{1... | collective-permute-start | bytes 122888 | tf_op jit(solution)/shard_map/ppermute | solution.py:475
  20.7 1.4 %collective-permute-start.7 = (bf16[3,64,256]{2,1,0:T(8,128)(2,1)S(1)}, bf16[3,64,256]{2,1,0:T(8,128)(2,1)S(1)}, u32[]{:S(2)}, u32[]{:S(2)}) collective-permute-start(bf16[3,64,256]{2,1,0:T(8,128)(2,1)S(1)} %get-tuple-element.17), channel_id=1, source_target_pairs={{0,1},{1,0},{2,3},{3,2},{4,5},{5,4},{6,7},{7,6},{8,9},{9,8},{10,11... | collective-permute-start | bytes 294920 | tf_op jit(solution)/shard_map/ppermute | solution.py:475
  24.0 9.0 %collective-permute-start.8 = (bf16[256,256]{1,0:T(8,128)(2,1)S(1)}, bf16[256,256]{1,0:T(8,128)(2,1)S(1)}, u32[]{:S(2)}, u32[]{:S(2)}) collective-permute-start(bf16[256,256]{1,0:T(8,128)(2,1)S(1)} %get-tuple-element.23), channel_id=1, source_target_pairs={{0,8},{4,12},{8,0},{12,4},{1,9},{5,13},{9,1},{13,5},{2,10},{6,14},... | collective-permute-start | bytes 393224 | tf_op jit(solution)/shard_map/ppermute | solution.py:475

commit v26 on v25

--- a/solution.py
+++ b/solution.py
@@ -110,10 +110,8 @@
 
 
 def project_kernel(act, grad, pin, pout, keep_ref, send_ref, act_v, grad_v, pin_v, pout_v, sems):
-    unit = grad.shape[1] // 7
-    spans = [pl.ds(0, unit), pl.ds(unit, 2 * unit), pl.ds(3 * unit, 4 * unit)]
-    if grad.shape[1] % 7 or unit % 128:
-        spans = [pl.ds(0, grad.shape[1])]
+    chunk = grad.shape[1] // 2
+    spans = [pl.ds(0, chunk), pl.ds(chunk, chunk)]
     pairs = [(pin, pin_v), (act, act_v), (pout, pout_v)]
     pairs += [(grad.at[:, span], grad_v.at[:, span]) for span in spans]
     copies = [pltpu.make_async_copy(s, d, sems.at[n]) for n, (s, d) in enumerate(pairs)]
@@ -148,7 +146,7 @@
             pltpu.VMEM((tok, f_here), jnp.bfloat16),
             pltpu.VMEM((rank, d_here), jnp.bfloat16),
             pltpu.VMEM((rank, f_here), jnp.bfloat16),
-            pltpu.SemaphoreType.DMA((6,)),
+            pltpu.SemaphoreType.DMA((5,)),
         ],
         compiler_params=params(53.75),
     )(activations, out_grads, proj_in_t, proj_out_t)

time: 33.9 us -> 33.9 us (level)
  no operation moved by 1% of the time
where the time goes in v26:
time: 33.9 us; the launch traced here: 33.7 us
  Pallas kernels  16.8 us (50%)
  starting transfers between devices  10.4 us (31%)
  waiting for transfers between devices  4.93 us (15%)
  between operations  0.75 us (2%)
  other arithmetic  0.74 us (2%)
    ppermute x9, starting transfers between devices, swapped(): lax.ppermute(array, axis, [(i, i ^ distance) for i in range(lax.axis_size...  10.4 us
    pallas_call x1, Pallas kernels, hessian_rows(): pl.pallas_call(functools.partial(hessian_kernel, row_count, col_count), o...  7.88 us
    ppermute x9, waiting for transfers between devices, swapped(): lax.ppermute(array, axis, [(i, i ^ distance) for i in range(lax.axis_size...  4.93 us
    pallas_call x1, Pallas kernels, project(): pl.pallas_call(project_kernel, in_specs=[pl.BlockSpec(memory_space=pl.ANY...  2.66 us
    pallas_call x1, Pallas kernels, own_tokens_sum(): pl.pallas_call(functools.partial(own_kernel, row_count, col_count), out_s...  2.4 us
    pallas_call x1, Pallas kernels, score_shares(): pl.pallas_call(functools.partial(share_kernel, row_count), out_shape=[jax...  1.96 us
    pallas_call x1, Pallas kernels, finish_scores(): pl.pallas_call(finish_kernel, out_shape=jax.ShapeDtypeStruct((tok, count)...  0.77 us
    convert_element_type x1, other arithmetic, few_tokens(): jnp.where(live, credit[:, None], 0).astype(jnp.float32).reshape(1, -1)  0.74 us
  transfers between devices with their start and end apart: 9, of which 4 were waited for; matrix products, arithmetic and copies ran while one was open for 2% of the time, Pallas kernels for 42%

profile of v26, /device:TPU:0, one launch (start us, length us, event | category | flops | bytes accessed | tf_op | source)
XLA Modules:
  0.0 33.7 jit_solution(11002731177612131550)
XLA Ops:
  0.6 0.0 copy-start
  0.6 3.1 %collective-permute-start.3 = (bf16[1024,256]{1,0:T(8,128)(2,1)}, bf16[1024,256]{1,0:T(8,128)(2,1)S(1)}, u32[]{:S(2)}, u32[]{:S(2)}) collective-permute-start(bf16[1024,256]{1,0:T(8,128)(2,1)} %query.1), channel_id=1, source_target_pairs={{0,4},{4,0},{8,12},{12,8},{1,5},{5,1},{9,13},{13,9},{2,6},{6,2},{1... | collective-permute-start | bytes 1572872 | tf_op jit(solution)/shard_map/ppermute | solution.py:473
  3.7 2.7 %shard_map.86 = (f32[64,256]{1,0:T(8,128)S(1)}, f32[64,256]{1,0:T(8,128)S(1)}) custom-call(bf16[256,1024]{1,0:T(8,128)(2,1)} %act.1, bf16[256,3584]{1,0:T(8,128)(2,1)} %grad.1, bf16[64,1024]{1,0:T(8,128)(2,1)} %bitcast.5, bf16[64,3584]{1,0:T(8,128)(2,1)} %bitcast.4), custom_call_target="tpu_custom_call" | custom-call | tf_op jit(solution)/shard_map/pallas_call | solution.py:140
  6.4 0.1 collective-permute-start
  6.5 1.2 %collective-permute-done.other_ref = f32[64,256]{1,0:T(8,128)S(1)} collective-permute-done((f32[64,256]{1,0:T(8,128)S(1)}, f32[64,256]{1,0:T(8,128)S(1)}, u32[]{:S(2)}, u32[]{:S(2)}) %collective-permute-start) | collective-permute-done | bytes 65568 | tf_op jit(solution)/shard_map/ppermute | solution.py:473
  7.7 1.6 %collective-permute-start.1 = (f32[64,256]{1,0:T(8,128)S(1)}, f32[64,256]{1,0:T(8,128)S(1)}, u32[]{:S(2)}, u32[]{:S(2)}) collective-permute-start(f32[64,256]{1,0:T(8,128)S(1)} %shard_map.87.one_ref), channel_id=1, source_target_pairs={{0,2},{1,3},{2,0},{3,1},{4,6},{5,7},{6,4},{7,5},{8,10},{9,11},{10,... | collective-permute-start | bytes 196616 | tf_op jit(solution)/shard_map/ppermute | solution.py:473
  9.3 0.7 %fusion = f32[2,128]{1,0:T(2,128)S(1)} fusion(s32[2]{0:T(128)} %param.13, s32[2]{0:T(128)} %param.12), kind=kLoop, calls=%fused_computation.1 | loop fusion | flops 768 | bytes 1040 | tf_op jit(solution)/shard_map/convert_element_type | solution.py:483
  10.0 2.0 %collective-permute-done.1.other_ref = f32[64,256]{1,0:T(8,128)S(1)} collective-permute-done((f32[64,256]{1,0:T(8,128)S(1)}, f32[64,256]{1,0:T(8,128)S(1)}, u32[]{:S(2)}, u32[]{:S(2)}) %collective-permute-start.1) | collective-permute-done | bytes 65568 | tf_op jit(solution)/shard_map/ppermute | solution.py:473
  12.1 0.1 collective-permute-start.2
  12.2 2.5 %collective-permute-start.4 = (bf16[80,256]{1,0:T(8,128)(2,1)S(1)}, bf16[80,256]{1,0:T(8,128)(2,1)S(1)}, u32[]{:S(2)}, u32[]{:S(2)}) collective-permute-start(bf16[80,256]{1,0:T(8,128)(2,1)S(1)} %shard_map.88.own.payload_ref), channel_id=1, source_target_pairs={{0,12},{4,8},{8,4},{12,0},{1,13},{5,9},{9,5},{13,1},{2,14},{6,10},... | collective-permute-start | bytes 122888 | tf_op jit(solution)/shard_map/ppermute | solution.py:473
  14.7 0.2 collective-permute-start.5
  14.9 1.7 %collective-permute-start.6 = (bf16[80,256]{1,0:T(8,128)(2,1)S(1)}, bf16[80,256]{1,0:T(8,128)(2,1)S(1)}, u32[]{:S(2)}, u32[]{:S(2)}) collective-permute-start(bf16[80,256]{1,0:T(8,128)(2,1)S(1)} %shard_map.88.own.payload_ref), channel_id=1, source_target_pairs={{0,4},{4,0},{8,12},{12,8},{1,5},{5,1},{9,13},{13,9},{2,6},{6,2},{1... | collective-permute-start | bytes 122888 | tf_op jit(solution)/shard_map/ppermute | solution.py:473
  16.6 0.0 collective-permute-done.2.own_other
  16.6 2.4 %shard_map.89._.own_sum = f32[1024,4096]{1,0:T(8,128)S(1)} custom-call(bf16[80,256]{1,0:T(8,128)(2,1)S(1)} %shard_map.88.own.payload_ref, bf16[80,256]{1,0:T(8,128)(2,1)S(1)} %collective-permute-done.2.own_other), custom_call_target="tpu_custom_call" | custom-call | tf_op jit(solution)/shard_map/pallas_call | solution.py:387
  19.0 0.0 collective-permute-done.3.near_query
  19.0 0.0 copy-done
  19.0 0.5 %shard_map.90 = (bf16[256,2048]{1,0:T(8,128)(2,1)S(1)}, f32[256,256]{1,0:T(8,128)S(1)}) custom-call(bf16[1024,256]{1,0:T(8,128)(2,1)S(1)} %copy-done, bf16[1024,256]{1,0:T(8,128)(2,1)S(1)} %collective-permute-done.3.near_query, bf16[80,256]{1,0:T(8,128)(2,1)S(1)} %shard_map.88.own.payload_ref, bf16[80,256]{1,0:T(8,128)(2,1)S(1)} %collective-permute-done.2.own_other), custom_call_target="tpu_custom_call" | custom-call | tf_op jit(solution)/shard_map/pallas_call | solution.py:262
  19.6 0.0 collective-permute-done.4.refs_0_
  19.6 1.0 %collective-permute-done.5.refs_1_ = bf16[80,256]{1,0:T(8,128)(2,1)S(1)} collective-permute-done((bf16[80,256]{1,0:T(8,128)(2,1)S(1)}, bf16[80,256]{1,0:T(8,128)(2,1)S(1)}, u32[]{:S(2)}, u32[]{:S(2)}) %collective-permute-start.5) | collective-permute-done | bytes 40992 | tf_op jit(solution)/shard_map/ppermute | solution.py:473
  20.6 0.0 collective-permute-done.6.refs_2_
  20.6 0.1 collective-permute-start.7
  20.7 0.6 %shard_map.93 = (f32[2,1024,256]{2,1,0:T(8,128)S(1)}, f32[8,1024]{1,0:T(8,128)S(1)}, f32[8,128]{1,0:T(8,128)S(1)}) custom-call(bf16[80,256]{1,0:T(8,128)(2,1)S(1)} %shard_map.88.own.payload_ref, bf16[3,80,256]{2,1,0:T(8,128)(2,1)S(1)} %get-tuple-element.16.mine), custom_call_target="tpu_custom_call" | custom-call | tf_op jit(solution)/shard_map/pallas_call | solution.py:300
  21.3 0.6 %collective-permute-done.7.other = bf16[3,64,256]{2,1,0:T(8,128)(2,1)S(1)} collective-permute-done((bf16[3,64,256]{2,1,0:T(8,128)(2,1)S(1)}, bf16[3,64,256]{2,1,0:T(8,128)(2,1)S(1)}, u32[]{:S(2)}, u32[]{:S(2)}) %collective-permute-start.7) | collective-permute-done | bytes 98336 | tf_op jit(solution)/shard_map/ppermute | solution.py:473
  21.9 2.0 %shard_map.94 = (f32[256,256]{1,0:T(8,128)S(1)}, bf16[256,256]{1,0:T(8,128)(2,1)S(1)}) custom-call(bf16[80,256]{1,0:T(8,128)(2,1)S(1)} %shard_map.88.own.payload_ref, bf16[80,256]{1,0:T(8,128)(2,1)S(1)} %collective-permute-done.2.own_other, bf16[3,80,256]{2,1,0:T(8,128)(2,1)S(1)} %get-tuple-element.16.mine, ...), custom_call_target="tpu_custom_call" | custom-call | tf_op jit(solution)/shard_map/pallas_call | solution.py:346
  23.9 1.1 %collective-permute-start.8 = (bf16[256,256]{1,0:T(8,128)(2,1)S(1)}, bf16[256,256]{1,0:T(8,128)(2,1)S(1)}, u32[]{:S(2)}, u32[]{:S(2)}) collective-permute-start(bf16[256,256]{1,0:T(8,128)(2,1)S(1)} %get-tuple-element.23), channel_id=1, source_target_pairs={{0,8},{4,12},{8,0},{12,4},{1,9},{5,13},{9,1},{13,5},{2,10},{6,14},... | collective-permute-start | bytes 393224 | tf_op jit(solution)/shard_map/ppermute | solution.py:473
  25.0 7.9 %shard_map.92 = f32[1024,4096]{1,0:T(8,128)} custom-call(bf16[3,80,256]{2,1,0:T(8,128)(2,1)S(1)} %get-tuple-element.16.mine, bf16[3,64,256]{2,1,0:T(8,128)(2,1)S(1)} %collective-permute-done.7.other, f32[1024,4096]{1,0:T(8,128)S(1)} %shard_map.89._.own_sum), custom_call_target="tpu_custom_call" | custom-call | tf_op jit(solution)/shard_map/pallas_call | solution.py:437
  32.9 0.0 collective-permute-done.8.refs_1_
  32.9 0.8 %shard_map.95 = bf16[256,256]{1,0:T(8,128)(2,1)} custom-call(bf16[80,256]{1,0:T(8,128)(2,1)S(1)} %shard_map.88.own.payload_ref, f32[256,256]{1,0:T(8,128)S(1)} %get-tuple-element.22.refs_0_, bf16[256,256]{1,0:T(8,128)(2,1)S(1)} %collective-permute-done.8.refs_1_), custom_call_target="tpu_custom_call" | custom-call | tf_op jit(solution)/shard_map/pallas_call | solution.py:465
  (3 shorter events, 0.0 us)
Async XLA Ops:
  0.6 18.4 %copy-start = (bf16[1024,256]{1,0:T(8,128)(2,1)S(1)}, bf16[1024,256]{1,0:T(8,128)(2,1)}, u32[]{:S(2)}) copy-start(bf16[1024,256]{1,0:T(8,128)(2,1)} %query.1) | copy-start | bytes 1572868
  0.6 18.4 %collective-permute-start.3 = (bf16[1024,256]{1,0:T(8,128)(2,1)}, bf16[1024,256]{1,0:T(8,128)(2,1)S(1)}, u32[]{:S(2)}, u32[]{:S(2)}) collective-permute-start(bf16[1024,256]{1,0:T(8,128)(2,1)} %query.1), channel_id=1, source_target_pairs={{0,4},{4,0},{8,12},{12,8},{1,5},{5,1},{9,13},{13,9},{2,6},{6,2},{1... | collective-permute-start | bytes 1572872 | tf_op jit(solution)/shard_map/ppermute | solution.py:473
  6.4 1.3 %collective-permute-start = (f32[64,256]{1,0:T(8,128)S(1)}, f32[64,256]{1,0:T(8,128)S(1)}, u32[]{:S(2)}, u32[]{:S(2)}) collective-permute-start(f32[64,256]{1,0:T(8,128)S(1)} %get-tuple-element.14), channel_id=1, source_target_pairs={{0,1},{1,0},{2,3},{3,2},{4,5},{5,4},{6,7},{7,6},{8,9},{9,8},{10,11... | collective-permute-start | bytes 196616 | tf_op jit(solution)/shard_map/ppermute | solution.py:473
  7.7 4.3 %collective-permute-start.1 = (f32[64,256]{1,0:T(8,128)S(1)}, f32[64,256]{1,0:T(8,128)S(1)}, u32[]{:S(2)}, u32[]{:S(2)}) collective-permute-start(f32[64,256]{1,0:T(8,128)S(1)} %shard_map.87.one_ref), channel_id=1, source_target_pairs={{0,2},{1,3},{2,0},{3,1},{4,6},{5,7},{6,4},{7,5},{8,10},{9,11},{10,... | collective-permute-start | bytes 196616 | tf_op jit(solution)/shard_map/ppermute | solution.py:473
  12.1 4.5 %collective-permute-start.2 = (bf16[80,256]{1,0:T(8,128)(2,1)S(1)}, bf16[80,256]{1,0:T(8,128)(2,1)S(1)}, u32[]{:S(2)}, u32[]{:S(2)}) collective-permute-start(bf16[80,256]{1,0:T(8,128)(2,1)S(1)} %shard_map.88.own.payload_ref), channel_id=1, source_target_pairs={{0,1},{1,0},{2,3},{3,2},{4,5},{5,4},{6,7},{7,6},{8,9},{9,8},{10,11... | collective-permute-start | bytes 122888 | tf_op jit(solution)/shard_map/ppermute | solution.py:473
  12.2 7.4 %collective-permute-start.4 = (bf16[80,256]{1,0:T(8,128)(2,1)S(1)}, bf16[80,256]{1,0:T(8,128)(2,1)S(1)}, u32[]{:S(2)}, u32[]{:S(2)}) collective-permute-start(bf16[80,256]{1,0:T(8,128)(2,1)S(1)} %shard_map.88.own.payload_ref), channel_id=1, source_target_pairs={{0,12},{4,8},{8,4},{12,0},{1,13},{5,9},{9,5},{13,1},{2,14},{6,10},... | collective-permute-start | bytes 122888 | tf_op jit(solution)/shard_map/ppermute | solution.py:473
  14.7 5.9 %collective-permute-start.5 = (bf16[80,256]{1,0:T(8,128)(2,1)S(1)}, bf16[80,256]{1,0:T(8,128)(2,1)S(1)}, u32[]{:S(2)}, u32[]{:S(2)}) collective-permute-start(bf16[80,256]{1,0:T(8,128)(2,1)S(1)} %shard_map.88.own.payload_ref), channel_id=1, source_target_pairs={{0,8},{4,12},{8,0},{12,4},{1,9},{5,13},{9,1},{13,5},{2,10},{6,14},... | collective-permute-start | bytes 122888 | tf_op jit(solution)/shard_map/ppermute | solution.py:473
  14.9 5.7 %collective-permute-start.6 = (bf16[80,256]{1,0:T(8,128)(2,1)S(1)}, bf16[80,256]{1,0:T(8,128)(2,1)S(1)}, u32[]{:S(2)}, u32[]{:S(2)}) collective-permute-start(bf16[80,256]{1,0:T(8,128)(2,1)S(1)} %shard_map.88.own.payload_ref), channel_id=1, source_target_pairs={{0,4},{4,0},{8,12},{12,8},{1,5},{5,1},{9,13},{13,9},{2,6},{6,2},{1... | collective-permute-start | bytes 122888 | tf_op jit(solution)/shard_map/ppermute | solution.py:473
  20.6 1.4 %collective-permute-start.7 = (bf16[3,64,256]{2,1,0:T(8,128)(2,1)S(1)}, bf16[3,64,256]{2,1,0:T(8,128)(2,1)S(1)}, u32[]{:S(2)}, u32[]{:S(2)}) collective-permute-start(bf16[3,64,256]{2,1,0:T(8,128)(2,1)S(1)} %get-tuple-element.17), channel_id=1, source_target_pairs={{0,1},{1,0},{2,3},{3,2},{4,5},{5,4},{6,7},{7,6},{8,9},{9,8},{10,11... | collective-permute-start | bytes 294920 | tf_op jit(solution)/shard_map/ppermute | solution.py:473
  23.9 9.0 %collective-permute-start.8 = (bf16[256,256]{1,0:T(8,128)(2,1)S(1)}, bf16[256,256]{1,0:T(8,128)(2,1)S(1)}, u32[]{:S(2)}, u32[]{:S(2)}) collective-permute-start(bf16[256,256]{1,0:T(8,128)(2,1)S(1)} %get-tuple-element.23), channel_id=1, source_target_pairs={{0,8},{4,12},{8,0},{12,4},{1,9},{5,13},{9,1},{13,5},{2,10},{6,14},... | collective-permute-start | bytes 393224 | tf_op jit(solution)/shard_map/ppermute | solution.py:473
